TPU v7x, 32 devices: a whole 2x2x4 slice. The times are simulated.
32 devices in a mesh: row: 8 (over y, x, core), col: 4 (over z).
Axes of the slice: x: 2, y: 2, z: 4, core: 2. Of those that a mesh axis runs over, the one named last changes fastest.
Arguments:
- p_cols: int32 [128, 16], P('row', 'col'), may hold values from -1 to 31, as said below
- p_data: float32 [8192, 1024], P('row', 'col'), may hold values from -1.5 to 1.5
Outputs:
- product: float32 [8192, 8192], P('row', 'col')
Inputs may be any that keep to these rules, and one draw needn't show every extreme that they name: `p_cols`: in each column tile, each block row has 1 to 4 used slots, the used ones first, with distinct columns; the first block row of each device's rows has all 4 used.
All inputs are finite; a program needn't handle non-finite values.
Results may differ from a plain program's by a relative error of at most 0.0003.
Values sent between devices are 32-bit elements; how exact they have to be, the bound alone decides.
No kernel may reach another device: no remote copies, remote signals or barrier semaphores. Data moves between devices by JAX's collectives and lax.ppermute only.
A program may use at most 192 MiB of HBM per device.

v0:
```python
import functools

import jax
import jax.numpy as jnp
import numpy as np
from jax import lax
from jax.experimental import pallas as pl
from jax.experimental.pallas import tpu as pltpu
from jax.sharding import PartitionSpec as P

BS = 64
STEPS = 4
UNROLL = 4
EXTRA = 8
PARTS = 8


def left_offsets(row, ratio, n_col):
    seen = []
    for step in range(STEPS):
        offset = (row + step) // ratio % n_col
        if offset not in seen:
            seen.append(offset)
    return seen


def shift(rows, step, count):
    return [((r, c), (r, (c + step) % count)) for r in rows for c in range(count)]


def left_plan(n_row, n_col, ratio):
    offsets = [left_offsets(row, ratio, n_col) for row in range(n_row)]
    if (n_row, n_col, ratio) != (8, 4, 2):
        perms = []
        for slot in range(max(len(o) for o in offsets)):
            pairs = [
                ((row, (col + offsets[row][slot]) % n_col), (row, col))
                for row in range(n_row)
                for col in range(n_col)
                if slot < len(offsets[row]) and offsets[row][slot] != 0
            ]
            perms.append((0, pairs))
        return perms
    whole = [r for r in range(8) if {1, 2, 3} <= set(offsets[r])]
    once, twice = {-1: [], 1: []}, {-1: [], 1: []}
    for r in range(8):
        for offset, step in ((1, -1), (3, 1)):
            if offset in offsets[r] and r not in whole:
                once[step].append(r)
                if 2 in offsets[r]:
                    twice[step].append(r)
    down = shift([r for r in once[-1] if r != 0], -1, 4) + [((3, c), (3, c - 1)) for c in (1, 2, 3)] + [((3, 0), (0, 0))]
    up = shift(once[1], 1, 4) + shift([0], -1, 4) + [((3, c), (3, c + 1)) for c in (0, 1, 2)] + [((3, 3), (1, 3))]
    again_down = shift(twice[-1], -1, 4) + [((3, 1), (3, 0)), ((3, 2), (3, 1)), ((0, 0), (3, 3))]
    again_up = shift(twice[1], 1, 4) + [((3, 1), (3, 2)), ((3, 2), (3, 3)), ((1, 3), (3, 0))]
    return [(0, down), (0, up), (1, again_down), (2, again_up)]


def right_plan(n_row, n_col, ratio):
    everyone = [(row, col) for row in range(n_row) for col in range(n_col)]
    if (n_row, n_col, ratio) != (8, 4, 2):
        return [
            (0, [(((r + ratio * c + step) % n_row, c), (r, c)) for r, c in everyone if (ratio * c + step) % n_row])
            for step in range(STEPS)
        ]
    first = [(((r + 2 * c) % 8, c), (r, c)) for r, c in everyone if c != 0]
    first += [((r + 1, 0), (r, 0)) for r in range(0, 8, 2)]
    second = [(((r + 2 * c + 2) % 8, c), (r, c)) for r, c in everyone if c != 3]
    second += [((r ^ 1, 3), (r, 3)) for r in range(8)]
    last = [(((r - 1 + 2 * c + 4) % 8, c), (r, c)) for r, c in everyone if r % 2 == 1]
    first_swap = [((r + 1, c), (r, c)) for r, c in everyone if r % 2 == 0 and c != 0]
    second_swap = [((r ^ 1, c), (r, c)) for r, c in everyone if c != 3]
    return [(0, first), (0, second), (0, last), (1, first_swap), (2, second_swap)]


def carry_out(perms, n_row, n_col):
    held = [{(r, c): (r, c) for r in range(n_row) for c in range(n_col)}]
    for source, pairs in perms:
        held.append({dst: held[source][src] for src, dst in pairs})
    return held


def device_table(left_perms, right_perms, n_row, n_col, ratio):
    left_held = carry_out(left_perms, n_row, n_col)
    right_held = carry_out(right_perms, n_row, n_col)
    slots = (ratio - 1 + STEPS - 1) // ratio + 1
    table = np.full((n_row, n_col, 2 * slots + STEPS), -1, np.int32)

    def find(held, device, tile):
        return [i for i, h in enumerate(held) if h.get(device) == tile][0]

    for r in range(n_row):
        for c in range(n_col):
            for slot, offset in enumerate(left_offsets(r, ratio, n_col)):
                tile_col = (c + offset) % n_col
                table[r, c, slot] = find(left_held, (r, c), (r, tile_col))
                table[r, c, slots + STEPS + slot] = (tile_col * ratio - r - ratio * c) % n_row
            for step in range(STEPS):
                table[r, c, slots + step] = find(right_held, (r, c), ((r + ratio * c + step) % n_row, c))
    return table, slots


def fetch(choice, bufs, target, sem):
    for number, buf in enumerate(bufs):
        @pl.when(choice == number)
        def _():
            pltpu.make_async_copy(buf, target, sem).start()


def join_kernel(cols_ref, data_ref, out_ref, sem):
    rows = data_ref.shape[0]
    data_copy = pltpu.make_async_copy(data_ref, out_ref.at[pl.ds(0, rows)], sem.at[0])
    cols_copy = pltpu.make_async_copy(cols_ref, out_ref.at[pl.ds(rows, EXTRA)], sem.at[1])
    data_copy.start()
    cols_copy.start()
    data_copy.wait()
    cols_copy.wait()


def product_kernel(slots, n_row, ratio, rb, w, n_right, info_ref, *refs):
    out_ref, left, right, acc, value, cols, coded, scalars, codes, lsem, rsem, osem, csem = refs[-13:]
    right_bufs, left_bufs = refs[:n_right], refs[:1] + refs[n_right:-13]
    rows, width = left.shape[1] - EXTRA, left.shape[2]
    names = pl.ds(rows, EXTRA)
    for slot in range(slots):
        fetch(info_ref[slot], [buf.at[names] for buf in left_bufs], cols.at[slot], csem.at[slot])
    for step in range(STEPS):
        choice = info_ref[slots + step]
        fetch(choice, [buf.at[names] for buf in right_bufs], cols.at[slots + step], csem.at[slots + step])
    for step in range(STEPS):
        fetch(info_ref[slots + step], right_bufs, right.at[step], rsem.at[step])
    for slot in range(slots):
        fetch(info_ref[slot], left_bufs, left.at[slot], lsem.at[slot])

    def clear(first, last):
        @pl.loop(first, last)
        def _(r):
            acc[pl.ds(pl.multiple_of(r * BS, BS), BS), :] = jnp.zeros((BS, acc.shape[1]), jnp.float32)

    clear(0, rb // 4)
    lanes = scalars.shape[1]
    row = lax.broadcasted_iota(jnp.int32, (w, lanes), 1)
    tile_slot = lax.broadcasted_iota(jnp.int32, (w, lanes), 0)
    for slot in range(slots):
        used = info_ref[slot] >= 0

        @pl.when(used)
        def _():
            pltpu.make_async_copy(left_bufs[0].at[names], cols.at[slot], csem.at[slot]).wait()

        inner = cols[slot, 0:w, 0:lanes].astype(jnp.int32)
        valid = (inner >= 0) & (row < rb)
        step = jnp.full(inner.shape, info_ref[slots + STEPS + slot], jnp.int32)
        for _ in range(ratio - 1):
            beyond = inner >= rb
            step = jnp.where(beyond, step + 1, step)
            inner = jnp.where(beyond, inner - rb, inner)
        step = jnp.where(step >= n_row, step - n_row, step)
        code = inner | tile_slot << 8 | slot << 12 | row << 16 | step << 24
        valid = valid & (step < STEPS)
        coded[slot * w : (slot + 1) * w, :] = jnp.where(valid, jnp.where(used, code, -1), -1)
    for step in range(STEPS):
        pltpu.make_async_copy(right_bufs[0].at[names], cols.at[slots + step], csem.at[slots + step]).wait()
        col = cols[slots + step, 0:w, 0:lanes].astype(jnp.int32)
        code = (col >> 1) * 2 * BS | (col & 1) << 16
        coded[(slots + step) * w : (slots + step + 1) * w, :] = jnp.where(col < 0, 2 << 16, code)
    coded[(slots + STEPS) * w : (slots + STEPS + 1) * w, :] = jnp.full((w, lanes), 2 << 16, jnp.int32)
    to_scalars = pltpu.make_async_copy(coded, scalars, csem.at[slots + STEPS])
    to_scalars.start()
    clear(rb // 4, rb)
    to_scalars.wait()

    part_rows = rb // PARTS
    for u in range(UNROLL):
        codes[u] = STEPS << 24
    bounds = [jnp.int32(UNROLL)]
    for part in range(PARTS):
        def listed(i, place):
            for slot in range(slots):
                for k in range(w):
                    code = scalars[slot * w + k, part * part_rows + i]
                    codes[place] = code
                    place = place + (code >= 0).astype(jnp.int32)
            return place

        bounds.append(lax.fori_loop(0, part_rows, listed, bounds[-1]))
    for u in range(2 * UNROLL):
        codes[bounds[-1] + u] = STEPS << 24

    for step in range(STEPS):
        pltpu.make_async_copy(right_bufs[0], right.at[step], rsem.at[step]).wait()
    for slot in range(slots):
        @pl.when(info_ref[slot] >= 0)
        def _():
            pltpu.make_async_copy(left_bufs[0], left.at[slot], lsem.at[slot]).wait()

    low = lax.broadcasted_iota(jnp.int32, (BS, 2 * BS), 1) < BS
    half = lax.broadcasted_iota(jnp.int32, (BS, 2 * BS), 1) // BS

    def block_at(index):
        return pl.ds(pl.multiple_of(index * BS, BS), BS)

    def product(code):
        slot = (code >> 8) & 15
        x = left[(code >> 12) & 15, block_at((code >> 16) & 255), pl.ds(pl.multiple_of((slot >> 1) * 2 * BS, 2 * BS), 2 * BS)]
        both = jnp.where(half == (slot & 1), x, pltpu.roll(x, BS, 1))
        hi = both.astype(jnp.bfloat16).astype(jnp.float32)
        lhs = jnp.where(low, hi, both - hi).astype(jnp.bfloat16)
        lhs = jnp.concatenate([lhs, lhs], axis=1)
        y = right[code >> 24, block_at(code & 255), :]
        hi = y.astype(jnp.bfloat16)
        lo = (y - hi.astype(jnp.float32)).astype(jnp.bfloat16)
        rhs = jnp.concatenate([hi, hi, lo, lo], axis=0)
        return jnp.dot(lhs, rhs, preferred_element_type=jnp.float32)

    def add(code, product):
        rows_at = block_at((code >> 16) & 255)
        for pair in range(w // 2):
            x = product[:, pair * 2 * BS : (pair + 1) * 2 * BS]
            turned = pltpu.roll(x, BS, 1)
            picked, at = [], []
            for side in range(2):
                place = scalars[(slots + (code >> 24)) * w + 2 * pair + side, code & 255]
                parity = place >> 16
                chosen = jnp.where(parity == side, x, turned)
                picked.append(jnp.where(half == parity, chosen, 0.0))
                at.append(place & 0xFFFF)
            picked[1] = jnp.where(at[0] == at[1], picked[0] + picked[1], picked[1])
            spots = [(rows_at, pl.ds(pl.multiple_of(base, 2 * BS), 2 * BS)) for base in at]
            sums = [acc[spot] + part for spot, part in zip(spots, picked)]
            for spot, total in zip(spots, sums):
                acc[spot] = total

    def out_copy(part):
        at = pl.ds(part * part_rows * BS, part_rows * BS)
        return pltpu.make_async_copy(acc.at[at], out_ref.at[at], osem.at[part])

    groups = [jnp.int32(0)] + [(bound + UNROLL - 1) // UNROLL for bound in bounds[1:]]
    for part in range(PARTS):
        @pl.loop(groups[part], groups[part + 1])
        def _(group):
            for u in range(UNROLL):
                add(codes[group * UNROLL + u], value[u])
            for u in range(UNROLL):
                value[u] = product(codes[(group + 1) * UNROLL + u])

        out_copy(part).start()
    for part in range(PARTS):
        out_copy(part).wait()


def local(p_cols, p_data):
    n_row, n_col = lax.axis_size("row"), lax.axis_size("col")
    ratio = n_row // n_col
    row_id, col_id = lax.axis_index("row"), lax.axis_index("col")
    rb, w = p_cols.shape
    rows, width = p_data.shape
    left_perms = left_plan(n_row, n_col, ratio)
    right_perms = right_plan(n_row, n_col, ratio)
    table, slots = device_table(left_perms, right_perms, n_row, n_col, ratio)
    info = jnp.asarray(table)[row_id, col_id]

    smem = pl.BlockSpec(memory_space=pltpu.SMEM)
    hbm = pl.BlockSpec(memory_space=pl.ANY)
    dma = pltpu.SemaphoreType.DMA
    own = pl.pallas_call(
        join_kernel,
        out_shape=jax.ShapeDtypeStruct((rows + EXTRA, width), jnp.float32),
        in_specs=[hbm, hbm],
        out_specs=hbm,
        scratch_shapes=[dma((2,))],
        compiler_params=pltpu.CompilerParams(vmem_limit_bytes=2 << 20),
        cost_estimate=pl.CostEstimate(flops=0, bytes_accessed=2 << 20, transcendentals=0),
    )(jnp.pad(p_cols.T.astype(jnp.float32), ((0, EXTRA - w), (0, width - rb))), p_data)

    def carry(perms):
        bufs = [own]
        for source, pairs in perms:
            flat = [(s[0] * n_col + s[1], d[0] * n_col + d[1]) for s, d in pairs]
            bufs.append(lax.ppermute(bufs[source], ("row", "col"), flat))
        return bufs

    left_bufs, right_bufs = carry(left_perms), carry(right_perms)
    out_shape = jax.ShapeDtypeStruct((rows, rb * ratio * BS), jnp.float32)
    bufs = right_bufs + left_bufs[1:]
    codings = -(-(slots + STEPS + 1) * w // 8) * 8
    return pl.pallas_call(
        functools.partial(product_kernel, slots, n_row, ratio, rb, w, len(right_bufs)),
        out_shape=out_shape,
        in_specs=[smem] + [hbm] * len(bufs),
        out_specs=hbm,
        scratch_shapes=[
            pltpu.VMEM((slots, rows + EXTRA, width), jnp.float32),
            pltpu.VMEM((STEPS + 1, rows + EXTRA, width), jnp.float32),
            pltpu.VMEM(out_shape.shape, jnp.float32),
            pltpu.VMEM((UNROLL, BS, width), jnp.float32),
            pltpu.VMEM((slots + STEPS, EXTRA, width), jnp.float32),
            pltpu.VMEM((codings, 128), jnp.int32),
            pltpu.SMEM((codings, 128), jnp.int32),
            pltpu.SMEM((slots * rb * w + 4 * UNROLL,), jnp.int32),
            dma((slots,)),
            dma((STEPS,)),
            dma((PARTS,)),
            dma((slots + STEPS + 1,)),
        ],
        compiler_params=pltpu.CompilerParams(vmem_limit_bytes=18 << 20),
        cost_estimate=pl.CostEstimate(flops=10**9, bytes_accessed=20 << 20, transcendentals=0),
    )(info, *bufs)


def solution(mesh):
    in_specs = (P("row", "col"), P("row", "col"))
    return jax.shard_map(local, mesh=mesh, in_specs=in_specs, out_specs=P("row", "col"), check_vma=False)
```

profile of v0, /device:TPU:11, one launch (start us, length us, event | category | flops | bytes accessed | tf_op | source)
XLA Modules:
  0.0 72.7 jit_solution(12197264331911488699)
XLA Ops:
  0.0 0.7 convert_bitcast_fusion
  0.7 0.0 copy-start
  0.7 1.2 %copy-done = f32[1024,256]{1,0:T(8,128)S(1)} copy-done((f32[1024,256]{1,0:T(8,128)S(1)}, f32[1024,256]{1,0:T(8,128)}, u32[]{:S(2)}) %copy-start) | copy-done | bytes 1048600
  1.9 0.1 shard_map.37.refs_0_
  2.0 3.2 %collective-permute-start.6 = (f32[1032,256]{1,0:T(8,128)S(1)}, f32[1032,256]{1,0:T(8,128)S(1)}, u32[]{:S(2)}, u32[]{:S(2)}) collective-permute-start(f32[1032,256]{1,0:T(8,128)S(1)} %shard_map.37.refs_0_), channel_id=1, source_target_pairs={{16,17},{17,18},{18,19},{19,16},{20,21},{21,22},{22,23},{23,20},{2... | collective-permute-start | bytes 3170312 | tf_op jit(solution)/shard_map/ppermute | solution.py:280
  5.2 2.1 %collective-permute-start.5 = (f32[1032,256]{1,0:T(8,128)S(1)}, f32[1032,256]{1,0:T(8,128)S(1)}, u32[]{:S(2)}, u32[]{:S(2)}) collective-permute-start(f32[1032,256]{1,0:T(8,128)S(1)} %shard_map.37.refs_0_), channel_id=1, source_target_pairs={{4,7},{5,4},{6,5},{7,6},{8,11},{9,8},{10,9},{11,10},{28,31},{29,28... | collective-permute-start | bytes 3170312 | tf_op jit(solution)/shard_map/ppermute | solution.py:280
  7.4 1.2 %collective-permute-start.1 = (f32[1032,256]{1,0:T(8,128)S(1)}, f32[1032,256]{1,0:T(8,128)}, u32[]{:S(2)}, u32[]{:S(2)}) collective-permute-start(f32[1032,256]{1,0:T(8,128)S(1)} %shard_map.37.refs_0_), channel_id=1, source_target_pairs={{8,0},{17,1},{26,2},{12,4},{21,5},{30,6},{16,8},{25,9},{2,10},{20,... | collective-permute-start | bytes 3170312 | tf_op jit(solution)/shard_map/ppermute | solution.py:280
  8.6 1.9 %collective-permute-start = (f32[1032,256]{1,0:T(8,128)S(1)}, f32[1032,256]{1,0:T(8,128)}, u32[]{:S(2)}, u32[]{:S(2)}) collective-permute-start(f32[1032,256]{1,0:T(8,128)S(1)} %shard_map.37.refs_0_), channel_id=1, source_target_pairs={{9,1},{18,2},{27,3},{13,5},{22,6},{31,7},{17,9},{26,10},{3,11},{21... | collective-permute-start | bytes 3170312 | tf_op jit(solution)/shard_map/ppermute | solution.py:280
  10.5 1.3 %collective-permute-start.2 = (f32[1032,256]{1,0:T(8,128)S(1)}, f32[1032,256]{1,0:T(8,128)}, u32[]{:S(2)}, u32[]{:S(2)}) collective-permute-start(f32[1032,256]{1,0:T(8,128)S(1)} %shard_map.37.refs_0_), channel_id=1, source_target_pairs={{16,4},{25,5},{2,6},{11,7},{24,12},{1,13},{10,14},{19,15},{0,20},{... | collective-permute-start | bytes 3170312 | tf_op jit(solution)/shard_map/ppermute | solution.py:280
  11.8 13.6 %collective-permute-done.6.refs_7_ = f32[1032,256]{1,0:T(8,128)S(1)} collective-permute-done((f32[1032,256]{1,0:T(8,128)S(1)}, f32[1032,256]{1,0:T(8,128)S(1)}, u32[]{:S(2)}, u32[]{:S(2)}) %collective-permute-start.6) | collective-permute-done | bytes 1056800 | tf_op jit(solution)/shard_map/ppermute | solution.py:280
  25.4 8.2 %collective-permute-start.8 = (f32[1032,256]{1,0:T(8,128)S(1)}, f32[1032,256]{1,0:T(8,128)}, u32[]{:S(2)}, u32[]{:S(2)}) collective-permute-start(f32[1032,256]{1,0:T(8,128)S(1)} %collective-permute-done.6.refs_7_), channel_id=1, source_target_pairs={{16,17},{17,18},{18,19},{19,16},{20,21},{21,22},{22,23},{23,20},{1... | collective-permute-start | bytes 3170312 | tf_op jit(solution)/shard_map/ppermute | solution.py:280
  33.6 0.0 collective-permute-done.5.refs_6_
  33.6 1.9 %collective-permute-start.7 = (f32[1032,256]{1,0:T(8,128)S(1)}, f32[1032,256]{1,0:T(8,128)}, u32[]{:S(2)}, u32[]{:S(2)}) collective-permute-start(f32[1032,256]{1,0:T(8,128)S(1)} %collective-permute-done.5.refs_6_), channel_id=1, source_target_pairs={{4,7},{5,4},{6,5},{7,6},{8,11},{9,8},{10,9},{11,10},{13,12},{14,13... | collective-permute-start | bytes 3170312 | tf_op jit(solution)/shard_map/ppermute | solution.py:280
  35.5 19.4 %collective-permute-done.1.refs_2_ = f32[1032,256]{1,0:T(8,128)} collective-permute-done((f32[1032,256]{1,0:T(8,128)S(1)}, f32[1032,256]{1,0:T(8,128)}, u32[]{:S(2)}, u32[]{:S(2)}) %collective-permute-start.1) | collective-permute-done | bytes 1056800 | tf_op jit(solution)/shard_map/ppermute | solution.py:280
  54.9 2.0 %collective-permute-start.4 = (f32[1032,256]{1,0:T(8,128)}, f32[1032,256]{1,0:T(8,128)}, u32[]{:S(2)}, u32[]{:S(2)}) collective-permute-start(f32[1032,256]{1,0:T(8,128)} %collective-permute-done.1.refs_2_), channel_id=1, source_target_pairs={{4,0},{5,1},{6,2},{0,4},{1,5},{2,6},{12,8},{13,9},{14,10},{8,12},{... | collective-permute-start | bytes 3170312 | tf_op jit(solution)/shard_map/ppermute | solution.py:280
  56.9 0.0 collective-permute-done.refs_1_
  56.9 3.3 %collective-permute-start.3 = (f32[1032,256]{1,0:T(8,128)}, f32[1032,256]{1,0:T(8,128)}, u32[]{:S(2)}, u32[]{:S(2)}) collective-permute-start(f32[1032,256]{1,0:T(8,128)} %collective-permute-done.refs_1_), channel_id=1, source_target_pairs={{5,1},{6,2},{7,3},{13,9},{14,10},{15,11},{21,17},{22,18},{23,19},{... | collective-permute-start | bytes 3170312 | tf_op jit(solution)/shard_map/ppermute | solution.py:280
  60.2 0.7 dynamic-slice_bitcast_fusion.info_ref
  60.9 0.0 collective-permute-done.2.refs_3_
  60.9 0.0 collective-permute-done.8.refs_9_
  60.9 0.0 collective-permute-done.7.refs_8_
  61.0 0.0 collective-permute-done.4.refs_5_
  61.0 0.9 %collective-permute-done.3.refs_4_ = f32[1032,256]{1,0:T(8,128)} collective-permute-done((f32[1032,256]{1,0:T(8,128)}, f32[1032,256]{1,0:T(8,128)}, u32[]{:S(2)}, u32[]{:S(2)}) %collective-permute-start.3) | collective-permute-done | bytes 1056800 | tf_op jit(solution)/shard_map/ppermute | solution.py:280
  61.9 10.8 %shard_map.38 = f32[1024,2048]{1,0:T(8,128)} custom-call(s32[10]{0:T(128)S(1)} %dynamic-slice_bitcast_fusion.info_ref, f32[1032,256]{1,0:T(8,128)S(1)} %shard_map.37.refs_0_, f32[1032,256]{1,0:T(8,128)} %collective-permute-done.refs_1_, f32[1032,256]{1,0:T(8,128)} %collective-permute-done.1.refs_2_, f32[1032,256]{1,0:T(8,128)} %collective-permute-done.2.refs_3_, ...), custom_call_target="tpu_custom_call" | custom-call | flops 1000000000 | bytes 20971520 | tf_op jit(solution)/shard_map/pallas_call | solution.py:287
  (1 shorter events, 0.0 us)
Async XLA Ops:
  0.7 1.2 %copy-start = (f32[1024,256]{1,0:T(8,128)S(1)}, f32[1024,256]{1,0:T(8,128)}, u32[]{:S(2)}) copy-start(f32[1024,256]{1,0:T(8,128)} %data_ref.1) | copy-start | bytes 3145732
  2.0 23.4 %collective-permute-start.6 = (f32[1032,256]{1,0:T(8,128)S(1)}, f32[1032,256]{1,0:T(8,128)S(1)}, u32[]{:S(2)}, u32[]{:S(2)}) collective-permute-start(f32[1032,256]{1,0:T(8,128)S(1)} %shard_map.37.refs_0_), channel_id=1, source_target_pairs={{16,17},{17,18},{18,19},{19,16},{20,21},{21,22},{22,23},{23,20},{2... | collective-permute-start | bytes 3170312 | tf_op jit(solution)/shard_map/ppermute | solution.py:280
  5.2 28.3 %collective-permute-start.5 = (f32[1032,256]{1,0:T(8,128)S(1)}, f32[1032,256]{1,0:T(8,128)S(1)}, u32[]{:S(2)}, u32[]{:S(2)}) collective-permute-start(f32[1032,256]{1,0:T(8,128)S(1)} %shard_map.37.refs_0_), channel_id=1, source_target_pairs={{4,7},{5,4},{6,5},{7,6},{8,11},{9,8},{10,9},{11,10},{28,31},{29,28... | collective-permute-start | bytes 3170312 | tf_op jit(solution)/shard_map/ppermute | solution.py:280
  7.4 47.5 %collective-permute-start.1 = (f32[1032,256]{1,0:T(8,128)S(1)}, f32[1032,256]{1,0:T(8,128)}, u32[]{:S(2)}, u32[]{:S(2)}) collective-permute-start(f32[1032,256]{1,0:T(8,128)S(1)} %shard_map.37.refs_0_), channel_id=1, source_target_pairs={{8,0},{17,1},{26,2},{12,4},{21,5},{30,6},{16,8},{25,9},{2,10},{20,... | collective-permute-start | bytes 3170312 | tf_op jit(solution)/shard_map/ppermute | solution.py:280
  8.6 48.3 %collective-permute-start = (f32[1032,256]{1,0:T(8,128)S(1)}, f32[1032,256]{1,0:T(8,128)}, u32[]{:S(2)}, u32[]{:S(2)}) collective-permute-start(f32[1032,256]{1,0:T(8,128)S(1)} %shard_map.37.refs_0_), channel_id=1, source_target_pairs={{9,1},{18,2},{27,3},{13,5},{22,6},{31,7},{17,9},{26,10},{3,11},{21... | collective-permute-start | bytes 3170312 | tf_op jit(solution)/shard_map/ppermute | solution.py:280
  10.5 50.4 %collective-permute-start.2 = (f32[1032,256]{1,0:T(8,128)S(1)}, f32[1032,256]{1,0:T(8,128)}, u32[]{:S(2)}, u32[]{:S(2)}) collective-permute-start(f32[1032,256]{1,0:T(8,128)S(1)} %shard_map.37.refs_0_), channel_id=1, source_target_pairs={{16,4},{25,5},{2,6},{11,7},{24,12},{1,13},{10,14},{19,15},{0,20},{... | collective-permute-start | bytes 3170312 | tf_op jit(solution)/shard_map/ppermute | solution.py:280
  25.4 35.5 %collective-permute-start.8 = (f32[1032,256]{1,0:T(8,128)S(1)}, f32[1032,256]{1,0:T(8,128)}, u32[]{:S(2)}, u32[]{:S(2)}) collective-permute-start(f32[1032,256]{1,0:T(8,128)S(1)} %collective-permute-done.6.refs_7_), channel_id=1, source_target_pairs={{16,17},{17,18},{18,19},{19,16},{20,21},{21,22},{22,23},{23,20},{1... | collective-permute-start | bytes 3170312 | tf_op jit(solution)/shard_map/ppermute | solution.py:280
  33.6 27.4 %collective-permute-start.7 = (f32[1032,256]{1,0:T(8,128)S(1)}, f32[1032,256]{1,0:T(8,128)}, u32[]{:S(2)}, u32[]{:S(2)}) collective-permute-start(f32[1032,256]{1,0:T(8,128)S(1)} %collective-permute-done.5.refs_6_), channel_id=1, source_target_pairs={{4,7},{5,4},{6,5},{7,6},{8,11},{9,8},{10,9},{11,10},{13,12},{14,13... | collective-permute-start | bytes 3170312 | tf_op jit(solution)/shard_map/ppermute | solution.py:280
  54.9 6.0 %collective-permute-start.4 = (f32[1032,256]{1,0:T(8,128)}, f32[1032,256]{1,0:T(8,128)}, u32[]{:S(2)}, u32[]{:S(2)}) collective-permute-start(f32[1032,256]{1,0:T(8,128)} %collective-permute-done.1.refs_2_), channel_id=1, source_target_pairs={{4,0},{5,1},{6,2},{0,4},{1,5},{2,6},{12,8},{13,9},{14,10},{8,12},{... | collective-permute-start | bytes 3170312 | tf_op jit(solution)/shard_map/ppermute | solution.py:280
  56.9 4.9 %collective-permute-start.3 = (f32[1032,256]{1,0:T(8,128)}, f32[1032,256]{1,0:T(8,128)}, u32[]{:S(2)}, u32[]{:S(2)}) collective-permute-start(f32[1032,256]{1,0:T(8,128)} %collective-permute-done.refs_1_), channel_id=1, source_target_pairs={{5,1},{6,2},{7,3},{13,9},{14,10},{15,11},{21,17},{22,18},{23,19},{... | collective-permute-start | bytes 3170312 | tf_op jit(solution)/shard_map/ppermute | solution.py:280
where the time goes:
time: 73.6 us; the launch traced here: 72.7 us
  waiting for transfers between devices  33.9 us (46%)
  starting transfers between devices  25.2 us (34%)
  Pallas kernels  10.9 us (15%)
  local copies, waits for them, and re-layouts  1.92 us (3%)
    ppermute x9, waiting for transfers between devices, carry(): bufs.append(lax.ppermute(bufs[source], ('row', 'col'), flat))  33.9 us
    ppermute x9, starting transfers between devices, carry(): bufs.append(lax.ppermute(bufs[source], ('row', 'col'), flat))  25.2 us
    pallas_call x1, Pallas kernels, local(): pl.pallas_call(functools.partial(product_kernel, slots, n_row, ratio, rb,...  10.8 us
  transfers between devices with their start and end apart: 9, of which 3 were waited for; matrix products, arithmetic and copies ran while one was open for 1% of the time, Pallas kernels for 0%

commit v1 on v0

--- a/solution.py
+++ b/solution.py
@@ -10,7 +10,7 @@
 
 BS = 64
 STEPS = 4
-UNROLL = 4
+UNROLL = 8
 EXTRA = 8
 PARTS = 8
 
@@ -107,14 +107,16 @@
             pltpu.make_async_copy(buf, target, sem).start()
 
 
-def join_kernel(cols_ref, data_ref, out_ref, sem):
+def join_kernel(cols_ref, data_ref, out_ref, cols, sem):
     rows = data_ref.shape[0]
     data_copy = pltpu.make_async_copy(data_ref, out_ref.at[pl.ds(0, rows)], sem.at[0])
-    cols_copy = pltpu.make_async_copy(cols_ref, out_ref.at[pl.ds(rows, EXTRA)], sem.at[1])
+    cols_copy = pltpu.make_async_copy(cols_ref, cols, sem.at[1])
     data_copy.start()
     cols_copy.start()
+    out_ref[pl.ds(rows, EXTRA), :] = jnp.zeros((EXTRA, out_ref.shape[1]), jnp.float32)
+    cols_copy.wait()
+    out_ref[pl.ds(rows, cols.shape[0]), pl.ds(0, cols.shape[1])] = cols[...].astype(jnp.float32)
     data_copy.wait()
-    cols_copy.wait()
 
 
 def product_kernel(slots, n_row, ratio, rb, w, n_right, info_ref, *refs):
@@ -266,12 +268,12 @@
     own = pl.pallas_call(
         join_kernel,
         out_shape=jax.ShapeDtypeStruct((rows + EXTRA, width), jnp.float32),
-        in_specs=[hbm, hbm],
-        out_specs=hbm,
-        scratch_shapes=[dma((2,))],
-        compiler_params=pltpu.CompilerParams(vmem_limit_bytes=2 << 20),
+        in_specs=[pl.BlockSpec(memory_space=pltpu.HBM)] * 2,
+        out_specs=pl.BlockSpec(memory_space=pltpu.VMEM),
+        scratch_shapes=[pltpu.VMEM((w, rb), jnp.int32), dma((2,))],
+        compiler_params=pltpu.CompilerParams(vmem_limit_bytes=4 << 20),
         cost_estimate=pl.CostEstimate(flops=0, bytes_accessed=2 << 20, transcendentals=0),
-    )(jnp.pad(p_cols.T.astype(jnp.float32), ((0, EXTRA - w), (0, width - rb))), p_data)
+    )(p_cols.T, p_data)
 
     def carry(perms):
         bufs = [own]

time: 73.6 us -> 73 us (level)
  the two profiles are of different devices: /device:TPU:11 before, /device:TPU:15 now
where the time goes in v1:
time: 73 us; the launch traced here: 72.4 us
  waiting for transfers between devices  42.1 us (58%)
  starting transfers between devices  17.5 us (24%)
  Pallas kernels  10.1 us (14%)
  local copies, waits for them, and re-layouts  2.59 us (4%)
    ppermute x9, waiting for transfers between devices, carry(): bufs.append(lax.ppermute(bufs[source], ('row', 'col'), flat))  42.1 us
    ppermute x9, starting transfers between devices, carry(): bufs.append(lax.ppermute(bufs[source], ('row', 'col'), flat))  17.5 us
    pallas_call x1, Pallas kernels, local(): pl.pallas_call(functools.partial(product_kernel, slots, n_row, ratio, rb,...  10 us
    unnamed x4, local copies, waits for them, and re-layouts  1.91 us
  transfers between devices with their start and end apart: 9, of which 4 were waited for; matrix products, arithmetic and copies ran while one was open for 1% of the time, Pallas kernels for 0%

profile of v1, /device:TPU:15, one launch (start us, length us, event | category | flops | bytes accessed | tf_op | source)
XLA Modules:
  0.0 72.4 jit_solution(2890469396005173816)
XLA Ops:
  0.0 0.0 copy-start
  0.0 1.2 %copy-done = f32[1024,256]{1,0:T(8,128)S(1)} copy-done((f32[1024,256]{1,0:T(8,128)S(1)}, f32[1024,256]{1,0:T(8,128)}, u32[]{:S(2)}) %copy-start) | copy-done | bytes 1048600
  1.2 0.7 copy-done.1
  1.9 0.1 shard_map.37.refs_0_
  2.0 3.2 %collective-permute-start.6 = (f32[1032,256]{1,0:T(8,128)S(1)}, f32[1032,256]{1,0:T(8,128)S(1)}, u32[]{:S(2)}, u32[]{:S(2)}) collective-permute-start(f32[1032,256]{1,0:T(8,128)S(1)} %shard_map.37.refs_0_), channel_id=1, source_target_pairs={{16,17},{17,18},{18,19},{19,16},{20,21},{21,22},{22,23},{23,20},{2... | collective-permute-start | bytes 3170312 | tf_op jit(solution)/shard_map/ppermute | solution.py:282
  5.2 2.1 %collective-permute-start.5 = (f32[1032,256]{1,0:T(8,128)S(1)}, f32[1032,256]{1,0:T(8,128)S(1)}, u32[]{:S(2)}, u32[]{:S(2)}) collective-permute-start(f32[1032,256]{1,0:T(8,128)S(1)} %shard_map.37.refs_0_), channel_id=1, source_target_pairs={{4,7},{5,4},{6,5},{7,6},{8,11},{9,8},{10,9},{11,10},{28,31},{29,28... | collective-permute-start | bytes 3170312 | tf_op jit(solution)/shard_map/ppermute | solution.py:282
  7.3 0.3 collective-permute-start.1
  7.6 1.9 %collective-permute-start = (f32[1032,256]{1,0:T(8,128)S(1)}, f32[1032,256]{1,0:T(8,128)}, u32[]{:S(2)}, u32[]{:S(2)}) collective-permute-start(f32[1032,256]{1,0:T(8,128)S(1)} %shard_map.37.refs_0_), channel_id=1, source_target_pairs={{9,1},{18,2},{27,3},{13,5},{22,6},{31,7},{17,9},{26,10},{3,11},{21... | collective-permute-start | bytes 3170312 | tf_op jit(solution)/shard_map/ppermute | solution.py:282
  9.6 1.3 %collective-permute-start.2 = (f32[1032,256]{1,0:T(8,128)S(1)}, f32[1032,256]{1,0:T(8,128)}, u32[]{:S(2)}, u32[]{:S(2)}) collective-permute-start(f32[1032,256]{1,0:T(8,128)S(1)} %shard_map.37.refs_0_), channel_id=1, source_target_pairs={{16,4},{25,5},{2,6},{11,7},{24,12},{1,13},{10,14},{19,15},{0,20},{... | collective-permute-start | bytes 3170312 | tf_op jit(solution)/shard_map/ppermute | solution.py:282
  10.9 17.3 %collective-permute-done.6.refs_7_ = f32[1032,256]{1,0:T(8,128)S(1)} collective-permute-done((f32[1032,256]{1,0:T(8,128)S(1)}, f32[1032,256]{1,0:T(8,128)S(1)}, u32[]{:S(2)}, u32[]{:S(2)}) %collective-permute-start.6) | collective-permute-done | bytes 1056800 | tf_op jit(solution)/shard_map/ppermute | solution.py:282
  28.2 1.7 %collective-permute-start.8 = (f32[1032,256]{1,0:T(8,128)S(1)}, f32[1032,256]{1,0:T(8,128)}, u32[]{:S(2)}, u32[]{:S(2)}) collective-permute-start(f32[1032,256]{1,0:T(8,128)S(1)} %collective-permute-done.6.refs_7_), channel_id=1, source_target_pairs={{16,17},{17,18},{18,19},{19,16},{20,21},{21,22},{22,23},{23,20},{1... | collective-permute-start | bytes 3170312 | tf_op jit(solution)/shard_map/ppermute | solution.py:282
  29.9 11.7 %collective-permute-done.5.refs_6_ = f32[1032,256]{1,0:T(8,128)S(1)} collective-permute-done((f32[1032,256]{1,0:T(8,128)S(1)}, f32[1032,256]{1,0:T(8,128)S(1)}, u32[]{:S(2)}, u32[]{:S(2)}) %collective-permute-start.5) | collective-permute-done | bytes 1056800 | tf_op jit(solution)/shard_map/ppermute | solution.py:282
  41.5 1.7 %collective-permute-start.7 = (f32[1032,256]{1,0:T(8,128)S(1)}, f32[1032,256]{1,0:T(8,128)}, u32[]{:S(2)}, u32[]{:S(2)}) collective-permute-start(f32[1032,256]{1,0:T(8,128)S(1)} %collective-permute-done.5.refs_6_), channel_id=1, source_target_pairs={{4,7},{5,4},{6,5},{7,6},{8,11},{9,8},{10,9},{11,10},{13,12},{14,13... | collective-permute-start | bytes 3170312 | tf_op jit(solution)/shard_map/ppermute | solution.py:282
  43.2 12.2 %collective-permute-done.1.refs_2_ = f32[1032,256]{1,0:T(8,128)} collective-permute-done((f32[1032,256]{1,0:T(8,128)S(1)}, f32[1032,256]{1,0:T(8,128)}, u32[]{:S(2)}, u32[]{:S(2)}) %collective-permute-start.1) | collective-permute-done | bytes 1056800 | tf_op jit(solution)/shard_map/ppermute | solution.py:282
  55.4 2.4 %collective-permute-start.4 = (f32[1032,256]{1,0:T(8,128)}, f32[1032,256]{1,0:T(8,128)}, u32[]{:S(2)}, u32[]{:S(2)}) collective-permute-start(f32[1032,256]{1,0:T(8,128)} %collective-permute-done.1.refs_2_), channel_id=1, source_target_pairs={{4,0},{5,1},{6,2},{0,4},{1,5},{2,6},{12,8},{13,9},{14,10},{8,12},{... | collective-permute-start | bytes 3170312 | tf_op jit(solution)/shard_map/ppermute | solution.py:282
  57.8 0.0 collective-permute-done.refs_1_
  57.8 3.0 %collective-permute-start.3 = (f32[1032,256]{1,0:T(8,128)}, f32[1032,256]{1,0:T(8,128)}, u32[]{:S(2)}, u32[]{:S(2)}) collective-permute-start(f32[1032,256]{1,0:T(8,128)} %collective-permute-done.refs_1_), channel_id=1, source_target_pairs={{5,1},{6,2},{7,3},{13,9},{14,10},{15,11},{21,17},{22,18},{23,19},{... | collective-permute-start | bytes 3170312 | tf_op jit(solution)/shard_map/ppermute | solution.py:282
  60.7 0.7 dynamic-slice_bitcast_fusion.info_ref
  61.4 0.0 collective-permute-done.2.refs_3_
  61.4 0.0 collective-permute-done.8.refs_9_
  61.4 0.0 collective-permute-done.7.refs_8_
  61.4 0.0 collective-permute-done.4.refs_5_
  61.5 0.9 %collective-permute-done.3.refs_4_ = f32[1032,256]{1,0:T(8,128)} collective-permute-done((f32[1032,256]{1,0:T(8,128)}, f32[1032,256]{1,0:T(8,128)}, u32[]{:S(2)}, u32[]{:S(2)}) %collective-permute-start.3) | collective-permute-done | bytes 1056800 | tf_op jit(solution)/shard_map/ppermute | solution.py:282
  62.4 10.0 %shard_map.38 = f32[1024,2048]{1,0:T(8,128)} custom-call(s32[10]{0:T(128)S(1)} %dynamic-slice_bitcast_fusion.info_ref, f32[1032,256]{1,0:T(8,128)S(1)} %shard_map.37.refs_0_, f32[1032,256]{1,0:T(8,128)} %collective-permute-done.refs_1_, f32[1032,256]{1,0:T(8,128)} %collective-permute-done.1.refs_2_, f32[1032,256]{1,0:T(8,128)} %collective-permute-done.2.refs_3_, ...), custom_call_target="tpu_custom_call" | custom-call | flops 1000000000 | bytes 20971520 | tf_op jit(solution)/shard_map/pallas_call | solution.py:289
  (1 shorter events, 0.0 us)
Async XLA Ops:
  0.0 1.2 %copy-start = (f32[1024,256]{1,0:T(8,128)S(1)}, f32[1024,256]{1,0:T(8,128)}, u32[]{:S(2)}) copy-start(f32[1024,256]{1,0:T(8,128)} %data_ref.1) | copy-start | bytes 3145732
  1.2 0.7 copy-start.1
  2.0 26.2 %collective-permute-start.6 = (f32[1032,256]{1,0:T(8,128)S(1)}, f32[1032,256]{1,0:T(8,128)S(1)}, u32[]{:S(2)}, u32[]{:S(2)}) collective-permute-start(f32[1032,256]{1,0:T(8,128)S(1)} %shard_map.37.refs_0_), channel_id=1, source_target_pairs={{16,17},{17,18},{18,19},{19,16},{20,21},{21,22},{22,23},{23,20},{2... | collective-permute-start | bytes 3170312 | tf_op jit(solution)/shard_map/ppermute | solution.py:282
  5.2 36.3 %collective-permute-start.5 = (f32[1032,256]{1,0:T(8,128)S(1)}, f32[1032,256]{1,0:T(8,128)S(1)}, u32[]{:S(2)}, u32[]{:S(2)}) collective-permute-start(f32[1032,256]{1,0:T(8,128)S(1)} %shard_map.37.refs_0_), channel_id=1, source_target_pairs={{4,7},{5,4},{6,5},{7,6},{8,11},{9,8},{10,9},{11,10},{28,31},{29,28... | collective-permute-start | bytes 3170312 | tf_op jit(solution)/shard_map/ppermute | solution.py:282
  7.3 48.1 %collective-permute-start.1 = (f32[1032,256]{1,0:T(8,128)S(1)}, f32[1032,256]{1,0:T(8,128)}, u32[]{:S(2)}, u32[]{:S(2)}) collective-permute-start(f32[1032,256]{1,0:T(8,128)S(1)} %shard_map.37.refs_0_), channel_id=1, source_target_pairs={{8,0},{17,1},{26,2},{12,4},{21,5},{30,6},{16,8},{25,9},{2,10},{20,... | collective-permute-start | bytes 3170312 | tf_op jit(solution)/shard_map/ppermute | solution.py:282
  7.6 50.1 %collective-permute-start = (f32[1032,256]{1,0:T(8,128)S(1)}, f32[1032,256]{1,0:T(8,128)}, u32[]{:S(2)}, u32[]{:S(2)}) collective-permute-start(f32[1032,256]{1,0:T(8,128)S(1)} %shard_map.37.refs_0_), channel_id=1, source_target_pairs={{9,1},{18,2},{27,3},{13,5},{22,6},{31,7},{17,9},{26,10},{3,11},{21... | collective-permute-start | bytes 3170312 | tf_op jit(solution)/shard_map/ppermute | solution.py:282
  9.6 51.9 %collective-permute-start.2 = (f32[1032,256]{1,0:T(8,128)S(1)}, f32[1032,256]{1,0:T(8,128)}, u32[]{:S(2)}, u32[]{:S(2)}) collective-permute-start(f32[1032,256]{1,0:T(8,128)S(1)} %shard_map.37.refs_0_), channel_id=1, source_target_pairs={{16,4},{25,5},{2,6},{11,7},{24,12},{1,13},{10,14},{19,15},{0,20},{... | collective-permute-start | bytes 3170312 | tf_op jit(solution)/shard_map/ppermute | solution.py:282
  28.2 33.2 %collective-permute-start.8 = (f32[1032,256]{1,0:T(8,128)S(1)}, f32[1032,256]{1,0:T(8,128)}, u32[]{:S(2)}, u32[]{:S(2)}) collective-permute-start(f32[1032,256]{1,0:T(8,128)S(1)} %collective-permute-done.6.refs_7_), channel_id=1, source_target_pairs={{16,17},{17,18},{18,19},{19,16},{20,21},{21,22},{22,23},{23,20},{1... | collective-permute-start | bytes 3170312 | tf_op jit(solution)/shard_map/ppermute | solution.py:282
  41.5 19.9 %collective-permute-start.7 = (f32[1032,256]{1,0:T(8,128)S(1)}, f32[1032,256]{1,0:T(8,128)}, u32[]{:S(2)}, u32[]{:S(2)}) collective-permute-start(f32[1032,256]{1,0:T(8,128)S(1)} %collective-permute-done.5.refs_6_), channel_id=1, source_target_pairs={{4,7},{5,4},{6,5},{7,6},{8,11},{9,8},{10,9},{11,10},{13,12},{14,13... | collective-permute-start | bytes 3170312 | tf_op jit(solution)/shard_map/ppermute | solution.py:282
  55.4 6.0 %collective-permute-start.4 = (f32[1032,256]{1,0:T(8,128)}, f32[1032,256]{1,0:T(8,128)}, u32[]{:S(2)}, u32[]{:S(2)}) collective-permute-start(f32[1032,256]{1,0:T(8,128)} %collective-permute-done.1.refs_2_), channel_id=1, source_target_pairs={{4,0},{5,1},{6,2},{0,4},{1,5},{2,6},{12,8},{13,9},{14,10},{8,12},{... | collective-permute-start | bytes 3170312 | tf_op jit(solution)/shard_map/ppermute | solution.py:282
  57.8 4.6 %collective-permute-start.3 = (f32[1032,256]{1,0:T(8,128)}, f32[1032,256]{1,0:T(8,128)}, u32[]{:S(2)}, u32[]{:S(2)}) collective-permute-start(f32[1032,256]{1,0:T(8,128)} %collective-permute-done.refs_1_), channel_id=1, source_target_pairs={{5,1},{6,2},{7,3},{13,9},{14,10},{15,11},{21,17},{22,18},{23,19},{... | collective-permute-start | bytes 3170312 | tf_op jit(solution)/shard_map/ppermute | solution.py:282

commit v2 on v1

--- a/solution.py
+++ b/solution.py
@@ -10,7 +10,7 @@
 
 BS = 64
 STEPS = 4
-UNROLL = 8
+UNROLL = 16
 EXTRA = 8
 PARTS = 8
 

time: 73 us -> 73 us (level)
  no operation moved by 1% of the time
where the time goes in v2:
time: 73 us; the launch traced here: 71.7 us
  waiting for transfers between devices  42.1 us (58%)
  starting transfers between devices  17.5 us (24%)
  Pallas kernels  9.43 us (13%)
  local copies, waits for them, and re-layouts  2.59 us (4%)
    ppermute x9, waiting for transfers between devices, carry(): bufs.append(lax.ppermute(bufs[source], ('row', 'col'), flat))  42.1 us
    ppermute x9, starting transfers between devices, carry(): bufs.append(lax.ppermute(bufs[source], ('row', 'col'), flat))  17.5 us
    pallas_call x1, Pallas kernels, local(): pl.pallas_call(functools.partial(product_kernel, slots, n_row, ratio, rb,...  9.34 us
    unnamed x4, local copies, waits for them, and re-layouts  1.91 us
  transfers between devices with their start and end apart: 9, of which 4 were waited for; matrix products, arithmetic and copies ran while one was open for 1% of the time, Pallas kernels for 0%

profile of v2, /device:TPU:15, one launch (start us, length us, event | category | flops | bytes accessed | tf_op | source)
XLA Modules:
  0.0 71.7 jit_solution(2159479468008200177)
XLA Ops:
  0.0 0.0 copy-start
  0.0 1.2 %copy-done = f32[1024,256]{1,0:T(8,128)S(1)} copy-done((f32[1024,256]{1,0:T(8,128)S(1)}, f32[1024,256]{1,0:T(8,128)}, u32[]{:S(2)}) %copy-start) | copy-done | bytes 1048600
  1.2 0.7 copy-done.1
  1.9 0.1 shard_map.37.refs_0_
  2.0 3.2 %collective-permute-start.6 = (f32[1032,256]{1,0:T(8,128)S(1)}, f32[1032,256]{1,0:T(8,128)S(1)}, u32[]{:S(2)}, u32[]{:S(2)}) collective-permute-start(f32[1032,256]{1,0:T(8,128)S(1)} %shard_map.37.refs_0_), channel_id=1, source_target_pairs={{16,17},{17,18},{18,19},{19,16},{20,21},{21,22},{22,23},{23,20},{2... | collective-permute-start | bytes 3170312 | tf_op jit(solution)/shard_map/ppermute | solution.py:282
  5.2 2.1 %collective-permute-start.5 = (f32[1032,256]{1,0:T(8,128)S(1)}, f32[1032,256]{1,0:T(8,128)S(1)}, u32[]{:S(2)}, u32[]{:S(2)}) collective-permute-start(f32[1032,256]{1,0:T(8,128)S(1)} %shard_map.37.refs_0_), channel_id=1, source_target_pairs={{4,7},{5,4},{6,5},{7,6},{8,11},{9,8},{10,9},{11,10},{28,31},{29,28... | collective-permute-start | bytes 3170312 | tf_op jit(solution)/shard_map/ppermute | solution.py:282
  7.3 0.3 collective-permute-start.1
  7.6 1.9 %collective-permute-start = (f32[1032,256]{1,0:T(8,128)S(1)}, f32[1032,256]{1,0:T(8,128)}, u32[]{:S(2)}, u32[]{:S(2)}) collective-permute-start(f32[1032,256]{1,0:T(8,128)S(1)} %shard_map.37.refs_0_), channel_id=1, source_target_pairs={{9,1},{18,2},{27,3},{13,5},{22,6},{31,7},{17,9},{26,10},{3,11},{21... | collective-permute-start | bytes 3170312 | tf_op jit(solution)/shard_map/ppermute | solution.py:282
  9.6 1.3 %collective-permute-start.2 = (f32[1032,256]{1,0:T(8,128)S(1)}, f32[1032,256]{1,0:T(8,128)}, u32[]{:S(2)}, u32[]{:S(2)}) collective-permute-start(f32[1032,256]{1,0:T(8,128)S(1)} %shard_map.37.refs_0_), channel_id=1, source_target_pairs={{16,4},{25,5},{2,6},{11,7},{24,12},{1,13},{10,14},{19,15},{0,20},{... | collective-permute-start | bytes 3170312 | tf_op jit(solution)/shard_map/ppermute | solution.py:282
  10.9 17.3 %collective-permute-done.6.refs_7_ = f32[1032,256]{1,0:T(8,128)S(1)} collective-permute-done((f32[1032,256]{1,0:T(8,128)S(1)}, f32[1032,256]{1,0:T(8,128)S(1)}, u32[]{:S(2)}, u32[]{:S(2)}) %collective-permute-start.6) | collective-permute-done | bytes 1056800 | tf_op jit(solution)/shard_map/ppermute | solution.py:282
  28.2 1.7 %collective-permute-start.8 = (f32[1032,256]{1,0:T(8,128)S(1)}, f32[1032,256]{1,0:T(8,128)}, u32[]{:S(2)}, u32[]{:S(2)}) collective-permute-start(f32[1032,256]{1,0:T(8,128)S(1)} %collective-permute-done.6.refs_7_), channel_id=1, source_target_pairs={{16,17},{17,18},{18,19},{19,16},{20,21},{21,22},{22,23},{23,20},{1... | collective-permute-start | bytes 3170312 | tf_op jit(solution)/shard_map/ppermute | solution.py:282
  29.9 11.7 %collective-permute-done.5.refs_6_ = f32[1032,256]{1,0:T(8,128)S(1)} collective-permute-done((f32[1032,256]{1,0:T(8,128)S(1)}, f32[1032,256]{1,0:T(8,128)S(1)}, u32[]{:S(2)}, u32[]{:S(2)}) %collective-permute-start.5) | collective-permute-done | bytes 1056800 | tf_op jit(solution)/shard_map/ppermute | solution.py:282
  41.5 1.7 %collective-permute-start.7 = (f32[1032,256]{1,0:T(8,128)S(1)}, f32[1032,256]{1,0:T(8,128)}, u32[]{:S(2)}, u32[]{:S(2)}) collective-permute-start(f32[1032,256]{1,0:T(8,128)S(1)} %collective-permute-done.5.refs_6_), channel_id=1, source_target_pairs={{4,7},{5,4},{6,5},{7,6},{8,11},{9,8},{10,9},{11,10},{13,12},{14,13... | collective-permute-start | bytes 3170312 | tf_op jit(solution)/shard_map/ppermute | solution.py:282
  43.2 12.2 %collective-permute-done.1.refs_2_ = f32[1032,256]{1,0:T(8,128)} collective-permute-done((f32[1032,256]{1,0:T(8,128)S(1)}, f32[1032,256]{1,0:T(8,128)}, u32[]{:S(2)}, u32[]{:S(2)}) %collective-permute-start.1) | collective-permute-done | bytes 1056800 | tf_op jit(solution)/shard_map/ppermute | solution.py:282
  55.4 2.4 %collective-permute-start.4 = (f32[1032,256]{1,0:T(8,128)}, f32[1032,256]{1,0:T(8,128)}, u32[]{:S(2)}, u32[]{:S(2)}) collective-permute-start(f32[1032,256]{1,0:T(8,128)} %collective-permute-done.1.refs_2_), channel_id=1, source_target_pairs={{4,0},{5,1},{6,2},{0,4},{1,5},{2,6},{12,8},{13,9},{14,10},{8,12},{... | collective-permute-start | bytes 3170312 | tf_op jit(solution)/shard_map/ppermute | solution.py:282
  57.8 0.0 collective-permute-done.refs_1_
  57.8 3.0 %collective-permute-start.3 = (f32[1032,256]{1,0:T(8,128)}, f32[1032,256]{1,0:T(8,128)}, u32[]{:S(2)}, u32[]{:S(2)}) collective-permute-start(f32[1032,256]{1,0:T(8,128)} %collective-permute-done.refs_1_), channel_id=1, source_target_pairs={{5,1},{6,2},{7,3},{13,9},{14,10},{15,11},{21,17},{22,18},{23,19},{... | collective-permute-start | bytes 3170312 | tf_op jit(solution)/shard_map/ppermute | solution.py:282
  60.7 0.7 dynamic-slice_bitcast_fusion.info_ref
  61.4 0.0 collective-permute-done.2.refs_3_
  61.4 0.0 collective-permute-done.8.refs_9_
  61.4 0.0 collective-permute-done.7.refs_8_
  61.4 0.0 collective-permute-done.4.refs_5_
  61.5 0.9 %collective-permute-done.3.refs_4_ = f32[1032,256]{1,0:T(8,128)} collective-permute-done((f32[1032,256]{1,0:T(8,128)}, f32[1032,256]{1,0:T(8,128)}, u32[]{:S(2)}, u32[]{:S(2)}) %collective-permute-start.3) | collective-permute-done | bytes 1056800 | tf_op jit(solution)/shard_map/ppermute | solution.py:282
  62.4 9.3 %shard_map.38 = f32[1024,2048]{1,0:T(8,128)} custom-call(s32[10]{0:T(128)S(1)} %dynamic-slice_bitcast_fusion.info_ref, f32[1032,256]{1,0:T(8,128)S(1)} %shard_map.37.refs_0_, f32[1032,256]{1,0:T(8,128)} %collective-permute-done.refs_1_, f32[1032,256]{1,0:T(8,128)} %collective-permute-done.1.refs_2_, f32[1032,256]{1,0:T(8,128)} %collective-permute-done.2.refs_3_, ...), custom_call_target="tpu_custom_call" | custom-call | flops 1000000000 | bytes 20971520 | tf_op jit(solution)/shard_map/pallas_call | solution.py:289
  (1 shorter events, 0.0 us)
Async XLA Ops:
  0.0 1.2 %copy-start = (f32[1024,256]{1,0:T(8,128)S(1)}, f32[1024,256]{1,0:T(8,128)}, u32[]{:S(2)}) copy-start(f32[1024,256]{1,0:T(8,128)} %data_ref.1) | copy-start | bytes 3145732
  1.2 0.7 copy-start.1
  2.0 26.2 %collective-permute-start.6 = (f32[1032,256]{1,0:T(8,128)S(1)}, f32[1032,256]{1,0:T(8,128)S(1)}, u32[]{:S(2)}, u32[]{:S(2)}) collective-permute-start(f32[1032,256]{1,0:T(8,128)S(1)} %shard_map.37.refs_0_), channel_id=1, source_target_pairs={{16,17},{17,18},{18,19},{19,16},{20,21},{21,22},{22,23},{23,20},{2... | collective-permute-start | bytes 3170312 | tf_op jit(solution)/shard_map/ppermute | solution.py:282
  5.2 36.3 %collective-permute-start.5 = (f32[1032,256]{1,0:T(8,128)S(1)}, f32[1032,256]{1,0:T(8,128)S(1)}, u32[]{:S(2)}, u32[]{:S(2)}) collective-permute-start(f32[1032,256]{1,0:T(8,128)S(1)} %shard_map.37.refs_0_), channel_id=1, source_target_pairs={{4,7},{5,4},{6,5},{7,6},{8,11},{9,8},{10,9},{11,10},{28,31},{29,28... | collective-permute-start | bytes 3170312 | tf_op jit(solution)/shard_map/ppermute | solution.py:282
  7.3 48.1 %collective-permute-start.1 = (f32[1032,256]{1,0:T(8,128)S(1)}, f32[1032,256]{1,0:T(8,128)}, u32[]{:S(2)}, u32[]{:S(2)}) collective-permute-start(f32[1032,256]{1,0:T(8,128)S(1)} %shard_map.37.refs_0_), channel_id=1, source_target_pairs={{8,0},{17,1},{26,2},{12,4},{21,5},{30,6},{16,8},{25,9},{2,10},{20,... | collective-permute-start | bytes 3170312 | tf_op jit(solution)/shard_map/ppermute | solution.py:282
  7.6 50.1 %collective-permute-start = (f32[1032,256]{1,0:T(8,128)S(1)}, f32[1032,256]{1,0:T(8,128)}, u32[]{:S(2)}, u32[]{:S(2)}) collective-permute-start(f32[1032,256]{1,0:T(8,128)S(1)} %shard_map.37.refs_0_), channel_id=1, source_target_pairs={{9,1},{18,2},{27,3},{13,5},{22,6},{31,7},{17,9},{26,10},{3,11},{21... | collective-permute-start | bytes 3170312 | tf_op jit(solution)/shard_map/ppermute | solution.py:282
  9.6 51.9 %collective-permute-start.2 = (f32[1032,256]{1,0:T(8,128)S(1)}, f32[1032,256]{1,0:T(8,128)}, u32[]{:S(2)}, u32[]{:S(2)}) collective-permute-start(f32[1032,256]{1,0:T(8,128)S(1)} %shard_map.37.refs_0_), channel_id=1, source_target_pairs={{16,4},{25,5},{2,6},{11,7},{24,12},{1,13},{10,14},{19,15},{0,20},{... | collective-permute-start | bytes 3170312 | tf_op jit(solution)/shard_map/ppermute | solution.py:282
  28.2 33.2 %collective-permute-start.8 = (f32[1032,256]{1,0:T(8,128)S(1)}, f32[1032,256]{1,0:T(8,128)}, u32[]{:S(2)}, u32[]{:S(2)}) collective-permute-start(f32[1032,256]{1,0:T(8,128)S(1)} %collective-permute-done.6.refs_7_), channel_id=1, source_target_pairs={{16,17},{17,18},{18,19},{19,16},{20,21},{21,22},{22,23},{23,20},{1... | collective-permute-start | bytes 3170312 | tf_op jit(solution)/shard_map/ppermute | solution.py:282
  41.5 19.9 %collective-permute-start.7 = (f32[1032,256]{1,0:T(8,128)S(1)}, f32[1032,256]{1,0:T(8,128)}, u32[]{:S(2)}, u32[]{:S(2)}) collective-permute-start(f32[1032,256]{1,0:T(8,128)S(1)} %collective-permute-done.5.refs_6_), channel_id=1, source_target_pairs={{4,7},{5,4},{6,5},{7,6},{8,11},{9,8},{10,9},{11,10},{13,12},{14,13... | collective-permute-start | bytes 3170312 | tf_op jit(solution)/shard_map/ppermute | solution.py:282
  55.4 6.0 %collective-permute-start.4 = (f32[1032,256]{1,0:T(8,128)}, f32[1032,256]{1,0:T(8,128)}, u32[]{:S(2)}, u32[]{:S(2)}) collective-permute-start(f32[1032,256]{1,0:T(8,128)} %collective-permute-done.1.refs_2_), channel_id=1, source_target_pairs={{4,0},{5,1},{6,2},{0,4},{1,5},{2,6},{12,8},{13,9},{14,10},{8,12},{... | collective-permute-start | bytes 3170312 | tf_op jit(solution)/shard_map/ppermute | solution.py:282
  57.8 4.6 %collective-permute-start.3 = (f32[1032,256]{1,0:T(8,128)}, f32[1032,256]{1,0:T(8,128)}, u32[]{:S(2)}, u32[]{:S(2)}) collective-permute-start(f32[1032,256]{1,0:T(8,128)} %collective-permute-done.refs_1_), channel_id=1, source_target_pairs={{5,1},{6,2},{7,3},{13,9},{14,10},{15,11},{21,17},{22,18},{23,19},{... | collective-permute-start | bytes 3170312 | tf_op jit(solution)/shard_map/ppermute | solution.py:282

commit v3 on v1

--- a/solution.py
+++ b/solution.py
@@ -100,11 +100,11 @@
     return table, slots
 
 
-def fetch(choice, bufs, target, sem):
-    for number, buf in enumerate(bufs):
+def fetch(choice, among, bufs, target, sem):
+    for number in among:
         @pl.when(choice == number)
         def _():
-            pltpu.make_async_copy(buf, target, sem).start()
+            pltpu.make_async_copy(bufs[number], target, sem).start()
 
 
 def join_kernel(cols_ref, data_ref, out_ref, cols, sem):
@@ -119,28 +119,12 @@
     data_copy.wait()
 
 
-def product_kernel(slots, n_row, ratio, rb, w, n_right, info_ref, *refs):
-    out_ref, left, right, acc, value, cols, coded, scalars, codes, lsem, rsem, osem, csem = refs[-13:]
-    right_bufs, left_bufs = refs[:n_right], refs[:1] + refs[n_right:-13]
-    rows, width = left.shape[1] - EXTRA, left.shape[2]
-    names = pl.ds(rows, EXTRA)
+def code_kernel(slots, n_row, ratio, rb, w, among, info_ref, *refs):
+    bufs, code_ref, (cols, sem) = refs[:-3], refs[-3], refs[-2:]
+    names = pl.ds(bufs[0].shape[0] - EXTRA, EXTRA)
     for slot in range(slots):
-        fetch(info_ref[slot], [buf.at[names] for buf in left_bufs], cols.at[slot], csem.at[slot])
-    for step in range(STEPS):
-        choice = info_ref[slots + step]
-        fetch(choice, [buf.at[names] for buf in right_bufs], cols.at[slots + step], csem.at[slots + step])
-    for step in range(STEPS):
-        fetch(info_ref[slots + step], right_bufs, right.at[step], rsem.at[step])
-    for slot in range(slots):
-        fetch(info_ref[slot], left_bufs, left.at[slot], lsem.at[slot])
-
-    def clear(first, last):
-        @pl.loop(first, last)
-        def _(r):
-            acc[pl.ds(pl.multiple_of(r * BS, BS), BS), :] = jnp.zeros((BS, acc.shape[1]), jnp.float32)
-
-    clear(0, rb // 4)
-    lanes = scalars.shape[1]
+        fetch(info_ref[slot], among[slot], [buf.at[names] for buf in bufs], cols.at[slot], sem.at[slot])
+    lanes = code_ref.shape[1]
     row = lax.broadcasted_iota(jnp.int32, (w, lanes), 1)
     tile_slot = lax.broadcasted_iota(jnp.int32, (w, lanes), 0)
     for slot in range(slots):
@@ -148,7 +132,7 @@
 
         @pl.when(used)
         def _():
-            pltpu.make_async_copy(left_bufs[0].at[names], cols.at[slot], csem.at[slot]).wait()
+            pltpu.make_async_copy(bufs[0].at[names], cols.at[slot], sem.at[slot]).wait()
 
         inner = cols[slot, 0:w, 0:lanes].astype(jnp.int32)
         valid = (inner >= 0) & (row < rb)
@@ -160,17 +144,40 @@
         step = jnp.where(step >= n_row, step - n_row, step)
         code = inner | tile_slot << 8 | slot << 12 | row << 16 | step << 24
         valid = valid & (step < STEPS)
-        coded[slot * w : (slot + 1) * w, :] = jnp.where(valid, jnp.where(used, code, -1), -1)
-    for step in range(STEPS):
-        pltpu.make_async_copy(right_bufs[0].at[names], cols.at[slots + step], csem.at[slots + step]).wait()
-        col = cols[slots + step, 0:w, 0:lanes].astype(jnp.int32)
-        code = (col >> 1) * 2 * BS | (col & 1) << 16
-        coded[(slots + step) * w : (slots + step + 1) * w, :] = jnp.where(col < 0, 2 << 16, code)
-    coded[(slots + STEPS) * w : (slots + STEPS + 1) * w, :] = jnp.full((w, lanes), 2 << 16, jnp.int32)
-    to_scalars = pltpu.make_async_copy(coded, scalars, csem.at[slots + STEPS])
-    to_scalars.start()
-    clear(rb // 4, rb)
-    to_scalars.wait()
+        code_ref[slot * w : (slot + 1) * w, :] = jnp.where(valid, jnp.where(used, code, -1), -1)
+
+
+def product_kernel(slots, rb, w, n_right, among, info_ref, code_ref, *refs):
+    out_ref, left, right, acc, value, cols, places, left_codes, right_places, codes, lsem, rsem, osem, csem = refs[-14:]
+    right_bufs, left_bufs = refs[:n_right], refs[:1] + refs[n_right:-14]
+    rows, width = left.shape[1] - EXTRA, left.shape[2]
+    names = pl.ds(rows, EXTRA)
+    left_codes_copy = pltpu.make_async_copy(code_ref, left_codes, csem.at[STEPS])
+    left_codes_copy.start()
+    for step in range(STEPS):
+        choice = info_ref[slots + step]
+        fetch(choice, among[slots + step], [buf.at[names] for buf in right_bufs], cols.at[step], csem.at[step])
+    for step in range(STEPS):
+        fetch(info_ref[slots + step], among[slots + step], right_bufs, right.at[step], rsem.at[step])
+    for slot in range(slots):
+        fetch(info_ref[slot], among[slot], left_bufs, left.at[slot], lsem.at[slot])
+
+    def clear(first, last):
+        @pl.loop(first, last)
+        def _(r):
+            acc[pl.ds(pl.multiple_of(r * BS, BS), BS), :] = jnp.zeros((BS, acc.shape[1]), jnp.float32)
+
+    clear(0, rb // 2)
+    lanes = places.shape[1]
+    for step in range(STEPS):
+        pltpu.make_async_copy(right_bufs[0].at[names], cols.at[step], csem.at[step]).wait()
+        col = cols[step, 0:w, 0:lanes].astype(jnp.int32)
+        place = (col >> 1) * 2 * BS | (col & 1) << 16
+        places[step * w : (step + 1) * w, :] = jnp.where(col < 0, 2 << 16, place)
+    places[STEPS * w : (STEPS + 1) * w, :] = jnp.full((w, lanes), 2 << 16, jnp.int32)
+    places_copy = pltpu.make_async_copy(places, right_places, csem.at[STEPS + 1])
+    places_copy.start()
+    left_codes_copy.wait()
 
     part_rows = rb // PARTS
     for u in range(UNROLL):
@@ -180,7 +187,7 @@
         def listed(i, place):
             for slot in range(slots):
                 for k in range(w):
-                    code = scalars[slot * w + k, part * part_rows + i]
+                    code = left_codes[slot * w + k, part * part_rows + i]
                     codes[place] = code
                     place = place + (code >= 0).astype(jnp.int32)
             return place
@@ -189,6 +196,8 @@
     for u in range(2 * UNROLL):
         codes[bounds[-1] + u] = STEPS << 24
 
+    clear(rb // 2, rb)
+    places_copy.wait()
     for step in range(STEPS):
         pltpu.make_async_copy(right_bufs[0], right.at[step], rsem.at[step]).wait()
     for slot in range(slots):
@@ -222,7 +231,7 @@
             turned = pltpu.roll(x, BS, 1)
             picked, at = [], []
             for side in range(2):
-                place = scalars[(slots + (code >> 24)) * w + 2 * pair + side, code & 255]
+                place = right_places[(code >> 24) * w + 2 * pair + side, code & 255]
                 parity = place >> 16
                 chosen = jnp.where(parity == side, x, turned)
                 picked.append(jnp.where(half == parity, chosen, 0.0))
@@ -285,29 +294,40 @@
     left_bufs, right_bufs = carry(left_perms), carry(right_perms)
     out_shape = jax.ShapeDtypeStruct((rows, rb * ratio * BS), jnp.float32)
     bufs = right_bufs + left_bufs[1:]
-    codings = -(-(slots + STEPS + 1) * w // 8) * 8
+    among = [sorted(set(table[:, :, i].ravel().tolist()) - {-1}) for i in range(slots + STEPS)]
+    left_lines, right_lines = -(-slots * w // 8) * 8, -(-(STEPS + 1) * w // 8) * 8
+    left_codes = pl.pallas_call(
+        functools.partial(code_kernel, slots, n_row, ratio, rb, w, among),
+        out_shape=jax.ShapeDtypeStruct((left_lines, 128), jnp.int32),
+        in_specs=[smem] + [hbm] * len(left_bufs),
+        out_specs=pl.BlockSpec(memory_space=pltpu.VMEM),
+        scratch_shapes=[pltpu.VMEM((slots, EXTRA, width), jnp.float32), dma((slots,))],
+        compiler_params=pltpu.CompilerParams(vmem_limit_bytes=2 << 20),
+        cost_estimate=pl.CostEstimate(flops=10**9, bytes_accessed=1 << 16, transcendentals=0),
+    )(info, *left_bufs)
     return pl.pallas_call(
-        functools.partial(product_kernel, slots, n_row, ratio, rb, w, len(right_bufs)),
+        functools.partial(product_kernel, slots, rb, w, len(right_bufs), among),
         out_shape=out_shape,
-        in_specs=[smem] + [hbm] * len(bufs),
+        in_specs=[smem] + [hbm] * (1 + len(bufs)),
         out_specs=hbm,
         scratch_shapes=[
             pltpu.VMEM((slots, rows + EXTRA, width), jnp.float32),
             pltpu.VMEM((STEPS + 1, rows + EXTRA, width), jnp.float32),
             pltpu.VMEM(out_shape.shape, jnp.float32),
             pltpu.VMEM((UNROLL, BS, width), jnp.float32),
-            pltpu.VMEM((slots + STEPS, EXTRA, width), jnp.float32),
-            pltpu.VMEM((codings, 128), jnp.int32),
-            pltpu.SMEM((codings, 128), jnp.int32),
+            pltpu.VMEM((STEPS, EXTRA, width), jnp.float32),
+            pltpu.VMEM((right_lines, 128), jnp.int32),
+            pltpu.SMEM((left_lines, 128), jnp.int32),
+            pltpu.SMEM((right_lines, 128), jnp.int32),
             pltpu.SMEM((slots * rb * w + 4 * UNROLL,), jnp.int32),
             dma((slots,)),
             dma((STEPS,)),
             dma((PARTS,)),
-            dma((slots + STEPS + 1,)),
+            dma((STEPS + 2,)),
         ],
-        compiler_params=pltpu.CompilerParams(vmem_limit_bytes=18 << 20),
+        compiler_params=pltpu.CompilerParams(vmem_limit_bytes=20 << 20),
         cost_estimate=pl.CostEstimate(flops=10**9, bytes_accessed=20 << 20, transcendentals=0),
-    )(info, *bufs)
+    )(info, left_codes, *bufs)
 
 
 def solution(mesh):

time: 73 us -> 75.7 us (1.037)
  the two profiles are of different devices: /device:TPU:15 before, /device:TPU:31 now
where the time goes in v3:
time: 75.7 us; the launch traced here: 75.2 us
  waiting for transfers between devices  42.4 us (56%)
  starting transfers between devices  19.8 us (26%)
  Pallas kernels  10.4 us (14%)
  local copies, waits for them, and re-layouts  2.59 us (3%)
    ppermute x9, waiting for transfers between devices, carry(): bufs.append(lax.ppermute(bufs[source], ('row', 'col'), flat))  42.4 us
    ppermute x9, starting transfers between devices, carry(): bufs.append(lax.ppermute(bufs[source], ('row', 'col'), flat))  19.8 us
    pallas_call x1, Pallas kernels, local(): pl.pallas_call(functools.partial(product_kernel, slots, rb, w, len(right_...  9.56 us
    unnamed x4, local copies, waits for them, and re-layouts  1.91 us
  transfers between devices with their start and end apart: 9, of which 3 were waited for; matrix products, arithmetic and copies ran while one was open for 1% of the time, Pallas kernels for 1%

profile of v3, /device:TPU:31, one launch (start us, length us, event | category | flops | bytes accessed | tf_op | source)
XLA Modules:
  0.0 75.2 jit_solution(7094932838999124653)
XLA Ops:
  0.0 1.2 %copy-done = f32[1024,256]{1,0:T(8,128)S(1)} copy-done((f32[1024,256]{1,0:T(8,128)S(1)}, f32[1024,256]{1,0:T(8,128)}, u32[]{:S(2)}) %copy-start) | copy-done | bytes 1048600
  1.2 0.7 copy-done.1
  1.9 0.1 shard_map.37.refs_0_
  2.0 1.9 %collective-permute-start.1 = (f32[1032,256]{1,0:T(8,128)S(1)}, f32[1032,256]{1,0:T(8,128)S(1)}, u32[]{:S(2)}, u32[]{:S(2)}) collective-permute-start(f32[1032,256]{1,0:T(8,128)S(1)} %shard_map.37.refs_0_), channel_id=1, source_target_pairs={{16,17},{17,18},{18,19},{19,16},{20,21},{21,22},{22,23},{23,20},{2... | collective-permute-start | bytes 3170312 | tf_op jit(solution)/shard_map/ppermute | solution.py:291
  3.9 3.4 %collective-permute-start = (f32[1032,256]{1,0:T(8,128)S(1)}, f32[1032,256]{1,0:T(8,128)S(1)}, u32[]{:S(2)}, u32[]{:S(2)}) collective-permute-start(f32[1032,256]{1,0:T(8,128)S(1)} %shard_map.37.refs_0_), channel_id=1, source_target_pairs={{4,7},{5,4},{6,5},{7,6},{8,11},{9,8},{10,9},{11,10},{28,31},{29,28... | collective-permute-start | bytes 3170312 | tf_op jit(solution)/shard_map/ppermute | solution.py:291
  7.3 0.1 collective-permute-start.5
  7.4 1.9 %collective-permute-start.4 = (f32[1032,256]{1,0:T(8,128)S(1)}, f32[1032,256]{1,0:T(8,128)}, u32[]{:S(2)}, u32[]{:S(2)}) collective-permute-start(f32[1032,256]{1,0:T(8,128)S(1)} %shard_map.37.refs_0_), channel_id=1, source_target_pairs={{9,1},{18,2},{27,3},{13,5},{22,6},{31,7},{17,9},{26,10},{3,11},{21... | collective-permute-start | bytes 3170312 | tf_op jit(solution)/shard_map/ppermute | solution.py:291
  9.3 19.1 %collective-permute-done.1.refs_2_.refs_7_ = f32[1032,256]{1,0:T(8,128)S(1)} collective-permute-done((f32[1032,256]{1,0:T(8,128)S(1)}, f32[1032,256]{1,0:T(8,128)S(1)}, u32[]{:S(2)}, u32[]{:S(2)}) %collective-permute-start.1) | collective-permute-done | bytes 1056800 | tf_op jit(solution)/shard_map/ppermute | solution.py:291
  28.4 1.7 %collective-permute-start.3 = (f32[1032,256]{1,0:T(8,128)S(1)}, f32[1032,256]{1,0:T(8,128)}, u32[]{:S(2)}, u32[]{:S(2)}) collective-permute-start(f32[1032,256]{1,0:T(8,128)S(1)} %collective-permute-done.1.refs_2_.refs_7_), channel_id=1, source_target_pairs={{16,17},{17,18},{18,19},{19,16},{20,21},{21,22},{22,23},{23,20},{1... | collective-permute-start | bytes 3170312 | tf_op jit(solution)/shard_map/ppermute | solution.py:291
  30.1 10.1 %collective-permute-done.refs_1_.refs_6_ = f32[1032,256]{1,0:T(8,128)S(1)} collective-permute-done((f32[1032,256]{1,0:T(8,128)S(1)}, f32[1032,256]{1,0:T(8,128)S(1)}, u32[]{:S(2)}, u32[]{:S(2)}) %collective-permute-start) | collective-permute-done | bytes 1056800 | tf_op jit(solution)/shard_map/ppermute | solution.py:291
  40.2 1.6 %collective-permute-start.2 = (f32[1032,256]{1,0:T(8,128)S(1)}, f32[1032,256]{1,0:T(8,128)}, u32[]{:S(2)}, u32[]{:S(2)}) collective-permute-start(f32[1032,256]{1,0:T(8,128)S(1)} %collective-permute-done.refs_1_.refs_6_), channel_id=1, source_target_pairs={{4,7},{5,4},{6,5},{7,6},{8,11},{9,8},{10,9},{11,10},{13,12},{14,13... | collective-permute-start | bytes 3170312 | tf_op jit(solution)/shard_map/ppermute | solution.py:291
  41.9 1.3 %collective-permute-start.6 = (f32[1032,256]{1,0:T(8,128)S(1)}, f32[1032,256]{1,0:T(8,128)}, u32[]{:S(2)}, u32[]{:S(2)}) collective-permute-start(f32[1032,256]{1,0:T(8,128)S(1)} %shard_map.37.refs_0_), channel_id=1, source_target_pairs={{16,4},{25,5},{2,6},{11,7},{24,12},{1,13},{10,14},{19,15},{0,20},{... | collective-permute-start | bytes 3170312 | tf_op jit(solution)/shard_map/ppermute | solution.py:291
  43.1 0.0 collective-permute-done.5.refs_2_
  43.2 1.7 %collective-permute-start.8 = (f32[1032,256]{1,0:T(8,128)}, f32[1032,256]{1,0:T(8,128)}, u32[]{:S(2)}, u32[]{:S(2)}) collective-permute-start(f32[1032,256]{1,0:T(8,128)} %collective-permute-done.5.refs_2_), channel_id=1, source_target_pairs={{4,0},{5,1},{6,2},{0,4},{1,5},{2,6},{12,8},{13,9},{14,10},{8,12},{... | collective-permute-start | bytes 3170312 | tf_op jit(solution)/shard_map/ppermute | solution.py:291
  44.8 0.0 collective-permute-done.4.refs_1_
  44.8 6.3 %collective-permute-start.7 = (f32[1032,256]{1,0:T(8,128)}, f32[1032,256]{1,0:T(8,128)}, u32[]{:S(2)}, u32[]{:S(2)}) collective-permute-start(f32[1032,256]{1,0:T(8,128)} %collective-permute-done.4.refs_1_), channel_id=1, source_target_pairs={{5,1},{6,2},{7,3},{13,9},{14,10},{15,11},{21,17},{22,18},{23,19},{... | collective-permute-start | bytes 3170312 | tf_op jit(solution)/shard_map/ppermute | solution.py:291
  51.1 0.7 dynamic-slice_bitcast_fusion.info_ref
  51.8 0.0 collective-permute-done.3.refs_4_.refs_9_
  51.8 0.0 collective-permute-done.2.refs_3_.refs_8_
  51.8 0.7 shard_map.38.code_ref
  52.5 13.1 %collective-permute-done.6.refs_3_ = f32[1032,256]{1,0:T(8,128)} collective-permute-done((f32[1032,256]{1,0:T(8,128)S(1)}, f32[1032,256]{1,0:T(8,128)}, u32[]{:S(2)}, u32[]{:S(2)}) %collective-permute-start.6) | collective-permute-done | bytes 1056800 | tf_op jit(solution)/shard_map/ppermute | solution.py:291
  65.7 0.0 collective-permute-done.8.refs_5_
  65.7 0.0 collective-permute-done.7.refs_4_
  65.7 9.6 %shard_map.39 = f32[1024,2048]{1,0:T(8,128)} custom-call(s32[10]{0:T(128)S(1)} %dynamic-slice_bitcast_fusion.info_ref, s32[16,128]{1,0:T(8,128)S(1)} %shard_map.38.code_ref, f32[1032,256]{1,0:T(8,128)S(1)} %shard_map.37.refs_0_, f32[1032,256]{1,0:T(8,128)} %collective-permute-done.4.refs_1_, f32[1032,256]{1,0:T(8,128)} %collective-permute-done.5.refs_2_, ...), custom_call_target="tpu_custom_call" | custom-call | flops 1000000000 | bytes 20971520 | tf_op jit(solution)/shard_map/pallas_call | solution.py:308
  (2 shorter events, 0.0 us)
Async XLA Ops:
  0.0 1.2 %copy-start = (f32[1024,256]{1,0:T(8,128)S(1)}, f32[1024,256]{1,0:T(8,128)}, u32[]{:S(2)}) copy-start(f32[1024,256]{1,0:T(8,128)} %data_ref.1) | copy-start | bytes 3145732
  1.2 0.7 copy-start.1
  2.0 26.4 %collective-permute-start.1 = (f32[1032,256]{1,0:T(8,128)S(1)}, f32[1032,256]{1,0:T(8,128)S(1)}, u32[]{:S(2)}, u32[]{:S(2)}) collective-permute-start(f32[1032,256]{1,0:T(8,128)S(1)} %shard_map.37.refs_0_), channel_id=1, source_target_pairs={{16,17},{17,18},{18,19},{19,16},{20,21},{21,22},{22,23},{23,20},{2... | collective-permute-start | bytes 3170312 | tf_op jit(solution)/shard_map/ppermute | solution.py:291
  3.9 36.3 %collective-permute-start = (f32[1032,256]{1,0:T(8,128)S(1)}, f32[1032,256]{1,0:T(8,128)S(1)}, u32[]{:S(2)}, u32[]{:S(2)}) collective-permute-start(f32[1032,256]{1,0:T(8,128)S(1)} %shard_map.37.refs_0_), channel_id=1, source_target_pairs={{4,7},{5,4},{6,5},{7,6},{8,11},{9,8},{10,9},{11,10},{28,31},{29,28... | collective-permute-start | bytes 3170312 | tf_op jit(solution)/shard_map/ppermute | solution.py:291
  7.3 35.8 %collective-permute-start.5 = (f32[1032,256]{1,0:T(8,128)S(1)}, f32[1032,256]{1,0:T(8,128)}, u32[]{:S(2)}, u32[]{:S(2)}) collective-permute-start(f32[1032,256]{1,0:T(8,128)S(1)} %shard_map.37.refs_0_), channel_id=1, source_target_pairs={{8,0},{17,1},{26,2},{12,4},{21,5},{30,6},{16,8},{25,9},{2,10},{20,... | collective-permute-start | bytes 3170312 | tf_op jit(solution)/shard_map/ppermute | solution.py:291
  7.4 37.5 %collective-permute-start.4 = (f32[1032,256]{1,0:T(8,128)S(1)}, f32[1032,256]{1,0:T(8,128)}, u32[]{:S(2)}, u32[]{:S(2)}) collective-permute-start(f32[1032,256]{1,0:T(8,128)S(1)} %shard_map.37.refs_0_), channel_id=1, source_target_pairs={{9,1},{18,2},{27,3},{13,5},{22,6},{31,7},{17,9},{26,10},{3,11},{21... | collective-permute-start | bytes 3170312 | tf_op jit(solution)/shard_map/ppermute | solution.py:291
  28.4 23.4 %collective-permute-start.3 = (f32[1032,256]{1,0:T(8,128)S(1)}, f32[1032,256]{1,0:T(8,128)}, u32[]{:S(2)}, u32[]{:S(2)}) collective-permute-start(f32[1032,256]{1,0:T(8,128)S(1)} %collective-permute-done.1.refs_2_.refs_7_), channel_id=1, source_target_pairs={{16,17},{17,18},{18,19},{19,16},{20,21},{21,22},{22,23},{23,20},{1... | collective-permute-start | bytes 3170312 | tf_op jit(solution)/shard_map/ppermute | solution.py:291
  40.2 11.6 %collective-permute-start.2 = (f32[1032,256]{1,0:T(8,128)S(1)}, f32[1032,256]{1,0:T(8,128)}, u32[]{:S(2)}, u32[]{:S(2)}) collective-permute-start(f32[1032,256]{1,0:T(8,128)S(1)} %collective-permute-done.refs_1_.refs_6_), channel_id=1, source_target_pairs={{4,7},{5,4},{6,5},{7,6},{8,11},{9,8},{10,9},{11,10},{13,12},{14,13... | collective-permute-start | bytes 3170312 | tf_op jit(solution)/shard_map/ppermute | solution.py:291
  41.9 23.8 %collective-permute-start.6 = (f32[1032,256]{1,0:T(8,128)S(1)}, f32[1032,256]{1,0:T(8,128)}, u32[]{:S(2)}, u32[]{:S(2)}) collective-permute-start(f32[1032,256]{1,0:T(8,128)S(1)} %shard_map.37.refs_0_), channel_id=1, source_target_pairs={{16,4},{25,5},{2,6},{11,7},{24,12},{1,13},{10,14},{19,15},{0,20},{... | collective-permute-start | bytes 3170312 | tf_op jit(solution)/shard_map/ppermute | solution.py:291
  43.2 22.5 %collective-permute-start.8 = (f32[1032,256]{1,0:T(8,128)}, f32[1032,256]{1,0:T(8,128)}, u32[]{:S(2)}, u32[]{:S(2)}) collective-permute-start(f32[1032,256]{1,0:T(8,128)} %collective-permute-done.5.refs_2_), channel_id=1, source_target_pairs={{4,0},{5,1},{6,2},{0,4},{1,5},{2,6},{12,8},{13,9},{14,10},{8,12},{... | collective-permute-start | bytes 3170312 | tf_op jit(solution)/shard_map/ppermute | solution.py:291
  44.8 20.8 %collective-permute-start.7 = (f32[1032,256]{1,0:T(8,128)}, f32[1032,256]{1,0:T(8,128)}, u32[]{:S(2)}, u32[]{:S(2)}) collective-permute-start(f32[1032,256]{1,0:T(8,128)} %collective-permute-done.4.refs_1_), channel_id=1, source_target_pairs={{5,1},{6,2},{7,3},{13,9},{14,10},{15,11},{21,17},{22,18},{23,19},{... | collective-permute-start | bytes 3170312 | tf_op jit(solution)/shard_map/ppermute | solution.py:291

commit v4 on v1

--- a/solution.py
+++ b/solution.py
@@ -13,6 +13,7 @@
 UNROLL = 8
 EXTRA = 8
 PARTS = 8
+EARLY = 2
 
 
 def left_offsets(row, ratio, n_col):
@@ -100,11 +101,11 @@
     return table, slots
 
 
-def fetch(choice, bufs, target, sem):
-    for number, buf in enumerate(bufs):
+def fetch(choice, among, bufs, target, sem):
+    for number in among:
         @pl.when(choice == number)
         def _():
-            pltpu.make_async_copy(buf, target, sem).start()
+            pltpu.make_async_copy(bufs[number], target, sem).start()
 
 
 def join_kernel(cols_ref, data_ref, out_ref, cols, sem):
@@ -119,20 +120,28 @@
     data_copy.wait()
 
 
-def product_kernel(slots, n_row, ratio, rb, w, n_right, info_ref, *refs):
+def product_kernel(slots, n_row, ratio, rb, w, n_right, among, info_ref, *refs):
     out_ref, left, right, acc, value, cols, coded, scalars, codes, lsem, rsem, osem, csem = refs[-13:]
     right_bufs, left_bufs = refs[:n_right], refs[:1] + refs[n_right:-13]
     rows, width = left.shape[1] - EXTRA, left.shape[2]
     names = pl.ds(rows, EXTRA)
+    def fetch_left(slot):
+        fetch(info_ref[slot], among[slot], left_bufs, left.at[slot], lsem.at[slot])
+
+    def fetch_right(step):
+        fetch(info_ref[slots + step], among[slots + step], right_bufs, right.at[step], rsem.at[step])
+
     for slot in range(slots):
-        fetch(info_ref[slot], [buf.at[names] for buf in left_bufs], cols.at[slot], csem.at[slot])
+        fetch(info_ref[slot], among[slot], [buf.at[names] for buf in left_bufs], cols.at[slot], csem.at[slot])
     for step in range(STEPS):
-        choice = info_ref[slots + step]
-        fetch(choice, [buf.at[names] for buf in right_bufs], cols.at[slots + step], csem.at[slots + step])
-    for step in range(STEPS):
-        fetch(info_ref[slots + step], right_bufs, right.at[step], rsem.at[step])
+        at = slots + step
+        fetch(info_ref[at], among[at], [buf.at[names] for buf in right_bufs], cols.at[at], csem.at[at])
+    for step in range(EARLY):
+        fetch_right(step)
     for slot in range(slots):
-        fetch(info_ref[slot], left_bufs, left.at[slot], lsem.at[slot])
+        fetch_left(slot)
+    for step in range(EARLY, STEPS):
+        fetch_right(step)
 
     def clear(first, last):
         @pl.loop(first, last)
@@ -173,24 +182,36 @@
     to_scalars.wait()
 
     part_rows = rb // PARTS
+    dummy, late = STEPS << 24, EARLY << 24
     for u in range(UNROLL):
-        codes[u] = STEPS << 24
-    bounds = [jnp.int32(UNROLL)]
-    for part in range(PARTS):
+        codes[u] = dummy
+
+    def listing(first_row, rows_count, wanted, place):
         def listed(i, place):
             for slot in range(slots):
                 for k in range(w):
-                    code = scalars[slot * w + k, part * part_rows + i]
+                    code = scalars[slot * w + k, first_row + i]
                     codes[place] = code
-                    place = place + (code >= 0).astype(jnp.int32)
+                    place = place + wanted(code).astype(jnp.int32)
             return place
 
-        bounds.append(lax.fori_loop(0, part_rows, listed, bounds[-1]))
+        return lax.fori_loop(0, rows_count, listed, place)
+
+    early_end = listing(0, rb, lambda code: (code >= 0) & (code < late), jnp.int32(UNROLL))
+    for u in range(UNROLL - 1):
+        codes[early_end + u] = dummy
+    early_groups = (early_end + UNROLL - 1) // UNROLL - 1
+    bounds = [(early_groups + 1) * UNROLL]
+    for part in range(PARTS):
+        bounds.append(listing(part * part_rows, part_rows, lambda code: code >= late, bounds[-1]))
     for u in range(2 * UNROLL):
-        codes[bounds[-1] + u] = STEPS << 24
-
-    for step in range(STEPS):
+        codes[bounds[-1] + u] = dummy
+
+    def wait_right(step):
         pltpu.make_async_copy(right_bufs[0], right.at[step], rsem.at[step]).wait()
+
+    for step in range(EARLY):
+        wait_right(step)
     for slot in range(slots):
         @pl.when(info_ref[slot] >= 0)
         def _():
@@ -237,15 +258,18 @@
         at = pl.ds(part * part_rows * BS, part_rows * BS)
         return pltpu.make_async_copy(acc.at[at], out_ref.at[at], osem.at[part])
 
-    groups = [jnp.int32(0)] + [(bound + UNROLL - 1) // UNROLL for bound in bounds[1:]]
+    def group_step(group):
+        for u in range(UNROLL):
+            add(codes[group * UNROLL + u], value[u])
+        for u in range(UNROLL):
+            value[u] = product(codes[(group + 1) * UNROLL + u])
+
+    pl.loop(0, early_groups)(group_step)
+    for step in range(EARLY, STEPS):
+        wait_right(step)
+    groups = [early_groups] + [(bound + UNROLL - 1) // UNROLL for bound in bounds[1:]]
     for part in range(PARTS):
-        @pl.loop(groups[part], groups[part + 1])
-        def _(group):
-            for u in range(UNROLL):
-                add(codes[group * UNROLL + u], value[u])
-            for u in range(UNROLL):
-                value[u] = product(codes[(group + 1) * UNROLL + u])
-
+        pl.loop(groups[part], groups[part + 1])(group_step)
         out_copy(part).start()
     for part in range(PARTS):
         out_copy(part).wait()
@@ -285,9 +309,10 @@
     left_bufs, right_bufs = carry(left_perms), carry(right_perms)
     out_shape = jax.ShapeDtypeStruct((rows, rb * ratio * BS), jnp.float32)
     bufs = right_bufs + left_bufs[1:]
+    among = [sorted(set(table[:, :, i].ravel().tolist()) - {-1}) for i in range(slots + STEPS)]
     codings = -(-(slots + STEPS + 1) * w // 8) * 8
     return pl.pallas_call(
-        functools.partial(product_kernel, slots, n_row, ratio, rb, w, len(right_bufs)),
+        functools.partial(product_kernel, slots, n_row, ratio, rb, w, len(right_bufs), among),
         out_shape=out_shape,
         in_specs=[smem] + [hbm] * len(bufs),
         out_specs=hbm,
@@ -299,7 +324,7 @@
             pltpu.VMEM((slots + STEPS, EXTRA, width), jnp.float32),
             pltpu.VMEM((codings, 128), jnp.int32),
             pltpu.SMEM((codings, 128), jnp.int32),
-            pltpu.SMEM((slots * rb * w + 4 * UNROLL,), jnp.int32),
+            pltpu.SMEM((slots * rb * w + 5 * UNROLL,), jnp.int32),
             dma((slots,)),
             dma((STEPS,)),
             dma((PARTS,)),

time: 73 us -> 74 us (1.014)
  Pallas kernels: 10.1 us -> 11.1 us
    pallas_call x1, Pallas kernels: 10 us -> 11.1 us  [local(): pl.pallas_call(functools.partial(product_kernel, slots, n_row, ratio, rb,...]
where the time goes in v4:
time: 74 us; the launch traced here: 73.4 us
  waiting for transfers between devices  42.1 us (57%)
  starting transfers between devices  17.5 us (24%)
  Pallas kernels  11.1 us (15%)
  local copies, waits for them, and re-layouts  2.59 us (4%)
    ppermute x9, waiting for transfers between devices, carry(): bufs.append(lax.ppermute(bufs[source], ('row', 'col'), flat))  42.1 us
    ppermute x9, starting transfers between devices, carry(): bufs.append(lax.ppermute(bufs[source], ('row', 'col'), flat))  17.5 us
    pallas_call x1, Pallas kernels, local(): pl.pallas_call(functools.partial(product_kernel, slots, n_row, ratio, rb,...  11.1 us
    unnamed x4, local copies, waits for them, and re-layouts  1.91 us
  transfers between devices with their start and end apart: 9, of which 4 were waited for; matrix products, arithmetic and copies ran while one was open for 1% of the time, Pallas kernels for 0%

profile of v4, /device:TPU:15, one launch (start us, length us, event | category | flops | bytes accessed | tf_op | source)
XLA Modules:
  0.0 73.4 jit_solution(3929369368596774480)
XLA Ops:
  0.0 0.0 copy-start
  0.0 1.2 %copy-done = f32[1024,256]{1,0:T(8,128)S(1)} copy-done((f32[1024,256]{1,0:T(8,128)S(1)}, f32[1024,256]{1,0:T(8,128)}, u32[]{:S(2)}) %copy-start) | copy-done | bytes 1048600
  1.2 0.7 copy-done.1
  1.9 0.1 shard_map.37.refs_0_
  2.0 3.2 %collective-permute-start.6 = (f32[1032,256]{1,0:T(8,128)S(1)}, f32[1032,256]{1,0:T(8,128)S(1)}, u32[]{:S(2)}, u32[]{:S(2)}) collective-permute-start(f32[1032,256]{1,0:T(8,128)S(1)} %shard_map.37.refs_0_), channel_id=1, source_target_pairs={{16,17},{17,18},{18,19},{19,16},{20,21},{21,22},{22,23},{23,20},{2... | collective-permute-start | bytes 3170312 | tf_op jit(solution)/shard_map/ppermute | solution.py:306
  5.2 2.1 %collective-permute-start.5 = (f32[1032,256]{1,0:T(8,128)S(1)}, f32[1032,256]{1,0:T(8,128)S(1)}, u32[]{:S(2)}, u32[]{:S(2)}) collective-permute-start(f32[1032,256]{1,0:T(8,128)S(1)} %shard_map.37.refs_0_), channel_id=1, source_target_pairs={{4,7},{5,4},{6,5},{7,6},{8,11},{9,8},{10,9},{11,10},{28,31},{29,28... | collective-permute-start | bytes 3170312 | tf_op jit(solution)/shard_map/ppermute | solution.py:306
  7.3 0.3 collective-permute-start.1
  7.6 1.9 %collective-permute-start = (f32[1032,256]{1,0:T(8,128)S(1)}, f32[1032,256]{1,0:T(8,128)}, u32[]{:S(2)}, u32[]{:S(2)}) collective-permute-start(f32[1032,256]{1,0:T(8,128)S(1)} %shard_map.37.refs_0_), channel_id=1, source_target_pairs={{9,1},{18,2},{27,3},{13,5},{22,6},{31,7},{17,9},{26,10},{3,11},{21... | collective-permute-start | bytes 3170312 | tf_op jit(solution)/shard_map/ppermute | solution.py:306
  9.6 1.3 %collective-permute-start.2 = (f32[1032,256]{1,0:T(8,128)S(1)}, f32[1032,256]{1,0:T(8,128)}, u32[]{:S(2)}, u32[]{:S(2)}) collective-permute-start(f32[1032,256]{1,0:T(8,128)S(1)} %shard_map.37.refs_0_), channel_id=1, source_target_pairs={{16,4},{25,5},{2,6},{11,7},{24,12},{1,13},{10,14},{19,15},{0,20},{... | collective-permute-start | bytes 3170312 | tf_op jit(solution)/shard_map/ppermute | solution.py:306
  10.9 17.3 %collective-permute-done.6.refs_7_ = f32[1032,256]{1,0:T(8,128)S(1)} collective-permute-done((f32[1032,256]{1,0:T(8,128)S(1)}, f32[1032,256]{1,0:T(8,128)S(1)}, u32[]{:S(2)}, u32[]{:S(2)}) %collective-permute-start.6) | collective-permute-done | bytes 1056800 | tf_op jit(solution)/shard_map/ppermute | solution.py:306
  28.2 1.7 %collective-permute-start.8 = (f32[1032,256]{1,0:T(8,128)S(1)}, f32[1032,256]{1,0:T(8,128)}, u32[]{:S(2)}, u32[]{:S(2)}) collective-permute-start(f32[1032,256]{1,0:T(8,128)S(1)} %collective-permute-done.6.refs_7_), channel_id=1, source_target_pairs={{16,17},{17,18},{18,19},{19,16},{20,21},{21,22},{22,23},{23,20},{1... | collective-permute-start | bytes 3170312 | tf_op jit(solution)/shard_map/ppermute | solution.py:306
  29.9 11.7 %collective-permute-done.5.refs_6_ = f32[1032,256]{1,0:T(8,128)S(1)} collective-permute-done((f32[1032,256]{1,0:T(8,128)S(1)}, f32[1032,256]{1,0:T(8,128)S(1)}, u32[]{:S(2)}, u32[]{:S(2)}) %collective-permute-start.5) | collective-permute-done | bytes 1056800 | tf_op jit(solution)/shard_map/ppermute | solution.py:306
  41.5 1.7 %collective-permute-start.7 = (f32[1032,256]{1,0:T(8,128)S(1)}, f32[1032,256]{1,0:T(8,128)}, u32[]{:S(2)}, u32[]{:S(2)}) collective-permute-start(f32[1032,256]{1,0:T(8,128)S(1)} %collective-permute-done.5.refs_6_), channel_id=1, source_target_pairs={{4,7},{5,4},{6,5},{7,6},{8,11},{9,8},{10,9},{11,10},{13,12},{14,13... | collective-permute-start | bytes 3170312 | tf_op jit(solution)/shard_map/ppermute | solution.py:306
  43.2 12.2 %collective-permute-done.1.refs_2_ = f32[1032,256]{1,0:T(8,128)} collective-permute-done((f32[1032,256]{1,0:T(8,128)S(1)}, f32[1032,256]{1,0:T(8,128)}, u32[]{:S(2)}, u32[]{:S(2)}) %collective-permute-start.1) | collective-permute-done | bytes 1056800 | tf_op jit(solution)/shard_map/ppermute | solution.py:306
  55.4 2.4 %collective-permute-start.4 = (f32[1032,256]{1,0:T(8,128)}, f32[1032,256]{1,0:T(8,128)}, u32[]{:S(2)}, u32[]{:S(2)}) collective-permute-start(f32[1032,256]{1,0:T(8,128)} %collective-permute-done.1.refs_2_), channel_id=1, source_target_pairs={{4,0},{5,1},{6,2},{0,4},{1,5},{2,6},{12,8},{13,9},{14,10},{8,12},{... | collective-permute-start | bytes 3170312 | tf_op jit(solution)/shard_map/ppermute | solution.py:306
  57.8 0.0 collective-permute-done.refs_1_
  57.8 3.0 %collective-permute-start.3 = (f32[1032,256]{1,0:T(8,128)}, f32[1032,256]{1,0:T(8,128)}, u32[]{:S(2)}, u32[]{:S(2)}) collective-permute-start(f32[1032,256]{1,0:T(8,128)} %collective-permute-done.refs_1_), channel_id=1, source_target_pairs={{5,1},{6,2},{7,3},{13,9},{14,10},{15,11},{21,17},{22,18},{23,19},{... | collective-permute-start | bytes 3170312 | tf_op jit(solution)/shard_map/ppermute | solution.py:306
  60.7 0.7 dynamic-slice_bitcast_fusion.info_ref
  61.4 0.0 collective-permute-done.2.refs_3_
  61.4 0.0 collective-permute-done.8.refs_9_
  61.4 0.0 collective-permute-done.7.refs_8_
  61.4 0.0 collective-permute-done.4.refs_5_
  61.5 0.9 %collective-permute-done.3.refs_4_ = f32[1032,256]{1,0:T(8,128)} collective-permute-done((f32[1032,256]{1,0:T(8,128)}, f32[1032,256]{1,0:T(8,128)}, u32[]{:S(2)}, u32[]{:S(2)}) %collective-permute-start.3) | collective-permute-done | bytes 1056800 | tf_op jit(solution)/shard_map/ppermute | solution.py:306
  62.4 11.1 %shard_map.38 = f32[1024,2048]{1,0:T(8,128)} custom-call(s32[10]{0:T(128)S(1)} %dynamic-slice_bitcast_fusion.info_ref, f32[1032,256]{1,0:T(8,128)S(1)} %shard_map.37.refs_0_, f32[1032,256]{1,0:T(8,128)} %collective-permute-done.refs_1_, f32[1032,256]{1,0:T(8,128)} %collective-permute-done.1.refs_2_, f32[1032,256]{1,0:T(8,128)} %collective-permute-done.2.refs_3_, ...), custom_call_target="tpu_custom_call" | custom-call | flops 1000000000 | bytes 20971520 | tf_op jit(solution)/shard_map/pallas_call | solution.py:314
  (1 shorter events, 0.0 us)
Async XLA Ops:
  0.0 1.2 %copy-start = (f32[1024,256]{1,0:T(8,128)S(1)}, f32[1024,256]{1,0:T(8,128)}, u32[]{:S(2)}) copy-start(f32[1024,256]{1,0:T(8,128)} %data_ref.1) | copy-start | bytes 3145732
  1.2 0.7 copy-start.1
  2.0 26.2 %collective-permute-start.6 = (f32[1032,256]{1,0:T(8,128)S(1)}, f32[1032,256]{1,0:T(8,128)S(1)}, u32[]{:S(2)}, u32[]{:S(2)}) collective-permute-start(f32[1032,256]{1,0:T(8,128)S(1)} %shard_map.37.refs_0_), channel_id=1, source_target_pairs={{16,17},{17,18},{18,19},{19,16},{20,21},{21,22},{22,23},{23,20},{2... | collective-permute-start | bytes 3170312 | tf_op jit(solution)/shard_map/ppermute | solution.py:306
  5.2 36.3 %collective-permute-start.5 = (f32[1032,256]{1,0:T(8,128)S(1)}, f32[1032,256]{1,0:T(8,128)S(1)}, u32[]{:S(2)}, u32[]{:S(2)}) collective-permute-start(f32[1032,256]{1,0:T(8,128)S(1)} %shard_map.37.refs_0_), channel_id=1, source_target_pairs={{4,7},{5,4},{6,5},{7,6},{8,11},{9,8},{10,9},{11,10},{28,31},{29,28... | collective-permute-start | bytes 3170312 | tf_op jit(solution)/shard_map/ppermute | solution.py:306
  7.3 48.1 %collective-permute-start.1 = (f32[1032,256]{1,0:T(8,128)S(1)}, f32[1032,256]{1,0:T(8,128)}, u32[]{:S(2)}, u32[]{:S(2)}) collective-permute-start(f32[1032,256]{1,0:T(8,128)S(1)} %shard_map.37.refs_0_), channel_id=1, source_target_pairs={{8,0},{17,1},{26,2},{12,4},{21,5},{30,6},{16,8},{25,9},{2,10},{20,... | collective-permute-start | bytes 3170312 | tf_op jit(solution)/shard_map/ppermute | solution.py:306
  7.6 50.1 %collective-permute-start = (f32[1032,256]{1,0:T(8,128)S(1)}, f32[1032,256]{1,0:T(8,128)}, u32[]{:S(2)}, u32[]{:S(2)}) collective-permute-start(f32[1032,256]{1,0:T(8,128)S(1)} %shard_map.37.refs_0_), channel_id=1, source_target_pairs={{9,1},{18,2},{27,3},{13,5},{22,6},{31,7},{17,9},{26,10},{3,11},{21... | collective-permute-start | bytes 3170312 | tf_op jit(solution)/shard_map/ppermute | solution.py:306
  9.6 51.9 %collective-permute-start.2 = (f32[1032,256]{1,0:T(8,128)S(1)}, f32[1032,256]{1,0:T(8,128)}, u32[]{:S(2)}, u32[]{:S(2)}) collective-permute-start(f32[1032,256]{1,0:T(8,128)S(1)} %shard_map.37.refs_0_), channel_id=1, source_target_pairs={{16,4},{25,5},{2,6},{11,7},{24,12},{1,13},{10,14},{19,15},{0,20},{... | collective-permute-start | bytes 3170312 | tf_op jit(solution)/shard_map/ppermute | solution.py:306
  28.2 33.2 %collective-permute-start.8 = (f32[1032,256]{1,0:T(8,128)S(1)}, f32[1032,256]{1,0:T(8,128)}, u32[]{:S(2)}, u32[]{:S(2)}) collective-permute-start(f32[1032,256]{1,0:T(8,128)S(1)} %collective-permute-done.6.refs_7_), channel_id=1, source_target_pairs={{16,17},{17,18},{18,19},{19,16},{20,21},{21,22},{22,23},{23,20},{1... | collective-permute-start | bytes 3170312 | tf_op jit(solution)/shard_map/ppermute | solution.py:306
  41.5 19.9 %collective-permute-start.7 = (f32[1032,256]{1,0:T(8,128)S(1)}, f32[1032,256]{1,0:T(8,128)}, u32[]{:S(2)}, u32[]{:S(2)}) collective-permute-start(f32[1032,256]{1,0:T(8,128)S(1)} %collective-permute-done.5.refs_6_), channel_id=1, source_target_pairs={{4,7},{5,4},{6,5},{7,6},{8,11},{9,8},{10,9},{11,10},{13,12},{14,13... | collective-permute-start | bytes 3170312 | tf_op jit(solution)/shard_map/ppermute | solution.py:306
  55.4 6.0 %collective-permute-start.4 = (f32[1032,256]{1,0:T(8,128)}, f32[1032,256]{1,0:T(8,128)}, u32[]{:S(2)}, u32[]{:S(2)}) collective-permute-start(f32[1032,256]{1,0:T(8,128)} %collective-permute-done.1.refs_2_), channel_id=1, source_target_pairs={{4,0},{5,1},{6,2},{0,4},{1,5},{2,6},{12,8},{13,9},{14,10},{8,12},{... | collective-permute-start | bytes 3170312 | tf_op jit(solution)/shard_map/ppermute | solution.py:306
  57.8 4.6 %collective-permute-start.3 = (f32[1032,256]{1,0:T(8,128)}, f32[1032,256]{1,0:T(8,128)}, u32[]{:S(2)}, u32[]{:S(2)}) collective-permute-start(f32[1032,256]{1,0:T(8,128)} %collective-permute-done.refs_1_), channel_id=1, source_target_pairs={{5,1},{6,2},{7,3},{13,9},{14,10},{15,11},{21,17},{22,18},{23,19},{... | collective-permute-start | bytes 3170312 | tf_op jit(solution)/shard_map/ppermute | solution.py:306

commit v5 on v1

--- a/solution.py
+++ b/solution.py
@@ -100,11 +100,11 @@
     return table, slots
 
 
-def fetch(choice, bufs, target, sem):
-    for number, buf in enumerate(bufs):
+def fetch(choice, among, bufs, target, sem):
+    for number in among:
         @pl.when(choice == number)
         def _():
-            pltpu.make_async_copy(buf, target, sem).start()
+            pltpu.make_async_copy(bufs[number], target, sem).start()
 
 
 def join_kernel(cols_ref, data_ref, out_ref, cols, sem):
@@ -119,20 +119,20 @@
     data_copy.wait()
 
 
-def product_kernel(slots, n_row, ratio, rb, w, n_right, info_ref, *refs):
+def product_kernel(slots, n_row, ratio, rb, w, n_right, among, info_ref, *refs):
     out_ref, left, right, acc, value, cols, coded, scalars, codes, lsem, rsem, osem, csem = refs[-13:]
     right_bufs, left_bufs = refs[:n_right], refs[:1] + refs[n_right:-13]
     rows, width = left.shape[1] - EXTRA, left.shape[2]
     names = pl.ds(rows, EXTRA)
     for slot in range(slots):
-        fetch(info_ref[slot], [buf.at[names] for buf in left_bufs], cols.at[slot], csem.at[slot])
-    for step in range(STEPS):
-        choice = info_ref[slots + step]
-        fetch(choice, [buf.at[names] for buf in right_bufs], cols.at[slots + step], csem.at[slots + step])
-    for step in range(STEPS):
-        fetch(info_ref[slots + step], right_bufs, right.at[step], rsem.at[step])
+        fetch(info_ref[slot], among[slot], [buf.at[names] for buf in left_bufs], cols.at[slot], csem.at[slot])
+    for step in range(STEPS):
+        at = slots + step
+        fetch(info_ref[at], among[at], [buf.at[names] for buf in right_bufs], cols.at[at], csem.at[at])
+    for step in range(STEPS):
+        fetch(info_ref[slots + step], among[slots + step], right_bufs, right.at[step], rsem.at[step])
     for slot in range(slots):
-        fetch(info_ref[slot], left_bufs, left.at[slot], lsem.at[slot])
+        fetch(info_ref[slot], among[slot], left_bufs, left.at[slot], lsem.at[slot])
 
     def clear(first, last):
         @pl.loop(first, last)
@@ -178,11 +178,10 @@
     bounds = [jnp.int32(UNROLL)]
     for part in range(PARTS):
         def listed(i, place):
-            for slot in range(slots):
-                for k in range(w):
-                    code = scalars[slot * w + k, part * part_rows + i]
-                    codes[place] = code
-                    place = place + (code >= 0).astype(jnp.int32)
+            row_codes = [scalars[line, part * part_rows + i] for line in range(slots * w)]
+            for code in row_codes:
+                codes[place] = code
+                place = place + (code >= 0).astype(jnp.int32)
             return place
 
         bounds.append(lax.fori_loop(0, part_rows, listed, bounds[-1]))
@@ -285,9 +284,10 @@
     left_bufs, right_bufs = carry(left_perms), carry(right_perms)
     out_shape = jax.ShapeDtypeStruct((rows, rb * ratio * BS), jnp.float32)
     bufs = right_bufs + left_bufs[1:]
+    among = [sorted(set(table[:, :, i].ravel().tolist()) - {-1}) for i in range(slots + STEPS)]
     codings = -(-(slots + STEPS + 1) * w // 8) * 8
     return pl.pallas_call(
-        functools.partial(product_kernel, slots, n_row, ratio, rb, w, len(right_bufs)),
+        functools.partial(product_kernel, slots, n_row, ratio, rb, w, len(right_bufs), among),
         out_shape=out_shape,
         in_specs=[smem] + [hbm] * len(bufs),
         out_specs=hbm,

time: 73 us -> 72.9 us (level)
  no operation moved by 1% of the time
where the time goes in v5:
time: 72.9 us
  waiting for transfers between devices  42.1 us (58%)
  starting transfers between devices  17.5 us (24%)
  Pallas kernels  10.6 us (15%)
  local copies, waits for them, and re-layouts  2.59 us (4%)
    ppermute x9, waiting for transfers between devices, carry(): bufs.append(lax.ppermute(bufs[source], ('row', 'col'), flat))  42.1 us
    ppermute x9, starting transfers between devices, carry(): bufs.append(lax.ppermute(bufs[source], ('row', 'col'), flat))  17.5 us
    pallas_call x1, Pallas kernels, local(): pl.pallas_call(functools.partial(product_kernel, slots, n_row, ratio, rb,...  10.5 us
    unnamed x4, local copies, waits for them, and re-layouts  1.91 us
  transfers between devices with their start and end apart: 9, of which 4 were waited for; matrix products, arithmetic and copies ran while one was open for 1% of the time, Pallas kernels for 0%

profile of v5, /device:TPU:15, one launch (start us, length us, event | category | flops | bytes accessed | tf_op | source)
XLA Modules:
  0.0 72.9 jit_solution(13398428846332018813)
XLA Ops:
  0.0 0.0 copy-start
  0.0 1.2 %copy-done = f32[1024,256]{1,0:T(8,128)S(1)} copy-done((f32[1024,256]{1,0:T(8,128)S(1)}, f32[1024,256]{1,0:T(8,128)}, u32[]{:S(2)}) %copy-start) | copy-done | bytes 1048600
  1.2 0.7 copy-done.1
  1.9 0.1 shard_map.37.refs_0_
  2.0 3.2 %collective-permute-start.6 = (f32[1032,256]{1,0:T(8,128)S(1)}, f32[1032,256]{1,0:T(8,128)S(1)}, u32[]{:S(2)}, u32[]{:S(2)}) collective-permute-start(f32[1032,256]{1,0:T(8,128)S(1)} %shard_map.37.refs_0_), channel_id=1, source_target_pairs={{16,17},{17,18},{18,19},{19,16},{20,21},{21,22},{22,23},{23,20},{2... | collective-permute-start | bytes 3170312 | tf_op jit(solution)/shard_map/ppermute | solution.py:281
  5.2 2.1 %collective-permute-start.5 = (f32[1032,256]{1,0:T(8,128)S(1)}, f32[1032,256]{1,0:T(8,128)S(1)}, u32[]{:S(2)}, u32[]{:S(2)}) collective-permute-start(f32[1032,256]{1,0:T(8,128)S(1)} %shard_map.37.refs_0_), channel_id=1, source_target_pairs={{4,7},{5,4},{6,5},{7,6},{8,11},{9,8},{10,9},{11,10},{28,31},{29,28... | collective-permute-start | bytes 3170312 | tf_op jit(solution)/shard_map/ppermute | solution.py:281
  7.3 0.3 collective-permute-start.1
  7.6 1.9 %collective-permute-start = (f32[1032,256]{1,0:T(8,128)S(1)}, f32[1032,256]{1,0:T(8,128)}, u32[]{:S(2)}, u32[]{:S(2)}) collective-permute-start(f32[1032,256]{1,0:T(8,128)S(1)} %shard_map.37.refs_0_), channel_id=1, source_target_pairs={{9,1},{18,2},{27,3},{13,5},{22,6},{31,7},{17,9},{26,10},{3,11},{21... | collective-permute-start | bytes 3170312 | tf_op jit(solution)/shard_map/ppermute | solution.py:281
  9.6 1.3 %collective-permute-start.2 = (f32[1032,256]{1,0:T(8,128)S(1)}, f32[1032,256]{1,0:T(8,128)}, u32[]{:S(2)}, u32[]{:S(2)}) collective-permute-start(f32[1032,256]{1,0:T(8,128)S(1)} %shard_map.37.refs_0_), channel_id=1, source_target_pairs={{16,4},{25,5},{2,6},{11,7},{24,12},{1,13},{10,14},{19,15},{0,20},{... | collective-permute-start | bytes 3170312 | tf_op jit(solution)/shard_map/ppermute | solution.py:281
  10.9 17.3 %collective-permute-done.6.refs_7_ = f32[1032,256]{1,0:T(8,128)S(1)} collective-permute-done((f32[1032,256]{1,0:T(8,128)S(1)}, f32[1032,256]{1,0:T(8,128)S(1)}, u32[]{:S(2)}, u32[]{:S(2)}) %collective-permute-start.6) | collective-permute-done | bytes 1056800 | tf_op jit(solution)/shard_map/ppermute | solution.py:281
  28.2 1.7 %collective-permute-start.8 = (f32[1032,256]{1,0:T(8,128)S(1)}, f32[1032,256]{1,0:T(8,128)}, u32[]{:S(2)}, u32[]{:S(2)}) collective-permute-start(f32[1032,256]{1,0:T(8,128)S(1)} %collective-permute-done.6.refs_7_), channel_id=1, source_target_pairs={{16,17},{17,18},{18,19},{19,16},{20,21},{21,22},{22,23},{23,20},{1... | collective-permute-start | bytes 3170312 | tf_op jit(solution)/shard_map/ppermute | solution.py:281
  29.9 11.7 %collective-permute-done.5.refs_6_ = f32[1032,256]{1,0:T(8,128)S(1)} collective-permute-done((f32[1032,256]{1,0:T(8,128)S(1)}, f32[1032,256]{1,0:T(8,128)S(1)}, u32[]{:S(2)}, u32[]{:S(2)}) %collective-permute-start.5) | collective-permute-done | bytes 1056800 | tf_op jit(solution)/shard_map/ppermute | solution.py:281
  41.5 1.7 %collective-permute-start.7 = (f32[1032,256]{1,0:T(8,128)S(1)}, f32[1032,256]{1,0:T(8,128)}, u32[]{:S(2)}, u32[]{:S(2)}) collective-permute-start(f32[1032,256]{1,0:T(8,128)S(1)} %collective-permute-done.5.refs_6_), channel_id=1, source_target_pairs={{4,7},{5,4},{6,5},{7,6},{8,11},{9,8},{10,9},{11,10},{13,12},{14,13... | collective-permute-start | bytes 3170312 | tf_op jit(solution)/shard_map/ppermute | solution.py:281
  43.2 12.2 %collective-permute-done.1.refs_2_ = f32[1032,256]{1,0:T(8,128)} collective-permute-done((f32[1032,256]{1,0:T(8,128)S(1)}, f32[1032,256]{1,0:T(8,128)}, u32[]{:S(2)}, u32[]{:S(2)}) %collective-permute-start.1) | collective-permute-done | bytes 1056800 | tf_op jit(solution)/shard_map/ppermute | solution.py:281
  55.4 2.4 %collective-permute-start.4 = (f32[1032,256]{1,0:T(8,128)}, f32[1032,256]{1,0:T(8,128)}, u32[]{:S(2)}, u32[]{:S(2)}) collective-permute-start(f32[1032,256]{1,0:T(8,128)} %collective-permute-done.1.refs_2_), channel_id=1, source_target_pairs={{4,0},{5,1},{6,2},{0,4},{1,5},{2,6},{12,8},{13,9},{14,10},{8,12},{... | collective-permute-start | bytes 3170312 | tf_op jit(solution)/shard_map/ppermute | solution.py:281
  57.8 0.0 collective-permute-done.refs_1_
  57.8 3.0 %collective-permute-start.3 = (f32[1032,256]{1,0:T(8,128)}, f32[1032,256]{1,0:T(8,128)}, u32[]{:S(2)}, u32[]{:S(2)}) collective-permute-start(f32[1032,256]{1,0:T(8,128)} %collective-permute-done.refs_1_), channel_id=1, source_target_pairs={{5,1},{6,2},{7,3},{13,9},{14,10},{15,11},{21,17},{22,18},{23,19},{... | collective-permute-start | bytes 3170312 | tf_op jit(solution)/shard_map/ppermute | solution.py:281
  60.7 0.7 dynamic-slice_bitcast_fusion.info_ref
  61.4 0.0 collective-permute-done.2.refs_3_
  61.4 0.0 collective-permute-done.8.refs_9_
  61.4 0.0 collective-permute-done.7.refs_8_
  61.4 0.0 collective-permute-done.4.refs_5_
  61.5 0.9 %collective-permute-done.3.refs_4_ = f32[1032,256]{1,0:T(8,128)} collective-permute-done((f32[1032,256]{1,0:T(8,128)}, f32[1032,256]{1,0:T(8,128)}, u32[]{:S(2)}, u32[]{:S(2)}) %collective-permute-start.3) | collective-permute-done | bytes 1056800 | tf_op jit(solution)/shard_map/ppermute | solution.py:281
  62.4 10.5 %shard_map.38 = f32[1024,2048]{1,0:T(8,128)} custom-call(s32[10]{0:T(128)S(1)} %dynamic-slice_bitcast_fusion.info_ref, f32[1032,256]{1,0:T(8,128)S(1)} %shard_map.37.refs_0_, f32[1032,256]{1,0:T(8,128)} %collective-permute-done.refs_1_, f32[1032,256]{1,0:T(8,128)} %collective-permute-done.1.refs_2_, f32[1032,256]{1,0:T(8,128)} %collective-permute-done.2.refs_3_, ...), custom_call_target="tpu_custom_call" | custom-call | flops 1000000000 | bytes 20971520 | tf_op jit(solution)/shard_map/pallas_call | solution.py:289
  (1 shorter events, 0.0 us)
Async XLA Ops:
  0.0 1.2 %copy-start = (f32[1024,256]{1,0:T(8,128)S(1)}, f32[1024,256]{1,0:T(8,128)}, u32[]{:S(2)}) copy-start(f32[1024,256]{1,0:T(8,128)} %data_ref.1) | copy-start | bytes 3145732
  1.2 0.7 copy-start.1
  2.0 26.2 %collective-permute-start.6 = (f32[1032,256]{1,0:T(8,128)S(1)}, f32[1032,256]{1,0:T(8,128)S(1)}, u32[]{:S(2)}, u32[]{:S(2)}) collective-permute-start(f32[1032,256]{1,0:T(8,128)S(1)} %shard_map.37.refs_0_), channel_id=1, source_target_pairs={{16,17},{17,18},{18,19},{19,16},{20,21},{21,22},{22,23},{23,20},{2... | collective-permute-start | bytes 3170312 | tf_op jit(solution)/shard_map/ppermute | solution.py:281
  5.2 36.3 %collective-permute-start.5 = (f32[1032,256]{1,0:T(8,128)S(1)}, f32[1032,256]{1,0:T(8,128)S(1)}, u32[]{:S(2)}, u32[]{:S(2)}) collective-permute-start(f32[1032,256]{1,0:T(8,128)S(1)} %shard_map.37.refs_0_), channel_id=1, source_target_pairs={{4,7},{5,4},{6,5},{7,6},{8,11},{9,8},{10,9},{11,10},{28,31},{29,28... | collective-permute-start | bytes 3170312 | tf_op jit(solution)/shard_map/ppermute | solution.py:281
  7.3 48.1 %collective-permute-start.1 = (f32[1032,256]{1,0:T(8,128)S(1)}, f32[1032,256]{1,0:T(8,128)}, u32[]{:S(2)}, u32[]{:S(2)}) collective-permute-start(f32[1032,256]{1,0:T(8,128)S(1)} %shard_map.37.refs_0_), channel_id=1, source_target_pairs={{8,0},{17,1},{26,2},{12,4},{21,5},{30,6},{16,8},{25,9},{2,10},{20,... | collective-permute-start | bytes 3170312 | tf_op jit(solution)/shard_map/ppermute | solution.py:281
  7.6 50.1 %collective-permute-start = (f32[1032,256]{1,0:T(8,128)S(1)}, f32[1032,256]{1,0:T(8,128)}, u32[]{:S(2)}, u32[]{:S(2)}) collective-permute-start(f32[1032,256]{1,0:T(8,128)S(1)} %shard_map.37.refs_0_), channel_id=1, source_target_pairs={{9,1},{18,2},{27,3},{13,5},{22,6},{31,7},{17,9},{26,10},{3,11},{21... | collective-permute-start | bytes 3170312 | tf_op jit(solution)/shard_map/ppermute | solution.py:281
  9.6 51.9 %collective-permute-start.2 = (f32[1032,256]{1,0:T(8,128)S(1)}, f32[1032,256]{1,0:T(8,128)}, u32[]{:S(2)}, u32[]{:S(2)}) collective-permute-start(f32[1032,256]{1,0:T(8,128)S(1)} %shard_map.37.refs_0_), channel_id=1, source_target_pairs={{16,4},{25,5},{2,6},{11,7},{24,12},{1,13},{10,14},{19,15},{0,20},{... | collective-permute-start | bytes 3170312 | tf_op jit(solution)/shard_map/ppermute | solution.py:281
  28.2 33.2 %collective-permute-start.8 = (f32[1032,256]{1,0:T(8,128)S(1)}, f32[1032,256]{1,0:T(8,128)}, u32[]{:S(2)}, u32[]{:S(2)}) collective-permute-start(f32[1032,256]{1,0:T(8,128)S(1)} %collective-permute-done.6.refs_7_), channel_id=1, source_target_pairs={{16,17},{17,18},{18,19},{19,16},{20,21},{21,22},{22,23},{23,20},{1... | collective-permute-start | bytes 3170312 | tf_op jit(solution)/shard_map/ppermute | solution.py:281
  41.5 19.9 %collective-permute-start.7 = (f32[1032,256]{1,0:T(8,128)S(1)}, f32[1032,256]{1,0:T(8,128)}, u32[]{:S(2)}, u32[]{:S(2)}) collective-permute-start(f32[1032,256]{1,0:T(8,128)S(1)} %collective-permute-done.5.refs_6_), channel_id=1, source_target_pairs={{4,7},{5,4},{6,5},{7,6},{8,11},{9,8},{10,9},{11,10},{13,12},{14,13... | collective-permute-start | bytes 3170312 | tf_op jit(solution)/shard_map/ppermute | solution.py:281
  55.4 6.0 %collective-permute-start.4 = (f32[1032,256]{1,0:T(8,128)}, f32[1032,256]{1,0:T(8,128)}, u32[]{:S(2)}, u32[]{:S(2)}) collective-permute-start(f32[1032,256]{1,0:T(8,128)} %collective-permute-done.1.refs_2_), channel_id=1, source_target_pairs={{4,0},{5,1},{6,2},{0,4},{1,5},{2,6},{12,8},{13,9},{14,10},{8,12},{... | collective-permute-start | bytes 3170312 | tf_op jit(solution)/shard_map/ppermute | solution.py:281
  57.8 4.6 %collective-permute-start.3 = (f32[1032,256]{1,0:T(8,128)}, f32[1032,256]{1,0:T(8,128)}, u32[]{:S(2)}, u32[]{:S(2)}) collective-permute-start(f32[1032,256]{1,0:T(8,128)} %collective-permute-done.refs_1_), channel_id=1, source_target_pairs={{5,1},{6,2},{7,3},{13,9},{14,10},{15,11},{21,17},{22,18},{23,19},{... | collective-permute-start | bytes 3170312 | tf_op jit(solution)/shard_map/ppermute | solution.py:281

commit v6 on v5

--- a/solution.py
+++ b/solution.py
@@ -173,9 +173,7 @@
     to_scalars.wait()
 
     part_rows = rb // PARTS
-    for u in range(UNROLL):
-        codes[u] = STEPS << 24
-    bounds = [jnp.int32(UNROLL)]
+    bounds = [jnp.int32(0)]
     for part in range(PARTS):
         def listed(i, place):
             row_codes = [scalars[line, part * part_rows + i] for line in range(slots * w)]
@@ -185,7 +183,7 @@
             return place
 
         bounds.append(lax.fori_loop(0, part_rows, listed, bounds[-1]))
-    for u in range(2 * UNROLL):
+    for u in range(UNROLL):
         codes[bounds[-1] + u] = STEPS << 24
 
     for step in range(STEPS):
@@ -195,7 +193,6 @@
         def _():
             pltpu.make_async_copy(left_bufs[0], left.at[slot], lsem.at[slot]).wait()
 
-    low = lax.broadcasted_iota(jnp.int32, (BS, 2 * BS), 1) < BS
     half = lax.broadcasted_iota(jnp.int32, (BS, 2 * BS), 1) // BS
 
     def block_at(index):
@@ -205,14 +202,15 @@
         slot = (code >> 8) & 15
         x = left[(code >> 12) & 15, block_at((code >> 16) & 255), pl.ds(pl.multiple_of((slot >> 1) * 2 * BS, 2 * BS), 2 * BS)]
         both = jnp.where(half == (slot & 1), x, pltpu.roll(x, BS, 1))
-        hi = both.astype(jnp.bfloat16).astype(jnp.float32)
-        lhs = jnp.where(low, hi, both - hi).astype(jnp.bfloat16)
-        lhs = jnp.concatenate([lhs, lhs], axis=1)
+        hi = both.astype(jnp.bfloat16)
+        lo = (both - hi.astype(jnp.float32)).astype(jnp.bfloat16)
         y = right[code >> 24, block_at(code & 255), :]
-        hi = y.astype(jnp.bfloat16)
-        lo = (y - hi.astype(jnp.float32)).astype(jnp.bfloat16)
-        rhs = jnp.concatenate([hi, hi, lo, lo], axis=0)
-        return jnp.dot(lhs, rhs, preferred_element_type=jnp.float32)
+        right_hi = y.astype(jnp.bfloat16)
+        right_lo = (y - right_hi.astype(jnp.float32)).astype(jnp.bfloat16)
+        lhs = jnp.concatenate([hi, lo], axis=0)
+        rhs = jnp.concatenate([right_hi, right_lo], axis=0)
+        terms = jnp.dot(lhs, rhs, preferred_element_type=jnp.float32)
+        return terms[:BS] + terms[BS:]
 
     def add(code, product):
         rows_at = block_at((code >> 16) & 255)
@@ -236,16 +234,31 @@
         at = pl.ds(part * part_rows * BS, part_rows * BS)
         return pltpu.make_async_copy(acc.at[at], out_ref.at[at], osem.at[part])
 
-    groups = [jnp.int32(0)] + [(bound + UNROLL - 1) // UNROLL for bound in bounds[1:]]
+    def products(group):
+        for u in range(UNROLL):
+            value[u] = product(codes[group * UNROLL + u])
+
+    def sums(group):
+        for u in range(UNROLL):
+            add(codes[group * UNROLL + u], value[u])
+
+    ends = [(bound + UNROLL - 1) // UNROLL for bound in bounds]
+    last = jnp.maximum(ends[-1] - 1, 0)
+    products(0)
     for part in range(PARTS):
-        @pl.loop(groups[part], groups[part + 1])
+        @pl.loop(jnp.minimum(ends[part], last), jnp.minimum(ends[part + 1], last))
         def _(group):
-            for u in range(UNROLL):
-                add(codes[group * UNROLL + u], value[u])
-            for u in range(UNROLL):
-                value[u] = product(codes[(group + 1) * UNROLL + u])
-
-        out_copy(part).start()
+            sums(group)
+            products(group + 1)
+
+        @pl.when(ends[part + 1] <= last)
+        def _():
+            out_copy(part).start()
+    sums(last)
+    for part in range(PARTS):
+        @pl.when(ends[part + 1] > last)
+        def _():
+            out_copy(part).start()
     for part in range(PARTS):
         out_copy(part).wait()
 

time: 72.9 us -> 72.2 us (level)
  Pallas kernels: 10.6 us -> 9.22 us
    pallas_call x1, Pallas kernels: 10.5 us -> 9.12 us  [local(): pl.pallas_call(functools.partial(product_kernel, slots, n_row, ratio, rb,...]
where the time goes in v6:
time: 72.2 us; the launch traced here: 71.5 us
  waiting for transfers between devices  42.1 us (58%)
  starting transfers between devices  17.5 us (24%)
  Pallas kernels  9.22 us (13%)
  local copies, waits for them, and re-layouts  2.59 us (4%)
    ppermute x9, waiting for transfers between devices, carry(): bufs.append(lax.ppermute(bufs[source], ('row', 'col'), flat))  42.1 us
    ppermute x9, starting transfers between devices, carry(): bufs.append(lax.ppermute(bufs[source], ('row', 'col'), flat))  17.5 us
    pallas_call x1, Pallas kernels, local(): pl.pallas_call(functools.partial(product_kernel, slots, n_row, ratio, rb,...  9.12 us
    unnamed x4, local copies, waits for them, and re-layouts  1.91 us
  transfers between devices with their start and end apart: 9, of which 4 were waited for; matrix products, arithmetic and copies ran while one was open for 1% of the time, Pallas kernels for 0%

profile of v6, /device:TPU:15, one launch (start us, length us, event | category | flops | bytes accessed | tf_op | source)
XLA Modules:
  0.0 71.5 jit_solution(2424605979813471087)
XLA Ops:
  0.0 0.0 copy-start
  0.0 1.2 %copy-done = f32[1024,256]{1,0:T(8,128)S(1)} copy-done((f32[1024,256]{1,0:T(8,128)S(1)}, f32[1024,256]{1,0:T(8,128)}, u32[]{:S(2)}) %copy-start) | copy-done | bytes 1048600
  1.2 0.7 copy-done.1
  1.9 0.1 shard_map.37.refs_0_
  2.0 3.2 %collective-permute-start.6 = (f32[1032,256]{1,0:T(8,128)S(1)}, f32[1032,256]{1,0:T(8,128)S(1)}, u32[]{:S(2)}, u32[]{:S(2)}) collective-permute-start(f32[1032,256]{1,0:T(8,128)S(1)} %shard_map.37.refs_0_), channel_id=1, source_target_pairs={{16,17},{17,18},{18,19},{19,16},{20,21},{21,22},{22,23},{23,20},{2... | collective-permute-start | bytes 3170312 | tf_op jit(solution)/shard_map/ppermute | solution.py:294
  5.2 2.1 %collective-permute-start.5 = (f32[1032,256]{1,0:T(8,128)S(1)}, f32[1032,256]{1,0:T(8,128)S(1)}, u32[]{:S(2)}, u32[]{:S(2)}) collective-permute-start(f32[1032,256]{1,0:T(8,128)S(1)} %shard_map.37.refs_0_), channel_id=1, source_target_pairs={{4,7},{5,4},{6,5},{7,6},{8,11},{9,8},{10,9},{11,10},{28,31},{29,28... | collective-permute-start | bytes 3170312 | tf_op jit(solution)/shard_map/ppermute | solution.py:294
  7.3 0.3 collective-permute-start.1
  7.6 1.9 %collective-permute-start = (f32[1032,256]{1,0:T(8,128)S(1)}, f32[1032,256]{1,0:T(8,128)}, u32[]{:S(2)}, u32[]{:S(2)}) collective-permute-start(f32[1032,256]{1,0:T(8,128)S(1)} %shard_map.37.refs_0_), channel_id=1, source_target_pairs={{9,1},{18,2},{27,3},{13,5},{22,6},{31,7},{17,9},{26,10},{3,11},{21... | collective-permute-start | bytes 3170312 | tf_op jit(solution)/shard_map/ppermute | solution.py:294
  9.6 1.3 %collective-permute-start.2 = (f32[1032,256]{1,0:T(8,128)S(1)}, f32[1032,256]{1,0:T(8,128)}, u32[]{:S(2)}, u32[]{:S(2)}) collective-permute-start(f32[1032,256]{1,0:T(8,128)S(1)} %shard_map.37.refs_0_), channel_id=1, source_target_pairs={{16,4},{25,5},{2,6},{11,7},{24,12},{1,13},{10,14},{19,15},{0,20},{... | collective-permute-start | bytes 3170312 | tf_op jit(solution)/shard_map/ppermute | solution.py:294
  10.9 17.3 %collective-permute-done.6.refs_7_ = f32[1032,256]{1,0:T(8,128)S(1)} collective-permute-done((f32[1032,256]{1,0:T(8,128)S(1)}, f32[1032,256]{1,0:T(8,128)S(1)}, u32[]{:S(2)}, u32[]{:S(2)}) %collective-permute-start.6) | collective-permute-done | bytes 1056800 | tf_op jit(solution)/shard_map/ppermute | solution.py:294
  28.2 1.7 %collective-permute-start.8 = (f32[1032,256]{1,0:T(8,128)S(1)}, f32[1032,256]{1,0:T(8,128)}, u32[]{:S(2)}, u32[]{:S(2)}) collective-permute-start(f32[1032,256]{1,0:T(8,128)S(1)} %collective-permute-done.6.refs_7_), channel_id=1, source_target_pairs={{16,17},{17,18},{18,19},{19,16},{20,21},{21,22},{22,23},{23,20},{1... | collective-permute-start | bytes 3170312 | tf_op jit(solution)/shard_map/ppermute | solution.py:294
  29.9 11.7 %collective-permute-done.5.refs_6_ = f32[1032,256]{1,0:T(8,128)S(1)} collective-permute-done((f32[1032,256]{1,0:T(8,128)S(1)}, f32[1032,256]{1,0:T(8,128)S(1)}, u32[]{:S(2)}, u32[]{:S(2)}) %collective-permute-start.5) | collective-permute-done | bytes 1056800 | tf_op jit(solution)/shard_map/ppermute | solution.py:294
  41.5 1.7 %collective-permute-start.7 = (f32[1032,256]{1,0:T(8,128)S(1)}, f32[1032,256]{1,0:T(8,128)}, u32[]{:S(2)}, u32[]{:S(2)}) collective-permute-start(f32[1032,256]{1,0:T(8,128)S(1)} %collective-permute-done.5.refs_6_), channel_id=1, source_target_pairs={{4,7},{5,4},{6,5},{7,6},{8,11},{9,8},{10,9},{11,10},{13,12},{14,13... | collective-permute-start | bytes 3170312 | tf_op jit(solution)/shard_map/ppermute | solution.py:294
  43.2 12.2 %collective-permute-done.1.refs_2_ = f32[1032,256]{1,0:T(8,128)} collective-permute-done((f32[1032,256]{1,0:T(8,128)S(1)}, f32[1032,256]{1,0:T(8,128)}, u32[]{:S(2)}, u32[]{:S(2)}) %collective-permute-start.1) | collective-permute-done | bytes 1056800 | tf_op jit(solution)/shard_map/ppermute | solution.py:294
  55.4 2.4 %collective-permute-start.4 = (f32[1032,256]{1,0:T(8,128)}, f32[1032,256]{1,0:T(8,128)}, u32[]{:S(2)}, u32[]{:S(2)}) collective-permute-start(f32[1032,256]{1,0:T(8,128)} %collective-permute-done.1.refs_2_), channel_id=1, source_target_pairs={{4,0},{5,1},{6,2},{0,4},{1,5},{2,6},{12,8},{13,9},{14,10},{8,12},{... | collective-permute-start | bytes 3170312 | tf_op jit(solution)/shard_map/ppermute | solution.py:294
  57.8 0.0 collective-permute-done.refs_1_
  57.8 3.0 %collective-permute-start.3 = (f32[1032,256]{1,0:T(8,128)}, f32[1032,256]{1,0:T(8,128)}, u32[]{:S(2)}, u32[]{:S(2)}) collective-permute-start(f32[1032,256]{1,0:T(8,128)} %collective-permute-done.refs_1_), channel_id=1, source_target_pairs={{5,1},{6,2},{7,3},{13,9},{14,10},{15,11},{21,17},{22,18},{23,19},{... | collective-permute-start | bytes 3170312 | tf_op jit(solution)/shard_map/ppermute | solution.py:294
  60.7 0.7 dynamic-slice_bitcast_fusion.info_ref
  61.4 0.0 collective-permute-done.2.refs_3_
  61.4 0.0 collective-permute-done.8.refs_9_
  61.4 0.0 collective-permute-done.7.refs_8_
  61.4 0.0 collective-permute-done.4.refs_5_
  61.5 0.9 %collective-permute-done.3.refs_4_ = f32[1032,256]{1,0:T(8,128)} collective-permute-done((f32[1032,256]{1,0:T(8,128)}, f32[1032,256]{1,0:T(8,128)}, u32[]{:S(2)}, u32[]{:S(2)}) %collective-permute-start.3) | collective-permute-done | bytes 1056800 | tf_op jit(solution)/shard_map/ppermute | solution.py:294
  62.4 9.1 %shard_map.38 = f32[1024,2048]{1,0:T(8,128)} custom-call(s32[10]{0:T(128)S(1)} %dynamic-slice_bitcast_fusion.info_ref, f32[1032,256]{1,0:T(8,128)S(1)} %shard_map.37.refs_0_, f32[1032,256]{1,0:T(8,128)} %collective-permute-done.refs_1_, f32[1032,256]{1,0:T(8,128)} %collective-permute-done.1.refs_2_, f32[1032,256]{1,0:T(8,128)} %collective-permute-done.2.refs_3_, ...), custom_call_target="tpu_custom_call" | custom-call | flops 1000000000 | bytes 20971520 | tf_op jit(solution)/shard_map/pallas_call | solution.py:302
  (1 shorter events, 0.0 us)
Async XLA Ops:
  0.0 1.2 %copy-start = (f32[1024,256]{1,0:T(8,128)S(1)}, f32[1024,256]{1,0:T(8,128)}, u32[]{:S(2)}) copy-start(f32[1024,256]{1,0:T(8,128)} %data_ref.1) | copy-start | bytes 3145732
  1.2 0.7 copy-start.1
  2.0 26.2 %collective-permute-start.6 = (f32[1032,256]{1,0:T(8,128)S(1)}, f32[1032,256]{1,0:T(8,128)S(1)}, u32[]{:S(2)}, u32[]{:S(2)}) collective-permute-start(f32[1032,256]{1,0:T(8,128)S(1)} %shard_map.37.refs_0_), channel_id=1, source_target_pairs={{16,17},{17,18},{18,19},{19,16},{20,21},{21,22},{22,23},{23,20},{2... | collective-permute-start | bytes 3170312 | tf_op jit(solution)/shard_map/ppermute | solution.py:294
  5.2 36.3 %collective-permute-start.5 = (f32[1032,256]{1,0:T(8,128)S(1)}, f32[1032,256]{1,0:T(8,128)S(1)}, u32[]{:S(2)}, u32[]{:S(2)}) collective-permute-start(f32[1032,256]{1,0:T(8,128)S(1)} %shard_map.37.refs_0_), channel_id=1, source_target_pairs={{4,7},{5,4},{6,5},{7,6},{8,11},{9,8},{10,9},{11,10},{28,31},{29,28... | collective-permute-start | bytes 3170312 | tf_op jit(solution)/shard_map/ppermute | solution.py:294
  7.3 48.1 %collective-permute-start.1 = (f32[1032,256]{1,0:T(8,128)S(1)}, f32[1032,256]{1,0:T(8,128)}, u32[]{:S(2)}, u32[]{:S(2)}) collective-permute-start(f32[1032,256]{1,0:T(8,128)S(1)} %shard_map.37.refs_0_), channel_id=1, source_target_pairs={{8,0},{17,1},{26,2},{12,4},{21,5},{30,6},{16,8},{25,9},{2,10},{20,... | collective-permute-start | bytes 3170312 | tf_op jit(solution)/shard_map/ppermute | solution.py:294
  7.6 50.1 %collective-permute-start = (f32[1032,256]{1,0:T(8,128)S(1)}, f32[1032,256]{1,0:T(8,128)}, u32[]{:S(2)}, u32[]{:S(2)}) collective-permute-start(f32[1032,256]{1,0:T(8,128)S(1)} %shard_map.37.refs_0_), channel_id=1, source_target_pairs={{9,1},{18,2},{27,3},{13,5},{22,6},{31,7},{17,9},{26,10},{3,11},{21... | collective-permute-start | bytes 3170312 | tf_op jit(solution)/shard_map/ppermute | solution.py:294
  9.6 51.9 %collective-permute-start.2 = (f32[1032,256]{1,0:T(8,128)S(1)}, f32[1032,256]{1,0:T(8,128)}, u32[]{:S(2)}, u32[]{:S(2)}) collective-permute-start(f32[1032,256]{1,0:T(8,128)S(1)} %shard_map.37.refs_0_), channel_id=1, source_target_pairs={{16,4},{25,5},{2,6},{11,7},{24,12},{1,13},{10,14},{19,15},{0,20},{... | collective-permute-start | bytes 3170312 | tf_op jit(solution)/shard_map/ppermute | solution.py:294
  28.2 33.2 %collective-permute-start.8 = (f32[1032,256]{1,0:T(8,128)S(1)}, f32[1032,256]{1,0:T(8,128)}, u32[]{:S(2)}, u32[]{:S(2)}) collective-permute-start(f32[1032,256]{1,0:T(8,128)S(1)} %collective-permute-done.6.refs_7_), channel_id=1, source_target_pairs={{16,17},{17,18},{18,19},{19,16},{20,21},{21,22},{22,23},{23,20},{1... | collective-permute-start | bytes 3170312 | tf_op jit(solution)/shard_map/ppermute | solution.py:294
  41.5 19.9 %collective-permute-start.7 = (f32[1032,256]{1,0:T(8,128)S(1)}, f32[1032,256]{1,0:T(8,128)}, u32[]{:S(2)}, u32[]{:S(2)}) collective-permute-start(f32[1032,256]{1,0:T(8,128)S(1)} %collective-permute-done.5.refs_6_), channel_id=1, source_target_pairs={{4,7},{5,4},{6,5},{7,6},{8,11},{9,8},{10,9},{11,10},{13,12},{14,13... | collective-permute-start | bytes 3170312 | tf_op jit(solution)/shard_map/ppermute | solution.py:294
  55.4 6.0 %collective-permute-start.4 = (f32[1032,256]{1,0:T(8,128)}, f32[1032,256]{1,0:T(8,128)}, u32[]{:S(2)}, u32[]{:S(2)}) collective-permute-start(f32[1032,256]{1,0:T(8,128)} %collective-permute-done.1.refs_2_), channel_id=1, source_target_pairs={{4,0},{5,1},{6,2},{0,4},{1,5},{2,6},{12,8},{13,9},{14,10},{8,12},{... | collective-permute-start | bytes 3170312 | tf_op jit(solution)/shard_map/ppermute | solution.py:294
  57.8 4.6 %collective-permute-start.3 = (f32[1032,256]{1,0:T(8,128)}, f32[1032,256]{1,0:T(8,128)}, u32[]{:S(2)}, u32[]{:S(2)}) collective-permute-start(f32[1032,256]{1,0:T(8,128)} %collective-permute-done.refs_1_), channel_id=1, source_target_pairs={{5,1},{6,2},{7,3},{13,9},{14,10},{15,11},{21,17},{22,18},{23,19},{... | collective-permute-start | bytes 3170312 | tf_op jit(solution)/shard_map/ppermute | solution.py:294

commit v7 on v6

--- a/solution.py
+++ b/solution.py
@@ -202,15 +202,14 @@
         slot = (code >> 8) & 15
         x = left[(code >> 12) & 15, block_at((code >> 16) & 255), pl.ds(pl.multiple_of((slot >> 1) * 2 * BS, 2 * BS), 2 * BS)]
         both = jnp.where(half == (slot & 1), x, pltpu.roll(x, BS, 1))
-        hi = both.astype(jnp.bfloat16)
-        lo = (both - hi.astype(jnp.float32)).astype(jnp.bfloat16)
+        hi = both.astype(jnp.bfloat16).astype(jnp.float32)
+        lhs = jnp.where(half == 0, hi, both - hi).astype(jnp.bfloat16)
         y = right[code >> 24, block_at(code & 255), :]
-        right_hi = y.astype(jnp.bfloat16)
-        right_lo = (y - right_hi.astype(jnp.float32)).astype(jnp.bfloat16)
-        lhs = jnp.concatenate([hi, lo], axis=0)
-        rhs = jnp.concatenate([right_hi, right_lo], axis=0)
-        terms = jnp.dot(lhs, rhs, preferred_element_type=jnp.float32)
-        return terms[:BS] + terms[BS:]
+        hi = y.astype(jnp.bfloat16)
+        lo = (y - hi.astype(jnp.float32)).astype(jnp.bfloat16)
+        lhs = jnp.concatenate([lhs, lhs], axis=1)
+        rhs = jnp.concatenate([hi, hi, lo, lo], axis=0)
+        return jnp.dot(lhs, rhs, preferred_element_type=jnp.float32)
 
     def add(code, product):
         rows_at = block_at((code >> 16) & 255)

time: 72.2 us -> 72.3 us (level)
  no operation moved by 1% of the time
where the time goes in v7:
time: 72.3 us; the launch traced here: 72.1 us
  waiting for transfers between devices  42.1 us (58%)
  starting transfers between devices  17.5 us (24%)
  Pallas kernels  9.81 us (14%)
  local copies, waits for them, and re-layouts  2.59 us (4%)
    ppermute x9, waiting for transfers between devices, carry(): bufs.append(lax.ppermute(bufs[source], ('row', 'col'), flat))  42.1 us
    ppermute x9, starting transfers between devices, carry(): bufs.append(lax.ppermute(bufs[source], ('row', 'col'), flat))  17.5 us
    pallas_call x1, Pallas kernels, local(): pl.pallas_call(functools.partial(product_kernel, slots, n_row, ratio, rb,...  9.72 us
    unnamed x4, local copies, waits for them, and re-layouts  1.91 us
  transfers between devices with their start and end apart: 9, of which 4 were waited for; matrix products, arithmetic and copies ran while one was open for 1% of the time, Pallas kernels for 0%

profile of v7, /device:TPU:15, one launch (start us, length us, event | category | flops | bytes accessed | tf_op | source)
XLA Modules:
  0.0 72.1 jit_solution(4445314358951661486)
XLA Ops:
  0.0 1.2 %copy-done = f32[1024,256]{1,0:T(8,128)S(1)} copy-done((f32[1024,256]{1,0:T(8,128)S(1)}, f32[1024,256]{1,0:T(8,128)}, u32[]{:S(2)}) %copy-start) | copy-done | bytes 1048600
  1.2 0.0 copy-start.1
  1.2 0.7 copy-done.1
  1.9 0.1 shard_map.37.refs_0_
  2.0 3.2 %collective-permute-start.6 = (f32[1032,256]{1,0:T(8,128)S(1)}, f32[1032,256]{1,0:T(8,128)S(1)}, u32[]{:S(2)}, u32[]{:S(2)}) collective-permute-start(f32[1032,256]{1,0:T(8,128)S(1)} %shard_map.37.refs_0_), channel_id=1, source_target_pairs={{16,17},{17,18},{18,19},{19,16},{20,21},{21,22},{22,23},{23,20},{2... | collective-permute-start | bytes 3170312 | tf_op jit(solution)/shard_map/ppermute | solution.py:293
  5.2 2.1 %collective-permute-start.5 = (f32[1032,256]{1,0:T(8,128)S(1)}, f32[1032,256]{1,0:T(8,128)S(1)}, u32[]{:S(2)}, u32[]{:S(2)}) collective-permute-start(f32[1032,256]{1,0:T(8,128)S(1)} %shard_map.37.refs_0_), channel_id=1, source_target_pairs={{4,7},{5,4},{6,5},{7,6},{8,11},{9,8},{10,9},{11,10},{28,31},{29,28... | collective-permute-start | bytes 3170312 | tf_op jit(solution)/shard_map/ppermute | solution.py:293
  7.3 0.3 collective-permute-start.1
  7.6 1.9 %collective-permute-start = (f32[1032,256]{1,0:T(8,128)S(1)}, f32[1032,256]{1,0:T(8,128)}, u32[]{:S(2)}, u32[]{:S(2)}) collective-permute-start(f32[1032,256]{1,0:T(8,128)S(1)} %shard_map.37.refs_0_), channel_id=1, source_target_pairs={{9,1},{18,2},{27,3},{13,5},{22,6},{31,7},{17,9},{26,10},{3,11},{21... | collective-permute-start | bytes 3170312 | tf_op jit(solution)/shard_map/ppermute | solution.py:293
  9.6 1.3 %collective-permute-start.2 = (f32[1032,256]{1,0:T(8,128)S(1)}, f32[1032,256]{1,0:T(8,128)}, u32[]{:S(2)}, u32[]{:S(2)}) collective-permute-start(f32[1032,256]{1,0:T(8,128)S(1)} %shard_map.37.refs_0_), channel_id=1, source_target_pairs={{16,4},{25,5},{2,6},{11,7},{24,12},{1,13},{10,14},{19,15},{0,20},{... | collective-permute-start | bytes 3170312 | tf_op jit(solution)/shard_map/ppermute | solution.py:293
  10.9 17.3 %collective-permute-done.6.refs_7_ = f32[1032,256]{1,0:T(8,128)S(1)} collective-permute-done((f32[1032,256]{1,0:T(8,128)S(1)}, f32[1032,256]{1,0:T(8,128)S(1)}, u32[]{:S(2)}, u32[]{:S(2)}) %collective-permute-start.6) | collective-permute-done | bytes 1056800 | tf_op jit(solution)/shard_map/ppermute | solution.py:293
  28.2 1.7 %collective-permute-start.8 = (f32[1032,256]{1,0:T(8,128)S(1)}, f32[1032,256]{1,0:T(8,128)}, u32[]{:S(2)}, u32[]{:S(2)}) collective-permute-start(f32[1032,256]{1,0:T(8,128)S(1)} %collective-permute-done.6.refs_7_), channel_id=1, source_target_pairs={{16,17},{17,18},{18,19},{19,16},{20,21},{21,22},{22,23},{23,20},{1... | collective-permute-start | bytes 3170312 | tf_op jit(solution)/shard_map/ppermute | solution.py:293
  29.9 11.7 %collective-permute-done.5.refs_6_ = f32[1032,256]{1,0:T(8,128)S(1)} collective-permute-done((f32[1032,256]{1,0:T(8,128)S(1)}, f32[1032,256]{1,0:T(8,128)S(1)}, u32[]{:S(2)}, u32[]{:S(2)}) %collective-permute-start.5) | collective-permute-done | bytes 1056800 | tf_op jit(solution)/shard_map/ppermute | solution.py:293
  41.5 1.7 %collective-permute-start.7 = (f32[1032,256]{1,0:T(8,128)S(1)}, f32[1032,256]{1,0:T(8,128)}, u32[]{:S(2)}, u32[]{:S(2)}) collective-permute-start(f32[1032,256]{1,0:T(8,128)S(1)} %collective-permute-done.5.refs_6_), channel_id=1, source_target_pairs={{4,7},{5,4},{6,5},{7,6},{8,11},{9,8},{10,9},{11,10},{13,12},{14,13... | collective-permute-start | bytes 3170312 | tf_op jit(solution)/shard_map/ppermute | solution.py:293
  43.2 12.2 %collective-permute-done.1.refs_2_ = f32[1032,256]{1,0:T(8,128)} collective-permute-done((f32[1032,256]{1,0:T(8,128)S(1)}, f32[1032,256]{1,0:T(8,128)}, u32[]{:S(2)}, u32[]{:S(2)}) %collective-permute-start.1) | collective-permute-done | bytes 1056800 | tf_op jit(solution)/shard_map/ppermute | solution.py:293
  55.4 2.4 %collective-permute-start.4 = (f32[1032,256]{1,0:T(8,128)}, f32[1032,256]{1,0:T(8,128)}, u32[]{:S(2)}, u32[]{:S(2)}) collective-permute-start(f32[1032,256]{1,0:T(8,128)} %collective-permute-done.1.refs_2_), channel_id=1, source_target_pairs={{4,0},{5,1},{6,2},{0,4},{1,5},{2,6},{12,8},{13,9},{14,10},{8,12},{... | collective-permute-start | bytes 3170312 | tf_op jit(solution)/shard_map/ppermute | solution.py:293
  57.8 0.0 collective-permute-done.refs_1_
  57.8 3.0 %collective-permute-start.3 = (f32[1032,256]{1,0:T(8,128)}, f32[1032,256]{1,0:T(8,128)}, u32[]{:S(2)}, u32[]{:S(2)}) collective-permute-start(f32[1032,256]{1,0:T(8,128)} %collective-permute-done.refs_1_), channel_id=1, source_target_pairs={{5,1},{6,2},{7,3},{13,9},{14,10},{15,11},{21,17},{22,18},{23,19},{... | collective-permute-start | bytes 3170312 | tf_op jit(solution)/shard_map/ppermute | solution.py:293
  60.7 0.7 dynamic-slice_bitcast_fusion.info_ref
  61.4 0.0 collective-permute-done.2.refs_3_
  61.4 0.0 collective-permute-done.8.refs_9_
  61.4 0.0 collective-permute-done.7.refs_8_
  61.4 0.0 collective-permute-done.4.refs_5_
  61.5 0.9 %collective-permute-done.3.refs_4_ = f32[1032,256]{1,0:T(8,128)} collective-permute-done((f32[1032,256]{1,0:T(8,128)}, f32[1032,256]{1,0:T(8,128)}, u32[]{:S(2)}, u32[]{:S(2)}) %collective-permute-start.3) | collective-permute-done | bytes 1056800 | tf_op jit(solution)/shard_map/ppermute | solution.py:293
  62.4 9.7 %shard_map.38 = f32[1024,2048]{1,0:T(8,128)} custom-call(s32[10]{0:T(128)S(1)} %dynamic-slice_bitcast_fusion.info_ref, f32[1032,256]{1,0:T(8,128)S(1)} %shard_map.37.refs_0_, f32[1032,256]{1,0:T(8,128)} %collective-permute-done.refs_1_, f32[1032,256]{1,0:T(8,128)} %collective-permute-done.1.refs_2_, f32[1032,256]{1,0:T(8,128)} %collective-permute-done.2.refs_3_, ...), custom_call_target="tpu_custom_call" | custom-call | flops 1000000000 | bytes 20971520 | tf_op jit(solution)/shard_map/pallas_call | solution.py:301
  (1 shorter events, 0.0 us)
Async XLA Ops:
  0.0 1.2 %copy-start = (f32[1024,256]{1,0:T(8,128)S(1)}, f32[1024,256]{1,0:T(8,128)}, u32[]{:S(2)}) copy-start(f32[1024,256]{1,0:T(8,128)} %data_ref.1) | copy-start | bytes 3145732
  1.2 0.7 copy-start.1
  2.0 26.2 %collective-permute-start.6 = (f32[1032,256]{1,0:T(8,128)S(1)}, f32[1032,256]{1,0:T(8,128)S(1)}, u32[]{:S(2)}, u32[]{:S(2)}) collective-permute-start(f32[1032,256]{1,0:T(8,128)S(1)} %shard_map.37.refs_0_), channel_id=1, source_target_pairs={{16,17},{17,18},{18,19},{19,16},{20,21},{21,22},{22,23},{23,20},{2... | collective-permute-start | bytes 3170312 | tf_op jit(solution)/shard_map/ppermute | solution.py:293
  5.2 36.3 %collective-permute-start.5 = (f32[1032,256]{1,0:T(8,128)S(1)}, f32[1032,256]{1,0:T(8,128)S(1)}, u32[]{:S(2)}, u32[]{:S(2)}) collective-permute-start(f32[1032,256]{1,0:T(8,128)S(1)} %shard_map.37.refs_0_), channel_id=1, source_target_pairs={{4,7},{5,4},{6,5},{7,6},{8,11},{9,8},{10,9},{11,10},{28,31},{29,28... | collective-permute-start | bytes 3170312 | tf_op jit(solution)/shard_map/ppermute | solution.py:293
  7.3 48.1 %collective-permute-start.1 = (f32[1032,256]{1,0:T(8,128)S(1)}, f32[1032,256]{1,0:T(8,128)}, u32[]{:S(2)}, u32[]{:S(2)}) collective-permute-start(f32[1032,256]{1,0:T(8,128)S(1)} %shard_map.37.refs_0_), channel_id=1, source_target_pairs={{8,0},{17,1},{26,2},{12,4},{21,5},{30,6},{16,8},{25,9},{2,10},{20,... | collective-permute-start | bytes 3170312 | tf_op jit(solution)/shard_map/ppermute | solution.py:293
  7.6 50.1 %collective-permute-start = (f32[1032,256]{1,0:T(8,128)S(1)}, f32[1032,256]{1,0:T(8,128)}, u32[]{:S(2)}, u32[]{:S(2)}) collective-permute-start(f32[1032,256]{1,0:T(8,128)S(1)} %shard_map.37.refs_0_), channel_id=1, source_target_pairs={{9,1},{18,2},{27,3},{13,5},{22,6},{31,7},{17,9},{26,10},{3,11},{21... | collective-permute-start | bytes 3170312 | tf_op jit(solution)/shard_map/ppermute | solution.py:293
  9.6 51.9 %collective-permute-start.2 = (f32[1032,256]{1,0:T(8,128)S(1)}, f32[1032,256]{1,0:T(8,128)}, u32[]{:S(2)}, u32[]{:S(2)}) collective-permute-start(f32[1032,256]{1,0:T(8,128)S(1)} %shard_map.37.refs_0_), channel_id=1, source_target_pairs={{16,4},{25,5},{2,6},{11,7},{24,12},{1,13},{10,14},{19,15},{0,20},{... | collective-permute-start | bytes 3170312 | tf_op jit(solution)/shard_map/ppermute | solution.py:293
  28.2 33.2 %collective-permute-start.8 = (f32[1032,256]{1,0:T(8,128)S(1)}, f32[1032,256]{1,0:T(8,128)}, u32[]{:S(2)}, u32[]{:S(2)}) collective-permute-start(f32[1032,256]{1,0:T(8,128)S(1)} %collective-permute-done.6.refs_7_), channel_id=1, source_target_pairs={{16,17},{17,18},{18,19},{19,16},{20,21},{21,22},{22,23},{23,20},{1... | collective-permute-start | bytes 3170312 | tf_op jit(solution)/shard_map/ppermute | solution.py:293
  41.5 19.9 %collective-permute-start.7 = (f32[1032,256]{1,0:T(8,128)S(1)}, f32[1032,256]{1,0:T(8,128)}, u32[]{:S(2)}, u32[]{:S(2)}) collective-permute-start(f32[1032,256]{1,0:T(8,128)S(1)} %collective-permute-done.5.refs_6_), channel_id=1, source_target_pairs={{4,7},{5,4},{6,5},{7,6},{8,11},{9,8},{10,9},{11,10},{13,12},{14,13... | collective-permute-start | bytes 3170312 | tf_op jit(solution)/shard_map/ppermute | solution.py:293
  55.4 6.0 %collective-permute-start.4 = (f32[1032,256]{1,0:T(8,128)}, f32[1032,256]{1,0:T(8,128)}, u32[]{:S(2)}, u32[]{:S(2)}) collective-permute-start(f32[1032,256]{1,0:T(8,128)} %collective-permute-done.1.refs_2_), channel_id=1, source_target_pairs={{4,0},{5,1},{6,2},{0,4},{1,5},{2,6},{12,8},{13,9},{14,10},{8,12},{... | collective-permute-start | bytes 3170312 | tf_op jit(solution)/shard_map/ppermute | solution.py:293
  57.8 4.6 %collective-permute-start.3 = (f32[1032,256]{1,0:T(8,128)}, f32[1032,256]{1,0:T(8,128)}, u32[]{:S(2)}, u32[]{:S(2)}) collective-permute-start(f32[1032,256]{1,0:T(8,128)} %collective-permute-done.refs_1_), channel_id=1, source_target_pairs={{5,1},{6,2},{7,3},{13,9},{14,10},{15,11},{21,17},{22,18},{23,19},{... | collective-permute-start | bytes 3170312 | tf_op jit(solution)/shard_map/ppermute | solution.py:293

commit v8 on v7

--- a/solution.py
+++ b/solution.py
@@ -120,8 +120,8 @@
 
 
 def product_kernel(slots, n_row, ratio, rb, w, n_right, among, info_ref, *refs):
-    out_ref, left, right, acc, value, cols, coded, scalars, codes, lsem, rsem, osem, csem = refs[-13:]
-    right_bufs, left_bufs = refs[:n_right], refs[:1] + refs[n_right:-13]
+    out_ref, left, right, acc, value, cols, coded, scalars, codes, ends, lsem, rsem, osem, csem = refs[-14:]
+    right_bufs, left_bufs = refs[:n_right], refs[:1] + refs[n_right:-14]
     rows, width = left.shape[1] - EXTRA, left.shape[2]
     names = pl.ds(rows, EXTRA)
     for slot in range(slots):
@@ -173,18 +173,17 @@
     to_scalars.wait()
 
     part_rows = rb // PARTS
-    bounds = [jnp.int32(0)]
-    for part in range(PARTS):
-        def listed(i, place):
-            row_codes = [scalars[line, part * part_rows + i] for line in range(slots * w)]
-            for code in row_codes:
-                codes[place] = code
-                place = place + (code >= 0).astype(jnp.int32)
-            return place
-
-        bounds.append(lax.fori_loop(0, part_rows, listed, bounds[-1]))
+
+    def listed(row, place):
+        for code in [scalars[line, row] for line in range(slots * w)]:
+            codes[place] = code
+            place = place + (code >= 0).astype(jnp.int32)
+        ends[row] = (place + UNROLL - 1) // UNROLL
+        return place
+
+    listed_end = lax.fori_loop(0, rb, listed, jnp.int32(0))
     for u in range(UNROLL):
-        codes[bounds[-1] + u] = STEPS << 24
+        codes[listed_end + u] = STEPS << 24
 
     for step in range(STEPS):
         pltpu.make_async_copy(right_bufs[0], right.at[step], rsem.at[step]).wait()
@@ -241,23 +240,24 @@
         for u in range(UNROLL):
             add(codes[group * UNROLL + u], value[u])
 
-    ends = [(bound + UNROLL - 1) // UNROLL for bound in bounds]
-    last = jnp.maximum(ends[-1] - 1, 0)
+    last = jnp.maximum(ends[rb - 1] - 1, 0)
+
+    def leave(group):
+        for part in range(PARTS):
+            @pl.when(jnp.maximum(ends[(part + 1) * part_rows - 1] - 1, 0) == group)
+            def _():
+                out_copy(part).start()
+
     products(0)
-    for part in range(PARTS):
-        @pl.loop(jnp.minimum(ends[part], last), jnp.minimum(ends[part + 1], last))
-        def _(group):
-            sums(group)
-            products(group + 1)
-
-        @pl.when(ends[part + 1] <= last)
-        def _():
-            out_copy(part).start()
+
+    @pl.loop(0, last)
+    def _(group):
+        sums(group)
+        products(group + 1)
+        leave(group)
+
     sums(last)
-    for part in range(PARTS):
-        @pl.when(ends[part + 1] > last)
-        def _():
-            out_copy(part).start()
+    leave(last)
     for part in range(PARTS):
         out_copy(part).wait()
 
@@ -311,7 +311,8 @@
             pltpu.VMEM((slots + STEPS, EXTRA, width), jnp.float32),
             pltpu.VMEM((codings, 128), jnp.int32),
             pltpu.SMEM((codings, 128), jnp.int32),
-            pltpu.SMEM((slots * rb * w + 4 * UNROLL,), jnp.int32),
+            pltpu.SMEM((slots * rb * w + UNROLL,), jnp.int32),
+            pltpu.SMEM((rb,), jnp.int32),
             dma((slots,)),
             dma((STEPS,)),
             dma((PARTS,)),

time: 72.3 us -> 72.3 us (level)
  no operation moved by 1% of the time
where the time goes in v8:
time: 72.3 us; the launch traced here: 71.5 us
  waiting for transfers between devices  42.1 us (58%)
  starting transfers between devices  17.5 us (24%)
  Pallas kernels  9.23 us (13%)
  local copies, waits for them, and re-layouts  2.59 us (4%)
    ppermute x9, waiting for transfers between devices, carry(): bufs.append(lax.ppermute(bufs[source], ('row', 'col'), flat))  42.1 us
    ppermute x9, starting transfers between devices, carry(): bufs.append(lax.ppermute(bufs[source], ('row', 'col'), flat))  17.5 us
    pallas_call x1, Pallas kernels, local(): pl.pallas_call(functools.partial(product_kernel, slots, n_row, ratio, rb,...  9.13 us
    unnamed x4, local copies, waits for them, and re-layouts  1.91 us
  transfers between devices with their start and end apart: 9, of which 4 were waited for; matrix products, arithmetic and copies ran while one was open for 1% of the time, Pallas kernels for 0%

profile of v8, /device:TPU:15, one launch (start us, length us, event | category | flops | bytes accessed | tf_op | source)
XLA Modules:
  0.0 71.5 jit_solution(14198354481398159512)
XLA Ops:
  0.0 0.0 copy-start
  0.0 1.2 %copy-done = f32[1024,256]{1,0:T(8,128)S(1)} copy-done((f32[1024,256]{1,0:T(8,128)S(1)}, f32[1024,256]{1,0:T(8,128)}, u32[]{:S(2)}) %copy-start) | copy-done | bytes 1048600
  1.2 0.7 copy-done.1
  1.9 0.1 shard_map.37.refs_0_
  2.0 3.2 %collective-permute-start.6 = (f32[1032,256]{1,0:T(8,128)S(1)}, f32[1032,256]{1,0:T(8,128)S(1)}, u32[]{:S(2)}, u32[]{:S(2)}) collective-permute-start(f32[1032,256]{1,0:T(8,128)S(1)} %shard_map.37.refs_0_), channel_id=1, source_target_pairs={{16,17},{17,18},{18,19},{19,16},{20,21},{21,22},{22,23},{23,20},{2... | collective-permute-start | bytes 3170312 | tf_op jit(solution)/shard_map/ppermute | solution.py:293
  5.2 2.1 %collective-permute-start.5 = (f32[1032,256]{1,0:T(8,128)S(1)}, f32[1032,256]{1,0:T(8,128)S(1)}, u32[]{:S(2)}, u32[]{:S(2)}) collective-permute-start(f32[1032,256]{1,0:T(8,128)S(1)} %shard_map.37.refs_0_), channel_id=1, source_target_pairs={{4,7},{5,4},{6,5},{7,6},{8,11},{9,8},{10,9},{11,10},{28,31},{29,28... | collective-permute-start | bytes 3170312 | tf_op jit(solution)/shard_map/ppermute | solution.py:293
  7.3 0.3 collective-permute-start.1
  7.6 1.9 %collective-permute-start = (f32[1032,256]{1,0:T(8,128)S(1)}, f32[1032,256]{1,0:T(8,128)}, u32[]{:S(2)}, u32[]{:S(2)}) collective-permute-start(f32[1032,256]{1,0:T(8,128)S(1)} %shard_map.37.refs_0_), channel_id=1, source_target_pairs={{9,1},{18,2},{27,3},{13,5},{22,6},{31,7},{17,9},{26,10},{3,11},{21... | collective-permute-start | bytes 3170312 | tf_op jit(solution)/shard_map/ppermute | solution.py:293
  9.6 1.3 %collective-permute-start.2 = (f32[1032,256]{1,0:T(8,128)S(1)}, f32[1032,256]{1,0:T(8,128)}, u32[]{:S(2)}, u32[]{:S(2)}) collective-permute-start(f32[1032,256]{1,0:T(8,128)S(1)} %shard_map.37.refs_0_), channel_id=1, source_target_pairs={{16,4},{25,5},{2,6},{11,7},{24,12},{1,13},{10,14},{19,15},{0,20},{... | collective-permute-start | bytes 3170312 | tf_op jit(solution)/shard_map/ppermute | solution.py:293
  10.9 17.3 %collective-permute-done.6.refs_7_ = f32[1032,256]{1,0:T(8,128)S(1)} collective-permute-done((f32[1032,256]{1,0:T(8,128)S(1)}, f32[1032,256]{1,0:T(8,128)S(1)}, u32[]{:S(2)}, u32[]{:S(2)}) %collective-permute-start.6) | collective-permute-done | bytes 1056800 | tf_op jit(solution)/shard_map/ppermute | solution.py:293
  28.2 1.7 %collective-permute-start.8 = (f32[1032,256]{1,0:T(8,128)S(1)}, f32[1032,256]{1,0:T(8,128)}, u32[]{:S(2)}, u32[]{:S(2)}) collective-permute-start(f32[1032,256]{1,0:T(8,128)S(1)} %collective-permute-done.6.refs_7_), channel_id=1, source_target_pairs={{16,17},{17,18},{18,19},{19,16},{20,21},{21,22},{22,23},{23,20},{1... | collective-permute-start | bytes 3170312 | tf_op jit(solution)/shard_map/ppermute | solution.py:293
  29.9 11.7 %collective-permute-done.5.refs_6_ = f32[1032,256]{1,0:T(8,128)S(1)} collective-permute-done((f32[1032,256]{1,0:T(8,128)S(1)}, f32[1032,256]{1,0:T(8,128)S(1)}, u32[]{:S(2)}, u32[]{:S(2)}) %collective-permute-start.5) | collective-permute-done | bytes 1056800 | tf_op jit(solution)/shard_map/ppermute | solution.py:293
  41.5 1.7 %collective-permute-start.7 = (f32[1032,256]{1,0:T(8,128)S(1)}, f32[1032,256]{1,0:T(8,128)}, u32[]{:S(2)}, u32[]{:S(2)}) collective-permute-start(f32[1032,256]{1,0:T(8,128)S(1)} %collective-permute-done.5.refs_6_), channel_id=1, source_target_pairs={{4,7},{5,4},{6,5},{7,6},{8,11},{9,8},{10,9},{11,10},{13,12},{14,13... | collective-permute-start | bytes 3170312 | tf_op jit(solution)/shard_map/ppermute | solution.py:293
  43.2 12.2 %collective-permute-done.1.refs_2_ = f32[1032,256]{1,0:T(8,128)} collective-permute-done((f32[1032,256]{1,0:T(8,128)S(1)}, f32[1032,256]{1,0:T(8,128)}, u32[]{:S(2)}, u32[]{:S(2)}) %collective-permute-start.1) | collective-permute-done | bytes 1056800 | tf_op jit(solution)/shard_map/ppermute | solution.py:293
  55.4 2.4 %collective-permute-start.4 = (f32[1032,256]{1,0:T(8,128)}, f32[1032,256]{1,0:T(8,128)}, u32[]{:S(2)}, u32[]{:S(2)}) collective-permute-start(f32[1032,256]{1,0:T(8,128)} %collective-permute-done.1.refs_2_), channel_id=1, source_target_pairs={{4,0},{5,1},{6,2},{0,4},{1,5},{2,6},{12,8},{13,9},{14,10},{8,12},{... | collective-permute-start | bytes 3170312 | tf_op jit(solution)/shard_map/ppermute | solution.py:293
  57.8 0.0 collective-permute-done.refs_1_
  57.8 3.0 %collective-permute-start.3 = (f32[1032,256]{1,0:T(8,128)}, f32[1032,256]{1,0:T(8,128)}, u32[]{:S(2)}, u32[]{:S(2)}) collective-permute-start(f32[1032,256]{1,0:T(8,128)} %collective-permute-done.refs_1_), channel_id=1, source_target_pairs={{5,1},{6,2},{7,3},{13,9},{14,10},{15,11},{21,17},{22,18},{23,19},{... | collective-permute-start | bytes 3170312 | tf_op jit(solution)/shard_map/ppermute | solution.py:293
  60.7 0.7 dynamic-slice_bitcast_fusion.info_ref
  61.4 0.0 collective-permute-done.2.refs_3_
  61.4 0.0 collective-permute-done.8.refs_9_
  61.4 0.0 collective-permute-done.7.refs_8_
  61.4 0.0 collective-permute-done.4.refs_5_
  61.5 0.9 %collective-permute-done.3.refs_4_ = f32[1032,256]{1,0:T(8,128)} collective-permute-done((f32[1032,256]{1,0:T(8,128)}, f32[1032,256]{1,0:T(8,128)}, u32[]{:S(2)}, u32[]{:S(2)}) %collective-permute-start.3) | collective-permute-done | bytes 1056800 | tf_op jit(solution)/shard_map/ppermute | solution.py:293
  62.4 9.1 %shard_map.38 = f32[1024,2048]{1,0:T(8,128)} custom-call(s32[10]{0:T(128)S(1)} %dynamic-slice_bitcast_fusion.info_ref, f32[1032,256]{1,0:T(8,128)S(1)} %shard_map.37.refs_0_, f32[1032,256]{1,0:T(8,128)} %collective-permute-done.refs_1_, f32[1032,256]{1,0:T(8,128)} %collective-permute-done.1.refs_2_, f32[1032,256]{1,0:T(8,128)} %collective-permute-done.2.refs_3_, ...), custom_call_target="tpu_custom_call" | custom-call | flops 1000000000 | bytes 20971520 | tf_op jit(solution)/shard_map/pallas_call | solution.py:301
  (1 shorter events, 0.0 us)
Async XLA Ops:
  0.0 1.2 %copy-start = (f32[1024,256]{1,0:T(8,128)S(1)}, f32[1024,256]{1,0:T(8,128)}, u32[]{:S(2)}) copy-start(f32[1024,256]{1,0:T(8,128)} %data_ref.1) | copy-start | bytes 3145732
  1.2 0.7 copy-start.1
  2.0 26.2 %collective-permute-start.6 = (f32[1032,256]{1,0:T(8,128)S(1)}, f32[1032,256]{1,0:T(8,128)S(1)}, u32[]{:S(2)}, u32[]{:S(2)}) collective-permute-start(f32[1032,256]{1,0:T(8,128)S(1)} %shard_map.37.refs_0_), channel_id=1, source_target_pairs={{16,17},{17,18},{18,19},{19,16},{20,21},{21,22},{22,23},{23,20},{2... | collective-permute-start | bytes 3170312 | tf_op jit(solution)/shard_map/ppermute | solution.py:293
  5.2 36.3 %collective-permute-start.5 = (f32[1032,256]{1,0:T(8,128)S(1)}, f32[1032,256]{1,0:T(8,128)S(1)}, u32[]{:S(2)}, u32[]{:S(2)}) collective-permute-start(f32[1032,256]{1,0:T(8,128)S(1)} %shard_map.37.refs_0_), channel_id=1, source_target_pairs={{4,7},{5,4},{6,5},{7,6},{8,11},{9,8},{10,9},{11,10},{28,31},{29,28... | collective-permute-start | bytes 3170312 | tf_op jit(solution)/shard_map/ppermute | solution.py:293
  7.3 48.1 %collective-permute-start.1 = (f32[1032,256]{1,0:T(8,128)S(1)}, f32[1032,256]{1,0:T(8,128)}, u32[]{:S(2)}, u32[]{:S(2)}) collective-permute-start(f32[1032,256]{1,0:T(8,128)S(1)} %shard_map.37.refs_0_), channel_id=1, source_target_pairs={{8,0},{17,1},{26,2},{12,4},{21,5},{30,6},{16,8},{25,9},{2,10},{20,... | collective-permute-start | bytes 3170312 | tf_op jit(solution)/shard_map/ppermute | solution.py:293
  7.6 50.1 %collective-permute-start = (f32[1032,256]{1,0:T(8,128)S(1)}, f32[1032,256]{1,0:T(8,128)}, u32[]{:S(2)}, u32[]{:S(2)}) collective-permute-start(f32[1032,256]{1,0:T(8,128)S(1)} %shard_map.37.refs_0_), channel_id=1, source_target_pairs={{9,1},{18,2},{27,3},{13,5},{22,6},{31,7},{17,9},{26,10},{3,11},{21... | collective-permute-start | bytes 3170312 | tf_op jit(solution)/shard_map/ppermute | solution.py:293
  9.6 51.9 %collective-permute-start.2 = (f32[1032,256]{1,0:T(8,128)S(1)}, f32[1032,256]{1,0:T(8,128)}, u32[]{:S(2)}, u32[]{:S(2)}) collective-permute-start(f32[1032,256]{1,0:T(8,128)S(1)} %shard_map.37.refs_0_), channel_id=1, source_target_pairs={{16,4},{25,5},{2,6},{11,7},{24,12},{1,13},{10,14},{19,15},{0,20},{... | collective-permute-start | bytes 3170312 | tf_op jit(solution)/shard_map/ppermute | solution.py:293
  28.2 33.2 %collective-permute-start.8 = (f32[1032,256]{1,0:T(8,128)S(1)}, f32[1032,256]{1,0:T(8,128)}, u32[]{:S(2)}, u32[]{:S(2)}) collective-permute-start(f32[1032,256]{1,0:T(8,128)S(1)} %collective-permute-done.6.refs_7_), channel_id=1, source_target_pairs={{16,17},{17,18},{18,19},{19,16},{20,21},{21,22},{22,23},{23,20},{1... | collective-permute-start | bytes 3170312 | tf_op jit(solution)/shard_map/ppermute | solution.py:293
  41.5 19.9 %collective-permute-start.7 = (f32[1032,256]{1,0:T(8,128)S(1)}, f32[1032,256]{1,0:T(8,128)}, u32[]{:S(2)}, u32[]{:S(2)}) collective-permute-start(f32[1032,256]{1,0:T(8,128)S(1)} %collective-permute-done.5.refs_6_), channel_id=1, source_target_pairs={{4,7},{5,4},{6,5},{7,6},{8,11},{9,8},{10,9},{11,10},{13,12},{14,13... | collective-permute-start | bytes 3170312 | tf_op jit(solution)/shard_map/ppermute | solution.py:293
  55.4 6.0 %collective-permute-start.4 = (f32[1032,256]{1,0:T(8,128)}, f32[1032,256]{1,0:T(8,128)}, u32[]{:S(2)}, u32[]{:S(2)}) collective-permute-start(f32[1032,256]{1,0:T(8,128)} %collective-permute-done.1.refs_2_), channel_id=1, source_target_pairs={{4,0},{5,1},{6,2},{0,4},{1,5},{2,6},{12,8},{13,9},{14,10},{8,12},{... | collective-permute-start | bytes 3170312 | tf_op jit(solution)/shard_map/ppermute | solution.py:293
  57.8 4.6 %collective-permute-start.3 = (f32[1032,256]{1,0:T(8,128)}, f32[1032,256]{1,0:T(8,128)}, u32[]{:S(2)}, u32[]{:S(2)}) collective-permute-start(f32[1032,256]{1,0:T(8,128)} %collective-permute-done.refs_1_), channel_id=1, source_target_pairs={{5,1},{6,2},{7,3},{13,9},{14,10},{15,11},{21,17},{22,18},{23,19},{... | collective-permute-start | bytes 3170312 | tf_op jit(solution)/shard_map/ppermute | solution.py:293

commit v9 on v8

--- a/solution.py
+++ b/solution.py
@@ -192,17 +192,21 @@
         def _():
             pltpu.make_async_copy(left_bufs[0], left.at[slot], lsem.at[slot]).wait()
 
-    half = lax.broadcasted_iota(jnp.int32, (BS, 2 * BS), 1) // BS
+    half = lax.broadcasted_iota(jnp.int32, (8, 2 * BS), 1) // BS
 
     def block_at(index):
         return pl.ds(pl.multiple_of(index * BS, BS), BS)
+
+    def in_half(side, kept, other):
+        tall = lambda x: x.reshape(BS // 8, 8, 2 * BS) if jnp.ndim(x) else x
+        return jnp.where((half == side)[None], tall(kept), tall(other)).reshape(BS, 2 * BS)
 
     def product(code):
         slot = (code >> 8) & 15
         x = left[(code >> 12) & 15, block_at((code >> 16) & 255), pl.ds(pl.multiple_of((slot >> 1) * 2 * BS, 2 * BS), 2 * BS)]
-        both = jnp.where(half == (slot & 1), x, pltpu.roll(x, BS, 1))
+        both = in_half(slot & 1, x, pltpu.roll(x, BS, 1))
         hi = both.astype(jnp.bfloat16).astype(jnp.float32)
-        lhs = jnp.where(half == 0, hi, both - hi).astype(jnp.bfloat16)
+        lhs = in_half(0, hi, both - hi).astype(jnp.bfloat16)
         y = right[code >> 24, block_at(code & 255), :]
         hi = y.astype(jnp.bfloat16)
         lo = (y - hi.astype(jnp.float32)).astype(jnp.bfloat16)
@@ -210,17 +214,15 @@
         rhs = jnp.concatenate([hi, hi, lo, lo], axis=0)
         return jnp.dot(lhs, rhs, preferred_element_type=jnp.float32)
 
-    def add(code, product):
+    def add(code, u):
         rows_at = block_at((code >> 16) & 255)
         for pair in range(w // 2):
-            x = product[:, pair * 2 * BS : (pair + 1) * 2 * BS]
-            turned = pltpu.roll(x, BS, 1)
+            lanes_at = pl.ds(pair * 2 * BS, 2 * BS)
             picked, at = [], []
             for side in range(2):
                 place = scalars[(slots + (code >> 24)) * w + 2 * pair + side, code & 255]
                 parity = place >> 16
-                chosen = jnp.where(parity == side, x, turned)
-                picked.append(jnp.where(half == parity, chosen, 0.0))
+                picked.append(in_half(parity, value[u, (parity ^ side) & 1, :, lanes_at], 0.0))
                 at.append(place & 0xFFFF)
             picked[1] = jnp.where(at[0] == at[1], picked[0] + picked[1], picked[1])
             spots = [(rows_at, pl.ds(pl.multiple_of(base, 2 * BS), 2 * BS)) for base in at]
@@ -234,11 +236,15 @@
 
     def products(group):
         for u in range(UNROLL):
-            value[u] = product(codes[group * UNROLL + u])
+            result = product(codes[group * UNROLL + u])
+            value[u, 0] = result
+            for pair in range(w // 2):
+                lanes_at = slice(pair * 2 * BS, (pair + 1) * 2 * BS)
+                value[u, 1, :, lanes_at] = pltpu.roll(result[:, lanes_at], BS, 1)
 
     def sums(group):
         for u in range(UNROLL):
-            add(codes[group * UNROLL + u], value[u])
+            add(codes[group * UNROLL + u], u)
 
     last = jnp.maximum(ends[rb - 1] - 1, 0)
 
@@ -307,7 +313,7 @@
             pltpu.VMEM((slots, rows + EXTRA, width), jnp.float32),
             pltpu.VMEM((STEPS + 1, rows + EXTRA, width), jnp.float32),
             pltpu.VMEM(out_shape.shape, jnp.float32),
-            pltpu.VMEM((UNROLL, BS, width), jnp.float32),
+            pltpu.VMEM((UNROLL, 2, BS, width), jnp.float32),
             pltpu.VMEM((slots + STEPS, EXTRA, width), jnp.float32),
             pltpu.VMEM((codings, 128), jnp.int32),
             pltpu.SMEM((codings, 128), jnp.int32),

time: 72.3 us -> 74.3 us (1.028)
  Pallas kernels: 9.23 us -> 10.7 us
    pallas_call x1, Pallas kernels: 9.13 us -> 10.6 us  [local(): pl.pallas_call(functools.partial(product_kernel, slots, n_row, ratio, rb,...]
where the time goes in v9:
time: 74.3 us; the launch traced here: 72.9 us
  waiting for transfers between devices  42.1 us (57%)
  starting transfers between devices  17.5 us (24%)
  Pallas kernels  10.7 us (14%)
  local copies, waits for them, and re-layouts  2.59 us (3%)
    ppermute x9, waiting for transfers between devices, carry(): bufs.append(lax.ppermute(bufs[source], ('row', 'col'), flat))  42.1 us
    ppermute x9, starting transfers between devices, carry(): bufs.append(lax.ppermute(bufs[source], ('row', 'col'), flat))  17.5 us
    pallas_call x1, Pallas kernels, local(): pl.pallas_call(functools.partial(product_kernel, slots, n_row, ratio, rb,...  10.6 us
    unnamed x4, local copies, waits for them, and re-layouts  1.91 us
  transfers between devices with their start and end apart: 9, of which 4 were waited for; matrix products, arithmetic and copies ran while one was open for 1% of the time, Pallas kernels for 0%

profile of v9, /device:TPU:15, one launch (start us, length us, event | category | flops | bytes accessed | tf_op | source)
XLA Modules:
  0.0 72.9 jit_solution(12738675362716065880)
XLA Ops:
  0.0 0.0 copy-start
  0.0 1.2 %copy-done = f32[1024,256]{1,0:T(8,128)S(1)} copy-done((f32[1024,256]{1,0:T(8,128)S(1)}, f32[1024,256]{1,0:T(8,128)}, u32[]{:S(2)}) %copy-start) | copy-done | bytes 1048600
  1.2 0.7 copy-done.1
  1.9 0.1 shard_map.37.refs_0_
  2.0 3.2 %collective-permute-start.6 = (f32[1032,256]{1,0:T(8,128)S(1)}, f32[1032,256]{1,0:T(8,128)S(1)}, u32[]{:S(2)}, u32[]{:S(2)}) collective-permute-start(f32[1032,256]{1,0:T(8,128)S(1)} %shard_map.37.refs_0_), channel_id=1, source_target_pairs={{16,17},{17,18},{18,19},{19,16},{20,21},{21,22},{22,23},{23,20},{2... | collective-permute-start | bytes 3170312 | tf_op jit(solution)/shard_map/ppermute | solution.py:299
  5.2 2.1 %collective-permute-start.5 = (f32[1032,256]{1,0:T(8,128)S(1)}, f32[1032,256]{1,0:T(8,128)S(1)}, u32[]{:S(2)}, u32[]{:S(2)}) collective-permute-start(f32[1032,256]{1,0:T(8,128)S(1)} %shard_map.37.refs_0_), channel_id=1, source_target_pairs={{4,7},{5,4},{6,5},{7,6},{8,11},{9,8},{10,9},{11,10},{28,31},{29,28... | collective-permute-start | bytes 3170312 | tf_op jit(solution)/shard_map/ppermute | solution.py:299
  7.3 0.3 collective-permute-start.1
  7.6 1.9 %collective-permute-start = (f32[1032,256]{1,0:T(8,128)S(1)}, f32[1032,256]{1,0:T(8,128)}, u32[]{:S(2)}, u32[]{:S(2)}) collective-permute-start(f32[1032,256]{1,0:T(8,128)S(1)} %shard_map.37.refs_0_), channel_id=1, source_target_pairs={{9,1},{18,2},{27,3},{13,5},{22,6},{31,7},{17,9},{26,10},{3,11},{21... | collective-permute-start | bytes 3170312 | tf_op jit(solution)/shard_map/ppermute | solution.py:299
  9.6 1.3 %collective-permute-start.2 = (f32[1032,256]{1,0:T(8,128)S(1)}, f32[1032,256]{1,0:T(8,128)}, u32[]{:S(2)}, u32[]{:S(2)}) collective-permute-start(f32[1032,256]{1,0:T(8,128)S(1)} %shard_map.37.refs_0_), channel_id=1, source_target_pairs={{16,4},{25,5},{2,6},{11,7},{24,12},{1,13},{10,14},{19,15},{0,20},{... | collective-permute-start | bytes 3170312 | tf_op jit(solution)/shard_map/ppermute | solution.py:299
  10.9 17.3 %collective-permute-done.6.refs_7_ = f32[1032,256]{1,0:T(8,128)S(1)} collective-permute-done((f32[1032,256]{1,0:T(8,128)S(1)}, f32[1032,256]{1,0:T(8,128)S(1)}, u32[]{:S(2)}, u32[]{:S(2)}) %collective-permute-start.6) | collective-permute-done | bytes 1056800 | tf_op jit(solution)/shard_map/ppermute | solution.py:299
  28.2 1.7 %collective-permute-start.8 = (f32[1032,256]{1,0:T(8,128)S(1)}, f32[1032,256]{1,0:T(8,128)}, u32[]{:S(2)}, u32[]{:S(2)}) collective-permute-start(f32[1032,256]{1,0:T(8,128)S(1)} %collective-permute-done.6.refs_7_), channel_id=1, source_target_pairs={{16,17},{17,18},{18,19},{19,16},{20,21},{21,22},{22,23},{23,20},{1... | collective-permute-start | bytes 3170312 | tf_op jit(solution)/shard_map/ppermute | solution.py:299
  29.9 11.7 %collective-permute-done.5.refs_6_ = f32[1032,256]{1,0:T(8,128)S(1)} collective-permute-done((f32[1032,256]{1,0:T(8,128)S(1)}, f32[1032,256]{1,0:T(8,128)S(1)}, u32[]{:S(2)}, u32[]{:S(2)}) %collective-permute-start.5) | collective-permute-done | bytes 1056800 | tf_op jit(solution)/shard_map/ppermute | solution.py:299
  41.5 1.7 %collective-permute-start.7 = (f32[1032,256]{1,0:T(8,128)S(1)}, f32[1032,256]{1,0:T(8,128)}, u32[]{:S(2)}, u32[]{:S(2)}) collective-permute-start(f32[1032,256]{1,0:T(8,128)S(1)} %collective-permute-done.5.refs_6_), channel_id=1, source_target_pairs={{4,7},{5,4},{6,5},{7,6},{8,11},{9,8},{10,9},{11,10},{13,12},{14,13... | collective-permute-start | bytes 3170312 | tf_op jit(solution)/shard_map/ppermute | solution.py:299
  43.2 12.2 %collective-permute-done.1.refs_2_ = f32[1032,256]{1,0:T(8,128)} collective-permute-done((f32[1032,256]{1,0:T(8,128)S(1)}, f32[1032,256]{1,0:T(8,128)}, u32[]{:S(2)}, u32[]{:S(2)}) %collective-permute-start.1) | collective-permute-done | bytes 1056800 | tf_op jit(solution)/shard_map/ppermute | solution.py:299
  55.4 2.4 %collective-permute-start.4 = (f32[1032,256]{1,0:T(8,128)}, f32[1032,256]{1,0:T(8,128)}, u32[]{:S(2)}, u32[]{:S(2)}) collective-permute-start(f32[1032,256]{1,0:T(8,128)} %collective-permute-done.1.refs_2_), channel_id=1, source_target_pairs={{4,0},{5,1},{6,2},{0,4},{1,5},{2,6},{12,8},{13,9},{14,10},{8,12},{... | collective-permute-start | bytes 3170312 | tf_op jit(solution)/shard_map/ppermute | solution.py:299
  57.8 0.0 collective-permute-done.refs_1_
  57.8 3.0 %collective-permute-start.3 = (f32[1032,256]{1,0:T(8,128)}, f32[1032,256]{1,0:T(8,128)}, u32[]{:S(2)}, u32[]{:S(2)}) collective-permute-start(f32[1032,256]{1,0:T(8,128)} %collective-permute-done.refs_1_), channel_id=1, source_target_pairs={{5,1},{6,2},{7,3},{13,9},{14,10},{15,11},{21,17},{22,18},{23,19},{... | collective-permute-start | bytes 3170312 | tf_op jit(solution)/shard_map/ppermute | solution.py:299
  60.7 0.7 dynamic-slice_bitcast_fusion.info_ref
  61.4 0.0 collective-permute-done.2.refs_3_
  61.4 0.0 collective-permute-done.8.refs_9_
  61.4 0.0 collective-permute-done.7.refs_8_
  61.4 0.0 collective-permute-done.4.refs_5_
  61.5 0.9 %collective-permute-done.3.refs_4_ = f32[1032,256]{1,0:T(8,128)} collective-permute-done((f32[1032,256]{1,0:T(8,128)}, f32[1032,256]{1,0:T(8,128)}, u32[]{:S(2)}, u32[]{:S(2)}) %collective-permute-start.3) | collective-permute-done | bytes 1056800 | tf_op jit(solution)/shard_map/ppermute | solution.py:299
  62.4 10.6 %shard_map.38 = f32[1024,2048]{1,0:T(8,128)} custom-call(s32[10]{0:T(128)S(1)} %dynamic-slice_bitcast_fusion.info_ref, f32[1032,256]{1,0:T(8,128)S(1)} %shard_map.37.refs_0_, f32[1032,256]{1,0:T(8,128)} %collective-permute-done.refs_1_, f32[1032,256]{1,0:T(8,128)} %collective-permute-done.1.refs_2_, f32[1032,256]{1,0:T(8,128)} %collective-permute-done.2.refs_3_, ...), custom_call_target="tpu_custom_call" | custom-call | flops 1000000000 | bytes 20971520 | tf_op jit(solution)/shard_map/pallas_call | solution.py:307
  (1 shorter events, 0.0 us)
Async XLA Ops:
  0.0 1.2 %copy-start = (f32[1024,256]{1,0:T(8,128)S(1)}, f32[1024,256]{1,0:T(8,128)}, u32[]{:S(2)}) copy-start(f32[1024,256]{1,0:T(8,128)} %data_ref.1) | copy-start | bytes 3145732
  1.2 0.7 copy-start.1
  2.0 26.2 %collective-permute-start.6 = (f32[1032,256]{1,0:T(8,128)S(1)}, f32[1032,256]{1,0:T(8,128)S(1)}, u32[]{:S(2)}, u32[]{:S(2)}) collective-permute-start(f32[1032,256]{1,0:T(8,128)S(1)} %shard_map.37.refs_0_), channel_id=1, source_target_pairs={{16,17},{17,18},{18,19},{19,16},{20,21},{21,22},{22,23},{23,20},{2... | collective-permute-start | bytes 3170312 | tf_op jit(solution)/shard_map/ppermute | solution.py:299
  5.2 36.3 %collective-permute-start.5 = (f32[1032,256]{1,0:T(8,128)S(1)}, f32[1032,256]{1,0:T(8,128)S(1)}, u32[]{:S(2)}, u32[]{:S(2)}) collective-permute-start(f32[1032,256]{1,0:T(8,128)S(1)} %shard_map.37.refs_0_), channel_id=1, source_target_pairs={{4,7},{5,4},{6,5},{7,6},{8,11},{9,8},{10,9},{11,10},{28,31},{29,28... | collective-permute-start | bytes 3170312 | tf_op jit(solution)/shard_map/ppermute | solution.py:299
  7.3 48.1 %collective-permute-start.1 = (f32[1032,256]{1,0:T(8,128)S(1)}, f32[1032,256]{1,0:T(8,128)}, u32[]{:S(2)}, u32[]{:S(2)}) collective-permute-start(f32[1032,256]{1,0:T(8,128)S(1)} %shard_map.37.refs_0_), channel_id=1, source_target_pairs={{8,0},{17,1},{26,2},{12,4},{21,5},{30,6},{16,8},{25,9},{2,10},{20,... | collective-permute-start | bytes 3170312 | tf_op jit(solution)/shard_map/ppermute | solution.py:299
  7.6 50.1 %collective-permute-start = (f32[1032,256]{1,0:T(8,128)S(1)}, f32[1032,256]{1,0:T(8,128)}, u32[]{:S(2)}, u32[]{:S(2)}) collective-permute-start(f32[1032,256]{1,0:T(8,128)S(1)} %shard_map.37.refs_0_), channel_id=1, source_target_pairs={{9,1},{18,2},{27,3},{13,5},{22,6},{31,7},{17,9},{26,10},{3,11},{21... | collective-permute-start | bytes 3170312 | tf_op jit(solution)/shard_map/ppermute | solution.py:299
  9.6 51.9 %collective-permute-start.2 = (f32[1032,256]{1,0:T(8,128)S(1)}, f32[1032,256]{1,0:T(8,128)}, u32[]{:S(2)}, u32[]{:S(2)}) collective-permute-start(f32[1032,256]{1,0:T(8,128)S(1)} %shard_map.37.refs_0_), channel_id=1, source_target_pairs={{16,4},{25,5},{2,6},{11,7},{24,12},{1,13},{10,14},{19,15},{0,20},{... | collective-permute-start | bytes 3170312 | tf_op jit(solution)/shard_map/ppermute | solution.py:299
  28.2 33.2 %collective-permute-start.8 = (f32[1032,256]{1,0:T(8,128)S(1)}, f32[1032,256]{1,0:T(8,128)}, u32[]{:S(2)}, u32[]{:S(2)}) collective-permute-start(f32[1032,256]{1,0:T(8,128)S(1)} %collective-permute-done.6.refs_7_), channel_id=1, source_target_pairs={{16,17},{17,18},{18,19},{19,16},{20,21},{21,22},{22,23},{23,20},{1... | collective-permute-start | bytes 3170312 | tf_op jit(solution)/shard_map/ppermute | solution.py:299
  41.5 19.9 %collective-permute-start.7 = (f32[1032,256]{1,0:T(8,128)S(1)}, f32[1032,256]{1,0:T(8,128)}, u32[]{:S(2)}, u32[]{:S(2)}) collective-permute-start(f32[1032,256]{1,0:T(8,128)S(1)} %collective-permute-done.5.refs_6_), channel_id=1, source_target_pairs={{4,7},{5,4},{6,5},{7,6},{8,11},{9,8},{10,9},{11,10},{13,12},{14,13... | collective-permute-start | bytes 3170312 | tf_op jit(solution)/shard_map/ppermute | solution.py:299
  55.4 6.0 %collective-permute-start.4 = (f32[1032,256]{1,0:T(8,128)}, f32[1032,256]{1,0:T(8,128)}, u32[]{:S(2)}, u32[]{:S(2)}) collective-permute-start(f32[1032,256]{1,0:T(8,128)} %collective-permute-done.1.refs_2_), channel_id=1, source_target_pairs={{4,0},{5,1},{6,2},{0,4},{1,5},{2,6},{12,8},{13,9},{14,10},{8,12},{... | collective-permute-start | bytes 3170312 | tf_op jit(solution)/shard_map/ppermute | solution.py:299
  57.8 4.6 %collective-permute-start.3 = (f32[1032,256]{1,0:T(8,128)}, f32[1032,256]{1,0:T(8,128)}, u32[]{:S(2)}, u32[]{:S(2)}) collective-permute-start(f32[1032,256]{1,0:T(8,128)} %collective-permute-done.refs_1_), channel_id=1, source_target_pairs={{5,1},{6,2},{7,3},{13,9},{14,10},{15,11},{21,17},{22,18},{23,19},{... | collective-permute-start | bytes 3170312 | tf_op jit(solution)/shard_map/ppermute | solution.py:299

commit v10 on v8

--- a/solution.py
+++ b/solution.py
@@ -11,6 +11,7 @@
 BS = 64
 STEPS = 4
 UNROLL = 8
+AHEAD = 2
 EXTRA = 8
 PARTS = 8
 
@@ -232,13 +233,18 @@
         at = pl.ds(part * part_rows * BS, part_rows * BS)
         return pltpu.make_async_copy(acc.at[at], out_ref.at[at], osem.at[part])
 
-    def products(group):
+    def first_products(group):
+        for u in range(AHEAD):
+            value[u] = product(codes[group * UNROLL + u])
+
+    def sums(group, more):
+        waiting = [value[u] for u in range(AHEAD)]
         for u in range(UNROLL):
-            value[u] = product(codes[group * UNROLL + u])
-
-    def sums(group):
-        for u in range(UNROLL):
-            add(codes[group * UNROLL + u], value[u])
+            if u + AHEAD < UNROLL or more:
+                waiting.append(product(codes[group * UNROLL + u + AHEAD]))
+            add(codes[group * UNROLL + u], waiting[u])
+        for u in range(AHEAD if more else 0):
+            value[u] = waiting[UNROLL + u]
 
     last = jnp.maximum(ends[rb - 1] - 1, 0)
 
@@ -248,15 +254,14 @@
             def _():
                 out_copy(part).start()
 
-    products(0)
+    first_products(0)
 
     @pl.loop(0, last)
     def _(group):
-        sums(group)
-        products(group + 1)
+        sums(group, True)
         leave(group)
 
-    sums(last)
+    sums(last, False)
     leave(last)
     for part in range(PARTS):
         out_copy(part).wait()
@@ -307,7 +312,7 @@
             pltpu.VMEM((slots, rows + EXTRA, width), jnp.float32),
             pltpu.VMEM((STEPS + 1, rows + EXTRA, width), jnp.float32),
             pltpu.VMEM(out_shape.shape, jnp.float32),
-            pltpu.VMEM((UNROLL, BS, width), jnp.float32),
+            pltpu.VMEM((AHEAD, BS, width), jnp.float32),
             pltpu.VMEM((slots + STEPS, EXTRA, width), jnp.float32),
             pltpu.VMEM((codings, 128), jnp.int32),
             pltpu.SMEM((codings, 128), jnp.int32),

time: 72.3 us -> 73.2 us (1.012)
  no operation moved by 1% of the time
where the time goes in v10:
time: 73.2 us; the launch traced here: 72.1 us
  waiting for transfers between devices  42.1 us (58%)
  starting transfers between devices  17.5 us (24%)
  Pallas kernels  9.88 us (13%)
  local copies, waits for them, and re-layouts  2.59 us (4%)
    ppermute x9, waiting for transfers between devices, carry(): bufs.append(lax.ppermute(bufs[source], ('row', 'col'), flat))  42.1 us
    ppermute x9, starting transfers between devices, carry(): bufs.append(lax.ppermute(bufs[source], ('row', 'col'), flat))  17.5 us
    pallas_call x1, Pallas kernels, local(): pl.pallas_call(functools.partial(product_kernel, slots, n_row, ratio, rb,...  9.78 us
    unnamed x4, local copies, waits for them, and re-layouts  1.91 us
  transfers between devices with their start and end apart: 9, of which 4 were waited for; matrix products, arithmetic and copies ran while one was open for 1% of the time, Pallas kernels for 0%

profile of v10, /device:TPU:15, one launch (start us, length us, event | category | flops | bytes accessed | tf_op | source)
XLA Modules:
  0.0 72.1 jit_solution(17284295185019513632)
XLA Ops:
  0.0 1.2 %copy-done = f32[1024,256]{1,0:T(8,128)S(1)} copy-done((f32[1024,256]{1,0:T(8,128)S(1)}, f32[1024,256]{1,0:T(8,128)}, u32[]{:S(2)}) %copy-start) | copy-done | bytes 1048600
  1.2 0.0 copy-start.1
  1.2 0.7 copy-done.1
  1.9 0.1 shard_map.37.refs_0_
  2.0 3.2 %collective-permute-start.6 = (f32[1032,256]{1,0:T(8,128)S(1)}, f32[1032,256]{1,0:T(8,128)S(1)}, u32[]{:S(2)}, u32[]{:S(2)}) collective-permute-start(f32[1032,256]{1,0:T(8,128)S(1)} %shard_map.37.refs_0_), channel_id=1, source_target_pairs={{16,17},{17,18},{18,19},{19,16},{20,21},{21,22},{22,23},{23,20},{2... | collective-permute-start | bytes 3170312 | tf_op jit(solution)/shard_map/ppermute | solution.py:298
  5.2 2.1 %collective-permute-start.5 = (f32[1032,256]{1,0:T(8,128)S(1)}, f32[1032,256]{1,0:T(8,128)S(1)}, u32[]{:S(2)}, u32[]{:S(2)}) collective-permute-start(f32[1032,256]{1,0:T(8,128)S(1)} %shard_map.37.refs_0_), channel_id=1, source_target_pairs={{4,7},{5,4},{6,5},{7,6},{8,11},{9,8},{10,9},{11,10},{28,31},{29,28... | collective-permute-start | bytes 3170312 | tf_op jit(solution)/shard_map/ppermute | solution.py:298
  7.3 0.3 collective-permute-start.1
  7.6 1.9 %collective-permute-start = (f32[1032,256]{1,0:T(8,128)S(1)}, f32[1032,256]{1,0:T(8,128)}, u32[]{:S(2)}, u32[]{:S(2)}) collective-permute-start(f32[1032,256]{1,0:T(8,128)S(1)} %shard_map.37.refs_0_), channel_id=1, source_target_pairs={{9,1},{18,2},{27,3},{13,5},{22,6},{31,7},{17,9},{26,10},{3,11},{21... | collective-permute-start | bytes 3170312 | tf_op jit(solution)/shard_map/ppermute | solution.py:298
  9.6 1.3 %collective-permute-start.2 = (f32[1032,256]{1,0:T(8,128)S(1)}, f32[1032,256]{1,0:T(8,128)}, u32[]{:S(2)}, u32[]{:S(2)}) collective-permute-start(f32[1032,256]{1,0:T(8,128)S(1)} %shard_map.37.refs_0_), channel_id=1, source_target_pairs={{16,4},{25,5},{2,6},{11,7},{24,12},{1,13},{10,14},{19,15},{0,20},{... | collective-permute-start | bytes 3170312 | tf_op jit(solution)/shard_map/ppermute | solution.py:298
  10.9 17.3 %collective-permute-done.6.refs_7_ = f32[1032,256]{1,0:T(8,128)S(1)} collective-permute-done((f32[1032,256]{1,0:T(8,128)S(1)}, f32[1032,256]{1,0:T(8,128)S(1)}, u32[]{:S(2)}, u32[]{:S(2)}) %collective-permute-start.6) | collective-permute-done | bytes 1056800 | tf_op jit(solution)/shard_map/ppermute | solution.py:298
  28.2 1.7 %collective-permute-start.8 = (f32[1032,256]{1,0:T(8,128)S(1)}, f32[1032,256]{1,0:T(8,128)}, u32[]{:S(2)}, u32[]{:S(2)}) collective-permute-start(f32[1032,256]{1,0:T(8,128)S(1)} %collective-permute-done.6.refs_7_), channel_id=1, source_target_pairs={{16,17},{17,18},{18,19},{19,16},{20,21},{21,22},{22,23},{23,20},{1... | collective-permute-start | bytes 3170312 | tf_op jit(solution)/shard_map/ppermute | solution.py:298
  29.9 11.7 %collective-permute-done.5.refs_6_ = f32[1032,256]{1,0:T(8,128)S(1)} collective-permute-done((f32[1032,256]{1,0:T(8,128)S(1)}, f32[1032,256]{1,0:T(8,128)S(1)}, u32[]{:S(2)}, u32[]{:S(2)}) %collective-permute-start.5) | collective-permute-done | bytes 1056800 | tf_op jit(solution)/shard_map/ppermute | solution.py:298
  41.5 1.7 %collective-permute-start.7 = (f32[1032,256]{1,0:T(8,128)S(1)}, f32[1032,256]{1,0:T(8,128)}, u32[]{:S(2)}, u32[]{:S(2)}) collective-permute-start(f32[1032,256]{1,0:T(8,128)S(1)} %collective-permute-done.5.refs_6_), channel_id=1, source_target_pairs={{4,7},{5,4},{6,5},{7,6},{8,11},{9,8},{10,9},{11,10},{13,12},{14,13... | collective-permute-start | bytes 3170312 | tf_op jit(solution)/shard_map/ppermute | solution.py:298
  43.2 12.2 %collective-permute-done.1.refs_2_ = f32[1032,256]{1,0:T(8,128)} collective-permute-done((f32[1032,256]{1,0:T(8,128)S(1)}, f32[1032,256]{1,0:T(8,128)}, u32[]{:S(2)}, u32[]{:S(2)}) %collective-permute-start.1) | collective-permute-done | bytes 1056800 | tf_op jit(solution)/shard_map/ppermute | solution.py:298
  55.4 2.4 %collective-permute-start.4 = (f32[1032,256]{1,0:T(8,128)}, f32[1032,256]{1,0:T(8,128)}, u32[]{:S(2)}, u32[]{:S(2)}) collective-permute-start(f32[1032,256]{1,0:T(8,128)} %collective-permute-done.1.refs_2_), channel_id=1, source_target_pairs={{4,0},{5,1},{6,2},{0,4},{1,5},{2,6},{12,8},{13,9},{14,10},{8,12},{... | collective-permute-start | bytes 3170312 | tf_op jit(solution)/shard_map/ppermute | solution.py:298
  57.8 0.0 collective-permute-done.refs_1_
  57.8 3.0 %collective-permute-start.3 = (f32[1032,256]{1,0:T(8,128)}, f32[1032,256]{1,0:T(8,128)}, u32[]{:S(2)}, u32[]{:S(2)}) collective-permute-start(f32[1032,256]{1,0:T(8,128)} %collective-permute-done.refs_1_), channel_id=1, source_target_pairs={{5,1},{6,2},{7,3},{13,9},{14,10},{15,11},{21,17},{22,18},{23,19},{... | collective-permute-start | bytes 3170312 | tf_op jit(solution)/shard_map/ppermute | solution.py:298
  60.7 0.7 dynamic-slice_bitcast_fusion.info_ref
  61.4 0.0 collective-permute-done.2.refs_3_
  61.4 0.0 collective-permute-done.8.refs_9_
  61.4 0.0 collective-permute-done.7.refs_8_
  61.4 0.0 collective-permute-done.4.refs_5_
  61.5 0.9 %collective-permute-done.3.refs_4_ = f32[1032,256]{1,0:T(8,128)} collective-permute-done((f32[1032,256]{1,0:T(8,128)}, f32[1032,256]{1,0:T(8,128)}, u32[]{:S(2)}, u32[]{:S(2)}) %collective-permute-start.3) | collective-permute-done | bytes 1056800 | tf_op jit(solution)/shard_map/ppermute | solution.py:298
  62.4 9.8 %shard_map.38 = f32[1024,2048]{1,0:T(8,128)} custom-call(s32[10]{0:T(128)S(1)} %dynamic-slice_bitcast_fusion.info_ref, f32[1032,256]{1,0:T(8,128)S(1)} %shard_map.37.refs_0_, f32[1032,256]{1,0:T(8,128)} %collective-permute-done.refs_1_, f32[1032,256]{1,0:T(8,128)} %collective-permute-done.1.refs_2_, f32[1032,256]{1,0:T(8,128)} %collective-permute-done.2.refs_3_, ...), custom_call_target="tpu_custom_call" | custom-call | flops 1000000000 | bytes 20971520 | tf_op jit(solution)/shard_map/pallas_call | solution.py:306
  (1 shorter events, 0.0 us)
Async XLA Ops:
  0.0 1.2 %copy-start = (f32[1024,256]{1,0:T(8,128)S(1)}, f32[1024,256]{1,0:T(8,128)}, u32[]{:S(2)}) copy-start(f32[1024,256]{1,0:T(8,128)} %data_ref.1) | copy-start | bytes 3145732
  1.2 0.7 copy-start.1
  2.0 26.2 %collective-permute-start.6 = (f32[1032,256]{1,0:T(8,128)S(1)}, f32[1032,256]{1,0:T(8,128)S(1)}, u32[]{:S(2)}, u32[]{:S(2)}) collective-permute-start(f32[1032,256]{1,0:T(8,128)S(1)} %shard_map.37.refs_0_), channel_id=1, source_target_pairs={{16,17},{17,18},{18,19},{19,16},{20,21},{21,22},{22,23},{23,20},{2... | collective-permute-start | bytes 3170312 | tf_op jit(solution)/shard_map/ppermute | solution.py:298
  5.2 36.3 %collective-permute-start.5 = (f32[1032,256]{1,0:T(8,128)S(1)}, f32[1032,256]{1,0:T(8,128)S(1)}, u32[]{:S(2)}, u32[]{:S(2)}) collective-permute-start(f32[1032,256]{1,0:T(8,128)S(1)} %shard_map.37.refs_0_), channel_id=1, source_target_pairs={{4,7},{5,4},{6,5},{7,6},{8,11},{9,8},{10,9},{11,10},{28,31},{29,28... | collective-permute-start | bytes 3170312 | tf_op jit(solution)/shard_map/ppermute | solution.py:298
  7.3 48.1 %collective-permute-start.1 = (f32[1032,256]{1,0:T(8,128)S(1)}, f32[1032,256]{1,0:T(8,128)}, u32[]{:S(2)}, u32[]{:S(2)}) collective-permute-start(f32[1032,256]{1,0:T(8,128)S(1)} %shard_map.37.refs_0_), channel_id=1, source_target_pairs={{8,0},{17,1},{26,2},{12,4},{21,5},{30,6},{16,8},{25,9},{2,10},{20,... | collective-permute-start | bytes 3170312 | tf_op jit(solution)/shard_map/ppermute | solution.py:298
  7.6 50.1 %collective-permute-start = (f32[1032,256]{1,0:T(8,128)S(1)}, f32[1032,256]{1,0:T(8,128)}, u32[]{:S(2)}, u32[]{:S(2)}) collective-permute-start(f32[1032,256]{1,0:T(8,128)S(1)} %shard_map.37.refs_0_), channel_id=1, source_target_pairs={{9,1},{18,2},{27,3},{13,5},{22,6},{31,7},{17,9},{26,10},{3,11},{21... | collective-permute-start | bytes 3170312 | tf_op jit(solution)/shard_map/ppermute | solution.py:298
  9.6 51.9 %collective-permute-start.2 = (f32[1032,256]{1,0:T(8,128)S(1)}, f32[1032,256]{1,0:T(8,128)}, u32[]{:S(2)}, u32[]{:S(2)}) collective-permute-start(f32[1032,256]{1,0:T(8,128)S(1)} %shard_map.37.refs_0_), channel_id=1, source_target_pairs={{16,4},{25,5},{2,6},{11,7},{24,12},{1,13},{10,14},{19,15},{0,20},{... | collective-permute-start | bytes 3170312 | tf_op jit(solution)/shard_map/ppermute | solution.py:298
  28.2 33.2 %collective-permute-start.8 = (f32[1032,256]{1,0:T(8,128)S(1)}, f32[1032,256]{1,0:T(8,128)}, u32[]{:S(2)}, u32[]{:S(2)}) collective-permute-start(f32[1032,256]{1,0:T(8,128)S(1)} %collective-permute-done.6.refs_7_), channel_id=1, source_target_pairs={{16,17},{17,18},{18,19},{19,16},{20,21},{21,22},{22,23},{23,20},{1... | collective-permute-start | bytes 3170312 | tf_op jit(solution)/shard_map/ppermute | solution.py:298
  41.5 19.9 %collective-permute-start.7 = (f32[1032,256]{1,0:T(8,128)S(1)}, f32[1032,256]{1,0:T(8,128)}, u32[]{:S(2)}, u32[]{:S(2)}) collective-permute-start(f32[1032,256]{1,0:T(8,128)S(1)} %collective-permute-done.5.refs_6_), channel_id=1, source_target_pairs={{4,7},{5,4},{6,5},{7,6},{8,11},{9,8},{10,9},{11,10},{13,12},{14,13... | collective-permute-start | bytes 3170312 | tf_op jit(solution)/shard_map/ppermute | solution.py:298
  55.4 6.0 %collective-permute-start.4 = (f32[1032,256]{1,0:T(8,128)}, f32[1032,256]{1,0:T(8,128)}, u32[]{:S(2)}, u32[]{:S(2)}) collective-permute-start(f32[1032,256]{1,0:T(8,128)} %collective-permute-done.1.refs_2_), channel_id=1, source_target_pairs={{4,0},{5,1},{6,2},{0,4},{1,5},{2,6},{12,8},{13,9},{14,10},{8,12},{... | collective-permute-start | bytes 3170312 | tf_op jit(solution)/shard_map/ppermute | solution.py:298
  57.8 4.6 %collective-permute-start.3 = (f32[1032,256]{1,0:T(8,128)}, f32[1032,256]{1,0:T(8,128)}, u32[]{:S(2)}, u32[]{:S(2)}) collective-permute-start(f32[1032,256]{1,0:T(8,128)} %collective-permute-done.refs_1_), channel_id=1, source_target_pairs={{5,1},{6,2},{7,3},{13,9},{14,10},{15,11},{21,17},{22,18},{23,19},{... | collective-permute-start | bytes 3170312 | tf_op jit(solution)/shard_map/ppermute | solution.py:298

commit v11 on v8

--- a/solution.py
+++ b/solution.py
@@ -68,7 +68,7 @@
     second = [(((r + 2 * c + 2) % 8, c), (r, c)) for r, c in everyone if c != 3]
     second += [((r ^ 1, 3), (r, 3)) for r in range(8)]
     last = [(((r - 1 + 2 * c + 4) % 8, c), (r, c)) for r, c in everyone if r % 2 == 1]
-    first_swap = [((r + 1, c), (r, c)) for r, c in everyone if r % 2 == 0 and c != 0]
+    first_swap = [((r ^ 1, c), (r, c)) for r, c in everyone]
     second_swap = [((r ^ 1, c), (r, c)) for r, c in everyone if c != 3]
     return [(0, first), (0, second), (0, last), (1, first_swap), (2, second_swap)]
 
@@ -76,7 +76,7 @@
 def carry_out(perms, n_row, n_col):
     held = [{(r, c): (r, c) for r in range(n_row) for c in range(n_col)}]
     for source, pairs in perms:
-        held.append({dst: held[source][src] for src, dst in pairs})
+        held.append({dst: held[source][src] for src, dst in pairs if src in held[source]})
     return held
 
 

time: 72.3 us -> 72.1 us (level); the launches traced: 71.5 us -> 72 us
  starting transfers between devices: 17.5 us -> 14.6 us
  waiting for transfers between devices: 42.1 us -> 44.5 us
  Pallas kernels: 9.23 us -> 10.2 us
    ppermute x9, starting transfers between devices: 17.5 us -> 14.6 us  [carry(): bufs.append(lax.ppermute(bufs[source], ('row', 'col'), flat))]
    ppermute x9, waiting for transfers between devices: 42.1 us -> 44.5 us  [carry(): bufs.append(lax.ppermute(bufs[source], ('row', 'col'), flat))]
    pallas_call x1, Pallas kernels: 9.13 us -> 10.1 us  [local(): pl.pallas_call(functools.partial(product_kernel, slots, n_row, ratio, rb,...]
  transfers between devices with their start and end apart: 9 -> 9, of which waited for: 4 -> 5; matrix products, arithmetic and copies ran while one was open for 1% -> 1% of each run, Pallas kernels for 0% -> 0%
where the time goes in v11:
time: 72.1 us; the launch traced here: 72 us
  waiting for transfers between devices  44.5 us (62%)
  starting transfers between devices  14.6 us (20%)
  Pallas kernels  10.2 us (14%)
  local copies, waits for them, and re-layouts  2.59 us (4%)
    ppermute x9, waiting for transfers between devices, carry(): bufs.append(lax.ppermute(bufs[source], ('row', 'col'), flat))  44.5 us
    ppermute x9, starting transfers between devices, carry(): bufs.append(lax.ppermute(bufs[source], ('row', 'col'), flat))  14.6 us
    pallas_call x1, Pallas kernels, local(): pl.pallas_call(functools.partial(product_kernel, slots, n_row, ratio, rb,...  10.1 us
    unnamed x4, local copies, waits for them, and re-layouts  1.91 us
  transfers between devices with their start and end apart: 9, of which 5 were waited for; matrix products, arithmetic and copies ran while one was open for 1% of the time, Pallas kernels for 0%

profile of v11, /device:TPU:15, one launch (start us, length us, event | category | flops | bytes accessed | tf_op | source)
XLA Modules:
  0.0 72.0 jit_solution(5992847553506978655)
XLA Ops:
  0.0 0.0 copy-start
  0.0 1.2 %copy-done = f32[1024,256]{1,0:T(8,128)S(1)} copy-done((f32[1024,256]{1,0:T(8,128)S(1)}, f32[1024,256]{1,0:T(8,128)}, u32[]{:S(2)}) %copy-start) | copy-done | bytes 1048600
  1.2 0.7 copy-done.1
  1.9 0.1 shard_map.37.refs_0_
  2.0 3.2 %collective-permute-start.6 = (f32[1032,256]{1,0:T(8,128)S(1)}, f32[1032,256]{1,0:T(8,128)S(1)}, u32[]{:S(2)}, u32[]{:S(2)}) collective-permute-start(f32[1032,256]{1,0:T(8,128)S(1)} %shard_map.37.refs_0_), channel_id=1, source_target_pairs={{16,17},{17,18},{18,19},{19,16},{20,21},{21,22},{22,23},{23,20},{2... | collective-permute-start | bytes 3170312 | tf_op jit(solution)/shard_map/ppermute | solution.py:293
  5.2 2.1 %collective-permute-start.5 = (f32[1032,256]{1,0:T(8,128)S(1)}, f32[1032,256]{1,0:T(8,128)S(1)}, u32[]{:S(2)}, u32[]{:S(2)}) collective-permute-start(f32[1032,256]{1,0:T(8,128)S(1)} %shard_map.37.refs_0_), channel_id=1, source_target_pairs={{4,7},{5,4},{6,5},{7,6},{8,11},{9,8},{10,9},{11,10},{28,31},{29,28... | collective-permute-start | bytes 3170312 | tf_op jit(solution)/shard_map/ppermute | solution.py:293
  7.3 0.3 collective-permute-start.1
  7.6 1.9 %collective-permute-start = (f32[1032,256]{1,0:T(8,128)S(1)}, f32[1032,256]{1,0:T(8,128)}, u32[]{:S(2)}, u32[]{:S(2)}) collective-permute-start(f32[1032,256]{1,0:T(8,128)S(1)} %shard_map.37.refs_0_), channel_id=1, source_target_pairs={{9,1},{18,2},{27,3},{13,5},{22,6},{31,7},{17,9},{26,10},{3,11},{21... | collective-permute-start | bytes 3170312 | tf_op jit(solution)/shard_map/ppermute | solution.py:293
  9.6 1.3 %collective-permute-start.2 = (f32[1032,256]{1,0:T(8,128)S(1)}, f32[1032,256]{1,0:T(8,128)}, u32[]{:S(2)}, u32[]{:S(2)}) collective-permute-start(f32[1032,256]{1,0:T(8,128)S(1)} %shard_map.37.refs_0_), channel_id=1, source_target_pairs={{16,4},{25,5},{2,6},{11,7},{24,12},{1,13},{10,14},{19,15},{0,20},{... | collective-permute-start | bytes 3170312 | tf_op jit(solution)/shard_map/ppermute | solution.py:293
  10.9 17.3 %collective-permute-done.6.refs_7_ = f32[1032,256]{1,0:T(8,128)S(1)} collective-permute-done((f32[1032,256]{1,0:T(8,128)S(1)}, f32[1032,256]{1,0:T(8,128)S(1)}, u32[]{:S(2)}, u32[]{:S(2)}) %collective-permute-start.6) | collective-permute-done | bytes 1056800 | tf_op jit(solution)/shard_map/ppermute | solution.py:293
  28.2 1.7 %collective-permute-start.8 = (f32[1032,256]{1,0:T(8,128)S(1)}, f32[1032,256]{1,0:T(8,128)}, u32[]{:S(2)}, u32[]{:S(2)}) collective-permute-start(f32[1032,256]{1,0:T(8,128)S(1)} %collective-permute-done.6.refs_7_), channel_id=1, source_target_pairs={{16,17},{17,18},{18,19},{19,16},{20,21},{21,22},{22,23},{23,20},{1... | collective-permute-start | bytes 3170312 | tf_op jit(solution)/shard_map/ppermute | solution.py:293
  29.9 11.7 %collective-permute-done.5.refs_6_ = f32[1032,256]{1,0:T(8,128)S(1)} collective-permute-done((f32[1032,256]{1,0:T(8,128)S(1)}, f32[1032,256]{1,0:T(8,128)S(1)}, u32[]{:S(2)}, u32[]{:S(2)}) %collective-permute-start.5) | collective-permute-done | bytes 1056800 | tf_op jit(solution)/shard_map/ppermute | solution.py:293
  41.5 1.7 %collective-permute-start.7 = (f32[1032,256]{1,0:T(8,128)S(1)}, f32[1032,256]{1,0:T(8,128)}, u32[]{:S(2)}, u32[]{:S(2)}) collective-permute-start(f32[1032,256]{1,0:T(8,128)S(1)} %collective-permute-done.5.refs_6_), channel_id=1, source_target_pairs={{4,7},{5,4},{6,5},{7,6},{8,11},{9,8},{10,9},{11,10},{13,12},{14,13... | collective-permute-start | bytes 3170312 | tf_op jit(solution)/shard_map/ppermute | solution.py:293
  43.2 12.2 %collective-permute-done.1.refs_2_ = f32[1032,256]{1,0:T(8,128)} collective-permute-done((f32[1032,256]{1,0:T(8,128)S(1)}, f32[1032,256]{1,0:T(8,128)}, u32[]{:S(2)}, u32[]{:S(2)}) %collective-permute-start.1) | collective-permute-done | bytes 1056800 | tf_op jit(solution)/shard_map/ppermute | solution.py:293
  55.4 2.4 %collective-permute-start.4 = (f32[1032,256]{1,0:T(8,128)}, f32[1032,256]{1,0:T(8,128)}, u32[]{:S(2)}, u32[]{:S(2)}) collective-permute-start(f32[1032,256]{1,0:T(8,128)} %collective-permute-done.1.refs_2_), channel_id=1, source_target_pairs={{4,0},{5,1},{6,2},{0,4},{1,5},{2,6},{12,8},{13,9},{14,10},{8,12},{... | collective-permute-start | bytes 3170312 | tf_op jit(solution)/shard_map/ppermute | solution.py:293
  57.8 0.0 collective-permute-done.refs_1_
  57.8 0.1 collective-permute-start.3
  57.9 0.7 dynamic-slice_bitcast_fusion.info_ref
  58.6 0.0 collective-permute-done.2.refs_3_
  58.6 0.0 collective-permute-done.8.refs_9_
  58.6 0.0 collective-permute-done.7.refs_8_
  58.6 1.8 %collective-permute-done.4.refs_5_ = f32[1032,256]{1,0:T(8,128)} collective-permute-done((f32[1032,256]{1,0:T(8,128)}, f32[1032,256]{1,0:T(8,128)}, u32[]{:S(2)}, u32[]{:S(2)}) %collective-permute-start.4) | collective-permute-done | bytes 1056800 | tf_op jit(solution)/shard_map/ppermute | solution.py:293
  60.4 1.5 %collective-permute-done.3.refs_4_ = f32[1032,256]{1,0:T(8,128)} collective-permute-done((f32[1032,256]{1,0:T(8,128)}, f32[1032,256]{1,0:T(8,128)}, u32[]{:S(2)}, u32[]{:S(2)}) %collective-permute-start.3) | collective-permute-done | bytes 1056800 | tf_op jit(solution)/shard_map/ppermute | solution.py:293
  61.9 10.1 %shard_map.38 = f32[1024,2048]{1,0:T(8,128)} custom-call(s32[10]{0:T(128)S(1)} %dynamic-slice_bitcast_fusion.info_ref, f32[1032,256]{1,0:T(8,128)S(1)} %shard_map.37.refs_0_, f32[1032,256]{1,0:T(8,128)} %collective-permute-done.refs_1_, f32[1032,256]{1,0:T(8,128)} %collective-permute-done.1.refs_2_, f32[1032,256]{1,0:T(8,128)} %collective-permute-done.2.refs_3_, ...), custom_call_target="tpu_custom_call" | custom-call | flops 1000000000 | bytes 20971520 | tf_op jit(solution)/shard_map/pallas_call | solution.py:301
  (1 shorter events, 0.0 us)
Async XLA Ops:
  0.0 1.2 %copy-start = (f32[1024,256]{1,0:T(8,128)S(1)}, f32[1024,256]{1,0:T(8,128)}, u32[]{:S(2)}) copy-start(f32[1024,256]{1,0:T(8,128)} %data_ref.1) | copy-start | bytes 3145732
  1.2 0.7 copy-start.1
  2.0 26.2 %collective-permute-start.6 = (f32[1032,256]{1,0:T(8,128)S(1)}, f32[1032,256]{1,0:T(8,128)S(1)}, u32[]{:S(2)}, u32[]{:S(2)}) collective-permute-start(f32[1032,256]{1,0:T(8,128)S(1)} %shard_map.37.refs_0_), channel_id=1, source_target_pairs={{16,17},{17,18},{18,19},{19,16},{20,21},{21,22},{22,23},{23,20},{2... | collective-permute-start | bytes 3170312 | tf_op jit(solution)/shard_map/ppermute | solution.py:293
  5.2 36.3 %collective-permute-start.5 = (f32[1032,256]{1,0:T(8,128)S(1)}, f32[1032,256]{1,0:T(8,128)S(1)}, u32[]{:S(2)}, u32[]{:S(2)}) collective-permute-start(f32[1032,256]{1,0:T(8,128)S(1)} %shard_map.37.refs_0_), channel_id=1, source_target_pairs={{4,7},{5,4},{6,5},{7,6},{8,11},{9,8},{10,9},{11,10},{28,31},{29,28... | collective-permute-start | bytes 3170312 | tf_op jit(solution)/shard_map/ppermute | solution.py:293
  7.3 48.1 %collective-permute-start.1 = (f32[1032,256]{1,0:T(8,128)S(1)}, f32[1032,256]{1,0:T(8,128)}, u32[]{:S(2)}, u32[]{:S(2)}) collective-permute-start(f32[1032,256]{1,0:T(8,128)S(1)} %shard_map.37.refs_0_), channel_id=1, source_target_pairs={{8,0},{17,1},{26,2},{12,4},{21,5},{30,6},{16,8},{25,9},{2,10},{20,... | collective-permute-start | bytes 3170312 | tf_op jit(solution)/shard_map/ppermute | solution.py:293
  7.6 50.1 %collective-permute-start = (f32[1032,256]{1,0:T(8,128)S(1)}, f32[1032,256]{1,0:T(8,128)}, u32[]{:S(2)}, u32[]{:S(2)}) collective-permute-start(f32[1032,256]{1,0:T(8,128)S(1)} %shard_map.37.refs_0_), channel_id=1, source_target_pairs={{9,1},{18,2},{27,3},{13,5},{22,6},{31,7},{17,9},{26,10},{3,11},{21... | collective-permute-start | bytes 3170312 | tf_op jit(solution)/shard_map/ppermute | solution.py:293
  9.6 49.0 %collective-permute-start.2 = (f32[1032,256]{1,0:T(8,128)S(1)}, f32[1032,256]{1,0:T(8,128)}, u32[]{:S(2)}, u32[]{:S(2)}) collective-permute-start(f32[1032,256]{1,0:T(8,128)S(1)} %shard_map.37.refs_0_), channel_id=1, source_target_pairs={{16,4},{25,5},{2,6},{11,7},{24,12},{1,13},{10,14},{19,15},{0,20},{... | collective-permute-start | bytes 3170312 | tf_op jit(solution)/shard_map/ppermute | solution.py:293
  28.2 30.4 %collective-permute-start.8 = (f32[1032,256]{1,0:T(8,128)S(1)}, f32[1032,256]{1,0:T(8,128)}, u32[]{:S(2)}, u32[]{:S(2)}) collective-permute-start(f32[1032,256]{1,0:T(8,128)S(1)} %collective-permute-done.6.refs_7_), channel_id=1, source_target_pairs={{16,17},{17,18},{18,19},{19,16},{20,21},{21,22},{22,23},{23,20},{1... | collective-permute-start | bytes 3170312 | tf_op jit(solution)/shard_map/ppermute | solution.py:293
  41.5 17.0 %collective-permute-start.7 = (f32[1032,256]{1,0:T(8,128)S(1)}, f32[1032,256]{1,0:T(8,128)}, u32[]{:S(2)}, u32[]{:S(2)}) collective-permute-start(f32[1032,256]{1,0:T(8,128)S(1)} %collective-permute-done.5.refs_6_), channel_id=1, source_target_pairs={{4,7},{5,4},{6,5},{7,6},{8,11},{9,8},{10,9},{11,10},{13,12},{14,13... | collective-permute-start | bytes 3170312 | tf_op jit(solution)/shard_map/ppermute | solution.py:293
  55.4 5.0 %collective-permute-start.4 = (f32[1032,256]{1,0:T(8,128)}, f32[1032,256]{1,0:T(8,128)}, u32[]{:S(2)}, u32[]{:S(2)}) collective-permute-start(f32[1032,256]{1,0:T(8,128)} %collective-permute-done.1.refs_2_), channel_id=1, source_target_pairs={{4,0},{5,1},{6,2},{0,4},{1,5},{2,6},{12,8},{13,9},{14,10},{8,12},{... | collective-permute-start | bytes 3170312 | tf_op jit(solution)/shard_map/ppermute | solution.py:293
  57.8 4.1 %collective-permute-start.3 = (f32[1032,256]{1,0:T(8,128)}, f32[1032,256]{1,0:T(8,128)}, u32[]{:S(2)}, u32[]{:S(2)}) collective-permute-start(f32[1032,256]{1,0:T(8,128)} %collective-permute-done.refs_1_), channel_id=1, source_target_pairs={{4,0},{5,1},{6,2},{7,3},{0,4},{1,5},{2,6},{3,7},{12,8},{13,9},{14,... | collective-permute-start | bytes 3170312 | tf_op jit(solution)/shard_map/ppermute | solution.py:293

commit v12 on v11

--- a/solution.py
+++ b/solution.py
@@ -53,7 +53,7 @@
     up = shift(once[1], 1, 4) + shift([0], -1, 4) + [((3, c), (3, c + 1)) for c in (0, 1, 2)] + [((3, 3), (1, 3))]
     again_down = shift(twice[-1], -1, 4) + [((3, 1), (3, 0)), ((3, 2), (3, 1)), ((0, 0), (3, 3))]
     again_up = shift(twice[1], 1, 4) + [((3, 1), (3, 2)), ((3, 2), (3, 3)), ((1, 3), (3, 0))]
-    return [(0, down), (0, up), (1, again_down), (2, again_up)]
+    return [(0, up), (0, down), (1, again_up), (2, again_down)]
 
 
 def right_plan(n_row, n_col, ratio):
@@ -64,13 +64,13 @@
             for step in range(STEPS)
         ]
     first = [(((r + 2 * c) % 8, c), (r, c)) for r, c in everyone if c != 0]
-    first += [((r + 1, 0), (r, 0)) for r in range(0, 8, 2)]
+    first += [((r ^ 1, 0), (r, 0)) for r in range(8)]
     second = [(((r + 2 * c + 2) % 8, c), (r, c)) for r, c in everyone if c != 3]
     second += [((r ^ 1, 3), (r, 3)) for r in range(8)]
     last = [(((r - 1 + 2 * c + 4) % 8, c), (r, c)) for r, c in everyone if r % 2 == 1]
-    first_swap = [((r ^ 1, c), (r, c)) for r, c in everyone]
-    second_swap = [((r ^ 1, c), (r, c)) for r, c in everyone if c != 3]
-    return [(0, first), (0, second), (0, last), (1, first_swap), (2, second_swap)]
+    last += [((r + 1, c), (r, c)) for r, c in everyone if r % 2 == 0]
+    swap = [((r ^ 1, c), (r, c)) for r, c in everyone]
+    return [(0, first), (0, second), (0, last), (1, swap), (2, swap)]
 
 
 def carry_out(perms, n_row, n_col):

time: 72.1 us -> 70.2 us (0.974)
  starting transfers between devices: 14.6 us -> 9.4 us
  waiting for transfers between devices: 44.5 us -> 47.9 us
    ppermute x9, starting transfers between devices: 14.6 us -> 9.4 us  [carry(): bufs.append(lax.ppermute(bufs[source], ('row', 'col'), flat))]
    ppermute x9, waiting for transfers between devices: 44.5 us -> 47.9 us  [carry(): bufs.append(lax.ppermute(bufs[source], ('row', 'col'), flat))]
where the time goes in v12:
time: 70.2 us; the launch traced here: 69.6 us
  waiting for transfers between devices  47.9 us (68%)
  Pallas kernels  9.65 us (14%)
  starting transfers between devices  9.4 us (13%)
  local copies, waits for them, and re-layouts  2.59 us (4%)
    ppermute x9, waiting for transfers between devices, carry(): bufs.append(lax.ppermute(bufs[source], ('row', 'col'), flat))  47.9 us
    pallas_call x1, Pallas kernels, local(): pl.pallas_call(functools.partial(product_kernel, slots, n_row, ratio, rb,...  9.56 us
    ppermute x9, starting transfers between devices, carry(): bufs.append(lax.ppermute(bufs[source], ('row', 'col'), flat))  9.4 us
    unnamed x4, local copies, waits for them, and re-layouts  1.91 us
  transfers between devices with their start and end apart: 9, of which 5 were waited for; matrix products, arithmetic and copies ran while one was open for 1% of the time, Pallas kernels for 0%

profile of v12, /device:TPU:15, one launch (start us, length us, event | category | flops | bytes accessed | tf_op | source)
XLA Modules:
  0.0 69.6 jit_solution(9413111609487839167)
XLA Ops:
  0.0 0.0 copy-start
  0.0 1.2 %copy-done = f32[1024,256]{1,0:T(8,128)S(1)} copy-done((f32[1024,256]{1,0:T(8,128)S(1)}, f32[1024,256]{1,0:T(8,128)}, u32[]{:S(2)}) %copy-start) | copy-done | bytes 1048600
  1.2 0.7 copy-done.1
  1.9 0.1 shard_map.37.refs_0_
  2.0 2.1 %collective-permute-start.6 = (f32[1032,256]{1,0:T(8,128)S(1)}, f32[1032,256]{1,0:T(8,128)S(1)}, u32[]{:S(2)}, u32[]{:S(2)}) collective-permute-start(f32[1032,256]{1,0:T(8,128)S(1)} %shard_map.37.refs_0_), channel_id=1, source_target_pairs={{4,7},{5,4},{6,5},{7,6},{8,11},{9,8},{10,9},{11,10},{28,31},{29,28... | collective-permute-start | bytes 3170312 | tf_op jit(solution)/shard_map/ppermute | solution.py:293
  4.1 3.2 %collective-permute-start.5 = (f32[1032,256]{1,0:T(8,128)S(1)}, f32[1032,256]{1,0:T(8,128)S(1)}, u32[]{:S(2)}, u32[]{:S(2)}) collective-permute-start(f32[1032,256]{1,0:T(8,128)S(1)} %shard_map.37.refs_0_), channel_id=1, source_target_pairs={{16,17},{17,18},{18,19},{19,16},{20,21},{21,22},{22,23},{23,20},{2... | collective-permute-start | bytes 3170312 | tf_op jit(solution)/shard_map/ppermute | solution.py:293
  7.3 0.3 collective-permute-start.1
  7.6 0.0 collective-permute-start
  7.6 0.0 collective-permute-start.2
  7.6 19.0 %collective-permute-done.6.refs_7_ = f32[1032,256]{1,0:T(8,128)S(1)} collective-permute-done((f32[1032,256]{1,0:T(8,128)S(1)}, f32[1032,256]{1,0:T(8,128)S(1)}, u32[]{:S(2)}, u32[]{:S(2)}) %collective-permute-start.6) | collective-permute-done | bytes 1056800 | tf_op jit(solution)/shard_map/ppermute | solution.py:293
  26.6 1.7 %collective-permute-start.8 = (f32[1032,256]{1,0:T(8,128)S(1)}, f32[1032,256]{1,0:T(8,128)}, u32[]{:S(2)}, u32[]{:S(2)}) collective-permute-start(f32[1032,256]{1,0:T(8,128)S(1)} %collective-permute-done.6.refs_7_), channel_id=1, source_target_pairs={{4,7},{5,4},{6,5},{7,6},{8,11},{9,8},{10,9},{11,10},{13,12},{14,13... | collective-permute-start | bytes 3170312 | tf_op jit(solution)/shard_map/ppermute | solution.py:293
  28.3 14.3 %collective-permute-done.5.refs_6_ = f32[1032,256]{1,0:T(8,128)S(1)} collective-permute-done((f32[1032,256]{1,0:T(8,128)S(1)}, f32[1032,256]{1,0:T(8,128)S(1)}, u32[]{:S(2)}, u32[]{:S(2)}) %collective-permute-start.5) | collective-permute-done | bytes 1056800 | tf_op jit(solution)/shard_map/ppermute | solution.py:293
  42.6 1.7 %collective-permute-start.7 = (f32[1032,256]{1,0:T(8,128)S(1)}, f32[1032,256]{1,0:T(8,128)}, u32[]{:S(2)}, u32[]{:S(2)}) collective-permute-start(f32[1032,256]{1,0:T(8,128)S(1)} %collective-permute-done.5.refs_6_), channel_id=1, source_target_pairs={{16,17},{17,18},{18,19},{19,16},{20,21},{21,22},{22,23},{23,20},{1... | collective-permute-start | bytes 3170312 | tf_op jit(solution)/shard_map/ppermute | solution.py:293
  44.2 11.2 %collective-permute-done.1.refs_2_ = f32[1032,256]{1,0:T(8,128)} collective-permute-done((f32[1032,256]{1,0:T(8,128)S(1)}, f32[1032,256]{1,0:T(8,128)}, u32[]{:S(2)}, u32[]{:S(2)}) %collective-permute-start.1) | collective-permute-done | bytes 1056800 | tf_op jit(solution)/shard_map/ppermute | solution.py:293
  55.4 0.5 collective-permute-start.4
  55.9 0.0 collective-permute-done.refs_1_
  55.9 0.0 collective-permute-start.3
  55.9 0.7 dynamic-slice_bitcast_fusion.info_ref
  56.6 0.0 collective-permute-done.2.refs_3_
  56.6 0.0 collective-permute-done.8.refs_9_
  56.6 0.0 collective-permute-done.7.refs_8_
  56.6 1.9 %collective-permute-done.4.refs_5_ = f32[1032,256]{1,0:T(8,128)} collective-permute-done((f32[1032,256]{1,0:T(8,128)}, f32[1032,256]{1,0:T(8,128)}, u32[]{:S(2)}, u32[]{:S(2)}) %collective-permute-start.4) | collective-permute-done | bytes 1056800 | tf_op jit(solution)/shard_map/ppermute | solution.py:293
  58.5 1.5 %collective-permute-done.3.refs_4_ = f32[1032,256]{1,0:T(8,128)} collective-permute-done((f32[1032,256]{1,0:T(8,128)}, f32[1032,256]{1,0:T(8,128)}, u32[]{:S(2)}, u32[]{:S(2)}) %collective-permute-start.3) | collective-permute-done | bytes 1056800 | tf_op jit(solution)/shard_map/ppermute | solution.py:293
  60.0 9.6 %shard_map.38 = f32[1024,2048]{1,0:T(8,128)} custom-call(s32[10]{0:T(128)S(1)} %dynamic-slice_bitcast_fusion.info_ref, f32[1032,256]{1,0:T(8,128)S(1)} %shard_map.37.refs_0_, f32[1032,256]{1,0:T(8,128)} %collective-permute-done.refs_1_, f32[1032,256]{1,0:T(8,128)} %collective-permute-done.1.refs_2_, f32[1032,256]{1,0:T(8,128)} %collective-permute-done.2.refs_3_, ...), custom_call_target="tpu_custom_call" | custom-call | flops 1000000000 | bytes 20971520 | tf_op jit(solution)/shard_map/pallas_call | solution.py:301
  (1 shorter events, 0.0 us)
Async XLA Ops:
  0.0 1.2 %copy-start = (f32[1024,256]{1,0:T(8,128)S(1)}, f32[1024,256]{1,0:T(8,128)}, u32[]{:S(2)}) copy-start(f32[1024,256]{1,0:T(8,128)} %data_ref.1) | copy-start | bytes 3145732
  1.2 0.7 copy-start.1
  2.0 24.6 %collective-permute-start.6 = (f32[1032,256]{1,0:T(8,128)S(1)}, f32[1032,256]{1,0:T(8,128)S(1)}, u32[]{:S(2)}, u32[]{:S(2)}) collective-permute-start(f32[1032,256]{1,0:T(8,128)S(1)} %shard_map.37.refs_0_), channel_id=1, source_target_pairs={{4,7},{5,4},{6,5},{7,6},{8,11},{9,8},{10,9},{11,10},{28,31},{29,28... | collective-permute-start | bytes 3170312 | tf_op jit(solution)/shard_map/ppermute | solution.py:293
  4.1 38.5 %collective-permute-start.5 = (f32[1032,256]{1,0:T(8,128)S(1)}, f32[1032,256]{1,0:T(8,128)S(1)}, u32[]{:S(2)}, u32[]{:S(2)}) collective-permute-start(f32[1032,256]{1,0:T(8,128)S(1)} %shard_map.37.refs_0_), channel_id=1, source_target_pairs={{16,17},{17,18},{18,19},{19,16},{20,21},{21,22},{22,23},{23,20},{2... | collective-permute-start | bytes 3170312 | tf_op jit(solution)/shard_map/ppermute | solution.py:293
  7.3 48.1 %collective-permute-start.1 = (f32[1032,256]{1,0:T(8,128)S(1)}, f32[1032,256]{1,0:T(8,128)}, u32[]{:S(2)}, u32[]{:S(2)}) collective-permute-start(f32[1032,256]{1,0:T(8,128)S(1)} %shard_map.37.refs_0_), channel_id=1, source_target_pairs={{8,0},{17,1},{26,2},{12,4},{21,5},{30,6},{16,8},{25,9},{2,10},{20,... | collective-permute-start | bytes 3170312 | tf_op jit(solution)/shard_map/ppermute | solution.py:293
  7.6 48.3 %collective-permute-start = (f32[1032,256]{1,0:T(8,128)S(1)}, f32[1032,256]{1,0:T(8,128)}, u32[]{:S(2)}, u32[]{:S(2)}) collective-permute-start(f32[1032,256]{1,0:T(8,128)S(1)} %shard_map.37.refs_0_), channel_id=1, source_target_pairs={{9,1},{18,2},{27,3},{13,5},{22,6},{31,7},{17,9},{26,10},{3,11},{21... | collective-permute-start | bytes 3170312 | tf_op jit(solution)/shard_map/ppermute | solution.py:293
  7.6 49.0 %collective-permute-start.2 = (f32[1032,256]{1,0:T(8,128)S(1)}, f32[1032,256]{1,0:T(8,128)}, u32[]{:S(2)}, u32[]{:S(2)}) collective-permute-start(f32[1032,256]{1,0:T(8,128)S(1)} %shard_map.37.refs_0_), channel_id=1, source_target_pairs={{16,4},{25,5},{2,6},{11,7},{24,12},{1,13},{10,14},{19,15},{0,20},{... | collective-permute-start | bytes 3170312 | tf_op jit(solution)/shard_map/ppermute | solution.py:293
  26.6 30.0 %collective-permute-start.8 = (f32[1032,256]{1,0:T(8,128)S(1)}, f32[1032,256]{1,0:T(8,128)}, u32[]{:S(2)}, u32[]{:S(2)}) collective-permute-start(f32[1032,256]{1,0:T(8,128)S(1)} %collective-permute-done.6.refs_7_), channel_id=1, source_target_pairs={{4,7},{5,4},{6,5},{7,6},{8,11},{9,8},{10,9},{11,10},{13,12},{14,13... | collective-permute-start | bytes 3170312 | tf_op jit(solution)/shard_map/ppermute | solution.py:293
  42.6 14.1 %collective-permute-start.7 = (f32[1032,256]{1,0:T(8,128)S(1)}, f32[1032,256]{1,0:T(8,128)}, u32[]{:S(2)}, u32[]{:S(2)}) collective-permute-start(f32[1032,256]{1,0:T(8,128)S(1)} %collective-permute-done.5.refs_6_), channel_id=1, source_target_pairs={{16,17},{17,18},{18,19},{19,16},{20,21},{21,22},{22,23},{23,20},{1... | collective-permute-start | bytes 3170312 | tf_op jit(solution)/shard_map/ppermute | solution.py:293
  55.4 3.1 %collective-permute-start.4 = (f32[1032,256]{1,0:T(8,128)}, f32[1032,256]{1,0:T(8,128)}, u32[]{:S(2)}, u32[]{:S(2)}) collective-permute-start(f32[1032,256]{1,0:T(8,128)} %collective-permute-done.1.refs_2_), channel_id=1, source_target_pairs={{4,0},{5,1},{6,2},{7,3},{0,4},{1,5},{2,6},{3,7},{12,8},{13,9},{14,... | collective-permute-start | bytes 3170312 | tf_op jit(solution)/shard_map/ppermute | solution.py:293
  55.9 4.1 %collective-permute-start.3 = (f32[1032,256]{1,0:T(8,128)}, f32[1032,256]{1,0:T(8,128)}, u32[]{:S(2)}, u32[]{:S(2)}) collective-permute-start(f32[1032,256]{1,0:T(8,128)} %collective-permute-done.refs_1_), channel_id=1, source_target_pairs={{4,0},{5,1},{6,2},{7,3},{0,4},{1,5},{2,6},{3,7},{12,8},{13,9},{14,... | collective-permute-start | bytes 3170312 | tf_op jit(solution)/shard_map/ppermute | solution.py:293

commit v13 on v12

--- a/solution.py
+++ b/solution.py
@@ -12,7 +12,7 @@
 STEPS = 4
 UNROLL = 8
 EXTRA = 8
-PARTS = 8
+PARTS = 16
 
 
 def left_offsets(row, ratio, n_col):
@@ -134,12 +134,19 @@
     for slot in range(slots):
         fetch(info_ref[slot], among[slot], left_bufs, left.at[slot], lsem.at[slot])
 
-    def clear(first, last):
+    def clear(first, rows_count):
+        at = pl.ds(pl.multiple_of(first, 8), rows_count)
+        acc[at, :] = jnp.zeros((rows_count, acc.shape[1]), jnp.float32)
+
+    beside = BS // 64 * 24
+    ahead = (BS - beside) * rb // BS
+
+    def clear_blocks(first, last):
         @pl.loop(first, last)
-        def _(r):
-            acc[pl.ds(pl.multiple_of(r * BS, BS), BS), :] = jnp.zeros((BS, acc.shape[1]), jnp.float32)
-
-    clear(0, rb // 4)
+        def _(block):
+            clear(block * BS, BS)
+
+    clear_blocks(0, ahead // 2)
     lanes = scalars.shape[1]
     row = lax.broadcasted_iota(jnp.int32, (w, lanes), 1)
     tile_slot = lax.broadcasted_iota(jnp.int32, (w, lanes), 0)
@@ -169,7 +176,7 @@
     coded[(slots + STEPS) * w : (slots + STEPS + 1) * w, :] = jnp.full((w, lanes), 2 << 16, jnp.int32)
     to_scalars = pltpu.make_async_copy(coded, scalars, csem.at[slots + STEPS])
     to_scalars.start()
-    clear(rb // 4, rb)
+    clear_blocks(ahead // 2, ahead)
     to_scalars.wait()
 
     part_rows = rb // PARTS
@@ -179,6 +186,7 @@
             codes[place] = code
             place = place + (code >= 0).astype(jnp.int32)
         ends[row] = (place + UNROLL - 1) // UNROLL
+        clear(ahead * BS + row * beside, beside)
         return place
 
     listed_end = lax.fori_loop(0, rb, listed, jnp.int32(0))

time: 70.2 us -> 70.4 us (level)
  no operation moved by 1% of the time
where the time goes in v13:
time: 70.4 us; the launch traced here: 69.9 us
  waiting for transfers between devices  47.9 us (68%)
  Pallas kernels  9.97 us (14%)
  starting transfers between devices  9.4 us (13%)
  local copies, waits for them, and re-layouts  2.59 us (4%)
    ppermute x9, waiting for transfers between devices, carry(): bufs.append(lax.ppermute(bufs[source], ('row', 'col'), flat))  47.9 us
    pallas_call x1, Pallas kernels, local(): pl.pallas_call(functools.partial(product_kernel, slots, n_row, ratio, rb,...  9.87 us
    ppermute x9, starting transfers between devices, carry(): bufs.append(lax.ppermute(bufs[source], ('row', 'col'), flat))  9.4 us
    unnamed x4, local copies, waits for them, and re-layouts  1.91 us
  transfers between devices with their start and end apart: 9, of which 5 were waited for; matrix products, arithmetic and copies ran while one was open for 1% of the time, Pallas kernels for 0%

profile of v13, /device:TPU:15, one launch (start us, length us, event | category | flops | bytes accessed | tf_op | source)
XLA Modules:
  0.0 69.9 jit_solution(8194654487295055216)
XLA Ops:
  0.0 0.0 copy-start
  0.0 1.2 %copy-done = f32[1024,256]{1,0:T(8,128)S(1)} copy-done((f32[1024,256]{1,0:T(8,128)S(1)}, f32[1024,256]{1,0:T(8,128)}, u32[]{:S(2)}) %copy-start) | copy-done | bytes 1048600
  1.2 0.7 copy-done.1
  1.9 0.1 shard_map.37.refs_0_
  2.0 2.1 %collective-permute-start.6 = (f32[1032,256]{1,0:T(8,128)S(1)}, f32[1032,256]{1,0:T(8,128)S(1)}, u32[]{:S(2)}, u32[]{:S(2)}) collective-permute-start(f32[1032,256]{1,0:T(8,128)S(1)} %shard_map.37.refs_0_), channel_id=1, source_target_pairs={{4,7},{5,4},{6,5},{7,6},{8,11},{9,8},{10,9},{11,10},{28,31},{29,28... | collective-permute-start | bytes 3170312 | tf_op jit(solution)/shard_map/ppermute | solution.py:301
  4.1 3.2 %collective-permute-start.5 = (f32[1032,256]{1,0:T(8,128)S(1)}, f32[1032,256]{1,0:T(8,128)S(1)}, u32[]{:S(2)}, u32[]{:S(2)}) collective-permute-start(f32[1032,256]{1,0:T(8,128)S(1)} %shard_map.37.refs_0_), channel_id=1, source_target_pairs={{16,17},{17,18},{18,19},{19,16},{20,21},{21,22},{22,23},{23,20},{2... | collective-permute-start | bytes 3170312 | tf_op jit(solution)/shard_map/ppermute | solution.py:301
  7.3 0.3 collective-permute-start.1
  7.6 0.0 collective-permute-start
  7.6 0.0 collective-permute-start.2
  7.6 19.0 %collective-permute-done.6.refs_7_ = f32[1032,256]{1,0:T(8,128)S(1)} collective-permute-done((f32[1032,256]{1,0:T(8,128)S(1)}, f32[1032,256]{1,0:T(8,128)S(1)}, u32[]{:S(2)}, u32[]{:S(2)}) %collective-permute-start.6) | collective-permute-done | bytes 1056800 | tf_op jit(solution)/shard_map/ppermute | solution.py:301
  26.6 1.7 %collective-permute-start.8 = (f32[1032,256]{1,0:T(8,128)S(1)}, f32[1032,256]{1,0:T(8,128)}, u32[]{:S(2)}, u32[]{:S(2)}) collective-permute-start(f32[1032,256]{1,0:T(8,128)S(1)} %collective-permute-done.6.refs_7_), channel_id=1, source_target_pairs={{4,7},{5,4},{6,5},{7,6},{8,11},{9,8},{10,9},{11,10},{13,12},{14,13... | collective-permute-start | bytes 3170312 | tf_op jit(solution)/shard_map/ppermute | solution.py:301
  28.3 14.3 %collective-permute-done.5.refs_6_ = f32[1032,256]{1,0:T(8,128)S(1)} collective-permute-done((f32[1032,256]{1,0:T(8,128)S(1)}, f32[1032,256]{1,0:T(8,128)S(1)}, u32[]{:S(2)}, u32[]{:S(2)}) %collective-permute-start.5) | collective-permute-done | bytes 1056800 | tf_op jit(solution)/shard_map/ppermute | solution.py:301
  42.6 1.7 %collective-permute-start.7 = (f32[1032,256]{1,0:T(8,128)S(1)}, f32[1032,256]{1,0:T(8,128)}, u32[]{:S(2)}, u32[]{:S(2)}) collective-permute-start(f32[1032,256]{1,0:T(8,128)S(1)} %collective-permute-done.5.refs_6_), channel_id=1, source_target_pairs={{16,17},{17,18},{18,19},{19,16},{20,21},{21,22},{22,23},{23,20},{1... | collective-permute-start | bytes 3170312 | tf_op jit(solution)/shard_map/ppermute | solution.py:301
  44.2 11.2 %collective-permute-done.1.refs_2_ = f32[1032,256]{1,0:T(8,128)} collective-permute-done((f32[1032,256]{1,0:T(8,128)S(1)}, f32[1032,256]{1,0:T(8,128)}, u32[]{:S(2)}, u32[]{:S(2)}) %collective-permute-start.1) | collective-permute-done | bytes 1056800 | tf_op jit(solution)/shard_map/ppermute | solution.py:301
  55.4 0.5 collective-permute-start.4
  55.9 0.0 collective-permute-done.refs_1_
  55.9 0.0 collective-permute-start.3
  55.9 0.7 dynamic-slice_bitcast_fusion.info_ref
  56.6 0.0 collective-permute-done.2.refs_3_
  56.6 0.0 collective-permute-done.8.refs_9_
  56.6 0.0 collective-permute-done.7.refs_8_
  56.6 1.9 %collective-permute-done.4.refs_5_ = f32[1032,256]{1,0:T(8,128)} collective-permute-done((f32[1032,256]{1,0:T(8,128)}, f32[1032,256]{1,0:T(8,128)}, u32[]{:S(2)}, u32[]{:S(2)}) %collective-permute-start.4) | collective-permute-done | bytes 1056800 | tf_op jit(solution)/shard_map/ppermute | solution.py:301
  58.5 1.5 %collective-permute-done.3.refs_4_ = f32[1032,256]{1,0:T(8,128)} collective-permute-done((f32[1032,256]{1,0:T(8,128)}, f32[1032,256]{1,0:T(8,128)}, u32[]{:S(2)}, u32[]{:S(2)}) %collective-permute-start.3) | collective-permute-done | bytes 1056800 | tf_op jit(solution)/shard_map/ppermute | solution.py:301
  60.0 9.9 %shard_map.38 = f32[1024,2048]{1,0:T(8,128)} custom-call(s32[10]{0:T(128)S(1)} %dynamic-slice_bitcast_fusion.info_ref, f32[1032,256]{1,0:T(8,128)S(1)} %shard_map.37.refs_0_, f32[1032,256]{1,0:T(8,128)} %collective-permute-done.refs_1_, f32[1032,256]{1,0:T(8,128)} %collective-permute-done.1.refs_2_, f32[1032,256]{1,0:T(8,128)} %collective-permute-done.2.refs_3_, ...), custom_call_target="tpu_custom_call" | custom-call | flops 1000000000 | bytes 20971520 | tf_op jit(solution)/shard_map/pallas_call | solution.py:309
  (1 shorter events, 0.0 us)
Async XLA Ops:
  0.0 1.2 %copy-start = (f32[1024,256]{1,0:T(8,128)S(1)}, f32[1024,256]{1,0:T(8,128)}, u32[]{:S(2)}) copy-start(f32[1024,256]{1,0:T(8,128)} %data_ref.1) | copy-start | bytes 3145732
  1.2 0.7 copy-start.1
  2.0 24.6 %collective-permute-start.6 = (f32[1032,256]{1,0:T(8,128)S(1)}, f32[1032,256]{1,0:T(8,128)S(1)}, u32[]{:S(2)}, u32[]{:S(2)}) collective-permute-start(f32[1032,256]{1,0:T(8,128)S(1)} %shard_map.37.refs_0_), channel_id=1, source_target_pairs={{4,7},{5,4},{6,5},{7,6},{8,11},{9,8},{10,9},{11,10},{28,31},{29,28... | collective-permute-start | bytes 3170312 | tf_op jit(solution)/shard_map/ppermute | solution.py:301
  4.1 38.5 %collective-permute-start.5 = (f32[1032,256]{1,0:T(8,128)S(1)}, f32[1032,256]{1,0:T(8,128)S(1)}, u32[]{:S(2)}, u32[]{:S(2)}) collective-permute-start(f32[1032,256]{1,0:T(8,128)S(1)} %shard_map.37.refs_0_), channel_id=1, source_target_pairs={{16,17},{17,18},{18,19},{19,16},{20,21},{21,22},{22,23},{23,20},{2... | collective-permute-start | bytes 3170312 | tf_op jit(solution)/shard_map/ppermute | solution.py:301
  7.3 48.1 %collective-permute-start.1 = (f32[1032,256]{1,0:T(8,128)S(1)}, f32[1032,256]{1,0:T(8,128)}, u32[]{:S(2)}, u32[]{:S(2)}) collective-permute-start(f32[1032,256]{1,0:T(8,128)S(1)} %shard_map.37.refs_0_), channel_id=1, source_target_pairs={{8,0},{17,1},{26,2},{12,4},{21,5},{30,6},{16,8},{25,9},{2,10},{20,... | collective-permute-start | bytes 3170312 | tf_op jit(solution)/shard_map/ppermute | solution.py:301
  7.6 48.3 %collective-permute-start = (f32[1032,256]{1,0:T(8,128)S(1)}, f32[1032,256]{1,0:T(8,128)}, u32[]{:S(2)}, u32[]{:S(2)}) collective-permute-start(f32[1032,256]{1,0:T(8,128)S(1)} %shard_map.37.refs_0_), channel_id=1, source_target_pairs={{9,1},{18,2},{27,3},{13,5},{22,6},{31,7},{17,9},{26,10},{3,11},{21... | collective-permute-start | bytes 3170312 | tf_op jit(solution)/shard_map/ppermute | solution.py:301
  7.6 49.0 %collective-permute-start.2 = (f32[1032,256]{1,0:T(8,128)S(1)}, f32[1032,256]{1,0:T(8,128)}, u32[]{:S(2)}, u32[]{:S(2)}) collective-permute-start(f32[1032,256]{1,0:T(8,128)S(1)} %shard_map.37.refs_0_), channel_id=1, source_target_pairs={{16,4},{25,5},{2,6},{11,7},{24,12},{1,13},{10,14},{19,15},{0,20},{... | collective-permute-start | bytes 3170312 | tf_op jit(solution)/shard_map/ppermute | solution.py:301
  26.6 30.0 %collective-permute-start.8 = (f32[1032,256]{1,0:T(8,128)S(1)}, f32[1032,256]{1,0:T(8,128)}, u32[]{:S(2)}, u32[]{:S(2)}) collective-permute-start(f32[1032,256]{1,0:T(8,128)S(1)} %collective-permute-done.6.refs_7_), channel_id=1, source_target_pairs={{4,7},{5,4},{6,5},{7,6},{8,11},{9,8},{10,9},{11,10},{13,12},{14,13... | collective-permute-start | bytes 3170312 | tf_op jit(solution)/shard_map/ppermute | solution.py:301
  42.6 14.1 %collective-permute-start.7 = (f32[1032,256]{1,0:T(8,128)S(1)}, f32[1032,256]{1,0:T(8,128)}, u32[]{:S(2)}, u32[]{:S(2)}) collective-permute-start(f32[1032,256]{1,0:T(8,128)S(1)} %collective-permute-done.5.refs_6_), channel_id=1, source_target_pairs={{16,17},{17,18},{18,19},{19,16},{20,21},{21,22},{22,23},{23,20},{1... | collective-permute-start | bytes 3170312 | tf_op jit(solution)/shard_map/ppermute | solution.py:301
  55.4 3.1 %collective-permute-start.4 = (f32[1032,256]{1,0:T(8,128)}, f32[1032,256]{1,0:T(8,128)}, u32[]{:S(2)}, u32[]{:S(2)}) collective-permute-start(f32[1032,256]{1,0:T(8,128)} %collective-permute-done.1.refs_2_), channel_id=1, source_target_pairs={{4,0},{5,1},{6,2},{7,3},{0,4},{1,5},{2,6},{3,7},{12,8},{13,9},{14,... | collective-permute-start | bytes 3170312 | tf_op jit(solution)/shard_map/ppermute | solution.py:301
  55.9 4.1 %collective-permute-start.3 = (f32[1032,256]{1,0:T(8,128)}, f32[1032,256]{1,0:T(8,128)}, u32[]{:S(2)}, u32[]{:S(2)}) collective-permute-start(f32[1032,256]{1,0:T(8,128)} %collective-permute-done.refs_1_), channel_id=1, source_target_pairs={{4,0},{5,1},{6,2},{7,3},{0,4},{1,5},{2,6},{3,7},{12,8},{13,9},{14,... | collective-permute-start | bytes 3170312 | tf_op jit(solution)/shard_map/ppermute | solution.py:301

commit v14 on v13

--- a/solution.py
+++ b/solution.py
@@ -240,13 +240,12 @@
         at = pl.ds(part * part_rows * BS, part_rows * BS)
         return pltpu.make_async_copy(acc.at[at], out_ref.at[at], osem.at[part])
 
-    def products(group):
+    def step_of(group, adds, multiplies):
         for u in range(UNROLL):
-            value[u] = product(codes[group * UNROLL + u])
-
-    def sums(group):
-        for u in range(UNROLL):
-            add(codes[group * UNROLL + u], value[u])
+            if adds:
+                add(codes[group * UNROLL + u], value[u])
+            if multiplies:
+                value[u] = product(codes[(group + 1) * UNROLL + u])
 
     last = jnp.maximum(ends[rb - 1] - 1, 0)
 
@@ -256,15 +255,14 @@
             def _():
                 out_copy(part).start()
 
-    products(0)
+    step_of(-1, False, True)
 
     @pl.loop(0, last)
     def _(group):
-        sums(group)
-        products(group + 1)
+        step_of(group, True, True)
         leave(group)
 
-    sums(last)
+    step_of(last, True, False)
     leave(last)
     for part in range(PARTS):
         out_copy(part).wait()

time: 70.4 us -> 70.3 us (level)
  no operation moved by 1% of the time
where the time goes in v14:
time: 70.3 us; the launch traced here: 70 us
  waiting for transfers between devices  47.9 us (68%)
  Pallas kernels  10.1 us (14%)
  starting transfers between devices  9.4 us (13%)
  local copies, waits for them, and re-layouts  2.59 us (4%)
    ppermute x9, waiting for transfers between devices, carry(): bufs.append(lax.ppermute(bufs[source], ('row', 'col'), flat))  47.9 us
    pallas_call x1, Pallas kernels, local(): pl.pallas_call(functools.partial(product_kernel, slots, n_row, ratio, rb,...  10 us
    ppermute x9, starting transfers between devices, carry(): bufs.append(lax.ppermute(bufs[source], ('row', 'col'), flat))  9.4 us
    unnamed x4, local copies, waits for them, and re-layouts  1.91 us
  transfers between devices with their start and end apart: 9, of which 5 were waited for; matrix products, arithmetic and copies ran while one was open for 1% of the time, Pallas kernels for 0%

profile of v14, /device:TPU:15, one launch (start us, length us, event | category | flops | bytes accessed | tf_op | source)
XLA Modules:
  0.0 70.0 jit_solution(1983853253537469301)
XLA Ops:
  0.0 0.0 copy-start
  0.0 1.2 %copy-done = f32[1024,256]{1,0:T(8,128)S(1)} copy-done((f32[1024,256]{1,0:T(8,128)S(1)}, f32[1024,256]{1,0:T(8,128)}, u32[]{:S(2)}) %copy-start) | copy-done | bytes 1048600
  1.2 0.7 copy-done.1
  1.9 0.1 shard_map.37.refs_0_
  2.0 2.1 %collective-permute-start.6 = (f32[1032,256]{1,0:T(8,128)S(1)}, f32[1032,256]{1,0:T(8,128)S(1)}, u32[]{:S(2)}, u32[]{:S(2)}) collective-permute-start(f32[1032,256]{1,0:T(8,128)S(1)} %shard_map.37.refs_0_), channel_id=1, source_target_pairs={{4,7},{5,4},{6,5},{7,6},{8,11},{9,8},{10,9},{11,10},{28,31},{29,28... | collective-permute-start | bytes 3170312 | tf_op jit(solution)/shard_map/ppermute | solution.py:299
  4.1 3.2 %collective-permute-start.5 = (f32[1032,256]{1,0:T(8,128)S(1)}, f32[1032,256]{1,0:T(8,128)S(1)}, u32[]{:S(2)}, u32[]{:S(2)}) collective-permute-start(f32[1032,256]{1,0:T(8,128)S(1)} %shard_map.37.refs_0_), channel_id=1, source_target_pairs={{16,17},{17,18},{18,19},{19,16},{20,21},{21,22},{22,23},{23,20},{2... | collective-permute-start | bytes 3170312 | tf_op jit(solution)/shard_map/ppermute | solution.py:299
  7.3 0.3 collective-permute-start.1
  7.6 0.0 collective-permute-start
  7.6 0.0 collective-permute-start.2
  7.6 19.0 %collective-permute-done.6.refs_7_ = f32[1032,256]{1,0:T(8,128)S(1)} collective-permute-done((f32[1032,256]{1,0:T(8,128)S(1)}, f32[1032,256]{1,0:T(8,128)S(1)}, u32[]{:S(2)}, u32[]{:S(2)}) %collective-permute-start.6) | collective-permute-done | bytes 1056800 | tf_op jit(solution)/shard_map/ppermute | solution.py:299
  26.6 1.7 %collective-permute-start.8 = (f32[1032,256]{1,0:T(8,128)S(1)}, f32[1032,256]{1,0:T(8,128)}, u32[]{:S(2)}, u32[]{:S(2)}) collective-permute-start(f32[1032,256]{1,0:T(8,128)S(1)} %collective-permute-done.6.refs_7_), channel_id=1, source_target_pairs={{4,7},{5,4},{6,5},{7,6},{8,11},{9,8},{10,9},{11,10},{13,12},{14,13... | collective-permute-start | bytes 3170312 | tf_op jit(solution)/shard_map/ppermute | solution.py:299
  28.3 14.3 %collective-permute-done.5.refs_6_ = f32[1032,256]{1,0:T(8,128)S(1)} collective-permute-done((f32[1032,256]{1,0:T(8,128)S(1)}, f32[1032,256]{1,0:T(8,128)S(1)}, u32[]{:S(2)}, u32[]{:S(2)}) %collective-permute-start.5) | collective-permute-done | bytes 1056800 | tf_op jit(solution)/shard_map/ppermute | solution.py:299
  42.6 1.7 %collective-permute-start.7 = (f32[1032,256]{1,0:T(8,128)S(1)}, f32[1032,256]{1,0:T(8,128)}, u32[]{:S(2)}, u32[]{:S(2)}) collective-permute-start(f32[1032,256]{1,0:T(8,128)S(1)} %collective-permute-done.5.refs_6_), channel_id=1, source_target_pairs={{16,17},{17,18},{18,19},{19,16},{20,21},{21,22},{22,23},{23,20},{1... | collective-permute-start | bytes 3170312 | tf_op jit(solution)/shard_map/ppermute | solution.py:299
  44.2 11.2 %collective-permute-done.1.refs_2_ = f32[1032,256]{1,0:T(8,128)} collective-permute-done((f32[1032,256]{1,0:T(8,128)S(1)}, f32[1032,256]{1,0:T(8,128)}, u32[]{:S(2)}, u32[]{:S(2)}) %collective-permute-start.1) | collective-permute-done | bytes 1056800 | tf_op jit(solution)/shard_map/ppermute | solution.py:299
  55.4 0.5 collective-permute-start.4
  55.9 0.0 collective-permute-done.refs_1_
  55.9 0.0 collective-permute-start.3
  55.9 0.7 dynamic-slice_bitcast_fusion.info_ref
  56.6 0.0 collective-permute-done.2.refs_3_
  56.6 0.0 collective-permute-done.8.refs_9_
  56.6 0.0 collective-permute-done.7.refs_8_
  56.6 1.9 %collective-permute-done.4.refs_5_ = f32[1032,256]{1,0:T(8,128)} collective-permute-done((f32[1032,256]{1,0:T(8,128)}, f32[1032,256]{1,0:T(8,128)}, u32[]{:S(2)}, u32[]{:S(2)}) %collective-permute-start.4) | collective-permute-done | bytes 1056800 | tf_op jit(solution)/shard_map/ppermute | solution.py:299
  58.5 1.5 %collective-permute-done.3.refs_4_ = f32[1032,256]{1,0:T(8,128)} collective-permute-done((f32[1032,256]{1,0:T(8,128)}, f32[1032,256]{1,0:T(8,128)}, u32[]{:S(2)}, u32[]{:S(2)}) %collective-permute-start.3) | collective-permute-done | bytes 1056800 | tf_op jit(solution)/shard_map/ppermute | solution.py:299
  60.0 10.0 %shard_map.38 = f32[1024,2048]{1,0:T(8,128)} custom-call(s32[10]{0:T(128)S(1)} %dynamic-slice_bitcast_fusion.info_ref, f32[1032,256]{1,0:T(8,128)S(1)} %shard_map.37.refs_0_, f32[1032,256]{1,0:T(8,128)} %collective-permute-done.refs_1_, f32[1032,256]{1,0:T(8,128)} %collective-permute-done.1.refs_2_, f32[1032,256]{1,0:T(8,128)} %collective-permute-done.2.refs_3_, ...), custom_call_target="tpu_custom_call" | custom-call | flops 1000000000 | bytes 20971520 | tf_op jit(solution)/shard_map/pallas_call | solution.py:307
  (1 shorter events, 0.0 us)
Async XLA Ops:
  0.0 1.2 %copy-start = (f32[1024,256]{1,0:T(8,128)S(1)}, f32[1024,256]{1,0:T(8,128)}, u32[]{:S(2)}) copy-start(f32[1024,256]{1,0:T(8,128)} %data_ref.1) | copy-start | bytes 3145732
  1.2 0.7 copy-start.1
  2.0 24.6 %collective-permute-start.6 = (f32[1032,256]{1,0:T(8,128)S(1)}, f32[1032,256]{1,0:T(8,128)S(1)}, u32[]{:S(2)}, u32[]{:S(2)}) collective-permute-start(f32[1032,256]{1,0:T(8,128)S(1)} %shard_map.37.refs_0_), channel_id=1, source_target_pairs={{4,7},{5,4},{6,5},{7,6},{8,11},{9,8},{10,9},{11,10},{28,31},{29,28... | collective-permute-start | bytes 3170312 | tf_op jit(solution)/shard_map/ppermute | solution.py:299
  4.1 38.5 %collective-permute-start.5 = (f32[1032,256]{1,0:T(8,128)S(1)}, f32[1032,256]{1,0:T(8,128)S(1)}, u32[]{:S(2)}, u32[]{:S(2)}) collective-permute-start(f32[1032,256]{1,0:T(8,128)S(1)} %shard_map.37.refs_0_), channel_id=1, source_target_pairs={{16,17},{17,18},{18,19},{19,16},{20,21},{21,22},{22,23},{23,20},{2... | collective-permute-start | bytes 3170312 | tf_op jit(solution)/shard_map/ppermute | solution.py:299
  7.3 48.1 %collective-permute-start.1 = (f32[1032,256]{1,0:T(8,128)S(1)}, f32[1032,256]{1,0:T(8,128)}, u32[]{:S(2)}, u32[]{:S(2)}) collective-permute-start(f32[1032,256]{1,0:T(8,128)S(1)} %shard_map.37.refs_0_), channel_id=1, source_target_pairs={{8,0},{17,1},{26,2},{12,4},{21,5},{30,6},{16,8},{25,9},{2,10},{20,... | collective-permute-start | bytes 3170312 | tf_op jit(solution)/shard_map/ppermute | solution.py:299
  7.6 48.3 %collective-permute-start = (f32[1032,256]{1,0:T(8,128)S(1)}, f32[1032,256]{1,0:T(8,128)}, u32[]{:S(2)}, u32[]{:S(2)}) collective-permute-start(f32[1032,256]{1,0:T(8,128)S(1)} %shard_map.37.refs_0_), channel_id=1, source_target_pairs={{9,1},{18,2},{27,3},{13,5},{22,6},{31,7},{17,9},{26,10},{3,11},{21... | collective-permute-start | bytes 3170312 | tf_op jit(solution)/shard_map/ppermute | solution.py:299
  7.6 49.0 %collective-permute-start.2 = (f32[1032,256]{1,0:T(8,128)S(1)}, f32[1032,256]{1,0:T(8,128)}, u32[]{:S(2)}, u32[]{:S(2)}) collective-permute-start(f32[1032,256]{1,0:T(8,128)S(1)} %shard_map.37.refs_0_), channel_id=1, source_target_pairs={{16,4},{25,5},{2,6},{11,7},{24,12},{1,13},{10,14},{19,15},{0,20},{... | collective-permute-start | bytes 3170312 | tf_op jit(solution)/shard_map/ppermute | solution.py:299
  26.6 30.0 %collective-permute-start.8 = (f32[1032,256]{1,0:T(8,128)S(1)}, f32[1032,256]{1,0:T(8,128)}, u32[]{:S(2)}, u32[]{:S(2)}) collective-permute-start(f32[1032,256]{1,0:T(8,128)S(1)} %collective-permute-done.6.refs_7_), channel_id=1, source_target_pairs={{4,7},{5,4},{6,5},{7,6},{8,11},{9,8},{10,9},{11,10},{13,12},{14,13... | collective-permute-start | bytes 3170312 | tf_op jit(solution)/shard_map/ppermute | solution.py:299
  42.6 14.1 %collective-permute-start.7 = (f32[1032,256]{1,0:T(8,128)S(1)}, f32[1032,256]{1,0:T(8,128)}, u32[]{:S(2)}, u32[]{:S(2)}) collective-permute-start(f32[1032,256]{1,0:T(8,128)S(1)} %collective-permute-done.5.refs_6_), channel_id=1, source_target_pairs={{16,17},{17,18},{18,19},{19,16},{20,21},{21,22},{22,23},{23,20},{1... | collective-permute-start | bytes 3170312 | tf_op jit(solution)/shard_map/ppermute | solution.py:299
  55.4 3.1 %collective-permute-start.4 = (f32[1032,256]{1,0:T(8,128)}, f32[1032,256]{1,0:T(8,128)}, u32[]{:S(2)}, u32[]{:S(2)}) collective-permute-start(f32[1032,256]{1,0:T(8,128)} %collective-permute-done.1.refs_2_), channel_id=1, source_target_pairs={{4,0},{5,1},{6,2},{7,3},{0,4},{1,5},{2,6},{3,7},{12,8},{13,9},{14,... | collective-permute-start | bytes 3170312 | tf_op jit(solution)/shard_map/ppermute | solution.py:299
  55.9 4.1 %collective-permute-start.3 = (f32[1032,256]{1,0:T(8,128)}, f32[1032,256]{1,0:T(8,128)}, u32[]{:S(2)}, u32[]{:S(2)}) collective-permute-start(f32[1032,256]{1,0:T(8,128)} %collective-permute-done.refs_1_), channel_id=1, source_target_pairs={{4,0},{5,1},{6,2},{7,3},{0,4},{1,5},{2,6},{3,7},{12,8},{13,9},{14,... | collective-permute-start | bytes 3170312 | tf_op jit(solution)/shard_map/ppermute | solution.py:299

commit v15 on v13

--- a/solution.py
+++ b/solution.py
@@ -200,17 +200,21 @@
         def _():
             pltpu.make_async_copy(left_bufs[0], left.at[slot], lsem.at[slot]).wait()
 
-    half = lax.broadcasted_iota(jnp.int32, (BS, 2 * BS), 1) // BS
+    half = lax.broadcasted_iota(jnp.int32, (8, 2 * BS), 1) // BS
 
     def block_at(index):
         return pl.ds(pl.multiple_of(index * BS, BS), BS)
+
+    def in_half(side, kept, other):
+        tall = lambda x: x.reshape(BS // 8, 8, 2 * BS) if jnp.ndim(x) else x
+        return jnp.where((half == side)[None], tall(kept), tall(other)).reshape(BS, 2 * BS)
 
     def product(code):
         slot = (code >> 8) & 15
         x = left[(code >> 12) & 15, block_at((code >> 16) & 255), pl.ds(pl.multiple_of((slot >> 1) * 2 * BS, 2 * BS), 2 * BS)]
-        both = jnp.where(half == (slot & 1), x, pltpu.roll(x, BS, 1))
+        both = in_half(slot & 1, x, pltpu.roll(x, BS, 1))
         hi = both.astype(jnp.bfloat16).astype(jnp.float32)
-        lhs = jnp.where(half == 0, hi, both - hi).astype(jnp.bfloat16)
+        lhs = in_half(0, hi, both - hi).astype(jnp.bfloat16)
         y = right[code >> 24, block_at(code & 255), :]
         hi = y.astype(jnp.bfloat16)
         lo = (y - hi.astype(jnp.float32)).astype(jnp.bfloat16)
@@ -228,7 +232,7 @@
                 place = scalars[(slots + (code >> 24)) * w + 2 * pair + side, code & 255]
                 parity = place >> 16
                 chosen = jnp.where(parity == side, x, turned)
-                picked.append(jnp.where(half == parity, chosen, 0.0))
+                picked.append(in_half(parity, chosen, 0.0))
                 at.append(place & 0xFFFF)
             picked[1] = jnp.where(at[0] == at[1], picked[0] + picked[1], picked[1])
             spots = [(rows_at, pl.ds(pl.multiple_of(base, 2 * BS), 2 * BS)) for base in at]

time: 70.4 us -> 70.4 us (level)
  no operation moved by 1% of the time
where the time goes in v15:
time: 70.4 us; the launch traced here: 70.3 us
  waiting for transfers between devices  47.9 us (68%)
  Pallas kernels  10.4 us (15%)
  starting transfers between devices  9.4 us (13%)
  local copies, waits for them, and re-layouts  2.59 us (4%)
    ppermute x9, waiting for transfers between devices, carry(): bufs.append(lax.ppermute(bufs[source], ('row', 'col'), flat))  47.9 us
    pallas_call x1, Pallas kernels, local(): pl.pallas_call(functools.partial(product_kernel, slots, n_row, ratio, rb,...  10.3 us
    ppermute x9, starting transfers between devices, carry(): bufs.append(lax.ppermute(bufs[source], ('row', 'col'), flat))  9.4 us
    unnamed x4, local copies, waits for them, and re-layouts  1.91 us
  transfers between devices with their start and end apart: 9, of which 5 were waited for; matrix products, arithmetic and copies ran while one was open for 1% of the time, Pallas kernels for 0%

profile of v15, /device:TPU:15, one launch (start us, length us, event | category | flops | bytes accessed | tf_op | source)
XLA Modules:
  0.0 70.3 jit_solution(8194654487295055216)
XLA Ops:
  0.0 0.0 copy-start
  0.0 1.2 %copy-done = f32[1024,256]{1,0:T(8,128)S(1)} copy-done((f32[1024,256]{1,0:T(8,128)S(1)}, f32[1024,256]{1,0:T(8,128)}, u32[]{:S(2)}) %copy-start) | copy-done | bytes 1048600
  1.2 0.7 copy-done.1
  1.9 0.1 shard_map.37.refs_0_
  2.0 2.1 %collective-permute-start.6 = (f32[1032,256]{1,0:T(8,128)S(1)}, f32[1032,256]{1,0:T(8,128)S(1)}, u32[]{:S(2)}, u32[]{:S(2)}) collective-permute-start(f32[1032,256]{1,0:T(8,128)S(1)} %shard_map.37.refs_0_), channel_id=1, source_target_pairs={{4,7},{5,4},{6,5},{7,6},{8,11},{9,8},{10,9},{11,10},{28,31},{29,28... | collective-permute-start | bytes 3170312 | tf_op jit(solution)/shard_map/ppermute | solution.py:305
  4.1 3.2 %collective-permute-start.5 = (f32[1032,256]{1,0:T(8,128)S(1)}, f32[1032,256]{1,0:T(8,128)S(1)}, u32[]{:S(2)}, u32[]{:S(2)}) collective-permute-start(f32[1032,256]{1,0:T(8,128)S(1)} %shard_map.37.refs_0_), channel_id=1, source_target_pairs={{16,17},{17,18},{18,19},{19,16},{20,21},{21,22},{22,23},{23,20},{2... | collective-permute-start | bytes 3170312 | tf_op jit(solution)/shard_map/ppermute | solution.py:305
  7.3 0.3 collective-permute-start.1
  7.6 0.0 collective-permute-start
  7.6 0.0 collective-permute-start.2
  7.6 19.0 %collective-permute-done.6.refs_7_ = f32[1032,256]{1,0:T(8,128)S(1)} collective-permute-done((f32[1032,256]{1,0:T(8,128)S(1)}, f32[1032,256]{1,0:T(8,128)S(1)}, u32[]{:S(2)}, u32[]{:S(2)}) %collective-permute-start.6) | collective-permute-done | bytes 1056800 | tf_op jit(solution)/shard_map/ppermute | solution.py:305
  26.6 1.7 %collective-permute-start.8 = (f32[1032,256]{1,0:T(8,128)S(1)}, f32[1032,256]{1,0:T(8,128)}, u32[]{:S(2)}, u32[]{:S(2)}) collective-permute-start(f32[1032,256]{1,0:T(8,128)S(1)} %collective-permute-done.6.refs_7_), channel_id=1, source_target_pairs={{4,7},{5,4},{6,5},{7,6},{8,11},{9,8},{10,9},{11,10},{13,12},{14,13... | collective-permute-start | bytes 3170312 | tf_op jit(solution)/shard_map/ppermute | solution.py:305
  28.3 14.3 %collective-permute-done.5.refs_6_ = f32[1032,256]{1,0:T(8,128)S(1)} collective-permute-done((f32[1032,256]{1,0:T(8,128)S(1)}, f32[1032,256]{1,0:T(8,128)S(1)}, u32[]{:S(2)}, u32[]{:S(2)}) %collective-permute-start.5) | collective-permute-done | bytes 1056800 | tf_op jit(solution)/shard_map/ppermute | solution.py:305
  42.6 1.7 %collective-permute-start.7 = (f32[1032,256]{1,0:T(8,128)S(1)}, f32[1032,256]{1,0:T(8,128)}, u32[]{:S(2)}, u32[]{:S(2)}) collective-permute-start(f32[1032,256]{1,0:T(8,128)S(1)} %collective-permute-done.5.refs_6_), channel_id=1, source_target_pairs={{16,17},{17,18},{18,19},{19,16},{20,21},{21,22},{22,23},{23,20},{1... | collective-permute-start | bytes 3170312 | tf_op jit(solution)/shard_map/ppermute | solution.py:305
  44.2 11.2 %collective-permute-done.1.refs_2_ = f32[1032,256]{1,0:T(8,128)} collective-permute-done((f32[1032,256]{1,0:T(8,128)S(1)}, f32[1032,256]{1,0:T(8,128)}, u32[]{:S(2)}, u32[]{:S(2)}) %collective-permute-start.1) | collective-permute-done | bytes 1056800 | tf_op jit(solution)/shard_map/ppermute | solution.py:305
  55.4 0.5 collective-permute-start.4
  55.9 0.0 collective-permute-done.refs_1_
  55.9 0.0 collective-permute-start.3
  55.9 0.7 dynamic-slice_bitcast_fusion.info_ref
  56.6 0.0 collective-permute-done.2.refs_3_
  56.6 0.0 collective-permute-done.8.refs_9_
  56.6 0.0 collective-permute-done.7.refs_8_
  56.6 1.9 %collective-permute-done.4.refs_5_ = f32[1032,256]{1,0:T(8,128)} collective-permute-done((f32[1032,256]{1,0:T(8,128)}, f32[1032,256]{1,0:T(8,128)}, u32[]{:S(2)}, u32[]{:S(2)}) %collective-permute-start.4) | collective-permute-done | bytes 1056800 | tf_op jit(solution)/shard_map/ppermute | solution.py:305
  58.5 1.5 %collective-permute-done.3.refs_4_ = f32[1032,256]{1,0:T(8,128)} collective-permute-done((f32[1032,256]{1,0:T(8,128)}, f32[1032,256]{1,0:T(8,128)}, u32[]{:S(2)}, u32[]{:S(2)}) %collective-permute-start.3) | collective-permute-done | bytes 1056800 | tf_op jit(solution)/shard_map/ppermute | solution.py:305
  60.0 10.3 %shard_map.38 = f32[1024,2048]{1,0:T(8,128)} custom-call(s32[10]{0:T(128)S(1)} %dynamic-slice_bitcast_fusion.info_ref, f32[1032,256]{1,0:T(8,128)S(1)} %shard_map.37.refs_0_, f32[1032,256]{1,0:T(8,128)} %collective-permute-done.refs_1_, f32[1032,256]{1,0:T(8,128)} %collective-permute-done.1.refs_2_, f32[1032,256]{1,0:T(8,128)} %collective-permute-done.2.refs_3_, ...), custom_call_target="tpu_custom_call" | custom-call | flops 1000000000 | bytes 20971520 | tf_op jit(solution)/shard_map/pallas_call | solution.py:313
  (1 shorter events, 0.0 us)
Async XLA Ops:
  0.0 1.2 %copy-start = (f32[1024,256]{1,0:T(8,128)S(1)}, f32[1024,256]{1,0:T(8,128)}, u32[]{:S(2)}) copy-start(f32[1024,256]{1,0:T(8,128)} %data_ref.1) | copy-start | bytes 3145732
  1.2 0.7 copy-start.1
  2.0 24.6 %collective-permute-start.6 = (f32[1032,256]{1,0:T(8,128)S(1)}, f32[1032,256]{1,0:T(8,128)S(1)}, u32[]{:S(2)}, u32[]{:S(2)}) collective-permute-start(f32[1032,256]{1,0:T(8,128)S(1)} %shard_map.37.refs_0_), channel_id=1, source_target_pairs={{4,7},{5,4},{6,5},{7,6},{8,11},{9,8},{10,9},{11,10},{28,31},{29,28... | collective-permute-start | bytes 3170312 | tf_op jit(solution)/shard_map/ppermute | solution.py:305
  4.1 38.5 %collective-permute-start.5 = (f32[1032,256]{1,0:T(8,128)S(1)}, f32[1032,256]{1,0:T(8,128)S(1)}, u32[]{:S(2)}, u32[]{:S(2)}) collective-permute-start(f32[1032,256]{1,0:T(8,128)S(1)} %shard_map.37.refs_0_), channel_id=1, source_target_pairs={{16,17},{17,18},{18,19},{19,16},{20,21},{21,22},{22,23},{23,20},{2... | collective-permute-start | bytes 3170312 | tf_op jit(solution)/shard_map/ppermute | solution.py:305
  7.3 48.1 %collective-permute-start.1 = (f32[1032,256]{1,0:T(8,128)S(1)}, f32[1032,256]{1,0:T(8,128)}, u32[]{:S(2)}, u32[]{:S(2)}) collective-permute-start(f32[1032,256]{1,0:T(8,128)S(1)} %shard_map.37.refs_0_), channel_id=1, source_target_pairs={{8,0},{17,1},{26,2},{12,4},{21,5},{30,6},{16,8},{25,9},{2,10},{20,... | collective-permute-start | bytes 3170312 | tf_op jit(solution)/shard_map/ppermute | solution.py:305
  7.6 48.3 %collective-permute-start = (f32[1032,256]{1,0:T(8,128)S(1)}, f32[1032,256]{1,0:T(8,128)}, u32[]{:S(2)}, u32[]{:S(2)}) collective-permute-start(f32[1032,256]{1,0:T(8,128)S(1)} %shard_map.37.refs_0_), channel_id=1, source_target_pairs={{9,1},{18,2},{27,3},{13,5},{22,6},{31,7},{17,9},{26,10},{3,11},{21... | collective-permute-start | bytes 3170312 | tf_op jit(solution)/shard_map/ppermute | solution.py:305
  7.6 49.0 %collective-permute-start.2 = (f32[1032,256]{1,0:T(8,128)S(1)}, f32[1032,256]{1,0:T(8,128)}, u32[]{:S(2)}, u32[]{:S(2)}) collective-permute-start(f32[1032,256]{1,0:T(8,128)S(1)} %shard_map.37.refs_0_), channel_id=1, source_target_pairs={{16,4},{25,5},{2,6},{11,7},{24,12},{1,13},{10,14},{19,15},{0,20},{... | collective-permute-start | bytes 3170312 | tf_op jit(solution)/shard_map/ppermute | solution.py:305
  26.6 30.0 %collective-permute-start.8 = (f32[1032,256]{1,0:T(8,128)S(1)}, f32[1032,256]{1,0:T(8,128)}, u32[]{:S(2)}, u32[]{:S(2)}) collective-permute-start(f32[1032,256]{1,0:T(8,128)S(1)} %collective-permute-done.6.refs_7_), channel_id=1, source_target_pairs={{4,7},{5,4},{6,5},{7,6},{8,11},{9,8},{10,9},{11,10},{13,12},{14,13... | collective-permute-start | bytes 3170312 | tf_op jit(solution)/shard_map/ppermute | solution.py:305
  42.6 14.1 %collective-permute-start.7 = (f32[1032,256]{1,0:T(8,128)S(1)}, f32[1032,256]{1,0:T(8,128)}, u32[]{:S(2)}, u32[]{:S(2)}) collective-permute-start(f32[1032,256]{1,0:T(8,128)S(1)} %collective-permute-done.5.refs_6_), channel_id=1, source_target_pairs={{16,17},{17,18},{18,19},{19,16},{20,21},{21,22},{22,23},{23,20},{1... | collective-permute-start | bytes 3170312 | tf_op jit(solution)/shard_map/ppermute | solution.py:305
  55.4 3.1 %collective-permute-start.4 = (f32[1032,256]{1,0:T(8,128)}, f32[1032,256]{1,0:T(8,128)}, u32[]{:S(2)}, u32[]{:S(2)}) collective-permute-start(f32[1032,256]{1,0:T(8,128)} %collective-permute-done.1.refs_2_), channel_id=1, source_target_pairs={{4,0},{5,1},{6,2},{7,3},{0,4},{1,5},{2,6},{3,7},{12,8},{13,9},{14,... | collective-permute-start | bytes 3170312 | tf_op jit(solution)/shard_map/ppermute | solution.py:305
  55.9 4.1 %collective-permute-start.3 = (f32[1032,256]{1,0:T(8,128)}, f32[1032,256]{1,0:T(8,128)}, u32[]{:S(2)}, u32[]{:S(2)}) collective-permute-start(f32[1032,256]{1,0:T(8,128)} %collective-permute-done.refs_1_), channel_id=1, source_target_pairs={{4,0},{5,1},{6,2},{7,3},{0,4},{1,5},{2,6},{3,7},{12,8},{13,9},{14,... | collective-permute-start | bytes 3170312 | tf_op jit(solution)/shard_map/ppermute | solution.py:305

commit v16 on v13

--- a/solution.py
+++ b/solution.py
@@ -214,8 +214,8 @@
         y = right[code >> 24, block_at(code & 255), :]
         hi = y.astype(jnp.bfloat16)
         lo = (y - hi.astype(jnp.float32)).astype(jnp.bfloat16)
-        lhs = jnp.concatenate([lhs, lhs], axis=1)
-        rhs = jnp.concatenate([hi, hi, lo, lo], axis=0)
+        lhs = jnp.concatenate([lhs, lhs[:, :BS]], axis=1)
+        rhs = jnp.concatenate([hi, hi, lo], axis=0)
         return jnp.dot(lhs, rhs, preferred_element_type=jnp.float32)
 
     def add(code, product):

time: 70.4 us -> 70.5 us (level)
  no operation moved by 1% of the time
where the time goes in v16:
time: 70.5 us; the launch traced here: 69.8 us
  waiting for transfers between devices  47.9 us (68%)
  Pallas kernels  9.88 us (14%)
  starting transfers between devices  9.4 us (13%)
  local copies, waits for them, and re-layouts  2.59 us (4%)
    ppermute x9, waiting for transfers between devices, carry(): bufs.append(lax.ppermute(bufs[source], ('row', 'col'), flat))  47.9 us
    pallas_call x1, Pallas kernels, local(): pl.pallas_call(functools.partial(product_kernel, slots, n_row, ratio, rb,...  9.79 us
    ppermute x9, starting transfers between devices, carry(): bufs.append(lax.ppermute(bufs[source], ('row', 'col'), flat))  9.4 us
    unnamed x4, local copies, waits for them, and re-layouts  1.91 us
  transfers between devices with their start and end apart: 9, of which 5 were waited for; matrix products, arithmetic and copies ran while one was open for 1% of the time, Pallas kernels for 0%

profile of v16, /device:TPU:15, one launch (start us, length us, event | category | flops | bytes accessed | tf_op | source)
XLA Modules:
  0.0 69.8 jit_solution(9660873892582037660)
XLA Ops:
  0.0 0.0 copy-start
  0.0 1.2 %copy-done = f32[1024,256]{1,0:T(8,128)S(1)} copy-done((f32[1024,256]{1,0:T(8,128)S(1)}, f32[1024,256]{1,0:T(8,128)}, u32[]{:S(2)}) %copy-start) | copy-done | bytes 1048600
  1.2 0.7 copy-done.1
  1.9 0.1 shard_map.37.refs_0_
  2.0 2.1 %collective-permute-start.6 = (f32[1032,256]{1,0:T(8,128)S(1)}, f32[1032,256]{1,0:T(8,128)S(1)}, u32[]{:S(2)}, u32[]{:S(2)}) collective-permute-start(f32[1032,256]{1,0:T(8,128)S(1)} %shard_map.37.refs_0_), channel_id=1, source_target_pairs={{4,7},{5,4},{6,5},{7,6},{8,11},{9,8},{10,9},{11,10},{28,31},{29,28... | collective-permute-start | bytes 3170312 | tf_op jit(solution)/shard_map/ppermute | solution.py:301
  4.1 3.2 %collective-permute-start.5 = (f32[1032,256]{1,0:T(8,128)S(1)}, f32[1032,256]{1,0:T(8,128)S(1)}, u32[]{:S(2)}, u32[]{:S(2)}) collective-permute-start(f32[1032,256]{1,0:T(8,128)S(1)} %shard_map.37.refs_0_), channel_id=1, source_target_pairs={{16,17},{17,18},{18,19},{19,16},{20,21},{21,22},{22,23},{23,20},{2... | collective-permute-start | bytes 3170312 | tf_op jit(solution)/shard_map/ppermute | solution.py:301
  7.3 0.3 collective-permute-start.1
  7.6 0.0 collective-permute-start
  7.6 0.0 collective-permute-start.2
  7.6 19.0 %collective-permute-done.6.refs_7_ = f32[1032,256]{1,0:T(8,128)S(1)} collective-permute-done((f32[1032,256]{1,0:T(8,128)S(1)}, f32[1032,256]{1,0:T(8,128)S(1)}, u32[]{:S(2)}, u32[]{:S(2)}) %collective-permute-start.6) | collective-permute-done | bytes 1056800 | tf_op jit(solution)/shard_map/ppermute | solution.py:301
  26.6 1.7 %collective-permute-start.8 = (f32[1032,256]{1,0:T(8,128)S(1)}, f32[1032,256]{1,0:T(8,128)}, u32[]{:S(2)}, u32[]{:S(2)}) collective-permute-start(f32[1032,256]{1,0:T(8,128)S(1)} %collective-permute-done.6.refs_7_), channel_id=1, source_target_pairs={{4,7},{5,4},{6,5},{7,6},{8,11},{9,8},{10,9},{11,10},{13,12},{14,13... | collective-permute-start | bytes 3170312 | tf_op jit(solution)/shard_map/ppermute | solution.py:301
  28.3 14.3 %collective-permute-done.5.refs_6_ = f32[1032,256]{1,0:T(8,128)S(1)} collective-permute-done((f32[1032,256]{1,0:T(8,128)S(1)}, f32[1032,256]{1,0:T(8,128)S(1)}, u32[]{:S(2)}, u32[]{:S(2)}) %collective-permute-start.5) | collective-permute-done | bytes 1056800 | tf_op jit(solution)/shard_map/ppermute | solution.py:301
  42.6 1.7 %collective-permute-start.7 = (f32[1032,256]{1,0:T(8,128)S(1)}, f32[1032,256]{1,0:T(8,128)}, u32[]{:S(2)}, u32[]{:S(2)}) collective-permute-start(f32[1032,256]{1,0:T(8,128)S(1)} %collective-permute-done.5.refs_6_), channel_id=1, source_target_pairs={{16,17},{17,18},{18,19},{19,16},{20,21},{21,22},{22,23},{23,20},{1... | collective-permute-start | bytes 3170312 | tf_op jit(solution)/shard_map/ppermute | solution.py:301
  44.2 11.2 %collective-permute-done.1.refs_2_ = f32[1032,256]{1,0:T(8,128)} collective-permute-done((f32[1032,256]{1,0:T(8,128)S(1)}, f32[1032,256]{1,0:T(8,128)}, u32[]{:S(2)}, u32[]{:S(2)}) %collective-permute-start.1) | collective-permute-done | bytes 1056800 | tf_op jit(solution)/shard_map/ppermute | solution.py:301
  55.4 0.5 collective-permute-start.4
  55.9 0.0 collective-permute-done.refs_1_
  55.9 0.0 collective-permute-start.3
  55.9 0.7 dynamic-slice_bitcast_fusion.info_ref
  56.6 0.0 collective-permute-done.2.refs_3_
  56.6 0.0 collective-permute-done.8.refs_9_
  56.6 0.0 collective-permute-done.7.refs_8_
  56.6 1.9 %collective-permute-done.4.refs_5_ = f32[1032,256]{1,0:T(8,128)} collective-permute-done((f32[1032,256]{1,0:T(8,128)}, f32[1032,256]{1,0:T(8,128)}, u32[]{:S(2)}, u32[]{:S(2)}) %collective-permute-start.4) | collective-permute-done | bytes 1056800 | tf_op jit(solution)/shard_map/ppermute | solution.py:301
  58.5 1.5 %collective-permute-done.3.refs_4_ = f32[1032,256]{1,0:T(8,128)} collective-permute-done((f32[1032,256]{1,0:T(8,128)}, f32[1032,256]{1,0:T(8,128)}, u32[]{:S(2)}, u32[]{:S(2)}) %collective-permute-start.3) | collective-permute-done | bytes 1056800 | tf_op jit(solution)/shard_map/ppermute | solution.py:301
  60.0 9.8 %shard_map.38 = f32[1024,2048]{1,0:T(8,128)} custom-call(s32[10]{0:T(128)S(1)} %dynamic-slice_bitcast_fusion.info_ref, f32[1032,256]{1,0:T(8,128)S(1)} %shard_map.37.refs_0_, f32[1032,256]{1,0:T(8,128)} %collective-permute-done.refs_1_, f32[1032,256]{1,0:T(8,128)} %collective-permute-done.1.refs_2_, f32[1032,256]{1,0:T(8,128)} %collective-permute-done.2.refs_3_, ...), custom_call_target="tpu_custom_call" | custom-call | flops 1000000000 | bytes 20971520 | tf_op jit(solution)/shard_map/pallas_call | solution.py:309
  (1 shorter events, 0.0 us)
Async XLA Ops:
  0.0 1.2 %copy-start = (f32[1024,256]{1,0:T(8,128)S(1)}, f32[1024,256]{1,0:T(8,128)}, u32[]{:S(2)}) copy-start(f32[1024,256]{1,0:T(8,128)} %data_ref.1) | copy-start | bytes 3145732
  1.2 0.7 copy-start.1
  2.0 24.6 %collective-permute-start.6 = (f32[1032,256]{1,0:T(8,128)S(1)}, f32[1032,256]{1,0:T(8,128)S(1)}, u32[]{:S(2)}, u32[]{:S(2)}) collective-permute-start(f32[1032,256]{1,0:T(8,128)S(1)} %shard_map.37.refs_0_), channel_id=1, source_target_pairs={{4,7},{5,4},{6,5},{7,6},{8,11},{9,8},{10,9},{11,10},{28,31},{29,28... | collective-permute-start | bytes 3170312 | tf_op jit(solution)/shard_map/ppermute | solution.py:301
  4.1 38.5 %collective-permute-start.5 = (f32[1032,256]{1,0:T(8,128)S(1)}, f32[1032,256]{1,0:T(8,128)S(1)}, u32[]{:S(2)}, u32[]{:S(2)}) collective-permute-start(f32[1032,256]{1,0:T(8,128)S(1)} %shard_map.37.refs_0_), channel_id=1, source_target_pairs={{16,17},{17,18},{18,19},{19,16},{20,21},{21,22},{22,23},{23,20},{2... | collective-permute-start | bytes 3170312 | tf_op jit(solution)/shard_map/ppermute | solution.py:301
  7.3 48.1 %collective-permute-start.1 = (f32[1032,256]{1,0:T(8,128)S(1)}, f32[1032,256]{1,0:T(8,128)}, u32[]{:S(2)}, u32[]{:S(2)}) collective-permute-start(f32[1032,256]{1,0:T(8,128)S(1)} %shard_map.37.refs_0_), channel_id=1, source_target_pairs={{8,0},{17,1},{26,2},{12,4},{21,5},{30,6},{16,8},{25,9},{2,10},{20,... | collective-permute-start | bytes 3170312 | tf_op jit(solution)/shard_map/ppermute | solution.py:301
  7.6 48.3 %collective-permute-start = (f32[1032,256]{1,0:T(8,128)S(1)}, f32[1032,256]{1,0:T(8,128)}, u32[]{:S(2)}, u32[]{:S(2)}) collective-permute-start(f32[1032,256]{1,0:T(8,128)S(1)} %shard_map.37.refs_0_), channel_id=1, source_target_pairs={{9,1},{18,2},{27,3},{13,5},{22,6},{31,7},{17,9},{26,10},{3,11},{21... | collective-permute-start | bytes 3170312 | tf_op jit(solution)/shard_map/ppermute | solution.py:301
  7.6 49.0 %collective-permute-start.2 = (f32[1032,256]{1,0:T(8,128)S(1)}, f32[1032,256]{1,0:T(8,128)}, u32[]{:S(2)}, u32[]{:S(2)}) collective-permute-start(f32[1032,256]{1,0:T(8,128)S(1)} %shard_map.37.refs_0_), channel_id=1, source_target_pairs={{16,4},{25,5},{2,6},{11,7},{24,12},{1,13},{10,14},{19,15},{0,20},{... | collective-permute-start | bytes 3170312 | tf_op jit(solution)/shard_map/ppermute | solution.py:301
  26.6 30.0 %collective-permute-start.8 = (f32[1032,256]{1,0:T(8,128)S(1)}, f32[1032,256]{1,0:T(8,128)}, u32[]{:S(2)}, u32[]{:S(2)}) collective-permute-start(f32[1032,256]{1,0:T(8,128)S(1)} %collective-permute-done.6.refs_7_), channel_id=1, source_target_pairs={{4,7},{5,4},{6,5},{7,6},{8,11},{9,8},{10,9},{11,10},{13,12},{14,13... | collective-permute-start | bytes 3170312 | tf_op jit(solution)/shard_map/ppermute | solution.py:301
  42.6 14.1 %collective-permute-start.7 = (f32[1032,256]{1,0:T(8,128)S(1)}, f32[1032,256]{1,0:T(8,128)}, u32[]{:S(2)}, u32[]{:S(2)}) collective-permute-start(f32[1032,256]{1,0:T(8,128)S(1)} %collective-permute-done.5.refs_6_), channel_id=1, source_target_pairs={{16,17},{17,18},{18,19},{19,16},{20,21},{21,22},{22,23},{23,20},{1... | collective-permute-start | bytes 3170312 | tf_op jit(solution)/shard_map/ppermute | solution.py:301
  55.4 3.1 %collective-permute-start.4 = (f32[1032,256]{1,0:T(8,128)}, f32[1032,256]{1,0:T(8,128)}, u32[]{:S(2)}, u32[]{:S(2)}) collective-permute-start(f32[1032,256]{1,0:T(8,128)} %collective-permute-done.1.refs_2_), channel_id=1, source_target_pairs={{4,0},{5,1},{6,2},{7,3},{0,4},{1,5},{2,6},{3,7},{12,8},{13,9},{14,... | collective-permute-start | bytes 3170312 | tf_op jit(solution)/shard_map/ppermute | solution.py:301
  55.9 4.1 %collective-permute-start.3 = (f32[1032,256]{1,0:T(8,128)}, f32[1032,256]{1,0:T(8,128)}, u32[]{:S(2)}, u32[]{:S(2)}) collective-permute-start(f32[1032,256]{1,0:T(8,128)} %collective-permute-done.refs_1_), channel_id=1, source_target_pairs={{4,0},{5,1},{6,2},{7,3},{0,4},{1,5},{2,6},{3,7},{12,8},{13,9},{14,... | collective-permute-start | bytes 3170312 | tf_op jit(solution)/shard_map/ppermute | solution.py:301

commit v17 on v13

--- a/solution.py
+++ b/solution.py
@@ -10,7 +10,7 @@
 
 BS = 64
 STEPS = 4
-UNROLL = 8
+UNROLL = 12
 EXTRA = 8
 PARTS = 16
 
@@ -290,7 +290,7 @@
         in_specs=[pl.BlockSpec(memory_space=pltpu.HBM)] * 2,
         out_specs=pl.BlockSpec(memory_space=pltpu.VMEM),
         scratch_shapes=[pltpu.VMEM((w, rb), jnp.int32), dma((2,))],
-        compiler_params=pltpu.CompilerParams(vmem_limit_bytes=4 << 20),
+        compiler_params=pltpu.CompilerParams(vmem_limit_bytes=58 << 20),
         cost_estimate=pl.CostEstimate(flops=0, bytes_accessed=2 << 20, transcendentals=0),
     )(p_cols.T, p_data)
 

time: 70.4 us -> 71.6 us (1.017)
  the two profiles are of different devices: /device:TPU:15 before, /device:TPU:4 now
where the time goes in v17:
time: 71.6 us; the launch traced here: 70.7 us
  waiting for transfers between devices  43.7 us (61%)
  starting transfers between devices  13.5 us (19%)
  Pallas kernels  11.6 us (16%)
  local copies, waits for them, and re-layouts  1.91 us (3%)
    ppermute x9, waiting for transfers between devices, carry(): bufs.append(lax.ppermute(bufs[source], ('row', 'col'), flat))  43.7 us
    ppermute x9, starting transfers between devices, carry(): bufs.append(lax.ppermute(bufs[source], ('row', 'col'), flat))  13.5 us
    pallas_call x1, Pallas kernels, local(): pl.pallas_call(functools.partial(product_kernel, slots, n_row, ratio, rb,...  9.43 us
    pallas_call x1, Pallas kernels, local(): pl.pallas_call(join_kernel, out_shape=jax.ShapeDtypeStruct((rows + EXTRA,...  2.21 us
  transfers between devices with their start and end apart: 9, of which 2 were waited for; matrix products, arithmetic and copies ran while one was open for 1% of the time, Pallas kernels for 0%

profile of v17, /device:TPU:4, one launch (start us, length us, event | category | flops | bytes accessed | tf_op | source)
XLA Modules:
  0.0 70.7 jit_solution(9227216075640947571)
XLA Ops:
  0.0 2.2 %shard_map.37.refs_0_ = f32[1032,256]{1,0:T(8,128)} custom-call(s32[4,16]{1,0:T(4,128)} %bitcast.3, f32[1024,256]{1,0:T(8,128)} %data_ref.1), custom_call_target="tpu_custom_call" | custom-call | bytes 2097152 | tf_op jit(solution)/shard_map/pallas_call | solution.py:287
  2.2 0.7 %collective-permute-start.6 = (f32[1032,256]{1,0:T(8,128)}, f32[1032,256]{1,0:T(8,128)S(1)}, u32[]{:S(2)}, u32[]{:S(2)}) collective-permute-start(f32[1032,256]{1,0:T(8,128)} %shard_map.37.refs_0_), channel_id=1, source_target_pairs={{4,7},{5,4},{6,5},{7,6},{8,11},{9,8},{10,9},{11,10},{28,31},{29,28... | collective-permute-start | bytes 3170312 | tf_op jit(solution)/shard_map/ppermute | solution.py:301
  3.0 3.5 %collective-permute-start.5 = (f32[1032,256]{1,0:T(8,128)}, f32[1032,256]{1,0:T(8,128)S(1)}, u32[]{:S(2)}, u32[]{:S(2)}) collective-permute-start(f32[1032,256]{1,0:T(8,128)} %shard_map.37.refs_0_), channel_id=1, source_target_pairs={{16,17},{17,18},{18,19},{19,16},{20,21},{21,22},{22,23},{23,20},{2... | collective-permute-start | bytes 3170312 | tf_op jit(solution)/shard_map/ppermute | solution.py:301
  6.4 3.5 %collective-permute-start.1 = (f32[1032,256]{1,0:T(8,128)}, f32[1032,256]{1,0:T(8,128)S(1)}, u32[]{:S(2)}, u32[]{:S(2)}) collective-permute-start(f32[1032,256]{1,0:T(8,128)} %shard_map.37.refs_0_), channel_id=1, source_target_pairs={{8,0},{17,1},{26,2},{12,4},{21,5},{30,6},{16,8},{25,9},{2,10},{20,... | collective-permute-start | bytes 3170312 | tf_op jit(solution)/shard_map/ppermute | solution.py:301
  10.0 0.0 collective-permute-start
  10.0 1.6 %collective-permute-start.2 = (f32[1032,256]{1,0:T(8,128)}, f32[1032,256]{1,0:T(8,128)}, u32[]{:S(2)}, u32[]{:S(2)}) collective-permute-start(f32[1032,256]{1,0:T(8,128)} %shard_map.37.refs_0_), channel_id=1, source_target_pairs={{16,4},{25,5},{2,6},{11,7},{24,12},{1,13},{10,14},{19,15},{0,20},{... | collective-permute-start | bytes 3170312 | tf_op jit(solution)/shard_map/ppermute | solution.py:301
  11.6 0.0 collective-permute-done.6.refs_7_
  11.6 1.7 %collective-permute-start.8 = (f32[1032,256]{1,0:T(8,128)S(1)}, f32[1032,256]{1,0:T(8,128)}, u32[]{:S(2)}, u32[]{:S(2)}) collective-permute-start(f32[1032,256]{1,0:T(8,128)S(1)} %collective-permute-done.6.refs_7_), channel_id=1, source_target_pairs={{4,7},{5,4},{6,5},{7,6},{8,11},{9,8},{10,9},{11,10},{13,12},{14,13... | collective-permute-start | bytes 3170312 | tf_op jit(solution)/shard_map/ppermute | solution.py:301
  13.2 18.8 %collective-permute-done.5.refs_6_ = f32[1032,256]{1,0:T(8,128)S(1)} collective-permute-done((f32[1032,256]{1,0:T(8,128)}, f32[1032,256]{1,0:T(8,128)S(1)}, u32[]{:S(2)}, u32[]{:S(2)}) %collective-permute-start.5) | collective-permute-done | bytes 1056800 | tf_op jit(solution)/shard_map/ppermute | solution.py:301
  32.0 1.9 %collective-permute-start.7 = (f32[1032,256]{1,0:T(8,128)S(1)}, f32[1032,256]{1,0:T(8,128)}, u32[]{:S(2)}, u32[]{:S(2)}) collective-permute-start(f32[1032,256]{1,0:T(8,128)S(1)} %collective-permute-done.5.refs_6_), channel_id=1, source_target_pairs={{16,17},{17,18},{18,19},{19,16},{20,21},{21,22},{22,23},{23,20},{1... | collective-permute-start | bytes 3170312 | tf_op jit(solution)/shard_map/ppermute | solution.py:301
  33.9 0.0 collective-permute-done.1.refs_2_
  33.9 0.1 collective-permute-start.4
  34.0 0.0 collective-permute-done.refs_1_
  34.0 0.5 collective-permute-start.3
  34.5 0.7 dynamic-slice_bitcast_fusion.info_ref
  35.2 0.0 collective-permute-done.2.refs_3_
  35.2 0.0 collective-permute-done.8.refs_9_
  35.2 24.9 %collective-permute-done.7.refs_8_ = f32[1032,256]{1,0:T(8,128)} collective-permute-done((f32[1032,256]{1,0:T(8,128)S(1)}, f32[1032,256]{1,0:T(8,128)}, u32[]{:S(2)}, u32[]{:S(2)}) %collective-permute-start.7) | collective-permute-done | bytes 1056800 | tf_op jit(solution)/shard_map/ppermute | solution.py:301
  60.1 0.0 collective-permute-done.4.refs_5_
  60.1 0.0 collective-permute-done.3.refs_4_
  60.1 0.0 copy-start
  60.1 1.2 %copy-done = f32[1032,256]{1,0:T(8,128)S(1)} copy-done((f32[1032,256]{1,0:T(8,128)S(1)}, f32[1032,256]{1,0:T(8,128)}, u32[]{:S(2)}) %copy-start) | copy-done | bytes 1056792
  61.3 9.4 %shard_map.38 = f32[1024,2048]{1,0:T(8,128)} custom-call(s32[10]{0:T(128)S(1)} %dynamic-slice_bitcast_fusion.info_ref, f32[1032,256]{1,0:T(8,128)S(1)} %copy-done, f32[1032,256]{1,0:T(8,128)} %collective-permute-done.refs_1_, f32[1032,256]{1,0:T(8,128)S(1)} %collective-permute-done.1.refs_2_, f32[1032,256]{1,0:T(8,128)} %collective-permute-done.2.refs_3_, ...), custom_call_target="tpu_custom_call" | custom-call | flops 1000000000 | bytes 20971520 | tf_op jit(solution)/shard_map/pallas_call | solution.py:309
Async XLA Ops:
  2.2 9.3 %collective-permute-start.6 = (f32[1032,256]{1,0:T(8,128)}, f32[1032,256]{1,0:T(8,128)S(1)}, u32[]{:S(2)}, u32[]{:S(2)}) collective-permute-start(f32[1032,256]{1,0:T(8,128)} %shard_map.37.refs_0_), channel_id=1, source_target_pairs={{4,7},{5,4},{6,5},{7,6},{8,11},{9,8},{10,9},{11,10},{28,31},{29,28... | collective-permute-start | bytes 3170312 | tf_op jit(solution)/shard_map/ppermute | solution.py:301
  3.0 29.0 %collective-permute-start.5 = (f32[1032,256]{1,0:T(8,128)}, f32[1032,256]{1,0:T(8,128)S(1)}, u32[]{:S(2)}, u32[]{:S(2)}) collective-permute-start(f32[1032,256]{1,0:T(8,128)} %shard_map.37.refs_0_), channel_id=1, source_target_pairs={{16,17},{17,18},{18,19},{19,16},{20,21},{21,22},{22,23},{23,20},{2... | collective-permute-start | bytes 3170312 | tf_op jit(solution)/shard_map/ppermute | solution.py:301
  6.4 27.5 %collective-permute-start.1 = (f32[1032,256]{1,0:T(8,128)}, f32[1032,256]{1,0:T(8,128)S(1)}, u32[]{:S(2)}, u32[]{:S(2)}) collective-permute-start(f32[1032,256]{1,0:T(8,128)} %shard_map.37.refs_0_), channel_id=1, source_target_pairs={{8,0},{17,1},{26,2},{12,4},{21,5},{30,6},{16,8},{25,9},{2,10},{20,... | collective-permute-start | bytes 3170312 | tf_op jit(solution)/shard_map/ppermute | solution.py:301
  10.0 24.1 %collective-permute-start = (f32[1032,256]{1,0:T(8,128)}, f32[1032,256]{1,0:T(8,128)}, u32[]{:S(2)}, u32[]{:S(2)}) collective-permute-start(f32[1032,256]{1,0:T(8,128)} %shard_map.37.refs_0_), channel_id=1, source_target_pairs={{9,1},{18,2},{27,3},{13,5},{22,6},{31,7},{17,9},{26,10},{3,11},{21... | collective-permute-start | bytes 3170312 | tf_op jit(solution)/shard_map/ppermute | solution.py:301
  10.0 25.2 %collective-permute-start.2 = (f32[1032,256]{1,0:T(8,128)}, f32[1032,256]{1,0:T(8,128)}, u32[]{:S(2)}, u32[]{:S(2)}) collective-permute-start(f32[1032,256]{1,0:T(8,128)} %shard_map.37.refs_0_), channel_id=1, source_target_pairs={{16,4},{25,5},{2,6},{11,7},{24,12},{1,13},{10,14},{19,15},{0,20},{... | collective-permute-start | bytes 3170312 | tf_op jit(solution)/shard_map/ppermute | solution.py:301
  11.6 23.6 %collective-permute-start.8 = (f32[1032,256]{1,0:T(8,128)S(1)}, f32[1032,256]{1,0:T(8,128)}, u32[]{:S(2)}, u32[]{:S(2)}) collective-permute-start(f32[1032,256]{1,0:T(8,128)S(1)} %collective-permute-done.6.refs_7_), channel_id=1, source_target_pairs={{4,7},{5,4},{6,5},{7,6},{8,11},{9,8},{10,9},{11,10},{13,12},{14,13... | collective-permute-start | bytes 3170312 | tf_op jit(solution)/shard_map/ppermute | solution.py:301
  32.0 28.1 %collective-permute-start.7 = (f32[1032,256]{1,0:T(8,128)S(1)}, f32[1032,256]{1,0:T(8,128)}, u32[]{:S(2)}, u32[]{:S(2)}) collective-permute-start(f32[1032,256]{1,0:T(8,128)S(1)} %collective-permute-done.5.refs_6_), channel_id=1, source_target_pairs={{16,17},{17,18},{18,19},{19,16},{20,21},{21,22},{22,23},{23,20},{1... | collective-permute-start | bytes 3170312 | tf_op jit(solution)/shard_map/ppermute | solution.py:301
  33.9 26.1 %collective-permute-start.4 = (f32[1032,256]{1,0:T(8,128)S(1)}, f32[1032,256]{1,0:T(8,128)}, u32[]{:S(2)}, u32[]{:S(2)}) collective-permute-start(f32[1032,256]{1,0:T(8,128)S(1)} %collective-permute-done.1.refs_2_), channel_id=1, source_target_pairs={{4,0},{5,1},{6,2},{7,3},{0,4},{1,5},{2,6},{3,7},{12,8},{13,9},{14,... | collective-permute-start | bytes 3170312 | tf_op jit(solution)/shard_map/ppermute | solution.py:301
  34.0 26.1 %collective-permute-start.3 = (f32[1032,256]{1,0:T(8,128)}, f32[1032,256]{1,0:T(8,128)}, u32[]{:S(2)}, u32[]{:S(2)}) collective-permute-start(f32[1032,256]{1,0:T(8,128)} %collective-permute-done.refs_1_), channel_id=1, source_target_pairs={{4,0},{5,1},{6,2},{7,3},{0,4},{1,5},{2,6},{3,7},{12,8},{13,9},{14,... | collective-permute-start | bytes 3170312 | tf_op jit(solution)/shard_map/ppermute | solution.py:301
  60.1 1.2 %copy-start = (f32[1032,256]{1,0:T(8,128)S(1)}, f32[1032,256]{1,0:T(8,128)}, u32[]{:S(2)}) copy-start(f32[1032,256]{1,0:T(8,128)} %shard_map.37.refs_0_) | copy-start | bytes 3170308

commit v18 on v17

--- a/solution.py
+++ b/solution.py
@@ -49,11 +49,14 @@
                 once[step].append(r)
                 if 2 in offsets[r]:
                     twice[step].append(r)
-    down = shift([r for r in once[-1] if r != 0], -1, 4) + [((3, c), (3, c - 1)) for c in (1, 2, 3)] + [((3, 0), (0, 0))]
-    up = shift(once[1], 1, 4) + shift([0], -1, 4) + [((3, c), (3, c + 1)) for c in (0, 1, 2)] + [((3, 3), (1, 3))]
-    again_down = shift(twice[-1], -1, 4) + [((3, 1), (3, 0)), ((3, 2), (3, 1)), ((0, 0), (3, 3))]
-    again_up = shift(twice[1], 1, 4) + [((3, 1), (3, 2)), ((3, 2), (3, 3)), ((1, 3), (3, 0))]
-    return [(0, up), (0, down), (1, again_up), (2, again_down)]
+    plain = lambda step: [r for r in once[step] if r not in twice[step] and r != 7]
+    early = shift(twice[-1] + [7], -1, 4) + shift(twice[1], 1, 4)
+    early += [((3, c), (3, c - 1)) for c in (1, 2, 3)] + [((3, 0), (0, 0))]
+    late = shift(plain(-1), -1, 4) + shift(plain(1) + [7], 1, 4)
+    late += [((3, c), (3, c + 1)) for c in (0, 1, 2)] + [((3, 3), (1, 3))]
+    again_early = shift(twice[-1], -1, 4) + shift(twice[1], 1, 4) + [((3, 1), (3, 0)), ((3, 2), (3, 1)), ((0, 0), (3, 3))]
+    again_late = [((3, 1), (3, 2)), ((3, 2), (3, 3)), ((1, 3), (3, 0))]
+    return [(0, late), (0, early), (1, again_late), (2, again_early)]
 
 
 def right_plan(n_row, n_col, ratio):
@@ -290,7 +293,7 @@
         in_specs=[pl.BlockSpec(memory_space=pltpu.HBM)] * 2,
         out_specs=pl.BlockSpec(memory_space=pltpu.VMEM),
         scratch_shapes=[pltpu.VMEM((w, rb), jnp.int32), dma((2,))],
-        compiler_params=pltpu.CompilerParams(vmem_limit_bytes=58 << 20),
+        compiler_params=pltpu.CompilerParams(vmem_limit_bytes=4 << 20),
         cost_estimate=pl.CostEstimate(flops=0, bytes_accessed=2 << 20, transcendentals=0),
     )(p_cols.T, p_data)
 

time: 71.6 us -> 70.5 us (0.985)
  the two profiles are of different devices: /device:TPU:4 before, /device:TPU:15 now
where the time goes in v18:
time: 70.5 us; the launch traced here: 70.3 us
  waiting for transfers between devices  47.9 us (68%)
  Pallas kernels  10.4 us (15%)
  starting transfers between devices  9.4 us (13%)
  local copies, waits for them, and re-layouts  2.59 us (4%)
    ppermute x9, waiting for transfers between devices, carry(): bufs.append(lax.ppermute(bufs[source], ('row', 'col'), flat))  47.9 us
    pallas_call x1, Pallas kernels, local(): pl.pallas_call(functools.partial(product_kernel, slots, n_row, ratio, rb,...  10.3 us
    ppermute x9, starting transfers between devices, carry(): bufs.append(lax.ppermute(bufs[source], ('row', 'col'), flat))  9.4 us
    unnamed x4, local copies, waits for them, and re-layouts  1.91 us
  transfers between devices with their start and end apart: 9, of which 5 were waited for; matrix products, arithmetic and copies ran while one was open for 1% of the time, Pallas kernels for 0%

profile of v18, /device:TPU:15, one launch (start us, length us, event | category | flops | bytes accessed | tf_op | source)
XLA Modules:
  0.0 70.3 jit_solution(413774859025061054)
XLA Ops:
  0.0 0.0 copy-start
  0.0 1.2 %copy-done = f32[1024,256]{1,0:T(8,128)S(1)} copy-done((f32[1024,256]{1,0:T(8,128)S(1)}, f32[1024,256]{1,0:T(8,128)}, u32[]{:S(2)}) %copy-start) | copy-done | bytes 1048600
  1.2 0.7 copy-done.1
  1.9 0.1 shard_map.37.refs_0_
  2.0 2.1 %collective-permute-start.6 = (f32[1032,256]{1,0:T(8,128)S(1)}, f32[1032,256]{1,0:T(8,128)S(1)}, u32[]{:S(2)}, u32[]{:S(2)}) collective-permute-start(f32[1032,256]{1,0:T(8,128)S(1)} %shard_map.37.refs_0_), channel_id=1, source_target_pairs={{4,7},{5,4},{6,5},{7,6},{8,11},{9,8},{10,9},{11,10},{28,31},{29,28... | collective-permute-start | bytes 3170312 | tf_op jit(solution)/shard_map/ppermute | solution.py:304
  4.1 3.2 %collective-permute-start.5 = (f32[1032,256]{1,0:T(8,128)S(1)}, f32[1032,256]{1,0:T(8,128)S(1)}, u32[]{:S(2)}, u32[]{:S(2)}) collective-permute-start(f32[1032,256]{1,0:T(8,128)S(1)} %shard_map.37.refs_0_), channel_id=1, source_target_pairs={{0,3},{1,0},{2,1},{3,2},{24,25},{25,26},{26,27},{27,24},{28,29},{2... | collective-permute-start | bytes 3170312 | tf_op jit(solution)/shard_map/ppermute | solution.py:304
  7.3 0.3 collective-permute-start.1
  7.6 0.0 collective-permute-start
  7.6 0.0 collective-permute-start.2
  7.6 19.0 %collective-permute-done.6.refs_7_ = f32[1032,256]{1,0:T(8,128)S(1)} collective-permute-done((f32[1032,256]{1,0:T(8,128)S(1)}, f32[1032,256]{1,0:T(8,128)S(1)}, u32[]{:S(2)}, u32[]{:S(2)}) %collective-permute-start.6) | collective-permute-done | bytes 1056800 | tf_op jit(solution)/shard_map/ppermute | solution.py:304
  26.6 1.7 %collective-permute-start.8 = (f32[1032,256]{1,0:T(8,128)S(1)}, f32[1032,256]{1,0:T(8,128)}, u32[]{:S(2)}, u32[]{:S(2)}) collective-permute-start(f32[1032,256]{1,0:T(8,128)S(1)} %collective-permute-done.6.refs_7_), channel_id=1, source_target_pairs={{4,7},{5,4},{6,5},{7,6},{8,11},{9,8},{10,9},{11,10},{16,17},{17,18... | collective-permute-start | bytes 3170312 | tf_op jit(solution)/shard_map/ppermute | solution.py:304
  28.3 14.3 %collective-permute-done.5.refs_6_ = f32[1032,256]{1,0:T(8,128)S(1)} collective-permute-done((f32[1032,256]{1,0:T(8,128)S(1)}, f32[1032,256]{1,0:T(8,128)S(1)}, u32[]{:S(2)}, u32[]{:S(2)}) %collective-permute-start.5) | collective-permute-done | bytes 1056800 | tf_op jit(solution)/shard_map/ppermute | solution.py:304
  42.6 1.7 %collective-permute-start.7 = (f32[1032,256]{1,0:T(8,128)S(1)}, f32[1032,256]{1,0:T(8,128)}, u32[]{:S(2)}, u32[]{:S(2)}) collective-permute-start(f32[1032,256]{1,0:T(8,128)S(1)} %collective-permute-done.5.refs_6_), channel_id=1, source_target_pairs={{13,14},{14,15},{7,12}} | collective-permute-start | bytes 3170312 | tf_op jit(solution)/shard_map/ppermute | solution.py:304
  44.2 11.2 %collective-permute-done.1.refs_2_ = f32[1032,256]{1,0:T(8,128)} collective-permute-done((f32[1032,256]{1,0:T(8,128)S(1)}, f32[1032,256]{1,0:T(8,128)}, u32[]{:S(2)}, u32[]{:S(2)}) %collective-permute-start.1) | collective-permute-done | bytes 1056800 | tf_op jit(solution)/shard_map/ppermute | solution.py:304
  55.4 0.5 collective-permute-start.4
  55.9 0.0 collective-permute-done.refs_1_
  55.9 0.0 collective-permute-start.3
  55.9 0.7 dynamic-slice_bitcast_fusion.info_ref
  56.6 0.0 collective-permute-done.2.refs_3_
  56.6 0.0 collective-permute-done.8.refs_9_
  56.6 0.0 collective-permute-done.7.refs_8_
  56.6 1.9 %collective-permute-done.4.refs_5_ = f32[1032,256]{1,0:T(8,128)} collective-permute-done((f32[1032,256]{1,0:T(8,128)}, f32[1032,256]{1,0:T(8,128)}, u32[]{:S(2)}, u32[]{:S(2)}) %collective-permute-start.4) | collective-permute-done | bytes 1056800 | tf_op jit(solution)/shard_map/ppermute | solution.py:304
  58.5 1.5 %collective-permute-done.3.refs_4_ = f32[1032,256]{1,0:T(8,128)} collective-permute-done((f32[1032,256]{1,0:T(8,128)}, f32[1032,256]{1,0:T(8,128)}, u32[]{:S(2)}, u32[]{:S(2)}) %collective-permute-start.3) | collective-permute-done | bytes 1056800 | tf_op jit(solution)/shard_map/ppermute | solution.py:304
  60.0 10.3 %shard_map.38 = f32[1024,2048]{1,0:T(8,128)} custom-call(s32[10]{0:T(128)S(1)} %dynamic-slice_bitcast_fusion.info_ref, f32[1032,256]{1,0:T(8,128)S(1)} %shard_map.37.refs_0_, f32[1032,256]{1,0:T(8,128)} %collective-permute-done.refs_1_, f32[1032,256]{1,0:T(8,128)} %collective-permute-done.1.refs_2_, f32[1032,256]{1,0:T(8,128)} %collective-permute-done.2.refs_3_, ...), custom_call_target="tpu_custom_call" | custom-call | flops 1000000000 | bytes 20971520 | tf_op jit(solution)/shard_map/pallas_call | solution.py:312
  (1 shorter events, 0.0 us)
Async XLA Ops:
  0.0 1.2 %copy-start = (f32[1024,256]{1,0:T(8,128)S(1)}, f32[1024,256]{1,0:T(8,128)}, u32[]{:S(2)}) copy-start(f32[1024,256]{1,0:T(8,128)} %data_ref.1) | copy-start | bytes 3145732
  1.2 0.7 copy-start.1
  2.0 24.6 %collective-permute-start.6 = (f32[1032,256]{1,0:T(8,128)S(1)}, f32[1032,256]{1,0:T(8,128)S(1)}, u32[]{:S(2)}, u32[]{:S(2)}) collective-permute-start(f32[1032,256]{1,0:T(8,128)S(1)} %shard_map.37.refs_0_), channel_id=1, source_target_pairs={{4,7},{5,4},{6,5},{7,6},{8,11},{9,8},{10,9},{11,10},{28,31},{29,28... | collective-permute-start | bytes 3170312 | tf_op jit(solution)/shard_map/ppermute | solution.py:304
  4.1 38.5 %collective-permute-start.5 = (f32[1032,256]{1,0:T(8,128)S(1)}, f32[1032,256]{1,0:T(8,128)S(1)}, u32[]{:S(2)}, u32[]{:S(2)}) collective-permute-start(f32[1032,256]{1,0:T(8,128)S(1)} %shard_map.37.refs_0_), channel_id=1, source_target_pairs={{0,3},{1,0},{2,1},{3,2},{24,25},{25,26},{26,27},{27,24},{28,29},{2... | collective-permute-start | bytes 3170312 | tf_op jit(solution)/shard_map/ppermute | solution.py:304
  7.3 48.1 %collective-permute-start.1 = (f32[1032,256]{1,0:T(8,128)S(1)}, f32[1032,256]{1,0:T(8,128)}, u32[]{:S(2)}, u32[]{:S(2)}) collective-permute-start(f32[1032,256]{1,0:T(8,128)S(1)} %shard_map.37.refs_0_), channel_id=1, source_target_pairs={{8,0},{17,1},{26,2},{12,4},{21,5},{30,6},{16,8},{25,9},{2,10},{20,... | collective-permute-start | bytes 3170312 | tf_op jit(solution)/shard_map/ppermute | solution.py:304
  7.6 48.3 %collective-permute-start = (f32[1032,256]{1,0:T(8,128)S(1)}, f32[1032,256]{1,0:T(8,128)}, u32[]{:S(2)}, u32[]{:S(2)}) collective-permute-start(f32[1032,256]{1,0:T(8,128)S(1)} %shard_map.37.refs_0_), channel_id=1, source_target_pairs={{9,1},{18,2},{27,3},{13,5},{22,6},{31,7},{17,9},{26,10},{3,11},{21... | collective-permute-start | bytes 3170312 | tf_op jit(solution)/shard_map/ppermute | solution.py:304
  7.6 49.0 %collective-permute-start.2 = (f32[1032,256]{1,0:T(8,128)S(1)}, f32[1032,256]{1,0:T(8,128)}, u32[]{:S(2)}, u32[]{:S(2)}) collective-permute-start(f32[1032,256]{1,0:T(8,128)S(1)} %shard_map.37.refs_0_), channel_id=1, source_target_pairs={{16,4},{25,5},{2,6},{11,7},{24,12},{1,13},{10,14},{19,15},{0,20},{... | collective-permute-start | bytes 3170312 | tf_op jit(solution)/shard_map/ppermute | solution.py:304
  26.6 30.0 %collective-permute-start.8 = (f32[1032,256]{1,0:T(8,128)S(1)}, f32[1032,256]{1,0:T(8,128)}, u32[]{:S(2)}, u32[]{:S(2)}) collective-permute-start(f32[1032,256]{1,0:T(8,128)S(1)} %collective-permute-done.6.refs_7_), channel_id=1, source_target_pairs={{4,7},{5,4},{6,5},{7,6},{8,11},{9,8},{10,9},{11,10},{16,17},{17,18... | collective-permute-start | bytes 3170312 | tf_op jit(solution)/shard_map/ppermute | solution.py:304
  42.6 14.1 %collective-permute-start.7 = (f32[1032,256]{1,0:T(8,128)S(1)}, f32[1032,256]{1,0:T(8,128)}, u32[]{:S(2)}, u32[]{:S(2)}) collective-permute-start(f32[1032,256]{1,0:T(8,128)S(1)} %collective-permute-done.5.refs_6_), channel_id=1, source_target_pairs={{13,14},{14,15},{7,12}} | collective-permute-start | bytes 3170312 | tf_op jit(solution)/shard_map/ppermute | solution.py:304
  55.4 3.1 %collective-permute-start.4 = (f32[1032,256]{1,0:T(8,128)}, f32[1032,256]{1,0:T(8,128)}, u32[]{:S(2)}, u32[]{:S(2)}) collective-permute-start(f32[1032,256]{1,0:T(8,128)} %collective-permute-done.1.refs_2_), channel_id=1, source_target_pairs={{4,0},{5,1},{6,2},{7,3},{0,4},{1,5},{2,6},{3,7},{12,8},{13,9},{14,... | collective-permute-start | bytes 3170312 | tf_op jit(solution)/shard_map/ppermute | solution.py:304
  55.9 4.1 %collective-permute-start.3 = (f32[1032,256]{1,0:T(8,128)}, f32[1032,256]{1,0:T(8,128)}, u32[]{:S(2)}, u32[]{:S(2)}) collective-permute-start(f32[1032,256]{1,0:T(8,128)} %collective-permute-done.refs_1_), channel_id=1, source_target_pairs={{4,0},{5,1},{6,2},{7,3},{0,4},{1,5},{2,6},{3,7},{12,8},{13,9},{14,... | collective-permute-start | bytes 3170312 | tf_op jit(solution)/shard_map/ppermute | solution.py:304

commit v19 on v18

--- a/solution.py
+++ b/solution.py
@@ -10,7 +10,7 @@
 
 BS = 64
 STEPS = 4
-UNROLL = 12
+UNROLL = 8
 EXTRA = 8
 PARTS = 16
 

time: 70.5 us -> 70.1 us (level)
  no operation moved by 1% of the time
where the time goes in v19:
time: 70.1 us; the launch traced here: 70 us
  waiting for transfers between devices  47.9 us (68%)
  Pallas kernels  10 us (14%)
  starting transfers between devices  9.4 us (13%)
  local copies, waits for them, and re-layouts  2.59 us (4%)
    ppermute x9, waiting for transfers between devices, carry(): bufs.append(lax.ppermute(bufs[source], ('row', 'col'), flat))  47.9 us
    pallas_call x1, Pallas kernels, local(): pl.pallas_call(functools.partial(product_kernel, slots, n_row, ratio, rb,...  9.94 us
    ppermute x9, starting transfers between devices, carry(): bufs.append(lax.ppermute(bufs[source], ('row', 'col'), flat))  9.4 us
    unnamed x4, local copies, waits for them, and re-layouts  1.91 us
  transfers between devices with their start and end apart: 9, of which 5 were waited for; matrix products, arithmetic and copies ran while one was open for 1% of the time, Pallas kernels for 0%

profile of v19, /device:TPU:15, one launch (start us, length us, event | category | flops | bytes accessed | tf_op | source)
XLA Modules:
  0.0 70.0 jit_solution(12015455521946141414)
XLA Ops:
  0.0 0.0 copy-start
  0.0 1.2 %copy-done = f32[1024,256]{1,0:T(8,128)S(1)} copy-done((f32[1024,256]{1,0:T(8,128)S(1)}, f32[1024,256]{1,0:T(8,128)}, u32[]{:S(2)}) %copy-start) | copy-done | bytes 1048600
  1.2 0.7 copy-done.1
  1.9 0.1 shard_map.37.refs_0_
  2.0 2.1 %collective-permute-start.6 = (f32[1032,256]{1,0:T(8,128)S(1)}, f32[1032,256]{1,0:T(8,128)S(1)}, u32[]{:S(2)}, u32[]{:S(2)}) collective-permute-start(f32[1032,256]{1,0:T(8,128)S(1)} %shard_map.37.refs_0_), channel_id=1, source_target_pairs={{4,7},{5,4},{6,5},{7,6},{8,11},{9,8},{10,9},{11,10},{28,31},{29,28... | collective-permute-start | bytes 3170312 | tf_op jit(solution)/shard_map/ppermute | solution.py:304
  4.1 3.2 %collective-permute-start.5 = (f32[1032,256]{1,0:T(8,128)S(1)}, f32[1032,256]{1,0:T(8,128)S(1)}, u32[]{:S(2)}, u32[]{:S(2)}) collective-permute-start(f32[1032,256]{1,0:T(8,128)S(1)} %shard_map.37.refs_0_), channel_id=1, source_target_pairs={{0,3},{1,0},{2,1},{3,2},{24,25},{25,26},{26,27},{27,24},{28,29},{2... | collective-permute-start | bytes 3170312 | tf_op jit(solution)/shard_map/ppermute | solution.py:304
  7.3 0.3 collective-permute-start.1
  7.6 0.0 collective-permute-start
  7.6 0.0 collective-permute-start.2
  7.6 19.0 %collective-permute-done.6.refs_7_ = f32[1032,256]{1,0:T(8,128)S(1)} collective-permute-done((f32[1032,256]{1,0:T(8,128)S(1)}, f32[1032,256]{1,0:T(8,128)S(1)}, u32[]{:S(2)}, u32[]{:S(2)}) %collective-permute-start.6) | collective-permute-done | bytes 1056800 | tf_op jit(solution)/shard_map/ppermute | solution.py:304
  26.6 1.7 %collective-permute-start.8 = (f32[1032,256]{1,0:T(8,128)S(1)}, f32[1032,256]{1,0:T(8,128)}, u32[]{:S(2)}, u32[]{:S(2)}) collective-permute-start(f32[1032,256]{1,0:T(8,128)S(1)} %collective-permute-done.6.refs_7_), channel_id=1, source_target_pairs={{4,7},{5,4},{6,5},{7,6},{8,11},{9,8},{10,9},{11,10},{16,17},{17,18... | collective-permute-start | bytes 3170312 | tf_op jit(solution)/shard_map/ppermute | solution.py:304
  28.3 14.3 %collective-permute-done.5.refs_6_ = f32[1032,256]{1,0:T(8,128)S(1)} collective-permute-done((f32[1032,256]{1,0:T(8,128)S(1)}, f32[1032,256]{1,0:T(8,128)S(1)}, u32[]{:S(2)}, u32[]{:S(2)}) %collective-permute-start.5) | collective-permute-done | bytes 1056800 | tf_op jit(solution)/shard_map/ppermute | solution.py:304
  42.6 1.7 %collective-permute-start.7 = (f32[1032,256]{1,0:T(8,128)S(1)}, f32[1032,256]{1,0:T(8,128)}, u32[]{:S(2)}, u32[]{:S(2)}) collective-permute-start(f32[1032,256]{1,0:T(8,128)S(1)} %collective-permute-done.5.refs_6_), channel_id=1, source_target_pairs={{13,14},{14,15},{7,12}} | collective-permute-start | bytes 3170312 | tf_op jit(solution)/shard_map/ppermute | solution.py:304
  44.2 11.2 %collective-permute-done.1.refs_2_ = f32[1032,256]{1,0:T(8,128)} collective-permute-done((f32[1032,256]{1,0:T(8,128)S(1)}, f32[1032,256]{1,0:T(8,128)}, u32[]{:S(2)}, u32[]{:S(2)}) %collective-permute-start.1) | collective-permute-done | bytes 1056800 | tf_op jit(solution)/shard_map/ppermute | solution.py:304
  55.4 0.5 collective-permute-start.4
  55.9 0.0 collective-permute-done.refs_1_
  55.9 0.0 collective-permute-start.3
  55.9 0.7 dynamic-slice_bitcast_fusion.info_ref
  56.6 0.0 collective-permute-done.2.refs_3_
  56.6 0.0 collective-permute-done.8.refs_9_
  56.6 0.0 collective-permute-done.7.refs_8_
  56.6 1.9 %collective-permute-done.4.refs_5_ = f32[1032,256]{1,0:T(8,128)} collective-permute-done((f32[1032,256]{1,0:T(8,128)}, f32[1032,256]{1,0:T(8,128)}, u32[]{:S(2)}, u32[]{:S(2)}) %collective-permute-start.4) | collective-permute-done | bytes 1056800 | tf_op jit(solution)/shard_map/ppermute | solution.py:304
  58.5 1.5 %collective-permute-done.3.refs_4_ = f32[1032,256]{1,0:T(8,128)} collective-permute-done((f32[1032,256]{1,0:T(8,128)}, f32[1032,256]{1,0:T(8,128)}, u32[]{:S(2)}, u32[]{:S(2)}) %collective-permute-start.3) | collective-permute-done | bytes 1056800 | tf_op jit(solution)/shard_map/ppermute | solution.py:304
  60.0 9.9 %shard_map.38 = f32[1024,2048]{1,0:T(8,128)} custom-call(s32[10]{0:T(128)S(1)} %dynamic-slice_bitcast_fusion.info_ref, f32[1032,256]{1,0:T(8,128)S(1)} %shard_map.37.refs_0_, f32[1032,256]{1,0:T(8,128)} %collective-permute-done.refs_1_, f32[1032,256]{1,0:T(8,128)} %collective-permute-done.1.refs_2_, f32[1032,256]{1,0:T(8,128)} %collective-permute-done.2.refs_3_, ...), custom_call_target="tpu_custom_call" | custom-call | flops 1000000000 | bytes 20971520 | tf_op jit(solution)/shard_map/pallas_call | solution.py:312
  (1 shorter events, 0.0 us)
Async XLA Ops:
  0.0 1.2 %copy-start = (f32[1024,256]{1,0:T(8,128)S(1)}, f32[1024,256]{1,0:T(8,128)}, u32[]{:S(2)}) copy-start(f32[1024,256]{1,0:T(8,128)} %data_ref.1) | copy-start | bytes 3145732
  1.2 0.7 copy-start.1
  2.0 24.6 %collective-permute-start.6 = (f32[1032,256]{1,0:T(8,128)S(1)}, f32[1032,256]{1,0:T(8,128)S(1)}, u32[]{:S(2)}, u32[]{:S(2)}) collective-permute-start(f32[1032,256]{1,0:T(8,128)S(1)} %shard_map.37.refs_0_), channel_id=1, source_target_pairs={{4,7},{5,4},{6,5},{7,6},{8,11},{9,8},{10,9},{11,10},{28,31},{29,28... | collective-permute-start | bytes 3170312 | tf_op jit(solution)/shard_map/ppermute | solution.py:304
  4.1 38.5 %collective-permute-start.5 = (f32[1032,256]{1,0:T(8,128)S(1)}, f32[1032,256]{1,0:T(8,128)S(1)}, u32[]{:S(2)}, u32[]{:S(2)}) collective-permute-start(f32[1032,256]{1,0:T(8,128)S(1)} %shard_map.37.refs_0_), channel_id=1, source_target_pairs={{0,3},{1,0},{2,1},{3,2},{24,25},{25,26},{26,27},{27,24},{28,29},{2... | collective-permute-start | bytes 3170312 | tf_op jit(solution)/shard_map/ppermute | solution.py:304
  7.3 48.1 %collective-permute-start.1 = (f32[1032,256]{1,0:T(8,128)S(1)}, f32[1032,256]{1,0:T(8,128)}, u32[]{:S(2)}, u32[]{:S(2)}) collective-permute-start(f32[1032,256]{1,0:T(8,128)S(1)} %shard_map.37.refs_0_), channel_id=1, source_target_pairs={{8,0},{17,1},{26,2},{12,4},{21,5},{30,6},{16,8},{25,9},{2,10},{20,... | collective-permute-start | bytes 3170312 | tf_op jit(solution)/shard_map/ppermute | solution.py:304
  7.6 48.3 %collective-permute-start = (f32[1032,256]{1,0:T(8,128)S(1)}, f32[1032,256]{1,0:T(8,128)}, u32[]{:S(2)}, u32[]{:S(2)}) collective-permute-start(f32[1032,256]{1,0:T(8,128)S(1)} %shard_map.37.refs_0_), channel_id=1, source_target_pairs={{9,1},{18,2},{27,3},{13,5},{22,6},{31,7},{17,9},{26,10},{3,11},{21... | collective-permute-start | bytes 3170312 | tf_op jit(solution)/shard_map/ppermute | solution.py:304
  7.6 49.0 %collective-permute-start.2 = (f32[1032,256]{1,0:T(8,128)S(1)}, f32[1032,256]{1,0:T(8,128)}, u32[]{:S(2)}, u32[]{:S(2)}) collective-permute-start(f32[1032,256]{1,0:T(8,128)S(1)} %shard_map.37.refs_0_), channel_id=1, source_target_pairs={{16,4},{25,5},{2,6},{11,7},{24,12},{1,13},{10,14},{19,15},{0,20},{... | collective-permute-start | bytes 3170312 | tf_op jit(solution)/shard_map/ppermute | solution.py:304
  26.6 30.0 %collective-permute-start.8 = (f32[1032,256]{1,0:T(8,128)S(1)}, f32[1032,256]{1,0:T(8,128)}, u32[]{:S(2)}, u32[]{:S(2)}) collective-permute-start(f32[1032,256]{1,0:T(8,128)S(1)} %collective-permute-done.6.refs_7_), channel_id=1, source_target_pairs={{4,7},{5,4},{6,5},{7,6},{8,11},{9,8},{10,9},{11,10},{16,17},{17,18... | collective-permute-start | bytes 3170312 | tf_op jit(solution)/shard_map/ppermute | solution.py:304
  42.6 14.1 %collective-permute-start.7 = (f32[1032,256]{1,0:T(8,128)S(1)}, f32[1032,256]{1,0:T(8,128)}, u32[]{:S(2)}, u32[]{:S(2)}) collective-permute-start(f32[1032,256]{1,0:T(8,128)S(1)} %collective-permute-done.5.refs_6_), channel_id=1, source_target_pairs={{13,14},{14,15},{7,12}} | collective-permute-start | bytes 3170312 | tf_op jit(solution)/shard_map/ppermute | solution.py:304
  55.4 3.1 %collective-permute-start.4 = (f32[1032,256]{1,0:T(8,128)}, f32[1032,256]{1,0:T(8,128)}, u32[]{:S(2)}, u32[]{:S(2)}) collective-permute-start(f32[1032,256]{1,0:T(8,128)} %collective-permute-done.1.refs_2_), channel_id=1, source_target_pairs={{4,0},{5,1},{6,2},{7,3},{0,4},{1,5},{2,6},{3,7},{12,8},{13,9},{14,... | collective-permute-start | bytes 3170312 | tf_op jit(solution)/shard_map/ppermute | solution.py:304
  55.9 4.1 %collective-permute-start.3 = (f32[1032,256]{1,0:T(8,128)}, f32[1032,256]{1,0:T(8,128)}, u32[]{:S(2)}, u32[]{:S(2)}) collective-permute-start(f32[1032,256]{1,0:T(8,128)} %collective-permute-done.refs_1_), channel_id=1, source_target_pairs={{4,0},{5,1},{6,2},{7,3},{0,4},{1,5},{2,6},{3,7},{12,8},{13,9},{14,... | collective-permute-start | bytes 3170312 | tf_op jit(solution)/shard_map/ppermute | solution.py:304

commit v20 on v13

--- a/solution.py
+++ b/solution.py
@@ -119,20 +119,25 @@
     data_copy.wait()
 
 
+def bufs_rows(bufs):
+    return bufs[0].shape[0] - EXTRA
+
+
 def product_kernel(slots, n_row, ratio, rb, w, n_right, among, info_ref, *refs):
     out_ref, left, right, acc, value, cols, coded, scalars, codes, ends, lsem, rsem, osem, csem = refs[-14:]
     right_bufs, left_bufs = refs[:n_right], refs[:1] + refs[n_right:-14]
-    rows, width = left.shape[1] - EXTRA, left.shape[2]
-    names = pl.ds(rows, EXTRA)
+    rows, width = bufs_rows(right_bufs), left.shape[1]
+    names, tile = pl.ds(rows, EXTRA), pl.ds(0, rows)
+    place_of = lambda ref, index: ref.at[pl.ds(index * rows, rows)]
     for slot in range(slots):
         fetch(info_ref[slot], among[slot], [buf.at[names] for buf in left_bufs], cols.at[slot], csem.at[slot])
     for step in range(STEPS):
         at = slots + step
         fetch(info_ref[at], among[at], [buf.at[names] for buf in right_bufs], cols.at[at], csem.at[at])
     for step in range(STEPS):
-        fetch(info_ref[slots + step], among[slots + step], right_bufs, right.at[step], rsem.at[step])
+        fetch(info_ref[slots + step], among[slots + step], [buf.at[tile] for buf in right_bufs], place_of(right, step), rsem.at[step])
     for slot in range(slots):
-        fetch(info_ref[slot], among[slot], left_bufs, left.at[slot], lsem.at[slot])
+        fetch(info_ref[slot], among[slot], [buf.at[tile] for buf in left_bufs], place_of(left, slot), lsem.at[slot])
 
     def clear(first, rows_count):
         at = pl.ds(pl.multiple_of(first, 8), rows_count)
@@ -165,15 +170,17 @@
             step = jnp.where(beyond, step + 1, step)
             inner = jnp.where(beyond, inner - rb, inner)
         step = jnp.where(step >= n_row, step - n_row, step)
-        code = inner | tile_slot << 8 | slot << 12 | row << 16 | step << 24
+        code = step * rb + inner | tile_slot << 8 | slot * rb + row << 12 | row << 20
         valid = valid & (step < STEPS)
         coded[slot * w : (slot + 1) * w, :] = jnp.where(valid, jnp.where(used, code, -1), -1)
+    places = jnp.full((w, lanes), 2 << 16, jnp.int32)
     for step in range(STEPS):
         pltpu.make_async_copy(right_bufs[0].at[names], cols.at[slots + step], csem.at[slots + step]).wait()
         col = cols[slots + step, 0:w, 0:lanes].astype(jnp.int32)
-        code = (col >> 1) * 2 * BS | (col & 1) << 16
-        coded[(slots + step) * w : (slots + step + 1) * w, :] = jnp.where(col < 0, 2 << 16, code)
-    coded[(slots + STEPS) * w : (slots + STEPS + 1) * w, :] = jnp.full((w, lanes), 2 << 16, jnp.int32)
+        place = jnp.where(col < 0, 2 << 16, (col >> 1) * 2 * BS | (col & 1) << 16)
+        own_lanes = (row >= step * rb) & (row < (step + 1) * rb)
+        places = jnp.where(own_lanes, pltpu.roll(place, step * rb, 1) if step else place, places)
+    coded[slots * w : (slots + 1) * w, :] = places
     to_scalars = pltpu.make_async_copy(coded, scalars, csem.at[slots + STEPS])
     to_scalars.start()
     clear_blocks(ahead // 2, ahead)
@@ -191,14 +198,14 @@
 
     listed_end = lax.fori_loop(0, rb, listed, jnp.int32(0))
     for u in range(UNROLL):
-        codes[listed_end + u] = STEPS << 24
-
-    for step in range(STEPS):
-        pltpu.make_async_copy(right_bufs[0], right.at[step], rsem.at[step]).wait()
+        codes[listed_end + u] = STEPS * rb
+
+    for step in range(STEPS):
+        pltpu.make_async_copy(right_bufs[0].at[tile], place_of(right, step), rsem.at[step]).wait()
     for slot in range(slots):
         @pl.when(info_ref[slot] >= 0)
         def _():
-            pltpu.make_async_copy(left_bufs[0], left.at[slot], lsem.at[slot]).wait()
+            pltpu.make_async_copy(left_bufs[0].at[tile], place_of(left, slot), lsem.at[slot]).wait()
 
     half = lax.broadcasted_iota(jnp.int32, (BS, 2 * BS), 1) // BS
 
@@ -207,11 +214,11 @@
 
     def product(code):
         slot = (code >> 8) & 15
-        x = left[(code >> 12) & 15, block_at((code >> 16) & 255), pl.ds(pl.multiple_of((slot >> 1) * 2 * BS, 2 * BS), 2 * BS)]
+        x = left[block_at((code >> 12) & 255), pl.ds(pl.multiple_of((slot >> 1) * 2 * BS, 2 * BS), 2 * BS)]
         both = jnp.where(half == (slot & 1), x, pltpu.roll(x, BS, 1))
         hi = both.astype(jnp.bfloat16).astype(jnp.float32)
         lhs = jnp.where(half == 0, hi, both - hi).astype(jnp.bfloat16)
-        y = right[code >> 24, block_at(code & 255), :]
+        y = right[block_at(code & 255), :]
         hi = y.astype(jnp.bfloat16)
         lo = (y - hi.astype(jnp.float32)).astype(jnp.bfloat16)
         lhs = jnp.concatenate([lhs, lhs], axis=1)
@@ -219,13 +226,13 @@
         return jnp.dot(lhs, rhs, preferred_element_type=jnp.float32)
 
     def add(code, product):
-        rows_at = block_at((code >> 16) & 255)
+        rows_at = block_at(code >> 20)
         for pair in range(w // 2):
             x = product[:, pair * 2 * BS : (pair + 1) * 2 * BS]
             turned = pltpu.roll(x, BS, 1)
             picked, at = [], []
             for side in range(2):
-                place = scalars[(slots + (code >> 24)) * w + 2 * pair + side, code & 255]
+                place = scalars[slots * w + 2 * pair + side, code & 255]
                 parity = place >> 16
                 chosen = jnp.where(parity == side, x, turned)
                 picked.append(jnp.where(half == parity, chosen, 0.0))
@@ -305,15 +312,15 @@
     out_shape = jax.ShapeDtypeStruct((rows, rb * ratio * BS), jnp.float32)
     bufs = right_bufs + left_bufs[1:]
     among = [sorted(set(table[:, :, i].ravel().tolist()) - {-1}) for i in range(slots + STEPS)]
-    codings = -(-(slots + STEPS + 1) * w // 8) * 8
+    codings = -(-(slots + 1) * w // 8) * 8
     return pl.pallas_call(
         functools.partial(product_kernel, slots, n_row, ratio, rb, w, len(right_bufs), among),
         out_shape=out_shape,
         in_specs=[smem] + [hbm] * len(bufs),
         out_specs=hbm,
         scratch_shapes=[
-            pltpu.VMEM((slots, rows + EXTRA, width), jnp.float32),
-            pltpu.VMEM((STEPS + 1, rows + EXTRA, width), jnp.float32),
+            pltpu.VMEM((slots * rows, width), jnp.float32),
+            pltpu.VMEM((STEPS * rows + BS, width), jnp.float32),
             pltpu.VMEM(out_shape.shape, jnp.float32),
             pltpu.VMEM((UNROLL, BS, width), jnp.float32),
             pltpu.VMEM((slots + STEPS, EXTRA, width), jnp.float32),

time: 70.4 us -> 70.4 us (level)
  no operation moved by 1% of the time
where the time goes in v20:
time: 70.4 us; the launch traced here: 69.3 us
  waiting for transfers between devices  47.9 us (68%)
  starting transfers between devices  9.4 us (13%)
  Pallas kernels  9.36 us (13%)
  local copies, waits for them, and re-layouts  2.59 us (4%)
    ppermute x9, waiting for transfers between devices, carry(): bufs.append(lax.ppermute(bufs[source], ('row', 'col'), flat))  47.9 us
    ppermute x9, starting transfers between devices, carry(): bufs.append(lax.ppermute(bufs[source], ('row', 'col'), flat))  9.4 us
    pallas_call x1, Pallas kernels, local(): pl.pallas_call(functools.partial(product_kernel, slots, n_row, ratio, rb,...  9.26 us
    unnamed x4, local copies, waits for them, and re-layouts  1.91 us
  transfers between devices with their start and end apart: 9, of which 5 were waited for; matrix products, arithmetic and copies ran while one was open for 1% of the time, Pallas kernels for 0%

profile of v20, /device:TPU:15, one launch (start us, length us, event | category | flops | bytes accessed | tf_op | source)
XLA Modules:
  0.0 69.3 jit_solution(784955705296348836)
XLA Ops:
  0.0 0.0 copy-start
  0.0 1.2 %copy-done = f32[1024,256]{1,0:T(8,128)S(1)} copy-done((f32[1024,256]{1,0:T(8,128)S(1)}, f32[1024,256]{1,0:T(8,128)}, u32[]{:S(2)}) %copy-start) | copy-done | bytes 1048600
  1.2 0.7 copy-done.1
  1.9 0.1 shard_map.37.refs_0_
  2.0 2.1 %collective-permute-start.6 = (f32[1032,256]{1,0:T(8,128)S(1)}, f32[1032,256]{1,0:T(8,128)S(1)}, u32[]{:S(2)}, u32[]{:S(2)}) collective-permute-start(f32[1032,256]{1,0:T(8,128)S(1)} %shard_map.37.refs_0_), channel_id=1, source_target_pairs={{4,7},{5,4},{6,5},{7,6},{8,11},{9,8},{10,9},{11,10},{28,31},{29,28... | collective-permute-start | bytes 3170312 | tf_op jit(solution)/shard_map/ppermute | solution.py:308
  4.1 3.2 %collective-permute-start.5 = (f32[1032,256]{1,0:T(8,128)S(1)}, f32[1032,256]{1,0:T(8,128)S(1)}, u32[]{:S(2)}, u32[]{:S(2)}) collective-permute-start(f32[1032,256]{1,0:T(8,128)S(1)} %shard_map.37.refs_0_), channel_id=1, source_target_pairs={{16,17},{17,18},{18,19},{19,16},{20,21},{21,22},{22,23},{23,20},{2... | collective-permute-start | bytes 3170312 | tf_op jit(solution)/shard_map/ppermute | solution.py:308
  7.3 0.3 collective-permute-start.1
  7.6 0.0 collective-permute-start
  7.6 0.0 collective-permute-start.2
  7.6 19.0 %collective-permute-done.6.refs_7_ = f32[1032,256]{1,0:T(8,128)S(1)} collective-permute-done((f32[1032,256]{1,0:T(8,128)S(1)}, f32[1032,256]{1,0:T(8,128)S(1)}, u32[]{:S(2)}, u32[]{:S(2)}) %collective-permute-start.6) | collective-permute-done | bytes 1056800 | tf_op jit(solution)/shard_map/ppermute | solution.py:308
  26.6 1.7 %collective-permute-start.8 = (f32[1032,256]{1,0:T(8,128)S(1)}, f32[1032,256]{1,0:T(8,128)}, u32[]{:S(2)}, u32[]{:S(2)}) collective-permute-start(f32[1032,256]{1,0:T(8,128)S(1)} %collective-permute-done.6.refs_7_), channel_id=1, source_target_pairs={{4,7},{5,4},{6,5},{7,6},{8,11},{9,8},{10,9},{11,10},{13,12},{14,13... | collective-permute-start | bytes 3170312 | tf_op jit(solution)/shard_map/ppermute | solution.py:308
  28.3 14.3 %collective-permute-done.5.refs_6_ = f32[1032,256]{1,0:T(8,128)S(1)} collective-permute-done((f32[1032,256]{1,0:T(8,128)S(1)}, f32[1032,256]{1,0:T(8,128)S(1)}, u32[]{:S(2)}, u32[]{:S(2)}) %collective-permute-start.5) | collective-permute-done | bytes 1056800 | tf_op jit(solution)/shard_map/ppermute | solution.py:308
  42.6 1.7 %collective-permute-start.7 = (f32[1032,256]{1,0:T(8,128)S(1)}, f32[1032,256]{1,0:T(8,128)}, u32[]{:S(2)}, u32[]{:S(2)}) collective-permute-start(f32[1032,256]{1,0:T(8,128)S(1)} %collective-permute-done.5.refs_6_), channel_id=1, source_target_pairs={{16,17},{17,18},{18,19},{19,16},{20,21},{21,22},{22,23},{23,20},{1... | collective-permute-start | bytes 3170312 | tf_op jit(solution)/shard_map/ppermute | solution.py:308
  44.2 11.2 %collective-permute-done.1.refs_2_ = f32[1032,256]{1,0:T(8,128)} collective-permute-done((f32[1032,256]{1,0:T(8,128)S(1)}, f32[1032,256]{1,0:T(8,128)}, u32[]{:S(2)}, u32[]{:S(2)}) %collective-permute-start.1) | collective-permute-done | bytes 1056800 | tf_op jit(solution)/shard_map/ppermute | solution.py:308
  55.4 0.5 collective-permute-start.4
  55.9 0.0 collective-permute-done.refs_1_
  55.9 0.0 collective-permute-start.3
  55.9 0.7 dynamic-slice_bitcast_fusion.info_ref
  56.6 0.0 collective-permute-done.2.refs_3_
  56.6 0.0 collective-permute-done.8.refs_9_
  56.6 0.0 collective-permute-done.7.refs_8_
  56.6 1.9 %collective-permute-done.4.refs_5_ = f32[1032,256]{1,0:T(8,128)} collective-permute-done((f32[1032,256]{1,0:T(8,128)}, f32[1032,256]{1,0:T(8,128)}, u32[]{:S(2)}, u32[]{:S(2)}) %collective-permute-start.4) | collective-permute-done | bytes 1056800 | tf_op jit(solution)/shard_map/ppermute | solution.py:308
  58.5 1.5 %collective-permute-done.3.refs_4_ = f32[1032,256]{1,0:T(8,128)} collective-permute-done((f32[1032,256]{1,0:T(8,128)}, f32[1032,256]{1,0:T(8,128)}, u32[]{:S(2)}, u32[]{:S(2)}) %collective-permute-start.3) | collective-permute-done | bytes 1056800 | tf_op jit(solution)/shard_map/ppermute | solution.py:308
  60.0 9.3 %shard_map.38 = f32[1024,2048]{1,0:T(8,128)} custom-call(s32[10]{0:T(128)S(1)} %dynamic-slice_bitcast_fusion.info_ref, f32[1032,256]{1,0:T(8,128)S(1)} %shard_map.37.refs_0_, f32[1032,256]{1,0:T(8,128)} %collective-permute-done.refs_1_, f32[1032,256]{1,0:T(8,128)} %collective-permute-done.1.refs_2_, f32[1032,256]{1,0:T(8,128)} %collective-permute-done.2.refs_3_, ...), custom_call_target="tpu_custom_call" | custom-call | flops 1000000000 | bytes 20971520 | tf_op jit(solution)/shard_map/pallas_call | solution.py:316
  (1 shorter events, 0.0 us)
Async XLA Ops:
  0.0 1.2 %copy-start = (f32[1024,256]{1,0:T(8,128)S(1)}, f32[1024,256]{1,0:T(8,128)}, u32[]{:S(2)}) copy-start(f32[1024,256]{1,0:T(8,128)} %data_ref.1) | copy-start | bytes 3145732
  1.2 0.7 copy-start.1
  2.0 24.6 %collective-permute-start.6 = (f32[1032,256]{1,0:T(8,128)S(1)}, f32[1032,256]{1,0:T(8,128)S(1)}, u32[]{:S(2)}, u32[]{:S(2)}) collective-permute-start(f32[1032,256]{1,0:T(8,128)S(1)} %shard_map.37.refs_0_), channel_id=1, source_target_pairs={{4,7},{5,4},{6,5},{7,6},{8,11},{9,8},{10,9},{11,10},{28,31},{29,28... | collective-permute-start | bytes 3170312 | tf_op jit(solution)/shard_map/ppermute | solution.py:308
  4.1 38.5 %collective-permute-start.5 = (f32[1032,256]{1,0:T(8,128)S(1)}, f32[1032,256]{1,0:T(8,128)S(1)}, u32[]{:S(2)}, u32[]{:S(2)}) collective-permute-start(f32[1032,256]{1,0:T(8,128)S(1)} %shard_map.37.refs_0_), channel_id=1, source_target_pairs={{16,17},{17,18},{18,19},{19,16},{20,21},{21,22},{22,23},{23,20},{2... | collective-permute-start | bytes 3170312 | tf_op jit(solution)/shard_map/ppermute | solution.py:308
  7.3 48.1 %collective-permute-start.1 = (f32[1032,256]{1,0:T(8,128)S(1)}, f32[1032,256]{1,0:T(8,128)}, u32[]{:S(2)}, u32[]{:S(2)}) collective-permute-start(f32[1032,256]{1,0:T(8,128)S(1)} %shard_map.37.refs_0_), channel_id=1, source_target_pairs={{8,0},{17,1},{26,2},{12,4},{21,5},{30,6},{16,8},{25,9},{2,10},{20,... | collective-permute-start | bytes 3170312 | tf_op jit(solution)/shard_map/ppermute | solution.py:308
  7.6 48.3 %collective-permute-start = (f32[1032,256]{1,0:T(8,128)S(1)}, f32[1032,256]{1,0:T(8,128)}, u32[]{:S(2)}, u32[]{:S(2)}) collective-permute-start(f32[1032,256]{1,0:T(8,128)S(1)} %shard_map.37.refs_0_), channel_id=1, source_target_pairs={{9,1},{18,2},{27,3},{13,5},{22,6},{31,7},{17,9},{26,10},{3,11},{21... | collective-permute-start | bytes 3170312 | tf_op jit(solution)/shard_map/ppermute | solution.py:308
  7.6 49.0 %collective-permute-start.2 = (f32[1032,256]{1,0:T(8,128)S(1)}, f32[1032,256]{1,0:T(8,128)}, u32[]{:S(2)}, u32[]{:S(2)}) collective-permute-start(f32[1032,256]{1,0:T(8,128)S(1)} %shard_map.37.refs_0_), channel_id=1, source_target_pairs={{16,4},{25,5},{2,6},{11,7},{24,12},{1,13},{10,14},{19,15},{0,20},{... | collective-permute-start | bytes 3170312 | tf_op jit(solution)/shard_map/ppermute | solution.py:308
  26.6 30.0 %collective-permute-start.8 = (f32[1032,256]{1,0:T(8,128)S(1)}, f32[1032,256]{1,0:T(8,128)}, u32[]{:S(2)}, u32[]{:S(2)}) collective-permute-start(f32[1032,256]{1,0:T(8,128)S(1)} %collective-permute-done.6.refs_7_), channel_id=1, source_target_pairs={{4,7},{5,4},{6,5},{7,6},{8,11},{9,8},{10,9},{11,10},{13,12},{14,13... | collective-permute-start | bytes 3170312 | tf_op jit(solution)/shard_map/ppermute | solution.py:308
  42.6 14.1 %collective-permute-start.7 = (f32[1032,256]{1,0:T(8,128)S(1)}, f32[1032,256]{1,0:T(8,128)}, u32[]{:S(2)}, u32[]{:S(2)}) collective-permute-start(f32[1032,256]{1,0:T(8,128)S(1)} %collective-permute-done.5.refs_6_), channel_id=1, source_target_pairs={{16,17},{17,18},{18,19},{19,16},{20,21},{21,22},{22,23},{23,20},{1... | collective-permute-start | bytes 3170312 | tf_op jit(solution)/shard_map/ppermute | solution.py:308
  55.4 3.1 %collective-permute-start.4 = (f32[1032,256]{1,0:T(8,128)}, f32[1032,256]{1,0:T(8,128)}, u32[]{:S(2)}, u32[]{:S(2)}) collective-permute-start(f32[1032,256]{1,0:T(8,128)} %collective-permute-done.1.refs_2_), channel_id=1, source_target_pairs={{4,0},{5,1},{6,2},{7,3},{0,4},{1,5},{2,6},{3,7},{12,8},{13,9},{14,... | collective-permute-start | bytes 3170312 | tf_op jit(solution)/shard_map/ppermute | solution.py:308
  55.9 4.1 %collective-permute-start.3 = (f32[1032,256]{1,0:T(8,128)}, f32[1032,256]{1,0:T(8,128)}, u32[]{:S(2)}, u32[]{:S(2)}) collective-permute-start(f32[1032,256]{1,0:T(8,128)} %collective-permute-done.refs_1_), channel_id=1, source_target_pairs={{4,0},{5,1},{6,2},{7,3},{0,4},{1,5},{2,6},{3,7},{12,8},{13,9},{14,... | collective-permute-start | bytes 3170312 | tf_op jit(solution)/shard_map/ppermute | solution.py:308

commit v21 on v20

--- a/solution.py
+++ b/solution.py
@@ -10,7 +10,7 @@
 
 BS = 64
 STEPS = 4
-UNROLL = 8
+UNROLL = 12
 EXTRA = 8
 PARTS = 16
 
@@ -49,11 +49,14 @@
                 once[step].append(r)
                 if 2 in offsets[r]:
                     twice[step].append(r)
-    down = shift([r for r in once[-1] if r != 0], -1, 4) + [((3, c), (3, c - 1)) for c in (1, 2, 3)] + [((3, 0), (0, 0))]
-    up = shift(once[1], 1, 4) + shift([0], -1, 4) + [((3, c), (3, c + 1)) for c in (0, 1, 2)] + [((3, 3), (1, 3))]
-    again_down = shift(twice[-1], -1, 4) + [((3, 1), (3, 0)), ((3, 2), (3, 1)), ((0, 0), (3, 3))]
-    again_up = shift(twice[1], 1, 4) + [((3, 1), (3, 2)), ((3, 2), (3, 3)), ((1, 3), (3, 0))]
-    return [(0, up), (0, down), (1, again_up), (2, again_down)]
+    plain = lambda step: [r for r in once[step] if r not in twice[step] and r != 7]
+    early = shift(twice[-1] + [7], -1, 4) + shift(twice[1], 1, 4)
+    early += [((3, c), (3, c - 1)) for c in (1, 2, 3)] + [((3, 0), (0, 0))]
+    late = shift(plain(-1), -1, 4) + shift(plain(1) + [7], 1, 4)
+    late += [((3, c), (3, c + 1)) for c in (0, 1, 2)] + [((3, 3), (1, 3))]
+    again_early = shift(twice[-1], -1, 4) + shift(twice[1], 1, 4) + [((3, 1), (3, 0)), ((3, 2), (3, 1)), ((0, 0), (3, 3))]
+    again_late = [((3, 1), (3, 2)), ((3, 2), (3, 3)), ((1, 3), (3, 0))]
+    return [(0, late), (0, early), (1, again_late), (2, again_early)]
 
 
 def right_plan(n_row, n_col, ratio):

time: 70.4 us -> 70.2 us (level); the launches traced: 69.3 us -> 70 us
  Pallas kernels: 9.36 us -> 10.1 us
    pallas_call x1, Pallas kernels: 9.26 us -> 10 us  [local(): pl.pallas_call(functools.partial(product_kernel, slots, n_row, ratio, rb,...]
where the time goes in v21:
time: 70.2 us; the launch traced here: 70 us
  waiting for transfers between devices  47.9 us (68%)
  Pallas kernels  10.1 us (14%)
  starting transfers between devices  9.4 us (13%)
  local copies, waits for them, and re-layouts  2.59 us (4%)
    ppermute x9, waiting for transfers between devices, carry(): bufs.append(lax.ppermute(bufs[source], ('row', 'col'), flat))  47.9 us
    pallas_call x1, Pallas kernels, local(): pl.pallas_call(functools.partial(product_kernel, slots, n_row, ratio, rb,...  10 us
    ppermute x9, starting transfers between devices, carry(): bufs.append(lax.ppermute(bufs[source], ('row', 'col'), flat))  9.4 us
    unnamed x4, local copies, waits for them, and re-layouts  1.91 us
  transfers between devices with their start and end apart: 9, of which 5 were waited for; matrix products, arithmetic and copies ran while one was open for 1% of the time, Pallas kernels for 0%

profile of v21, /device:TPU:15, one launch (start us, length us, event | category | flops | bytes accessed | tf_op | source)
XLA Modules:
  0.0 70.0 jit_solution(988599077733438977)
XLA Ops:
  0.0 0.0 copy-start
  0.0 1.2 %copy-done = f32[1024,256]{1,0:T(8,128)S(1)} copy-done((f32[1024,256]{1,0:T(8,128)S(1)}, f32[1024,256]{1,0:T(8,128)}, u32[]{:S(2)}) %copy-start) | copy-done | bytes 1048600
  1.2 0.7 copy-done.1
  1.9 0.1 shard_map.37.refs_0_
  2.0 2.1 %collective-permute-start.6 = (f32[1032,256]{1,0:T(8,128)S(1)}, f32[1032,256]{1,0:T(8,128)S(1)}, u32[]{:S(2)}, u32[]{:S(2)}) collective-permute-start(f32[1032,256]{1,0:T(8,128)S(1)} %shard_map.37.refs_0_), channel_id=1, source_target_pairs={{4,7},{5,4},{6,5},{7,6},{8,11},{9,8},{10,9},{11,10},{28,31},{29,28... | collective-permute-start | bytes 3170312 | tf_op jit(solution)/shard_map/ppermute | solution.py:311
  4.1 3.2 %collective-permute-start.5 = (f32[1032,256]{1,0:T(8,128)S(1)}, f32[1032,256]{1,0:T(8,128)S(1)}, u32[]{:S(2)}, u32[]{:S(2)}) collective-permute-start(f32[1032,256]{1,0:T(8,128)S(1)} %shard_map.37.refs_0_), channel_id=1, source_target_pairs={{0,3},{1,0},{2,1},{3,2},{24,25},{25,26},{26,27},{27,24},{28,29},{2... | collective-permute-start | bytes 3170312 | tf_op jit(solution)/shard_map/ppermute | solution.py:311
  7.3 0.3 collective-permute-start.1
  7.6 0.0 collective-permute-start
  7.6 0.0 collective-permute-start.2
  7.6 19.0 %collective-permute-done.6.refs_7_ = f32[1032,256]{1,0:T(8,128)S(1)} collective-permute-done((f32[1032,256]{1,0:T(8,128)S(1)}, f32[1032,256]{1,0:T(8,128)S(1)}, u32[]{:S(2)}, u32[]{:S(2)}) %collective-permute-start.6) | collective-permute-done | bytes 1056800 | tf_op jit(solution)/shard_map/ppermute | solution.py:311
  26.6 1.7 %collective-permute-start.8 = (f32[1032,256]{1,0:T(8,128)S(1)}, f32[1032,256]{1,0:T(8,128)}, u32[]{:S(2)}, u32[]{:S(2)}) collective-permute-start(f32[1032,256]{1,0:T(8,128)S(1)} %collective-permute-done.6.refs_7_), channel_id=1, source_target_pairs={{4,7},{5,4},{6,5},{7,6},{8,11},{9,8},{10,9},{11,10},{16,17},{17,18... | collective-permute-start | bytes 3170312 | tf_op jit(solution)/shard_map/ppermute | solution.py:311
  28.3 14.3 %collective-permute-done.5.refs_6_ = f32[1032,256]{1,0:T(8,128)S(1)} collective-permute-done((f32[1032,256]{1,0:T(8,128)S(1)}, f32[1032,256]{1,0:T(8,128)S(1)}, u32[]{:S(2)}, u32[]{:S(2)}) %collective-permute-start.5) | collective-permute-done | bytes 1056800 | tf_op jit(solution)/shard_map/ppermute | solution.py:311
  42.6 1.7 %collective-permute-start.7 = (f32[1032,256]{1,0:T(8,128)S(1)}, f32[1032,256]{1,0:T(8,128)}, u32[]{:S(2)}, u32[]{:S(2)}) collective-permute-start(f32[1032,256]{1,0:T(8,128)S(1)} %collective-permute-done.5.refs_6_), channel_id=1, source_target_pairs={{13,14},{14,15},{7,12}} | collective-permute-start | bytes 3170312 | tf_op jit(solution)/shard_map/ppermute | solution.py:311
  44.2 11.2 %collective-permute-done.1.refs_2_ = f32[1032,256]{1,0:T(8,128)} collective-permute-done((f32[1032,256]{1,0:T(8,128)S(1)}, f32[1032,256]{1,0:T(8,128)}, u32[]{:S(2)}, u32[]{:S(2)}) %collective-permute-start.1) | collective-permute-done | bytes 1056800 | tf_op jit(solution)/shard_map/ppermute | solution.py:311
  55.4 0.5 collective-permute-start.4
  55.9 0.0 collective-permute-done.refs_1_
  55.9 0.0 collective-permute-start.3
  55.9 0.7 dynamic-slice_bitcast_fusion.info_ref
  56.6 0.0 collective-permute-done.2.refs_3_
  56.6 0.0 collective-permute-done.8.refs_9_
  56.6 0.0 collective-permute-done.7.refs_8_
  56.6 1.9 %collective-permute-done.4.refs_5_ = f32[1032,256]{1,0:T(8,128)} collective-permute-done((f32[1032,256]{1,0:T(8,128)}, f32[1032,256]{1,0:T(8,128)}, u32[]{:S(2)}, u32[]{:S(2)}) %collective-permute-start.4) | collective-permute-done | bytes 1056800 | tf_op jit(solution)/shard_map/ppermute | solution.py:311
  58.5 1.5 %collective-permute-done.3.refs_4_ = f32[1032,256]{1,0:T(8,128)} collective-permute-done((f32[1032,256]{1,0:T(8,128)}, f32[1032,256]{1,0:T(8,128)}, u32[]{:S(2)}, u32[]{:S(2)}) %collective-permute-start.3) | collective-permute-done | bytes 1056800 | tf_op jit(solution)/shard_map/ppermute | solution.py:311
  60.0 10.0 %shard_map.38 = f32[1024,2048]{1,0:T(8,128)} custom-call(s32[10]{0:T(128)S(1)} %dynamic-slice_bitcast_fusion.info_ref, f32[1032,256]{1,0:T(8,128)S(1)} %shard_map.37.refs_0_, f32[1032,256]{1,0:T(8,128)} %collective-permute-done.refs_1_, f32[1032,256]{1,0:T(8,128)} %collective-permute-done.1.refs_2_, f32[1032,256]{1,0:T(8,128)} %collective-permute-done.2.refs_3_, ...), custom_call_target="tpu_custom_call" | custom-call | flops 1000000000 | bytes 20971520 | tf_op jit(solution)/shard_map/pallas_call | solution.py:319
  (1 shorter events, 0.0 us)
Async XLA Ops:
  0.0 1.2 %copy-start = (f32[1024,256]{1,0:T(8,128)S(1)}, f32[1024,256]{1,0:T(8,128)}, u32[]{:S(2)}) copy-start(f32[1024,256]{1,0:T(8,128)} %data_ref.1) | copy-start | bytes 3145732
  1.2 0.7 copy-start.1
  2.0 24.6 %collective-permute-start.6 = (f32[1032,256]{1,0:T(8,128)S(1)}, f32[1032,256]{1,0:T(8,128)S(1)}, u32[]{:S(2)}, u32[]{:S(2)}) collective-permute-start(f32[1032,256]{1,0:T(8,128)S(1)} %shard_map.37.refs_0_), channel_id=1, source_target_pairs={{4,7},{5,4},{6,5},{7,6},{8,11},{9,8},{10,9},{11,10},{28,31},{29,28... | collective-permute-start | bytes 3170312 | tf_op jit(solution)/shard_map/ppermute | solution.py:311
  4.1 38.5 %collective-permute-start.5 = (f32[1032,256]{1,0:T(8,128)S(1)}, f32[1032,256]{1,0:T(8,128)S(1)}, u32[]{:S(2)}, u32[]{:S(2)}) collective-permute-start(f32[1032,256]{1,0:T(8,128)S(1)} %shard_map.37.refs_0_), channel_id=1, source_target_pairs={{0,3},{1,0},{2,1},{3,2},{24,25},{25,26},{26,27},{27,24},{28,29},{2... | collective-permute-start | bytes 3170312 | tf_op jit(solution)/shard_map/ppermute | solution.py:311
  7.3 48.1 %collective-permute-start.1 = (f32[1032,256]{1,0:T(8,128)S(1)}, f32[1032,256]{1,0:T(8,128)}, u32[]{:S(2)}, u32[]{:S(2)}) collective-permute-start(f32[1032,256]{1,0:T(8,128)S(1)} %shard_map.37.refs_0_), channel_id=1, source_target_pairs={{8,0},{17,1},{26,2},{12,4},{21,5},{30,6},{16,8},{25,9},{2,10},{20,... | collective-permute-start | bytes 3170312 | tf_op jit(solution)/shard_map/ppermute | solution.py:311
  7.6 48.3 %collective-permute-start = (f32[1032,256]{1,0:T(8,128)S(1)}, f32[1032,256]{1,0:T(8,128)}, u32[]{:S(2)}, u32[]{:S(2)}) collective-permute-start(f32[1032,256]{1,0:T(8,128)S(1)} %shard_map.37.refs_0_), channel_id=1, source_target_pairs={{9,1},{18,2},{27,3},{13,5},{22,6},{31,7},{17,9},{26,10},{3,11},{21... | collective-permute-start | bytes 3170312 | tf_op jit(solution)/shard_map/ppermute | solution.py:311
  7.6 49.0 %collective-permute-start.2 = (f32[1032,256]{1,0:T(8,128)S(1)}, f32[1032,256]{1,0:T(8,128)}, u32[]{:S(2)}, u32[]{:S(2)}) collective-permute-start(f32[1032,256]{1,0:T(8,128)S(1)} %shard_map.37.refs_0_), channel_id=1, source_target_pairs={{16,4},{25,5},{2,6},{11,7},{24,12},{1,13},{10,14},{19,15},{0,20},{... | collective-permute-start | bytes 3170312 | tf_op jit(solution)/shard_map/ppermute | solution.py:311
  26.6 30.0 %collective-permute-start.8 = (f32[1032,256]{1,0:T(8,128)S(1)}, f32[1032,256]{1,0:T(8,128)}, u32[]{:S(2)}, u32[]{:S(2)}) collective-permute-start(f32[1032,256]{1,0:T(8,128)S(1)} %collective-permute-done.6.refs_7_), channel_id=1, source_target_pairs={{4,7},{5,4},{6,5},{7,6},{8,11},{9,8},{10,9},{11,10},{16,17},{17,18... | collective-permute-start | bytes 3170312 | tf_op jit(solution)/shard_map/ppermute | solution.py:311
  42.6 14.1 %collective-permute-start.7 = (f32[1032,256]{1,0:T(8,128)S(1)}, f32[1032,256]{1,0:T(8,128)}, u32[]{:S(2)}, u32[]{:S(2)}) collective-permute-start(f32[1032,256]{1,0:T(8,128)S(1)} %collective-permute-done.5.refs_6_), channel_id=1, source_target_pairs={{13,14},{14,15},{7,12}} | collective-permute-start | bytes 3170312 | tf_op jit(solution)/shard_map/ppermute | solution.py:311
  55.4 3.1 %collective-permute-start.4 = (f32[1032,256]{1,0:T(8,128)}, f32[1032,256]{1,0:T(8,128)}, u32[]{:S(2)}, u32[]{:S(2)}) collective-permute-start(f32[1032,256]{1,0:T(8,128)} %collective-permute-done.1.refs_2_), channel_id=1, source_target_pairs={{4,0},{5,1},{6,2},{7,3},{0,4},{1,5},{2,6},{3,7},{12,8},{13,9},{14,... | collective-permute-start | bytes 3170312 | tf_op jit(solution)/shard_map/ppermute | solution.py:311
  55.9 4.1 %collective-permute-start.3 = (f32[1032,256]{1,0:T(8,128)}, f32[1032,256]{1,0:T(8,128)}, u32[]{:S(2)}, u32[]{:S(2)}) collective-permute-start(f32[1032,256]{1,0:T(8,128)} %collective-permute-done.refs_1_), channel_id=1, source_target_pairs={{4,0},{5,1},{6,2},{7,3},{0,4},{1,5},{2,6},{3,7},{12,8},{13,9},{14,... | collective-permute-start | bytes 3170312 | tf_op jit(solution)/shard_map/ppermute | solution.py:311

commit v22 on v21

--- a/solution.py
+++ b/solution.py
@@ -10,7 +10,7 @@
 
 BS = 64
 STEPS = 4
-UNROLL = 12
+UNROLL = 10
 EXTRA = 8
 PARTS = 16
 

time: 70.2 us -> 69.9 us (level)
  no operation moved by 1% of the time
where the time goes in v22:
time: 69.9 us; the launch traced here: 69.8 us
  waiting for transfers between devices  47.9 us (69%)
  Pallas kernels  9.87 us (14%)
  starting transfers between devices  9.4 us (13%)
  local copies, waits for them, and re-layouts  2.59 us (4%)
    ppermute x9, waiting for transfers between devices, carry(): bufs.append(lax.ppermute(bufs[source], ('row', 'col'), flat))  47.9 us
    pallas_call x1, Pallas kernels, local(): pl.pallas_call(functools.partial(product_kernel, slots, n_row, ratio, rb,...  9.77 us
    ppermute x9, starting transfers between devices, carry(): bufs.append(lax.ppermute(bufs[source], ('row', 'col'), flat))  9.4 us
    unnamed x4, local copies, waits for them, and re-layouts  1.91 us
  transfers between devices with their start and end apart: 9, of which 5 were waited for; matrix products, arithmetic and copies ran while one was open for 1% of the time, Pallas kernels for 0%

profile of v22, /device:TPU:15, one launch (start us, length us, event | category | flops | bytes accessed | tf_op | source)
XLA Modules:
  0.0 69.8 jit_solution(7971827496209785879)
XLA Ops:
  0.0 0.0 copy-start
  0.0 1.2 %copy-done = f32[1024,256]{1,0:T(8,128)S(1)} copy-done((f32[1024,256]{1,0:T(8,128)S(1)}, f32[1024,256]{1,0:T(8,128)}, u32[]{:S(2)}) %copy-start) | copy-done | bytes 1048600
  1.2 0.7 copy-done.1
  1.9 0.1 shard_map.37.refs_0_
  2.0 2.1 %collective-permute-start.6 = (f32[1032,256]{1,0:T(8,128)S(1)}, f32[1032,256]{1,0:T(8,128)S(1)}, u32[]{:S(2)}, u32[]{:S(2)}) collective-permute-start(f32[1032,256]{1,0:T(8,128)S(1)} %shard_map.37.refs_0_), channel_id=1, source_target_pairs={{4,7},{5,4},{6,5},{7,6},{8,11},{9,8},{10,9},{11,10},{28,31},{29,28... | collective-permute-start | bytes 3170312 | tf_op jit(solution)/shard_map/ppermute | solution.py:311
  4.1 3.2 %collective-permute-start.5 = (f32[1032,256]{1,0:T(8,128)S(1)}, f32[1032,256]{1,0:T(8,128)S(1)}, u32[]{:S(2)}, u32[]{:S(2)}) collective-permute-start(f32[1032,256]{1,0:T(8,128)S(1)} %shard_map.37.refs_0_), channel_id=1, source_target_pairs={{0,3},{1,0},{2,1},{3,2},{24,25},{25,26},{26,27},{27,24},{28,29},{2... | collective-permute-start | bytes 3170312 | tf_op jit(solution)/shard_map/ppermute | solution.py:311
  7.3 0.3 collective-permute-start.1
  7.6 0.0 collective-permute-start
  7.6 0.0 collective-permute-start.2
  7.6 19.0 %collective-permute-done.6.refs_7_ = f32[1032,256]{1,0:T(8,128)S(1)} collective-permute-done((f32[1032,256]{1,0:T(8,128)S(1)}, f32[1032,256]{1,0:T(8,128)S(1)}, u32[]{:S(2)}, u32[]{:S(2)}) %collective-permute-start.6) | collective-permute-done | bytes 1056800 | tf_op jit(solution)/shard_map/ppermute | solution.py:311
  26.6 1.7 %collective-permute-start.8 = (f32[1032,256]{1,0:T(8,128)S(1)}, f32[1032,256]{1,0:T(8,128)}, u32[]{:S(2)}, u32[]{:S(2)}) collective-permute-start(f32[1032,256]{1,0:T(8,128)S(1)} %collective-permute-done.6.refs_7_), channel_id=1, source_target_pairs={{4,7},{5,4},{6,5},{7,6},{8,11},{9,8},{10,9},{11,10},{16,17},{17,18... | collective-permute-start | bytes 3170312 | tf_op jit(solution)/shard_map/ppermute | solution.py:311
  28.3 14.3 %collective-permute-done.5.refs_6_ = f32[1032,256]{1,0:T(8,128)S(1)} collective-permute-done((f32[1032,256]{1,0:T(8,128)S(1)}, f32[1032,256]{1,0:T(8,128)S(1)}, u32[]{:S(2)}, u32[]{:S(2)}) %collective-permute-start.5) | collective-permute-done | bytes 1056800 | tf_op jit(solution)/shard_map/ppermute | solution.py:311
  42.6 1.7 %collective-permute-start.7 = (f32[1032,256]{1,0:T(8,128)S(1)}, f32[1032,256]{1,0:T(8,128)}, u32[]{:S(2)}, u32[]{:S(2)}) collective-permute-start(f32[1032,256]{1,0:T(8,128)S(1)} %collective-permute-done.5.refs_6_), channel_id=1, source_target_pairs={{13,14},{14,15},{7,12}} | collective-permute-start | bytes 3170312 | tf_op jit(solution)/shard_map/ppermute | solution.py:311
  44.2 11.2 %collective-permute-done.1.refs_2_ = f32[1032,256]{1,0:T(8,128)} collective-permute-done((f32[1032,256]{1,0:T(8,128)S(1)}, f32[1032,256]{1,0:T(8,128)}, u32[]{:S(2)}, u32[]{:S(2)}) %collective-permute-start.1) | collective-permute-done | bytes 1056800 | tf_op jit(solution)/shard_map/ppermute | solution.py:311
  55.4 0.5 collective-permute-start.4
  55.9 0.0 collective-permute-done.refs_1_
  55.9 0.0 collective-permute-start.3
  55.9 0.7 dynamic-slice_bitcast_fusion.info_ref
  56.6 0.0 collective-permute-done.2.refs_3_
  56.6 0.0 collective-permute-done.8.refs_9_
  56.6 0.0 collective-permute-done.7.refs_8_
  56.6 1.9 %collective-permute-done.4.refs_5_ = f32[1032,256]{1,0:T(8,128)} collective-permute-done((f32[1032,256]{1,0:T(8,128)}, f32[1032,256]{1,0:T(8,128)}, u32[]{:S(2)}, u32[]{:S(2)}) %collective-permute-start.4) | collective-permute-done | bytes 1056800 | tf_op jit(solution)/shard_map/ppermute | solution.py:311
  58.5 1.5 %collective-permute-done.3.refs_4_ = f32[1032,256]{1,0:T(8,128)} collective-permute-done((f32[1032,256]{1,0:T(8,128)}, f32[1032,256]{1,0:T(8,128)}, u32[]{:S(2)}, u32[]{:S(2)}) %collective-permute-start.3) | collective-permute-done | bytes 1056800 | tf_op jit(solution)/shard_map/ppermute | solution.py:311
  60.0 9.8 %shard_map.38 = f32[1024,2048]{1,0:T(8,128)} custom-call(s32[10]{0:T(128)S(1)} %dynamic-slice_bitcast_fusion.info_ref, f32[1032,256]{1,0:T(8,128)S(1)} %shard_map.37.refs_0_, f32[1032,256]{1,0:T(8,128)} %collective-permute-done.refs_1_, f32[1032,256]{1,0:T(8,128)} %collective-permute-done.1.refs_2_, f32[1032,256]{1,0:T(8,128)} %collective-permute-done.2.refs_3_, ...), custom_call_target="tpu_custom_call" | custom-call | flops 1000000000 | bytes 20971520 | tf_op jit(solution)/shard_map/pallas_call | solution.py:319
  (1 shorter events, 0.0 us)
Async XLA Ops:
  0.0 1.2 %copy-start = (f32[1024,256]{1,0:T(8,128)S(1)}, f32[1024,256]{1,0:T(8,128)}, u32[]{:S(2)}) copy-start(f32[1024,256]{1,0:T(8,128)} %data_ref.1) | copy-start | bytes 3145732
  1.2 0.7 copy-start.1
  2.0 24.6 %collective-permute-start.6 = (f32[1032,256]{1,0:T(8,128)S(1)}, f32[1032,256]{1,0:T(8,128)S(1)}, u32[]{:S(2)}, u32[]{:S(2)}) collective-permute-start(f32[1032,256]{1,0:T(8,128)S(1)} %shard_map.37.refs_0_), channel_id=1, source_target_pairs={{4,7},{5,4},{6,5},{7,6},{8,11},{9,8},{10,9},{11,10},{28,31},{29,28... | collective-permute-start | bytes 3170312 | tf_op jit(solution)/shard_map/ppermute | solution.py:311
  4.1 38.5 %collective-permute-start.5 = (f32[1032,256]{1,0:T(8,128)S(1)}, f32[1032,256]{1,0:T(8,128)S(1)}, u32[]{:S(2)}, u32[]{:S(2)}) collective-permute-start(f32[1032,256]{1,0:T(8,128)S(1)} %shard_map.37.refs_0_), channel_id=1, source_target_pairs={{0,3},{1,0},{2,1},{3,2},{24,25},{25,26},{26,27},{27,24},{28,29},{2... | collective-permute-start | bytes 3170312 | tf_op jit(solution)/shard_map/ppermute | solution.py:311
  7.3 48.1 %collective-permute-start.1 = (f32[1032,256]{1,0:T(8,128)S(1)}, f32[1032,256]{1,0:T(8,128)}, u32[]{:S(2)}, u32[]{:S(2)}) collective-permute-start(f32[1032,256]{1,0:T(8,128)S(1)} %shard_map.37.refs_0_), channel_id=1, source_target_pairs={{8,0},{17,1},{26,2},{12,4},{21,5},{30,6},{16,8},{25,9},{2,10},{20,... | collective-permute-start | bytes 3170312 | tf_op jit(solution)/shard_map/ppermute | solution.py:311
  7.6 48.3 %collective-permute-start = (f32[1032,256]{1,0:T(8,128)S(1)}, f32[1032,256]{1,0:T(8,128)}, u32[]{:S(2)}, u32[]{:S(2)}) collective-permute-start(f32[1032,256]{1,0:T(8,128)S(1)} %shard_map.37.refs_0_), channel_id=1, source_target_pairs={{9,1},{18,2},{27,3},{13,5},{22,6},{31,7},{17,9},{26,10},{3,11},{21... | collective-permute-start | bytes 3170312 | tf_op jit(solution)/shard_map/ppermute | solution.py:311
  7.6 49.0 %collective-permute-start.2 = (f32[1032,256]{1,0:T(8,128)S(1)}, f32[1032,256]{1,0:T(8,128)}, u32[]{:S(2)}, u32[]{:S(2)}) collective-permute-start(f32[1032,256]{1,0:T(8,128)S(1)} %shard_map.37.refs_0_), channel_id=1, source_target_pairs={{16,4},{25,5},{2,6},{11,7},{24,12},{1,13},{10,14},{19,15},{0,20},{... | collective-permute-start | bytes 3170312 | tf_op jit(solution)/shard_map/ppermute | solution.py:311
  26.6 30.0 %collective-permute-start.8 = (f32[1032,256]{1,0:T(8,128)S(1)}, f32[1032,256]{1,0:T(8,128)}, u32[]{:S(2)}, u32[]{:S(2)}) collective-permute-start(f32[1032,256]{1,0:T(8,128)S(1)} %collective-permute-done.6.refs_7_), channel_id=1, source_target_pairs={{4,7},{5,4},{6,5},{7,6},{8,11},{9,8},{10,9},{11,10},{16,17},{17,18... | collective-permute-start | bytes 3170312 | tf_op jit(solution)/shard_map/ppermute | solution.py:311
  42.6 14.1 %collective-permute-start.7 = (f32[1032,256]{1,0:T(8,128)S(1)}, f32[1032,256]{1,0:T(8,128)}, u32[]{:S(2)}, u32[]{:S(2)}) collective-permute-start(f32[1032,256]{1,0:T(8,128)S(1)} %collective-permute-done.5.refs_6_), channel_id=1, source_target_pairs={{13,14},{14,15},{7,12}} | collective-permute-start | bytes 3170312 | tf_op jit(solution)/shard_map/ppermute | solution.py:311
  55.4 3.1 %collective-permute-start.4 = (f32[1032,256]{1,0:T(8,128)}, f32[1032,256]{1,0:T(8,128)}, u32[]{:S(2)}, u32[]{:S(2)}) collective-permute-start(f32[1032,256]{1,0:T(8,128)} %collective-permute-done.1.refs_2_), channel_id=1, source_target_pairs={{4,0},{5,1},{6,2},{7,3},{0,4},{1,5},{2,6},{3,7},{12,8},{13,9},{14,... | collective-permute-start | bytes 3170312 | tf_op jit(solution)/shard_map/ppermute | solution.py:311
  55.9 4.1 %collective-permute-start.3 = (f32[1032,256]{1,0:T(8,128)}, f32[1032,256]{1,0:T(8,128)}, u32[]{:S(2)}, u32[]{:S(2)}) collective-permute-start(f32[1032,256]{1,0:T(8,128)} %collective-permute-done.refs_1_), channel_id=1, source_target_pairs={{4,0},{5,1},{6,2},{7,3},{0,4},{1,5},{2,6},{3,7},{12,8},{13,9},{14,... | collective-permute-start | bytes 3170312 | tf_op jit(solution)/shard_map/ppermute | solution.py:311
